TPU v7x, 32 devices: a whole 2x2x4 slice. The times are simulated.
32 devices in a mesh: prow: 4 (over z), pcol: 8 (over y, x, core).
Axes of the slice: x: 2, y: 2, z: 4, core: 2. Of those that a mesh axis runs over, the one named last changes fastest.
Arguments:
- inverse_tiles: float32 [8192, 8192], P('pcol', 'prow'), may hold values from -6 to 6
- factor: float32 [2, 8192, 512], P(None, ('pcol', 'prow')), may hold values from -0.09375 to 0.09375
- link_factor: float32 [1, 512, 512], replicated, may hold values from -0.25 to 0.25
- diag_inverse: float32 [2, 512, 512], replicated, may hold values from -3 to 3
- ancestors: int32 [2, 8], replicated, may hold values from 0 to 15, as said below
Outputs:
- offdiag: float32 [2, 8192, 512], P(None, ('pcol', 'prow'))
- diag: float32 [2, 512, 512], P(None, 'pcol')
- link_blocks: float32 [1, 512, 512], P(None, 'pcol')
Inputs may be any that keep to these rules, and one draw needn't show every extreme that they name: `ancestors`: row k lists 8 distinct stored block rows; every row lists block 15, and row 0 lists block 0.
All inputs are finite; a program needn't handle non-finite values.
Results may differ from a plain program's by a relative error of at most 0.0001.
Values sent between devices are 32-bit elements; how exact they have to be, the bound alone decides.
No kernel may reach another device: no remote copies, remote signals or barrier semaphores. Data moves between devices by JAX's collectives and lax.ppermute only.
A program may use at most 64 MiB of HBM per device.

v0:
```python
import jax
import jax.numpy as jnp
from jax import lax
from jax.sharding import PartitionSpec as P


def broadcast(value, axis, source):
    kept = jnp.where(lax.axis_index(axis) == source, value, 0).astype(value.dtype)
    return lax.psum(kept, axis)


def product(left_part, right_part):
    return jnp.dot(
        left_part, right_part, precision=lax.Precision.HIGHEST, preferred_element_type=jnp.float32
    )


def gather_columns(row_factor, ratio, prow_index, concat_dim):
    pieces = []
    for member in range(ratio):
        pieces.append(broadcast(row_factor, "pcol", prow_index * ratio + member))
    return jnp.concatenate(pieces, axis=concat_dim)


def body(inverse_tiles, factor, link_factor, diag_inverse, ancestors):
    row_count, col_count = inverse_tiles.shape
    nsuper, unit_rows, columns = factor.shape
    prow_count = lax.axis_size("prow")
    pcol_count = lax.axis_size("pcol")
    ratio = col_count // row_count
    prow_index = lax.axis_index("prow")
    pcol_index = lax.axis_index("pcol")
    first_row = (pcol_index * prow_count + prow_index) * unit_rows
    block_ids = (first_row + lax.iota(jnp.int32, unit_rows)) // columns
    selected = jnp.any(block_ids[None, :, None] == ancestors[:, None, :], axis=2).astype(
        jnp.float32
    )
    unit_factor = factor * selected[:, :, None]
    slice_rows = columns // pcol_count
    slice_start = pcol_index * slice_rows
    offdiag_list = []
    diag_list = []
    link_list = []
    prior_offdiag = None
    prior_diag = None
    for number in range(nsuper):
        row_factor = lax.all_gather(unit_factor[number], "prow", axis=0, tiled=True)
        col_factor = gather_columns(row_factor, ratio, prow_index, 0)

        def partial_term(begin_row, row_total, col_factor=col_factor):
            return product(inverse_tiles, col_factor)

        summed = lax.psum_scatter(
            partial_term(jnp.int32(0), lax.axis_size("prow") * unit_rows),
            "prow",
            scatter_dimension=0,
            tiled=True,
        )
        local_factor = unit_factor[number]
        gram_part = product(local_factor.T, summed)
        keep_rows = selected[number][:, None]
        if number == 0:
            gram_sum = lax.psum(gram_part, ("prow", "pcol"))
            result = -(keep_rows * summed)
            diag_block = diag_inverse[0] + gram_sum
        else:
            link_block = link_factor[number - 1]
            cross_part = product(prior_offdiag.T, local_factor)
            gram_sum, cross_sum = lax.psum((gram_part, cross_part), ("prow", "pcol"))
            result = -(keep_rows * (summed + product(prior_offdiag, link_block)))
            link_out = -(cross_sum + product(prior_diag, link_block))
            diag_block = (
                diag_inverse[number]
                + gram_sum
                + product(cross_sum.T, link_block)
                - product(link_block.T, link_out)
            )
            link_list.append(lax.dynamic_slice_in_dim(link_out, slice_start, slice_rows, 0))
        offdiag_list.append(result)
        diag_list.append(lax.dynamic_slice_in_dim(diag_block, slice_start, slice_rows, 0))
        prior_offdiag = result
        prior_diag = diag_block
    return (jnp.stack(offdiag_list), jnp.stack(diag_list), jnp.stack(link_list))


def solution(mesh):
    in_specs = (P("pcol", "prow"), P(None, ("pcol", "prow"), None), P(), P(), P())
    out_specs = (P(None, ("pcol", "prow"), None), P(None, "pcol", None), P(None, "pcol", None))
    return jax.shard_map(body, mesh=mesh, in_specs=in_specs, out_specs=out_specs, check_vma=False)
```

profile of v0, /device:TPU:0, one launch (start us, length us, event | category | flops | bytes accessed | tf_op | source)
XLA Modules:
  0.0 517.7 jit_solution(16546581840661393173)
XLA Ops:
  7.2 0.8 compare_reduce_fusion
  8.1 1.4 broadcast_multiply_fusion
  9.5 1.1 fusion.38
  10.6 0.0 all-gather.7.cloned.1.call-start
  10.6 0.7 all-gather.7.cloned.1.call-update
  11.3 0.0 all-reduce.7.cloned.1.call-start
  11.4 48.0 %all-gather.5.cloned.1.call-done = f32[1,1024,512]{2,1,0:T(8,128)} async-done(((f32[1,256,512]{2,1,0:T(8,128)}), f32[1,1024,512]{2,1,0:T(8,128)}) %all-gather.5.cloned.1.call-update) | async-done | bytes 2097168 | tf_op jit(solution)/shard_map/all_gather | solution.py:47
  59.4 4.2 select_bitcast_fusion.3
  63.6 42.0 %all-gather.7.cloned.1.call-done = f32[1,1024,512]{2,1,0:T(8,128)} async-done(((f32[1,256,512]{2,1,0:T(8,128)}), f32[1,1024,512]{2,1,0:T(8,128)}) %all-gather.7.cloned.1.call-update) | async-done | bytes 2097168 | tf_op jit(solution)/shard_map/all_gather | solution.py:47
  105.6 4.2 select_bitcast_fusion.1
  109.8 0.0 reduce-scatter.3.cloned.1.call-start
  109.8 126.3 %all-reduce.7.cloned.1.call-done = (f32[1024,512]{1,0:T(8,128)}, f32[1024,512]{1,0:T(8,128)}, f32[1024,512]{1,0:T(8,128)}, f32[1024,512]{1,0:T(8,128)}) async-done(((f32[1024,512]{1,0:T(8,128)}, f32[1024,512]{1,0:T(8,128)}, f32[1024,512]{1,0:T(8,128)}, f32[1024,512]{1,0:T(8,128)}), (f32[1024,512]{1,0:T(8,128)}, f32[1024,512]{1,0:T(8,128)}, f32[1024,512]{1,0:T(8,128)}, ...) | async-done | bytes 8388624 | tf_op jit(solution)/shard_map/psum | solution.py:9
  236.2 30.4 %fusion.11 = f32[1024,512]{0,1:T(8,128)} fusion(f32[1024,2048]{1,0:T(8,128)} %param.5, f32[1024,512]{1,0:T(8,128)} %get-tuple-element.14, f32[1024,512]{1,0:T(8,128)} %get-tuple-element.15), kind=kOutput, calls=%fused_computation.13 | convolution fusion | flops 12885950464 | bytes 14680064 | tf_op jit(solution)/shard_map/dot_general | solution.py:13
  266.6 0.2 reduce-scatter.5.cloned.1.call-start
  266.8 30.4 %fusion.8 = f32[1024,512]{0,1:T(8,128)} fusion(f32[1024,2048]{1,0:T(8,128)} %param.5, f32[1024,512]{1,0:T(8,128)} %get-tuple-element.12, f32[1024,512]{1,0:T(8,128)} %get-tuple-element.13), kind=kOutput, calls=%fused_computation.12 | convolution fusion | flops 12885950464 | bytes 14680064 | tf_op jit(solution)/shard_map/dot_general | solution.py:13
  297.2 0.3 all-reduce.5.cloned.1.call-start
  297.5 13.3 %reduce-scatter.3.cloned.1.call-done = f32[256,512]{0,1:T(8,128)} async-done(((f32[1024,512]{0,1:T(8,128)}), f32[256,512]{0,1:T(8,128)}) %reduce-scatter.3.cloned.1.call-update) | async-done | bytes 524304 | tf_op jit(solution)/shard_map/reduce_scatter | solution.py:53
  310.8 3.9 fusion.27
  314.7 2.0 fusion.25
  316.7 39.4 %reduce-scatter.5.cloned.1.call-done = f32[256,512]{0,1:T(8,128)} async-done(((f32[1024,512]{0,1:T(8,128)}), f32[256,512]{0,1:T(8,128)}) %reduce-scatter.5.cloned.1.call-update) | async-done | bytes 524304 | tf_op jit(solution)/shard_map/reduce_scatter | solution.py:53
  356.1 3.9 fusion.23
  360.1 2.3 slice_bitcast_fusion
  362.4 1.8 fusion.17
  364.3 0.1 pad_maximum_fusion
  364.4 1.3 copy.11
  365.7 135.3 %all-reduce.5.cloned.1.call-done = (f32[512,512]{1,0:T(8,128)}, f32[512,512]{1,0:T(8,128)}, f32[512,512]{1,0:T(8,128)}) async-done(((f32[512,512]{1,0:T(8,128)}, f32[512,512]{1,0:T(8,128)}, f32[512,512]{1,0:T(8,128)}), (f32[512,512]{1,0:T(8,128)}, f32[512,512]{1,0:T(8,128)}, f32[512,512]{1,0:T(8,128)})) %all-reduce.5.cloned.1.call-update) | async-done | bytes 3145744 | tf_op jit(solution)/shard_map/psum | solution.py:69
  501.0 1.8 bitcast_add_fusion
  502.8 1.8 fusion.20
  504.7 1.9 fusion.14
  506.5 1.9 convolution_bitcast_fusion
  508.4 1.7 fusion.32
  510.1 0.7 pad_maximum_fusion.1
  (19 shorter events, 0.2 us)
Async XLA Ops:
  7.2 355.2 %copy-start = (f32[1,512,512]{2,1,0:T(8,128)S(1)}, f32[1,512,512]{2,1,0:T(8,128)}, u32[]{:S(2)}) copy-start(f32[1,512,512]{2,1,0:T(8,128)} %param.7) | copy-start | bytes 3145732
  7.2 52.2 %all-gather.5.cloned.1.call-start = ((), (), s32[]{:S(2)}) async-start(), calls=%async_computation.4 | async-start | bytes 2621440 | tf_op jit(solution)/shard_map/all_gather | solution.py:47
  10.6 95.0 %all-gather.7.cloned.1.call-start = ((), (), s32[]{:S(2)}) async-start(), calls=%async_computation.5 | async-start | bytes 2621440 | tf_op jit(solution)/shard_map/all_gather | solution.py:47
  11.3 224.9 %all-reduce.7.cloned.1.call-start = ((), (), s32[]{:S(2)}) async-start(), calls=%async_computation.7 | async-start | bytes 16777216 | tf_op jit(solution)/shard_map/psum | solution.py:9
  109.8 201.0 %reduce-scatter.3.cloned.1.call-start = ((), (), s32[]{:S(2)}) async-start(), calls=%async_computation.2 | async-start | bytes 2621440 | tf_op jit(solution)/shard_map/reduce_scatter | solution.py:53
  266.6 89.6 %reduce-scatter.5.cloned.1.call-start = ((), (), s32[]{:S(2)}) async-start(), calls=%async_computation.3 | async-start | bytes 2621440 | tf_op jit(solution)/shard_map/reduce_scatter | solution.py:53
  297.2 203.7 %all-reduce.5.cloned.1.call-start = ((), (), s32[]{:S(2)}) async-start(), calls=%async_computation.6 | async-start | bytes 6291456 | tf_op jit(solution)/shard_map/psum | solution.py:69
  310.8 3.9 copy-start.1
  360.0 2.4 copy-start.3
  501.0 1.9 copy-start.2
Sparse Core Ops, SparseCore 0:
  10.7 48.6 all-gather.4
  60.9 44.6 all-gather.6
  109.9 126.2 all-reduce.6
  266.7 44.0 reduce-scatter.2
  312.9 43.1 reduce-scatter.4
  362.8 138.1 all-reduce.4
where the time goes:
time: 518 us
  waiting for transfers between devices  405 us (78%)
  matrix products  78 us (15%)
  other arithmetic  14.9 us (3%)
  between operations  14.2 us (3%)
    psum x1, waiting for transfers between devices, body(): gram_sum, cross_sum = lax.psum((gram_part, cross_part), ('prow', 'pcol'))  135 us
    psum x1, waiting for transfers between devices, broadcast(): return lax.psum(kept, axis)  126 us
    all_gather x2, waiting for transfers between devices, body(): row_factor = lax.all_gather(unit_factor[number], 'prow', axis=0, tiled=True)  90 us
    dot_general x9, matrix products, product(): jnp.dot(left_part, right_part, precision=lax.Precision.HIGHEST, preferred...  78 us
    reduce_scatter x2, waiting for transfers between devices, body(): lax.psum_scatter(partial_term(jnp.int32(0), lax.axis_size('prow') * unit_...  52.7 us
  transfers between devices with their start and end apart: 6, of which 6 were waited for; matrix products, arithmetic and copies ran while one was open for 9% of the time, Pallas kernels for 0%

commit v1 on v0

v1 whole, which is shorter than its diff:
```python
import functools

import jax
import jax.numpy as jnp
import numpy as np
from jax import lax
from jax.experimental import pallas as pl
from jax.experimental.pallas import tpu as pltpu
from jax.sharding import PartitionSpec as P

BOTH = ("prow", "pcol")
VMEM_LIMIT = 48 * 1024 * 1024
LANES = 128


def product(left_part, right_part):
    return jnp.dot(
        left_part, right_part, precision=lax.Precision.HIGH, preferred_element_type=jnp.float32
    )


def halves(value):
    high = value.astype(jnp.bfloat16)
    low = (value - high.astype(jnp.float32)).astype(jnp.bfloat16)
    return high, low


def flip(value, axis, bit):
    return lax.ppermute(value, axis, [(i, i ^ bit) for i in range(lax.axis_size(axis))])


def spread_kernel(meta, factor_ref, *out_refs):
    nsuper = factor_ref.shape[0]
    count = len(out_refs) // nsuper
    width = out_refs[0].shape[1]
    for number in range(nsuper):
        for r in range(count):
            start = pl.multiple_of((meta[1] ^ r) * width, width)
            out_refs[number * count + r][...] = factor_ref[number, :, pl.ds(start, width)]


def spread(meta, factor, count):
    nsuper, unit_rows, columns = factor.shape
    width = columns // count
    if width % LANES:
        pieces = []
        for number in range(nsuper):
            for r in range(count):
                start = (meta[1] ^ r) * width
                pieces.append(lax.dynamic_slice_in_dim(factor[number], start, width, 1))
        return pieces
    return pl.pallas_call(
        spread_kernel,
        grid_spec=pltpu.PrefetchScalarGridSpec(
            num_scalar_prefetch=1,
            grid=(1,),
            in_specs=[pl.BlockSpec(factor.shape, lambda i, m: (0, 0, 0))],
            out_specs=[pl.BlockSpec((unit_rows, width), lambda i, m: (0, 0))] * (nsuper * count),
        ),
        out_shape=[jax.ShapeDtypeStruct((unit_rows, width), factor.dtype)] * (nsuper * count),
        compiler_params=pltpu.CompilerParams(vmem_limit_bytes=VMEM_LIMIT),
        cost_estimate=pl.CostEstimate(
            flops=0, bytes_accessed=2 * factor.size * 4, transcendentals=0
        ),
        name="spread",
    )(meta, factor)


def split_kernel(tile_ref, high_ref, low_ref):
    high_ref[...], low_ref[...] = halves(tile_ref[...])


def split(tiles, steps):
    rows, cols = tiles.shape
    block = pl.BlockSpec((rows // steps, cols), lambda i: (i, 0))
    shape = jax.ShapeDtypeStruct((rows, cols), jnp.bfloat16)
    return pl.pallas_call(
        split_kernel,
        grid=(steps,),
        in_specs=[block],
        out_specs=[block, block],
        out_shape=[shape, shape],
        compiler_params=pltpu.CompilerParams(vmem_limit_bytes=VMEM_LIMIT),
        cost_estimate=pl.CostEstimate(flops=0, bytes_accessed=8 * rows * cols, transcendentals=0),
        name="split",
    )(tiles)


def partial_kernel(places, ratio, count, meta, high_ref, low_ref, *refs):
    piece_refs = refs[: len(places)]
    out_ref, right_high, right_low = refs[len(places) :]
    columns = out_ref.shape[1]
    blocks = high_ref.shape[1] // columns
    step = pl.program_id(0)

    @pl.when(step == 0)
    def _assemble():
        for ref, place in zip(piece_refs, places):
            if place is None:
                right_high[...], right_low[...] = halves(ref[...])
                continue
            offset, first = place
            unit_rows, width = ref.shape[1:]
            owner = meta[0] ^ offset
            column = owner // ratio
            lane = pl.multiple_of(column * width, width)
            for r in range(ref.shape[0]):
                unit = (owner % ratio) * count + (column ^ (first + r))
                rows = pl.ds(pl.multiple_of(unit * unit_rows, unit_rows), unit_rows)
                high, low = halves(ref[r])
                right_high[rows, pl.ds(lane, width)] = high
                right_low[rows, pl.ds(lane, width)] = low

    out_ref[...] = jnp.zeros_like(out_ref)

    @pl.when(meta[3 + blocks + step] != 0)
    def _multiply():
        def add(number, carry):
            span = pl.ds(pl.multiple_of(meta[3 + number] * columns, columns), columns)
            high, low = high_ref[:, span], low_ref[:, span]
            right = right_high[span, :]
            dot = functools.partial(jnp.dot, preferred_element_type=jnp.float32)
            out_ref[...] += dot(high, right) + (dot(high, right_low[span, :]) + dot(low, right))
            return carry

        lax.fori_loop(0, meta[2], add, 0)


def partial_product(meta, high, low, pieces, places, ratio, count, columns):
    rows, cols = high.shape
    chunk = rows // count
    tile = pl.BlockSpec((chunk, cols), lambda i, m: (i, 0))
    whole = [
        pl.BlockSpec(piece.shape, functools.partial(lambda n, i, m: (0,) * n, piece.ndim))
        for piece in pieces
    ]
    return pl.pallas_call(
        functools.partial(partial_kernel, places, ratio, count),
        grid_spec=pltpu.PrefetchScalarGridSpec(
            num_scalar_prefetch=1,
            grid=(count,),
            in_specs=[tile, tile] + whole,
            out_specs=pl.BlockSpec((chunk, columns), lambda i, m: (i, 0)),
            scratch_shapes=[pltpu.VMEM((cols, columns), jnp.bfloat16)] * 2,
        ),
        out_shape=jax.ShapeDtypeStruct((rows, columns), jnp.float32),
        compiler_params=pltpu.CompilerParams(vmem_limit_bytes=VMEM_LIMIT),
        cost_estimate=pl.CostEstimate(
            flops=6 * rows * cols * columns,
            bytes_accessed=4 * (rows * cols + cols * columns + rows * columns),
            transcendentals=0,
        ),
        name="partial_product",
    )(meta, high, low, *pieces)


def to_plane(sends, count, ratio):
    pcol_count = count * ratio
    received = []
    for r, piece in enumerate(sends):
        perm = []
        for z in range(count):
            for c in range(count):
                for k in range(ratio):
                    source = z * pcol_count + c * ratio + k
                    perm.append((source, c * pcol_count + (z ^ r) * ratio + k))
        received.append(lax.ppermute(piece, BOTH, perm))
    return jnp.stack(received)


def gather_plane(own, pcol_count):
    parts = own.shape[0]
    found = {0: [(own, 0)]}
    even = [o for o in range(2, pcol_count, 2)]
    for offset in sorted(even, key=lambda o: bin(o).count("1")):
        bits = [1 << b for b in range(1, pcol_count.bit_length()) if offset >> b & 1]
        if len(bits) == 2 and parts % 2 == 0:
            half = parts // 2
            found[offset] = [
                (flip(found[offset ^ bit][0][0][i * half : (i + 1) * half], "pcol", bit), i * half)
                for i, bit in enumerate(bits)
            ]
        else:
            found[offset] = [
                (flip(piece, "pcol", bits[0]), first) for piece, first in found[offset ^ bits[0]]
            ]
    for offset in [0] + even:
        if pcol_count > 1:
            found[offset ^ 1] = [(flip(piece, "pcol", 1), first) for piece, first in found[offset]]
    return [(piece, o, first) for o in sorted(found) for piece, first in found[o]]


def gather_whole(own, count, ratio):
    _, unit_rows, width = own.shape
    gathered = lax.all_gather(own, "pcol", axis=0)
    column = np.arange(count)[None, None, :]
    owner = column * ratio + np.arange(ratio)[:, None, None]
    part = np.broadcast_to(column ^ np.arange(count)[None, :, None], (ratio, count, count))
    rows = jnp.transpose(gathered[np.broadcast_to(owner, part.shape), part], (0, 1, 3, 2, 4))
    return rows.reshape(ratio * count * unit_rows, count * width)


def sum_over_line(partial, count, z):
    rows = partial.shape[0] // count

    def chunk(index):
        start = jnp.clip(index, 0, count - 1) * rows
        return lax.dynamic_slice_in_dim(partial, start, rows, 0)

    up = down = None
    for t in range(1, count):
        up_send, down_send = chunk(z + count - t), chunk(z + t - count)
        if up is not None:
            up_send, down_send = up_send + up, down_send + down
        up = lax.ppermute(up_send, "prow", [(i, i + 1) for i in range(min(t, count - 1))])
        down = lax.ppermute(
            down_send, "prow", [(i, i - 1) for i in range(max(count - t, 1), count)]
        )
    mine = chunk(z)
    return mine if up is None else mine + up + down


def sum_rows(matrix, pcol_count, count, pcol_index):
    rows, columns = matrix.shape
    if pcol_count > 1:
        paired = matrix.reshape(pcol_count // 2, 2, rows // pcol_count, columns)
        core = pcol_index % 2
        send = lax.dynamic_index_in_dim(paired, 1 - core, 1, keepdims=False)
        mine = lax.dynamic_index_in_dim(paired, core, 1, keepdims=False) + flip(send, "pcol", 1)
        chip = pcol_index // 2
        matrix = lax.dynamic_index_in_dim(mine, chip, 0, keepdims=False)
        for o in range(1, pcol_count // 2):
            send = lax.dynamic_index_in_dim(mine, chip ^ o, 0, keepdims=False)
            matrix = matrix + flip(send, "pcol", 2 * o)
    bit = 1
    while bit < count:
        matrix = matrix + flip(matrix, "prow", bit)
        bit *= 2
    return matrix


def body(inverse_tiles, factor, link_factor, diag_inverse, ancestors):
    row_count, col_count = inverse_tiles.shape
    nsuper, unit_rows, columns = factor.shape
    count = lax.axis_size("prow")
    pcol_count = lax.axis_size("pcol")
    ratio = col_count // row_count
    z = lax.axis_index("prow")
    pcol_index = lax.axis_index("pcol")
    slice_rows = columns // pcol_count
    slice_start = pcol_index * slice_rows
    width = columns // count

    listed = jnp.any(
        lax.iota(jnp.int32, count * col_count // columns)[None, :, None] == ancestors[:, None, :],
        axis=2,
    )
    unit_ids = (pcol_index * count + lax.iota(jnp.int32, count)) * unit_rows // columns
    chunk_kept = listed[:, unit_ids]
    keep = chunk_kept[:, z][:, None, None]
    blocks = col_count // columns
    block_kept = lax.dynamic_slice_in_dim(listed, z * blocks, blocks, 1)
    ids = lax.iota(jnp.int32, blocks)
    rank = jnp.cumsum(block_kept.astype(jnp.int32), axis=1) - 1
    taken = (rank[:, None, :] == ids[None, :, None]) & block_kept[:, None, :]
    order = jnp.sum(jnp.where(taken, ids[None, None, :], 0), axis=2)
    place = jnp.stack([pcol_index, z]).astype(jnp.int32)
    metas = [
        jnp.concatenate(
            [
                place,
                jnp.sum(block_kept[number], dtype=jnp.int32)[None],
                order[number].astype(jnp.int32),
                chunk_kept[number].astype(jnp.int32),
            ]
        )
        for number in range(nsuper)
    ]

    sends = spread(place, factor, count)
    high, low = split(inverse_tiles, count)
    local = jnp.where(keep, factor, 0.0)

    partials = []
    for number in range(nsuper):
        own = to_plane(sends[number * count : (number + 1) * count], count, ratio)
        if width % LANES:
            pieces, places = [gather_whole(own, count, ratio)], [None]
        else:
            found = gather_plane(own, pcol_count)
            pieces = [piece for piece, _, _ in found]
            places = [(offset, first) for _, offset, first in found]
        partials.append(
            partial_product(metas[number], high, low, pieces, places, ratio, count, columns)
        )

    offdiag_list, diag_list, link_list = [], [], []
    prior_offdiag = prior_part = prior_base = None
    for number in range(nsuper):
        summed = sum_over_line(partials[number], count, z)
        gram_part = product(local[number].T, summed)
        if number == 0:
            result = -jnp.where(keep[number], summed, 0.0)
            part = gram_part
            base = diag_inverse[0]
        else:
            link_block = link_factor[number - 1]
            result = -jnp.where(keep[number], summed + product(prior_offdiag, link_block), 0.0)
            cross_part = product(prior_offdiag.T, local[number])
            link_part = cross_part + product(prior_part, link_block)
            rest = product(cross_part.T, link_block) + product(link_block.T, link_part)
            part = gram_part + rest
            base_link = product(prior_base, link_block)
            base = diag_inverse[number] + product(link_block.T, base_link)
            link_sum = sum_rows(link_part, pcol_count, count, pcol_index)
            link_list.append(
                -(link_sum + lax.dynamic_slice_in_dim(base_link, slice_start, slice_rows, 0))
            )
        diag_sum = sum_rows(part, pcol_count, count, pcol_index)
        diag_list.append(diag_sum + lax.dynamic_slice_in_dim(base, slice_start, slice_rows, 0))
        offdiag_list.append(result)
        prior_offdiag, prior_part, prior_base = result, part, base
    return (jnp.stack(offdiag_list), jnp.stack(diag_list), jnp.stack(link_list))


def solution(mesh):
    in_specs = (P("pcol", "prow"), P(None, ("pcol", "prow"), None), P(), P(), P())
    out_specs = (P(None, ("pcol", "prow"), None), P(None, "pcol", None), P(None, "pcol", None))
    return jax.shard_map(body, mesh=mesh, in_specs=in_specs, out_specs=out_specs, check_vma=False)
```

time: 518 us -> 290 us (0.56)
  waiting for transfers between devices: 405 us -> 58 us
  starting transfers between devices: 0.65 us -> 162 us
  matrix products: 78 us -> 10.3 us
  Pallas kernels: 0 us -> 24.9 us
  local copies, waits for them, and re-layouts: 4.78 us -> 17.9 us
  between operations: 14.2 us -> 1.35 us
    psum x2 -> x0, waiting for transfers between devices: 262 us -> none  [the longest x1 135 us: body(): gram_sum, cross_sum = lax.psum((gram_part, cross_part), ('prow', 'pcol'))]
    ppermute x0 -> x56, starting transfers between devices: none -> 162 us  [the longest x36 80.9 us: flip(): lax.ppermute(value, axis, [(i, i ^ bit) for i in range(lax.axis_size(axis...]
    all_gather x2 -> x0, waiting for transfers between devices: 90 us -> none  [body(): row_factor = lax.all_gather(unit_factor[number], 'prow', axis=0, tiled=True)]
    dot_general x9, matrix products: 78 us -> 10.3 us  [product(): jnp.dot(left_part, right_part, precision=lax.Precision.HIGH, preferred_el...]
    ppermute x0 -> x56, waiting for transfers between devices: none -> 58 us  [the longest x36 23.5 us: flip(): lax.ppermute(value, axis, [(i, i ^ bit) for i in range(lax.axis_size(axis...]
    reduce_scatter x2 -> x0, waiting for transfers between devices: 52.7 us -> none  [body(): lax.psum_scatter(partial_term(jnp.int32(0), lax.axis_size('prow') * unit_...]
    pallas_call x0 -> x4, Pallas kernels: none -> 24.9 us  [the longest x2 18.2 us: partial_product(): pl.pallas_call(functools.partial(partial_kernel, places, ratio, count), g...]
    select_n x3 -> x2, other arithmetic: 8.39 us -> 0.21 us  [the longest x1 0.19 us: body(): local = jnp.where(keep, factor, 0.0)]
  transfers between devices with their start and end apart: 6 -> 56, of which waited for: 6 -> 13; matrix products, arithmetic and copies ran while one was open for 9% -> 12% of each run, Pallas kernels for 0% -> 8%
where the time goes in v1:
time: 290 us
  starting transfers between devices  162 us (56%)
  waiting for transfers between devices  58 us (20%)
  Pallas kernels  24.9 us (9%)
  local copies, waits for them, and re-layouts  17.9 us (6%)
  other arithmetic  15 us (5%)
  matrix products  10.3 us (4%)
    ppermute x36, starting transfers between devices, flip(): lax.ppermute(value, axis, [(i, i ^ bit) for i in range(lax.axis_size(axis...  80.9 us
    ppermute x8, starting transfers between devices, to_plane(): received.append(lax.ppermute(piece, BOTH, perm))  44.5 us
    ppermute x6, starting transfers between devices, sum_over_line(): lax.ppermute(up_send, 'prow', [(i, i + 1) for i in range(min(t, count - 1...  31.3 us
    ppermute x36, waiting for transfers between devices, flip(): lax.ppermute(value, axis, [(i, i ^ bit) for i in range(lax.axis_size(axis...  23.5 us
    pallas_call x2, Pallas kernels, partial_product(): pl.pallas_call(functools.partial(partial_kernel, places, ratio, count), g...  18.2 us
    ppermute x6, waiting for transfers between devices, sum_over_line(): lax.ppermute(up_send, 'prow', [(i, i + 1) for i in range(min(t, count - 1...  16.9 us
    dot_general x9, matrix products, product(): jnp.dot(left_part, right_part, precision=lax.Precision.HIGH, preferred_el...  10.3 us
    ppermute x6, waiting for transfers between devices, sum_over_line(): lax.ppermute(down_send, 'prow', [(i, i - 1) for i in range(max(count - t,...  9.34 us
  transfers between devices with their start and end apart: 56, of which 13 were waited for; matrix products, arithmetic and copies ran while one was open for 12% of the time, Pallas kernels for 8%

profile of v1, /device:TPU:0, one launch (start us, length us, event | category | flops | bytes accessed | tf_op | source)
XLA Modules:
  0.0 289.8 jit_solution(8167274176200360387)
XLA Ops:
  2.7 3.9 %collective-permute-start.3 = (f32[256,128]{1,0:T(8,128)S(1)}, f32[256,128]{1,0:T(8,128)S(1)}, u32[]{:S(2)}, u32[]{:S(2)}) collective-permute-start(f32[256,128]{1,0:T(8,128)S(1)} %get-tuple-element.18), channel_id=1, source_target_pairs={{0,6},{1,7},{2,14},{3,15},{4,22},{5,23},{6,30},{7,31},{8,4},{9,5},... | collective-permute-start | bytes 393224 | tf_op jit(solution)/shard_map/ppermute | solution.py:167
  6.7 2.6 collective-permute-start.2
  10.5 6.9 %collective-permute-start.22 = (f32[256,128]{1,0:T(8,128)S(1)}, f32[256,128]{1,0:T(8,128)S(1)}, u32[]{:S(2)}, u32[]{:S(2)}) collective-permute-start(f32[256,128]{1,0:T(8,128)S(1)} %get-tuple-element.22), channel_id=1, source_target_pairs={{0,6},{1,7},{2,14},{3,15},{4,22},{5,23},{6,30},{7,31},{8,4},{9,5},... | collective-permute-start | bytes 393224 | tf_op jit(solution)/shard_map/ppermute | solution.py:167
  17.3 29.2 %collective-permute-start.21 = (f32[256,128]{1,0:T(8,128)S(1)}, f32[256,128]{1,0:T(8,128)S(1)}, u32[]{:S(2)}, u32[]{:S(2)}) collective-permute-start(f32[256,128]{1,0:T(8,128)S(1)} %get-tuple-element.21), channel_id=1, source_target_pairs={{0,4},{1,5},{2,12},{3,13},{4,20},{5,21},{6,28},{7,29},{8,6},{9,7},... | collective-permute-start | bytes 393224 | tf_op jit(solution)/shard_map/ppermute | solution.py:167
  46.6 4.1 %collective-permute-done.1 = f32[256,128]{1,0:T(8,128)S(1)} collective-permute-done((f32[256,128]{1,0:T(8,128)S(1)}, f32[256,128]{1,0:T(8,128)S(1)}, u32[]{:S(2)}, u32[]{:S(2)}) %collective-permute-start.1) | collective-permute-done | bytes 131104 | tf_op jit(solution)/shard_map/ppermute | solution.py:167
  51.4 14.9 %collective-permute-start.5 = (f32[4,256,128]{2,1,0:T(8,128)S(1)}, f32[4,256,128]{2,1,0:T(8,128)S(1)}, u32[]{:S(2)}, u32[]{:S(2)}) collective-permute-start(f32[4,256,128]{2,1,0:T(8,128)S(1)} %pad_maximum_fusion.1.refs_0_), channel_id=1, source_target_pairs={{0,2},{1,3},{2,0},{3,1},{4,6},{5,7},{6,4},{7,5},{8,10},{9,11},{10,... | collective-permute-start | bytes 1572872 | tf_op jit(solution)/shard_map/ppermute | solution.py:29
  66.3 2.7 collective-permute-start.7
  69.0 4.2 %collective-permute-done.20 = f32[256,128]{1,0:T(8,128)S(1)} collective-permute-done((f32[256,128]{1,0:T(8,128)S(1)}, f32[256,128]{1,0:T(8,128)S(1)}, u32[]{:S(2)}, u32[]{:S(2)}) %collective-permute-start.20) | collective-permute-done | bytes 131104 | tf_op jit(solution)/shard_map/ppermute | solution.py:167
  73.4 3.5 %collective-permute-start.24 = (f32[4,256,128]{2,1,0:T(8,128)S(1)}, f32[4,256,128]{2,1,0:T(8,128)}, u32[]{:S(2)}, u32[]{:S(2)}) collective-permute-start(f32[4,256,128]{2,1,0:T(8,128)S(1)} %pad_maximum_fusion.2.refs_0_), channel_id=1, source_target_pairs={{0,2},{1,3},{2,0},{3,1},{4,6},{5,7},{6,4},{7,5},{8,10},{9,11},{10,... | collective-permute-start | bytes 1572872 | tf_op jit(solution)/shard_map/ppermute | solution.py:29
  77.1 13.4 %collective-permute-done.26.refs_4_ = f32[4,256,128]{2,1,0:T(8,128)S(1)} collective-permute-done((f32[4,256,128]{2,1,0:T(8,128)S(1)}, f32[4,256,128]{2,1,0:T(8,128)S(1)}, u32[]{:S(2)}, u32[]{:S(2)}) %collective-permute-start.26) | collective-permute-done | bytes 524320 | tf_op jit(solution)/shard_map/ppermute | solution.py:29
  101.6 2.4 collective-permute-done.9.refs_6_
  104.7 6.0 %split.1 = (bf16[1024,2048]{1,0:T(8,128)(2,1)S(1)}, bf16[1024,2048]{1,0:T(8,128)(2,1)}) custom-call(f32[1024,2048]{1,0:T(8,128)} %tile_ref.1), custom_call_target="tpu_custom_call" | custom-call | bytes 16777216 | tf_op jit(solution)/shard_map/split/pallas_call | solution.py:77
  115.4 11.7 %partial_product.2 = f32[1024,512]{1,0:T(8,128)} custom-call(s32[11]{0:T(128)S(1)} %concatenate.8.meta, bf16[1024,2048]{1,0:T(8,128)(2,1)} %copy-done.3, bf16[1024,2048]{1,0:T(8,128)(2,1)} %get-tuple-element.14.low_ref, f32[4,256,128]{2,1,0:T(8,128)S(1)} %pad_maximum_fusion.1.refs_0_, f32[4,256,128]{2,1,0:T(8,128)} %collective-permute-done.4.refs_1_, ...), custom_call_target="tpu_custom_call" | custom-call | flops 6442450944 | bytes 14680064 | tf_op jit(solution)/shard_map/partial_product/pallas_call | solution.py:137
  129.5 6.6 %partial_product.3 = f32[1024,512]{1,0:T(8,128)} custom-call(s32[11]{0:T(128)S(1)} %concatenate.9.meta, bf16[1024,2048]{1,0:T(8,128)(2,1)} %copy-done.3, bf16[1024,2048]{1,0:T(8,128)(2,1)} %get-tuple-element.14.low_ref, f32[4,256,128]{2,1,0:T(8,128)S(1)} %pad_maximum_fusion.2.refs_0_, f32[4,256,128]{2,1,0:T(8,128)S(1)} %collective-permute-done.23.refs_1_, ...), custom_call_target="tpu_custom_call" | custom-call | flops 6442450944 | bytes 14680064 | tf_op jit(solution)/shard_map/partial_product/pallas_call | solution.py:137
  142.7 5.2 %collective-permute-start.14 = (f32[256,512]{1,0:T(8,128)}, f32[256,512]{1,0:T(8,128)}, u32[]{:S(2)}, u32[]{:S(2)}) collective-permute-start(f32[256,512]{1,0:T(8,128)} %dynamic-slice_add_fusion.6), channel_id=1, source_target_pairs={{0,8},{8,16},{1,9},{9,17},{2,10},{10,18},{3,11},{11,19},{4,12},{12... | collective-permute-start | bytes 1572872 | tf_op jit(solution)/shard_map/ppermute | solution.py:215
  148.5 3.6 %collective-permute-done.32 = f32[256,512]{1,0:T(8,128)} collective-permute-done((f32[256,512]{1,0:T(8,128)}, f32[256,512]{1,0:T(8,128)}, u32[]{:S(2)}, u32[]{:S(2)}) %collective-permute-start.32) | collective-permute-done | bytes 524320 | tf_op jit(solution)/shard_map/ppermute | solution.py:215
  153.5 4.4 %collective-permute-start.33 = (f32[256,512]{1,0:T(8,128)S(1)}, f32[256,512]{1,0:T(8,128)S(1)}, u32[]{:S(2)}, u32[]{:S(2)}) collective-permute-start(f32[256,512]{1,0:T(8,128)S(1)} %dynamic-slice_add_fusion.2), channel_id=1, source_target_pairs={{0,8},{8,16},{1,9},{9,17},{2,10},{10,18},{3,11},{11,19},{4,12},{12... | collective-permute-start | bytes 1572872 | tf_op jit(solution)/shard_map/ppermute | solution.py:215
  157.9 5.5 %collective-permute-done.14 = f32[256,512]{1,0:T(8,128)} collective-permute-done((f32[256,512]{1,0:T(8,128)}, f32[256,512]{1,0:T(8,128)}, u32[]{:S(2)}, u32[]{:S(2)}) %collective-permute-start.14) | collective-permute-done | bytes 524320 | tf_op jit(solution)/shard_map/ppermute | solution.py:215
  166.5 7.0 %collective-permute-done.33 = f32[256,512]{1,0:T(8,128)S(1)} collective-permute-done((f32[256,512]{1,0:T(8,128)S(1)}, f32[256,512]{1,0:T(8,128)S(1)}, u32[]{:S(2)}, u32[]{:S(2)}) %collective-permute-start.33) | collective-permute-done | bytes 524320 | tf_op jit(solution)/shard_map/ppermute | solution.py:215
  177.2 5.1 %collective-permute-start.15 = (f32[256,512]{1,0:T(8,128)S(1)}, f32[256,512]{1,0:T(8,128)S(1)}, u32[]{:S(2)}, u32[]{:S(2)}) collective-permute-start(f32[256,512]{1,0:T(8,128)S(1)} %get-tuple-element.33), channel_id=1, source_target_pairs={{0,8},{8,16},{16,24},{1,9},{9,17},{17,25},{2,10},{10,18},{18,26},{... | collective-permute-start | bytes 1572872 | tf_op jit(solution)/shard_map/ppermute | solution.py:215
  184.8 13.1 %collective-permute-start.34 = (f32[256,512]{1,0:T(8,128)S(1)}, f32[256,512]{1,0:T(8,128)S(1)}, u32[]{:S(2)}, u32[]{:S(2)}) collective-permute-start(f32[256,512]{1,0:T(8,128)S(1)} %get-tuple-element.35), channel_id=1, source_target_pairs={{0,8},{8,16},{16,24},{1,9},{9,17},{17,25},{2,10},{10,18},{18,26},{... | collective-permute-start | bytes 1572872 | tf_op jit(solution)/shard_map/ppermute | solution.py:215
  199.5 4.5 %collective-permute-done.18 = f32[256,512]{1,0:T(8,128)S(1)} collective-permute-done((f32[256,512]{1,0:T(8,128)S(1)}, f32[256,512]{1,0:T(8,128)S(1)}, u32[]{:S(2)}, u32[]{:S(2)}) %collective-permute-start.18) | collective-permute-done | bytes 524320 | tf_op jit(solution)/shard_map/ppermute | solution.py:216
  210.5 4.8 %collective-permute-done.37 = f32[256,512]{1,0:T(8,128)S(1)} collective-permute-done((f32[256,512]{1,0:T(8,128)S(1)}, f32[256,512]{1,0:T(8,128)S(1)}, u32[]{:S(2)}, u32[]{:S(2)}) %collective-permute-start.37) | collective-permute-done | bytes 524320 | tf_op jit(solution)/shard_map/ppermute | solution.py:216
  223.6 3.0 %collective-permute-start.47 = (f32[64,512]{1,0:T(8,128)S(1)}, f32[64,512]{1,0:T(8,128)S(1)}, u32[]{:S(2)}, u32[]{:S(2)}) collective-permute-start(f32[64,512]{1,0:T(8,128)S(1)} %get-tuple-element.44), channel_id=1, source_target_pairs={{0,6},{1,7},{2,4},{3,5},{4,2},{5,3},{6,0},{7,1},{8,14},{9,15},{10,... | collective-permute-start | bytes 393224 | tf_op jit(solution)/shard_map/ppermute | solution.py:29
  226.5 2.6 collective-permute-start.46
  240.6 9.4 %collective-permute-start.48 = (f32[64,512]{1,0:T(8,128)S(1)}, f32[64,512]{1,0:T(8,128)S(1)}, u32[]{:S(2)}, u32[]{:S(2)}) collective-permute-start(f32[64,512]{1,0:T(8,128)S(1)} %fusion.25), channel_id=1, source_target_pairs={{0,8},{8,0},{16,24},{24,16},{1,9},{9,1},{17,25},{25,17},{2,10},{10... | collective-permute-start | bytes 393224 | tf_op jit(solution)/shard_map/ppermute | solution.py:29
  250.8 4.7 %collective-permute-start.54 = (f32[64,512]{1,0:T(8,128)S(1)}, f32[64,512]{1,0:T(8,128)S(1)}, u32[]{:S(2)}, u32[]{:S(2)}) collective-permute-start(f32[64,512]{1,0:T(8,128)S(1)} %fusion.23), channel_id=1, source_target_pairs={{0,8},{8,0},{16,24},{24,16},{1,9},{9,1},{17,25},{25,17},{2,10},{10... | collective-permute-start | bytes 393224 | tf_op jit(solution)/shard_map/ppermute | solution.py:29
  256.4 9.8 %collective-permute-start.43 = (f32[64,512]{1,0:T(8,128)S(1)}, f32[64,512]{1,0:T(8,128)S(1)}, u32[]{:S(2)}, u32[]{:S(2)}) collective-permute-start(f32[64,512]{1,0:T(8,128)S(1)} %add.295), channel_id=1, source_target_pairs={{0,16},{8,24},{16,0},{24,8},{1,17},{9,25},{17,1},{25,9},{2,18},{10... | collective-permute-start | bytes 393224 | tf_op jit(solution)/shard_map/ppermute | solution.py:29
  267.2 5.8 %collective-permute-start.49 = (f32[64,512]{1,0:T(8,128)S(1)}, f32[64,512]{1,0:T(8,128)S(1)}, u32[]{:S(2)}, u32[]{:S(2)}) collective-permute-start(f32[64,512]{1,0:T(8,128)S(1)} %add.306), channel_id=1, source_target_pairs={{0,16},{8,24},{16,0},{24,8},{1,17},{9,25},{17,1},{25,9},{2,18},{10... | collective-permute-start | bytes 393224 | tf_op jit(solution)/shard_map/ppermute | solution.py:29
  273.1 5.8 %collective-permute-start.55 = (f32[64,512]{1,0:T(8,128)S(1)}, f32[64,512]{1,0:T(8,128)S(1)}, u32[]{:S(2)}, u32[]{:S(2)}) collective-permute-start(f32[64,512]{1,0:T(8,128)S(1)} %add.314), channel_id=1, source_target_pairs={{0,16},{8,24},{16,0},{24,8},{1,17},{9,25},{17,1},{25,9},{2,18},{10... | collective-permute-start | bytes 393224 | tf_op jit(solution)/shard_map/ppermute | solution.py:29
  279.8 2.6 collective-permute-done.49
  284.2 4.1 %collective-permute-done.55 = f32[64,512]{1,0:T(8,128)S(1)} collective-permute-done((f32[64,512]{1,0:T(8,128)S(1)}, f32[64,512]{1,0:T(8,128)S(1)}, u32[]{:S(2)}, u32[]{:S(2)}) %collective-permute-start.55) | collective-permute-done | bytes 131104 | tf_op jit(solution)/shard_map/ppermute | solution.py:29
  (183 shorter events, 75.4 us)
Async XLA Ops:
  2.7 14.6 %collective-permute-start.3 = (f32[256,128]{1,0:T(8,128)S(1)}, f32[256,128]{1,0:T(8,128)S(1)}, u32[]{:S(2)}, u32[]{:S(2)}) collective-permute-start(f32[256,128]{1,0:T(8,128)S(1)} %get-tuple-element.18), channel_id=1, source_target_pairs={{0,6},{1,7},{2,14},{3,15},{4,22},{5,23},{6,30},{7,31},{8,4},{9,5},... | collective-permute-start | bytes 393224 | tf_op jit(solution)/shard_map/ppermute | solution.py:167
  6.7 39.9 %collective-permute-start.2 = (f32[256,128]{1,0:T(8,128)S(1)}, f32[256,128]{1,0:T(8,128)S(1)}, u32[]{:S(2)}, u32[]{:S(2)}) collective-permute-start(f32[256,128]{1,0:T(8,128)S(1)} %get-tuple-element.17), channel_id=1, source_target_pairs={{0,4},{1,5},{2,12},{3,13},{4,20},{5,21},{6,28},{7,29},{8,6},{9,7},... | collective-permute-start | bytes 393224 | tf_op jit(solution)/shard_map/ppermute | solution.py:167
  9.3 41.5 %collective-permute-start.1 = (f32[256,128]{1,0:T(8,128)S(1)}, f32[256,128]{1,0:T(8,128)S(1)}, u32[]{:S(2)}, u32[]{:S(2)}) collective-permute-start(f32[256,128]{1,0:T(8,128)S(1)} %get-tuple-element.16), channel_id=1, source_target_pairs={{0,2},{1,3},{2,10},{3,11},{4,18},{5,19},{6,26},{7,27},{8,0},{9,1},... | collective-permute-start | bytes 393224 | tf_op jit(solution)/shard_map/ppermute | solution.py:167
  9.8 41.6 %collective-permute-start = (f32[256,128]{1,0:T(8,128)S(1)}, f32[256,128]{1,0:T(8,128)S(1)}, u32[]{:S(2)}, u32[]{:S(2)}) collective-permute-start(f32[256,128]{1,0:T(8,128)S(1)} %get-tuple-element.15), channel_id=1, source_target_pairs={{0,0},{1,1},{2,8},{3,9},{4,16},{5,17},{6,24},{7,25},{8,2},{9,3},{1... | collective-permute-start | bytes 393224 | tf_op jit(solution)/shard_map/ppermute | solution.py:167
  10.5 55.9 %collective-permute-start.22 = (f32[256,128]{1,0:T(8,128)S(1)}, f32[256,128]{1,0:T(8,128)S(1)}, u32[]{:S(2)}, u32[]{:S(2)}) collective-permute-start(f32[256,128]{1,0:T(8,128)S(1)} %get-tuple-element.22), channel_id=1, source_target_pairs={{0,6},{1,7},{2,14},{3,15},{4,22},{5,23},{6,30},{7,31},{8,4},{9,5},... | collective-permute-start | bytes 393224 | tf_op jit(solution)/shard_map/ppermute | solution.py:167
  17.3 51.7 %collective-permute-start.21 = (f32[256,128]{1,0:T(8,128)S(1)}, f32[256,128]{1,0:T(8,128)S(1)}, u32[]{:S(2)}, u32[]{:S(2)}) collective-permute-start(f32[256,128]{1,0:T(8,128)S(1)} %get-tuple-element.21), channel_id=1, source_target_pairs={{0,4},{1,5},{2,12},{3,13},{4,20},{5,21},{6,28},{7,29},{8,6},{9,7},... | collective-permute-start | bytes 393224 | tf_op jit(solution)/shard_map/ppermute | solution.py:167
  46.6 26.6 %collective-permute-start.20 = (f32[256,128]{1,0:T(8,128)S(1)}, f32[256,128]{1,0:T(8,128)S(1)}, u32[]{:S(2)}, u32[]{:S(2)}) collective-permute-start(f32[256,128]{1,0:T(8,128)S(1)} %get-tuple-element.20), channel_id=1, source_target_pairs={{0,2},{1,3},{2,10},{3,11},{4,18},{5,19},{6,26},{7,27},{8,0},{9,1},... | collective-permute-start | bytes 393224 | tf_op jit(solution)/shard_map/ppermute | solution.py:167
  50.7 22.5 %collective-permute-start.19 = (f32[256,128]{1,0:T(8,128)S(1)}, f32[256,128]{1,0:T(8,128)S(1)}, u32[]{:S(2)}, u32[]{:S(2)}) collective-permute-start(f32[256,128]{1,0:T(8,128)S(1)} %get-tuple-element.19), channel_id=1, source_target_pairs={{0,0},{1,1},{2,8},{3,9},{4,16},{5,17},{6,24},{7,25},{8,2},{9,3},{1... | collective-permute-start | bytes 393224 | tf_op jit(solution)/shard_map/ppermute | solution.py:167
  51.4 43.5 %collective-permute-start.5 = (f32[4,256,128]{2,1,0:T(8,128)S(1)}, f32[4,256,128]{2,1,0:T(8,128)S(1)}, u32[]{:S(2)}, u32[]{:S(2)}) collective-permute-start(f32[4,256,128]{2,1,0:T(8,128)S(1)} %pad_maximum_fusion.1.refs_0_), channel_id=1, source_target_pairs={{0,2},{1,3},{2,0},{3,1},{4,6},{5,7},{6,4},{7,5},{8,10},{9,11},{10,... | collective-permute-start | bytes 1572872 | tf_op jit(solution)/shard_map/ppermute | solution.py:29
  66.3 24.9 %collective-permute-start.7 = (f32[4,256,128]{2,1,0:T(8,128)S(1)}, f32[4,256,128]{2,1,0:T(8,128)}, u32[]{:S(2)}, u32[]{:S(2)}) collective-permute-start(f32[4,256,128]{2,1,0:T(8,128)S(1)} %pad_maximum_fusion.1.refs_0_), channel_id=1, source_target_pairs={{0,4},{1,5},{2,6},{3,7},{4,0},{5,1},{6,2},{7,3},{8,12},{9,13},{10,... | collective-permute-start | bytes 1572872 | tf_op jit(solution)/shard_map/ppermute | solution.py:29
  73.2 17.3 %collective-permute-start.26 = (f32[4,256,128]{2,1,0:T(8,128)S(1)}, f32[4,256,128]{2,1,0:T(8,128)S(1)}, u32[]{:S(2)}, u32[]{:S(2)}) collective-permute-start(f32[4,256,128]{2,1,0:T(8,128)S(1)} %pad_maximum_fusion.2.refs_0_), channel_id=1, source_target_pairs={{0,4},{1,5},{2,6},{3,7},{4,0},{5,1},{6,2},{7,3},{8,12},{9,13},{10,... | collective-permute-start | bytes 1572872 | tf_op jit(solution)/shard_map/ppermute | solution.py:29
  73.4 24.7 %collective-permute-start.24 = (f32[4,256,128]{2,1,0:T(8,128)S(1)}, f32[4,256,128]{2,1,0:T(8,128)}, u32[]{:S(2)}, u32[]{:S(2)}) collective-permute-start(f32[4,256,128]{2,1,0:T(8,128)S(1)} %pad_maximum_fusion.2.refs_0_), channel_id=1, source_target_pairs={{0,2},{1,3},{2,0},{3,1},{4,6},{5,7},{6,4},{7,5},{8,10},{9,11},{10,... | collective-permute-start | bytes 1572872 | tf_op jit(solution)/shard_map/ppermute | solution.py:29
  76.9 21.3 %collective-permute-start.4 = (f32[4,256,128]{2,1,0:T(8,128)S(1)}, f32[4,256,128]{2,1,0:T(8,128)}, u32[]{:S(2)}, u32[]{:S(2)}) collective-permute-start(f32[4,256,128]{2,1,0:T(8,128)S(1)} %pad_maximum_fusion.1.refs_0_), channel_id=1, source_target_pairs={{0,1},{1,0},{2,3},{3,2},{4,5},{5,4},{6,7},{7,6},{8,9},{9,8},{10,11... | collective-permute-start | bytes 1572872 | tf_op jit(solution)/shard_map/ppermute | solution.py:29
  98.1 16.2 %collective-permute-start.6 = (f32[4,256,128]{2,1,0:T(8,128)S(1)}, f32[4,256,128]{2,1,0:T(8,128)}, u32[]{:S(2)}, u32[]{:S(2)}) collective-permute-start(f32[4,256,128]{2,1,0:T(8,128)S(1)} %collective-permute-done.5.refs_2_), channel_id=1, source_target_pairs={{0,1},{1,0},{2,3},{3,2},{4,5},{5,4},{6,7},{7,6},{8,9},{9,8},{10,11... | collective-permute-start | bytes 1572872 | tf_op jit(solution)/shard_map/ppermute | solution.py:29
  98.2 16.6 %collective-permute-start.8 = (f32[4,256,128]{2,1,0:T(8,128)}, f32[4,256,128]{2,1,0:T(8,128)}, u32[]{:S(2)}, u32[]{:S(2)}) collective-permute-start(f32[4,256,128]{2,1,0:T(8,128)} %collective-permute-done.7.refs_4_), channel_id=1, source_target_pairs={{0,1},{1,0},{2,3},{3,2},{4,5},{5,4},{6,7},{7,6},{8,9},{9,8},{10,11... | collective-permute-start | bytes 1572872 | tf_op jit(solution)/shard_map/ppermute | solution.py:29
  114.3 15.2 %collective-permute-start.25 = (f32[4,256,128]{2,1,0:T(8,128)}, f32[4,256,128]{2,1,0:T(8,128)S(1)}, u32[]{:S(2)}, u32[]{:S(2)}) collective-permute-start(f32[4,256,128]{2,1,0:T(8,128)} %collective-permute-done.24.refs_2_), channel_id=1, source_target_pairs={{0,1},{1,0},{2,3},{3,2},{4,5},{5,4},{6,7},{7,6},{8,9},{9,8},{10,11... | collective-permute-start | bytes 1572872 | tf_op jit(solution)/shard_map/ppermute | solution.py:29
  114.8 14.7 %collective-permute-start.27 = (f32[4,256,128]{2,1,0:T(8,128)S(1)}, f32[4,256,128]{2,1,0:T(8,128)S(1)}, u32[]{:S(2)}, u32[]{:S(2)}) collective-permute-start(f32[4,256,128]{2,1,0:T(8,128)S(1)} %collective-permute-done.26.refs_4_), channel_id=1, source_target_pairs={{0,1},{1,0},{2,3},{3,2},{4,5},{5,4},{6,7},{7,6},{8,9},{9,8},{10,11... | collective-permute-start | bytes 1572872 | tf_op jit(solution)/shard_map/ppermute | solution.py:29
  114.9 14.6 %collective-permute-start.30 = (f32[2,256,128]{2,1,0:T(8,128)S(1)}, f32[2,256,128]{2,1,0:T(8,128)S(1)}, u32[]{:S(2)}, u32[]{:S(2)}) collective-permute-start(f32[2,256,128]{2,1,0:T(8,128)S(1)} %collective-permute-done.28.refs_6_), channel_id=1, source_target_pairs={{0,1},{1,0},{2,3},{3,2},{4,5},{5,4},{6,7},{7,6},{8,9},{9,8},{10,11... | collective-permute-start | bytes 786440 | tf_op jit(solution)/shard_map/ppermute | solution.py:29
  142.7 20.7 %collective-permute-start.14 = (f32[256,512]{1,0:T(8,128)}, f32[256,512]{1,0:T(8,128)}, u32[]{:S(2)}, u32[]{:S(2)}) collective-permute-start(f32[256,512]{1,0:T(8,128)} %dynamic-slice_add_fusion.6), channel_id=1, source_target_pairs={{0,8},{8,16},{1,9},{9,17},{2,10},{10,18},{3,11},{11,19},{4,12},{12... | collective-permute-start | bytes 1572872 | tf_op jit(solution)/shard_map/ppermute | solution.py:215
  153.5 20.1 %collective-permute-start.33 = (f32[256,512]{1,0:T(8,128)S(1)}, f32[256,512]{1,0:T(8,128)S(1)}, u32[]{:S(2)}, u32[]{:S(2)}) collective-permute-start(f32[256,512]{1,0:T(8,128)S(1)} %dynamic-slice_add_fusion.2), channel_id=1, source_target_pairs={{0,8},{8,16},{1,9},{9,17},{2,10},{10,18},{3,11},{11,19},{4,12},{12... | collective-permute-start | bytes 1572872 | tf_op jit(solution)/shard_map/ppermute | solution.py:215
  177.2 22.3 %collective-permute-start.15 = (f32[256,512]{1,0:T(8,128)S(1)}, f32[256,512]{1,0:T(8,128)S(1)}, u32[]{:S(2)}, u32[]{:S(2)}) collective-permute-start(f32[256,512]{1,0:T(8,128)S(1)} %get-tuple-element.33), channel_id=1, source_target_pairs={{0,8},{8,16},{16,24},{1,9},{9,17},{17,25},{2,10},{10,18},{18,26},{... | collective-permute-start | bytes 1572872 | tf_op jit(solution)/shard_map/ppermute | solution.py:215
  182.5 15.4 %collective-permute-start.36 = (f32[256,512]{1,0:T(8,128)S(1)}, f32[256,512]{1,0:T(8,128)S(1)}, u32[]{:S(2)}, u32[]{:S(2)}) collective-permute-start(f32[256,512]{1,0:T(8,128)S(1)} %dynamic-slice_add_fusion), channel_id=1, source_target_pairs={{16,8},{24,16},{17,9},{25,17},{18,10},{26,18},{19,11},{27,19},{20,... | collective-permute-start | bytes 1572872 | tf_op jit(solution)/shard_map/ppermute | solution.py:216
  183.3 20.8 %collective-permute-start.18 = (f32[256,512]{1,0:T(8,128)S(1)}, f32[256,512]{1,0:T(8,128)S(1)}, u32[]{:S(2)}, u32[]{:S(2)}) collective-permute-start(f32[256,512]{1,0:T(8,128)S(1)} %dynamic-slice_add_fusion.5), channel_id=1, source_target_pairs={{8,0},{16,8},{24,16},{9,1},{17,9},{25,17},{10,2},{18,10},{26,18},{... | collective-permute-start | bytes 1572872 | tf_op jit(solution)/shard_map/ppermute | solution.py:216
  184.8 25.7 %collective-permute-start.34 = (f32[256,512]{1,0:T(8,128)S(1)}, f32[256,512]{1,0:T(8,128)S(1)}, u32[]{:S(2)}, u32[]{:S(2)}) collective-permute-start(f32[256,512]{1,0:T(8,128)S(1)} %get-tuple-element.35), channel_id=1, source_target_pairs={{0,8},{8,16},{16,24},{1,9},{9,17},{17,25},{2,10},{10,18},{18,26},{... | collective-permute-start | bytes 1572872 | tf_op jit(solution)/shard_map/ppermute | solution.py:215
  198.0 17.3 %collective-permute-start.37 = (f32[256,512]{1,0:T(8,128)S(1)}, f32[256,512]{1,0:T(8,128)S(1)}, u32[]{:S(2)}, u32[]{:S(2)}) collective-permute-start(f32[256,512]{1,0:T(8,128)S(1)} %dynamic-slice_add_fusion.1), channel_id=1, source_target_pairs={{8,0},{16,8},{24,16},{9,1},{17,9},{25,17},{10,2},{18,10},{26,18},{... | collective-permute-start | bytes 1572872 | tf_op jit(solution)/shard_map/ppermute | solution.py:216
  233.0 17.0 %collective-permute-start.39 = (f32[64,512]{1,0:T(8,128)S(1)}, f32[64,512]{1,0:T(8,128)S(1)}, u32[]{:S(2)}, u32[]{:S(2)}) collective-permute-start(f32[64,512]{1,0:T(8,128)S(1)} %get-tuple-element.40), channel_id=1, source_target_pairs={{0,2},{1,3},{2,0},{3,1},{4,6},{5,7},{6,4},{7,5},{8,10},{9,11},{10,... | collective-permute-start | bytes 393224 | tf_op jit(solution)/shard_map/ppermute | solution.py:29
  234.9 15.8 %collective-permute-start.53 = (f32[64,512]{1,0:T(8,128)S(1)}, f32[64,512]{1,0:T(8,128)S(1)}, u32[]{:S(2)}, u32[]{:S(2)}) collective-permute-start(f32[64,512]{1,0:T(8,128)S(1)} %get-tuple-element.38), channel_id=1, source_target_pairs={{0,6},{1,7},{2,4},{3,5},{4,2},{5,3},{6,0},{7,1},{8,14},{9,15},{10,... | collective-permute-start | bytes 393224 | tf_op jit(solution)/shard_map/ppermute | solution.py:29
  240.6 26.6 %collective-permute-start.48 = (f32[64,512]{1,0:T(8,128)S(1)}, f32[64,512]{1,0:T(8,128)S(1)}, u32[]{:S(2)}, u32[]{:S(2)}) collective-permute-start(f32[64,512]{1,0:T(8,128)S(1)} %fusion.25), channel_id=1, source_target_pairs={{0,8},{8,0},{16,24},{24,16},{1,9},{9,1},{17,25},{25,17},{2,10},{10... | collective-permute-start | bytes 393224 | tf_op jit(solution)/shard_map/ppermute | solution.py:29
  250.8 22.3 %collective-permute-start.54 = (f32[64,512]{1,0:T(8,128)S(1)}, f32[64,512]{1,0:T(8,128)S(1)}, u32[]{:S(2)}, u32[]{:S(2)}) collective-permute-start(f32[64,512]{1,0:T(8,128)S(1)} %fusion.23), channel_id=1, source_target_pairs={{0,8},{8,0},{16,24},{24,16},{1,9},{9,1},{17,25},{25,17},{2,10},{10... | collective-permute-start | bytes 393224 | tf_op jit(solution)/shard_map/ppermute | solution.py:29
  256.4 22.4 %collective-permute-start.43 = (f32[64,512]{1,0:T(8,128)S(1)}, f32[64,512]{1,0:T(8,128)S(1)}, u32[]{:S(2)}, u32[]{:S(2)}) collective-permute-start(f32[64,512]{1,0:T(8,128)S(1)} %add.295), channel_id=1, source_target_pairs={{0,16},{8,24},{16,0},{24,8},{1,17},{9,25},{17,1},{25,9},{2,18},{10... | collective-permute-start | bytes 393224 | tf_op jit(solution)/shard_map/ppermute | solution.py:29
  267.2 15.2 %collective-permute-start.49 = (f32[64,512]{1,0:T(8,128)S(1)}, f32[64,512]{1,0:T(8,128)S(1)}, u32[]{:S(2)}, u32[]{:S(2)}) collective-permute-start(f32[64,512]{1,0:T(8,128)S(1)} %add.306), channel_id=1, source_target_pairs={{0,16},{8,24},{16,0},{24,8},{1,17},{9,25},{17,1},{25,9},{2,18},{10... | collective-permute-start | bytes 393224 | tf_op jit(solution)/shard_map/ppermute | solution.py:29
  273.1 15.2 %collective-permute-start.55 = (f32[64,512]{1,0:T(8,128)S(1)}, f32[64,512]{1,0:T(8,128)S(1)}, u32[]{:S(2)}, u32[]{:S(2)}) collective-permute-start(f32[64,512]{1,0:T(8,128)S(1)} %add.314), channel_id=1, source_target_pairs={{0,16},{8,24},{16,0},{24,8},{1,17},{9,25},{17,1},{25,9},{2,18},{10... | collective-permute-start | bytes 393224 | tf_op jit(solution)/shard_map/ppermute | solution.py:29
  (40 other events, 603.7 us)

commit v2 on v1

v2 whole, which is shorter than its diff:
```python
import functools

import jax
import jax.numpy as jnp
import numpy as np
from jax import lax
from jax.experimental import pallas as pl
from jax.experimental.pallas import tpu as pltpu
from jax.sharding import PartitionSpec as P

BOTH = ("prow", "pcol")
VMEM_LIMIT = 48 * 1024 * 1024
LANES = 128


def product(left_part, right_part):
    return jnp.dot(
        left_part, right_part, precision=lax.Precision.HIGH, preferred_element_type=jnp.float32
    )


def halves(value):
    high = value.astype(jnp.bfloat16)
    low = (value - high.astype(jnp.float32)).astype(jnp.bfloat16)
    return high, low


def flip(value, axis, bit):
    return lax.ppermute(value, axis, [(i, i ^ bit) for i in range(lax.axis_size(axis))])


def spread_kernel(meta, factor_ref, *out_refs):
    nsuper = factor_ref.shape[0]
    count = len(out_refs) // nsuper
    width = out_refs[0].shape[1]
    for number in range(nsuper):
        for r in range(count):
            start = pl.multiple_of((meta[0] ^ r) * width, width)
            out_refs[number * count + r][...] = factor_ref[number, :, pl.ds(start, width)]


def spread(meta, factor, count):
    nsuper, unit_rows, columns = factor.shape
    width = columns // count
    if width % LANES:
        pieces = []
        for number in range(nsuper):
            for r in range(count):
                start = (meta[0] ^ r) * width
                pieces.append(lax.dynamic_slice_in_dim(factor[number], start, width, 1))
        return pieces
    return pl.pallas_call(
        spread_kernel,
        grid_spec=pltpu.PrefetchScalarGridSpec(
            num_scalar_prefetch=1,
            grid=(1,),
            in_specs=[pl.BlockSpec(factor.shape, lambda i, m: (0, 0, 0))],
            out_specs=[pl.BlockSpec((unit_rows, width), lambda i, m: (0, 0))] * (nsuper * count),
        ),
        out_shape=[jax.ShapeDtypeStruct((unit_rows, width), factor.dtype)] * (nsuper * count),
        compiler_params=pltpu.CompilerParams(vmem_limit_bytes=VMEM_LIMIT),
        cost_estimate=pl.CostEstimate(
            flops=0, bytes_accessed=2 * factor.size * 4, transcendentals=0
        ),
        name="spread",
    )(meta, factor)


def partial_kernel(places, ratio, count, meta, tile_ref, *refs):
    piece_refs = refs[: len(places)]
    out_refs = refs[len(places) : -2]
    right_high, right_low = refs[-2:]
    columns = out_refs[0].shape[1]
    blocks = tile_ref.shape[1] // columns
    step = pl.program_id(0)

    @pl.when(step == 0)
    def _assemble():
        for ref, offset in zip(piece_refs, places):
            if offset is None:
                right_high[...], right_low[...] = halves(ref[...])
                continue
            unit_rows, width = ref.shape[1:]
            owner = meta[0] ^ offset
            column = owner // ratio
            lane = pl.multiple_of(column * width, width)
            for r in range(ref.shape[0]):
                unit = (owner % ratio) * count + (column ^ meta[1] ^ r)
                rows = pl.ds(pl.multiple_of(unit * unit_rows, unit_rows), unit_rows)
                high, low = halves(ref[r])
                right_high[rows, pl.ds(lane, width)] = high
                right_low[rows, pl.ds(lane, width)] = low

    def multiply(out_ref):
        out_ref[...] = jnp.zeros_like(out_ref)

        def add(number, carry):
            span = pl.ds(pl.multiple_of(meta[3 + number] * columns, columns), columns)
            high, low = halves(tile_ref[:, span])
            right = right_high[span, :]
            dot = functools.partial(jnp.dot, preferred_element_type=jnp.float32)
            out_ref[...] += dot(high, right) + (dot(high, right_low[span, :]) + dot(low, right))
            return carry

        lax.fori_loop(0, jnp.where(meta[3 + blocks + count + step] != 0, meta[2], 0), add, 0)

    for number, out_ref in enumerate(out_refs):
        pl.when(step == number)(functools.partial(multiply, out_ref))


def partial_product(meta, tiles, pieces, places, ratio, count, columns):
    rows, cols = tiles.shape
    chunk = rows // count
    first = 3 + cols // columns
    whole = [
        pl.BlockSpec(piece.shape, functools.partial(lambda n, i, m: (0,) * n, piece.ndim))
        for piece in pieces
    ]
    return pl.pallas_call(
        functools.partial(partial_kernel, places, ratio, count),
        grid_spec=pltpu.PrefetchScalarGridSpec(
            num_scalar_prefetch=1,
            grid=(count,),
            in_specs=[pl.BlockSpec((chunk, cols), lambda i, m: (m[first + i], 0))] + whole,
            out_specs=[pl.BlockSpec((chunk, columns), lambda i, m: (0, 0))] * count,
            scratch_shapes=[pltpu.VMEM((cols, columns), jnp.bfloat16)] * 2,
        ),
        out_shape=[jax.ShapeDtypeStruct((chunk, columns), jnp.float32)] * count,
        compiler_params=pltpu.CompilerParams(vmem_limit_bytes=VMEM_LIMIT),
        cost_estimate=pl.CostEstimate(
            flops=6 * rows * cols * columns,
            bytes_accessed=4 * (rows * cols + cols * columns + rows * columns),
            transcendentals=0,
        ),
        name="partial_product",
    )(meta, tiles, *pieces)


def to_plane(sends, count, ratio):
    pcol_count = count * ratio
    received = []
    for r, piece in enumerate(sends):
        perm = []
        for z in range(count):
            for c in range(count):
                for k in range(ratio):
                    source = z * pcol_count + c * ratio + k
                    perm.append((source, c * pcol_count + (c ^ z ^ r) * ratio + k))
        received.append(lax.ppermute(piece, BOTH, perm))
    return jnp.stack(received)


def gather_plane(own, pcol_count):
    found = {0: own}
    for offset in range(2, pcol_count, 2):
        found[offset] = flip(own, "pcol", offset)
    for offset in range(0, pcol_count, 2):
        found[offset + 1] = flip(found[offset], "pcol", 1)
    return found


def gather_whole(own, count, ratio):
    _, unit_rows, width = own.shape
    gathered = lax.all_gather(own, "pcol", axis=0)
    column = np.arange(count)[None, None, :]
    owner = np.broadcast_to(
        column * ratio + np.arange(ratio)[:, None, None], (ratio, count, count)
    )
    part = jnp.asarray(column ^ np.arange(count)[None, :, None]) ^ lax.axis_index("prow")
    part = jnp.broadcast_to(part, owner.shape)
    rows = jnp.transpose(gathered[owner, part], (0, 1, 3, 2, 4))
    return rows.reshape(ratio * count * unit_rows, count * width)


FOUR_SLOTS = ((3, 2, 1, 0), (2, 0, 3, 1), (1, 3, 0, 2), (0, 1, 2, 3))


def slots_of(count):
    return FOUR_SLOTS if count == len(FOUR_SLOTS) else (tuple(range(count)),) * count


def sum_over_four(slots):
    near = lax.ppermute(slots[0], "prow", [(0, 1), (3, 2)])
    total = lax.ppermute(slots[1], "prow", [(0, 2), (2, 3), (3, 1), (1, 0)])
    middle = lax.ppermute(slots[0], "prow", [(1, 2), (2, 1)])
    last = lax.ppermute(slots[2] + near, "prow", [(1, 3), (2, 0), (0, 1), (3, 2)])
    return ((slots[3] + total) + middle) + last


def sum_over_line(slots, z):
    count = len(slots)
    if count == len(FOUR_SLOTS):
        return sum_over_four(slots)
    chunks = jnp.stack(slots)

    def chunk(index):
        return lax.dynamic_index_in_dim(chunks, jnp.clip(index, 0, count - 1), 0, keepdims=False)

    up = down = None
    for t in range(1, count):
        up_send, down_send = chunk(z + count - t), chunk(z + t - count)
        if up is not None:
            up_send, down_send = up_send + up, down_send + down
        up = lax.ppermute(up_send, "prow", [(i, i + 1) for i in range(min(t, count - 1))])
        down = lax.ppermute(
            down_send, "prow", [(i, i - 1) for i in range(max(count - t, 1), count)]
        )
    mine = chunk(z)
    return mine if up is None else mine + up + down


def sum_rows(matrices, pcol_count, count, pcol_index):
    number, rows, columns = matrices.shape
    if pcol_count > 1:
        paired = matrices.reshape(number, pcol_count // 2, 2, rows // pcol_count, columns)
        core = pcol_index % 2
        send = lax.dynamic_index_in_dim(paired, 1 - core, 2, keepdims=False)
        mine = lax.dynamic_index_in_dim(paired, core, 2, keepdims=False) + flip(send, "pcol", 1)
        chip = pcol_index // 2
        matrices = lax.dynamic_index_in_dim(mine, chip, 1, keepdims=False)
        for o in range(1, pcol_count // 2):
            send = lax.dynamic_index_in_dim(mine, chip ^ o, 1, keepdims=False)
            matrices = matrices + flip(send, "pcol", 2 * o)
    bit = 1
    while bit < count:
        matrices = matrices + flip(matrices, "prow", bit)
        bit *= 2
    return matrices


def body(inverse_tiles, factor, link_factor, diag_inverse, ancestors):
    row_count, col_count = inverse_tiles.shape
    nsuper, unit_rows, columns = factor.shape
    count = lax.axis_size("prow")
    pcol_count = lax.axis_size("pcol")
    ratio = col_count // row_count
    z = lax.axis_index("prow")
    pcol_index = lax.axis_index("pcol")
    slice_rows = columns // pcol_count
    slice_start = pcol_index * slice_rows
    width = columns // count

    listed = jnp.any(
        lax.iota(jnp.int32, count * col_count // columns)[None, :, None] == ancestors[:, None, :],
        axis=2,
    )
    unit_ids = (pcol_index * count + lax.iota(jnp.int32, count)) * unit_rows // columns
    chunk_kept = listed[:, unit_ids]
    keep = chunk_kept[:, z][:, None, None]
    blocks = col_count // columns
    block_kept = lax.dynamic_slice_in_dim(listed, z * blocks, blocks, 1)
    ids = lax.iota(jnp.int32, blocks)
    rank = jnp.cumsum(block_kept.astype(jnp.int32), axis=1) - 1
    taken = (rank[:, None, :] == ids[None, :, None]) & block_kept[:, None, :]
    order = jnp.sum(jnp.where(taken, ids[None, None, :], 0), axis=2)
    slots = jnp.asarray(slots_of(count), jnp.int32)[z]
    place = jnp.stack([pcol_index, z]).astype(jnp.int32)
    metas = [
        jnp.concatenate(
            [
                place,
                jnp.sum(block_kept[number], dtype=jnp.int32)[None],
                order[number].astype(jnp.int32),
                slots,
                chunk_kept[number][slots].astype(jnp.int32),
            ]
        )
        for number in range(nsuper)
    ]

    target = ((pcol_index // ratio) ^ z).astype(jnp.int32)
    sends = spread(target[None], factor, count)
    local = jnp.where(keep, factor, 0.0)

    partials = []
    for number in range(nsuper):
        own = to_plane(sends[number * count : (number + 1) * count], count, ratio)
        if width % LANES:
            pieces, places = [gather_whole(own, count, ratio)], [None]
        else:
            found = gather_plane(own, pcol_count)
            places, pieces = list(found.keys()), list(found.values())
        partials.append(
            partial_product(metas[number], inverse_tiles, pieces, places, ratio, count, columns)
        )

    def own_rows(matrices):
        return lax.dynamic_slice_in_dim(matrices, slice_start, slice_rows, -2)

    offdiag_list, sums, bases = [], [], []
    for number in range(nsuper):
        summed = sum_over_line(partials[number], z)
        part = product(local[number].T, summed)
        if number == 0:
            result = -jnp.where(keep[number], summed, 0.0)
            base = diag_inverse[0]
            ready = [part]
        else:
            link_block = link_factor[number - 1]
            result = -jnp.where(keep[number], summed + product(prior_offdiag, link_block), 0.0)
            cross_part = product(prior_offdiag.T, local[number])
            link_part = cross_part + product(prior_part, link_block)
            rest = product(cross_part.T, link_block) + product(link_block.T, link_part)
            base_link = product(prior_base, link_block)
            base = diag_inverse[number] + product(link_block.T, base_link)
            sums.append(sum_rows(jnp.stack(ready + [link_part]), pcol_count, count, pcol_index))
            bases += [own_rows(prior_base), own_rows(base_link)]
            part = part + rest
            ready = [part]
        offdiag_list.append(result)
        prior_offdiag, prior_part, prior_base = result, part, base
    sums.append(sum_rows(jnp.stack(ready), pcol_count, count, pcol_index))
    bases.append(own_rows(prior_base))
    totals = jnp.concatenate(sums) + jnp.stack(bases)
    return (jnp.stack(offdiag_list), totals[0::2], -totals[1::2])


def solution(mesh):
    in_specs = (P("pcol", "prow"), P(None, ("pcol", "prow"), None), P(), P(), P())
    out_specs = (P(None, ("pcol", "prow"), None), P(None, "pcol", None), P(None, "pcol", None))
    return jax.shard_map(body, mesh=mesh, in_specs=in_specs, out_specs=out_specs, check_vma=False)
```

time: 290 us -> 247 us (0.85)
  starting transfers between devices: 162 us -> 86.6 us
  waiting for transfers between devices: 58 us -> 110 us
  local copies, waits for them, and re-layouts: 17.9 us -> 9.99 us
  Pallas kernels: 24.9 us -> 18.3 us
  other arithmetic: 15 us -> 10.9 us
    ppermute x36 -> x26, starting transfers between devices: 80.9 us -> 28.3 us  [flip(): lax.ppermute(value, axis, [(i, i ^ bit) for i in range(lax.axis_size(axis...]
    ppermute x36 -> x26, waiting for transfers between devices: 23.5 us -> 60.3 us  [flip(): lax.ppermute(value, axis, [(i, i ^ bit) for i in range(lax.axis_size(axis...]
    ppermute x12 -> x8, starting transfers between devices: 36.9 us -> 12.6 us  [the longest x2 7.24 us: sum_over_four(): total = lax.ppermute(slots[1], 'prow', [(0, 2), (2, 3), (3, 1), (1, 0)])]
    ppermute x12 -> x8, waiting for transfers between devices: 26.2 us -> 45.5 us  [the longest x2 25.3 us: sum_over_four(): lax.ppermute(slots[2] + near, 'prow', [(1, 3), (2, 0), (0, 1), (3, 2)])]
    pallas_call x1 -> x0, Pallas kernels: 6.02 us -> none  [split(): pl.pallas_call(split_kernel, grid=(steps,), in_specs=[block], out_specs=[...]
    add x18 -> x12, other arithmetic: 6.46 us -> 0.98 us  [the longest x2 0.3 us: sum_rows(): lax.dynamic_index_in_dim(paired, core, 2, keepdims=False)]
    another operation x7 -> x3, other arithmetic: 6.91 us -> 1.99 us  [the longest x2 1.95 us: body(): return (jnp.stack(offdiag_list), totals[0::2], -totals[1::2])]
    slice x4 -> x2, local copies, waits for them, and re-layouts: 4.82 us -> 0.9 us  [the longest x1 0.72 us: body(): return (jnp.stack(offdiag_list), totals[0::2], -totals[1::2])]
  transfers between devices with their start and end apart: 56 -> 42, of which waited for: 13 -> 16; matrix products, arithmetic and copies ran while one was open for 12% -> 11% of each run, Pallas kernels for 8% -> 7%
where the time goes in v2:
time: 247 us
  waiting for transfers between devices  110 us (45%)
  starting transfers between devices  86.6 us (35%)
  Pallas kernels  18.3 us (7%)
  other arithmetic  10.9 us (4%)
  local copies, waits for them, and re-layouts  9.99 us (4%)
  matrix products  9.56 us (4%)
    ppermute x26, waiting for transfers between devices, flip(): lax.ppermute(value, axis, [(i, i ^ bit) for i in range(lax.axis_size(axis...  60.3 us
    ppermute x8, starting transfers between devices, to_plane(): received.append(lax.ppermute(piece, BOTH, perm))  45.7 us
    ppermute x26, starting transfers between devices, flip(): lax.ppermute(value, axis, [(i, i ^ bit) for i in range(lax.axis_size(axis...  28.3 us
    ppermute x2, waiting for transfers between devices, sum_over_four(): lax.ppermute(slots[2] + near, 'prow', [(1, 3), (2, 0), (0, 1), (3, 2)])  25.3 us
    pallas_call x2, Pallas kernels, partial_product(): pl.pallas_call(functools.partial(partial_kernel, places, ratio, count), g...  18.2 us
    ppermute x2, waiting for transfers between devices, sum_over_four(): total = lax.ppermute(slots[1], 'prow', [(0, 2), (2, 3), (3, 1), (1, 0)])  12.6 us
    dot_general x9, matrix products, product(): jnp.dot(left_part, right_part, precision=lax.Precision.HIGH, preferred_el...  9.56 us
    ppermute x2, waiting for transfers between devices, sum_over_four(): near = lax.ppermute(slots[0], 'prow', [(0, 1), (3, 2)])  7.51 us
  transfers between devices with their start and end apart: 42, of which 16 were waited for; matrix products, arithmetic and copies ran while one was open for 11% of the time, Pallas kernels for 7%

profile of v2, /device:TPU:0, one launch (start us, length us, event | category | flops | bytes accessed | tf_op | source)
XLA Modules:
  0.0 247.1 jit_solution(4431913696114628333)
XLA Ops:
  2.1 5.9 %collective-permute-start.18 = (f32[256,128]{1,0:T(8,128)S(1)}, f32[256,128]{1,0:T(8,128)S(1)}, u32[]{:S(2)}, u32[]{:S(2)}) collective-permute-start(f32[256,128]{1,0:T(8,128)S(1)} %get-tuple-element.30), channel_id=1, source_target_pairs={{0,6},{1,7},{2,12},{3,13},{4,18},{5,19},{6,24},{7,25},{8,4},{9,5},... | collective-permute-start | bytes 393224 | tf_op jit(solution)/shard_map/ppermute | solution.py:149
  8.1 4.4 %collective-permute-start.17 = (f32[256,128]{1,0:T(8,128)S(1)}, f32[256,128]{1,0:T(8,128)S(1)}, u32[]{:S(2)}, u32[]{:S(2)}) collective-permute-start(f32[256,128]{1,0:T(8,128)S(1)} %get-tuple-element.29), channel_id=1, source_target_pairs={{0,4},{1,5},{2,14},{3,15},{4,16},{5,17},{6,26},{7,27},{8,6},{9,7},... | collective-permute-start | bytes 393224 | tf_op jit(solution)/shard_map/ppermute | solution.py:149
  12.5 3.5 %collective-permute-start.16 = (f32[256,128]{1,0:T(8,128)S(1)}, f32[256,128]{1,0:T(8,128)}, u32[]{:S(2)}, u32[]{:S(2)}) collective-permute-start(f32[256,128]{1,0:T(8,128)S(1)} %get-tuple-element.28), channel_id=1, source_target_pairs={{0,2},{1,3},{2,8},{3,9},{4,22},{5,23},{6,28},{7,29},{8,0},{9,1},{1... | collective-permute-start | bytes 393224 | tf_op jit(solution)/shard_map/ppermute | solution.py:149
  17.3 4.9 %collective-permute-start.3 = (f32[256,128]{1,0:T(8,128)S(1)}, f32[256,128]{1,0:T(8,128)S(1)}, u32[]{:S(2)}, u32[]{:S(2)}) collective-permute-start(f32[256,128]{1,0:T(8,128)S(1)} %get-tuple-element.22), channel_id=1, source_target_pairs={{0,6},{1,7},{2,12},{3,13},{4,18},{5,19},{6,24},{7,25},{8,4},{9,5},... | collective-permute-start | bytes 393224 | tf_op jit(solution)/shard_map/ppermute | solution.py:149
  27.5 22.4 %collective-permute-start.2 = (f32[256,128]{1,0:T(8,128)S(1)}, f32[256,128]{1,0:T(8,128)}, u32[]{:S(2)}, u32[]{:S(2)}) collective-permute-start(f32[256,128]{1,0:T(8,128)S(1)} %get-tuple-element.21), channel_id=1, source_target_pairs={{0,4},{1,5},{2,14},{3,15},{4,16},{5,17},{6,26},{7,27},{8,6},{9,7},... | collective-permute-start | bytes 393224 | tf_op jit(solution)/shard_map/ppermute | solution.py:149
  49.8 1.9 collective-permute-start.1
  57.6 11.2 %collective-permute-start.19 = (f32[4,256,128]{2,1,0:T(8,128)S(1)}, f32[4,256,128]{2,1,0:T(8,128)}, u32[]{:S(2)}, u32[]{:S(2)}) collective-permute-start(f32[4,256,128]{2,1,0:T(8,128)S(1)} %pad_maximum_fusion.2.refs_0_), channel_id=1, source_target_pairs={{0,2},{1,3},{2,0},{3,1},{4,6},{5,7},{6,4},{7,5},{8,10},{9,11},{10,... | collective-permute-start | bytes 1572872 | tf_op jit(solution)/shard_map/ppermute | solution.py:29
  68.8 1.6 collective-permute-start.20
  70.4 4.3 %collective-permute-done.1 = f32[256,128]{1,0:T(8,128)} collective-permute-done((f32[256,128]{1,0:T(8,128)S(1)}, f32[256,128]{1,0:T(8,128)}, u32[]{:S(2)}, u32[]{:S(2)}) %collective-permute-start.1) | collective-permute-done | bytes 131104 | tf_op jit(solution)/shard_map/ppermute | solution.py:149
  75.8 3.5 %collective-permute-start.4 = (f32[4,256,128]{2,1,0:T(8,128)S(1)}, f32[4,256,128]{2,1,0:T(8,128)}, u32[]{:S(2)}, u32[]{:S(2)}) collective-permute-start(f32[4,256,128]{2,1,0:T(8,128)S(1)} %pad_maximum_fusion.1.refs_0_), channel_id=1, source_target_pairs={{0,2},{1,3},{2,0},{3,1},{4,6},{5,7},{6,4},{7,5},{8,10},{9,11},{10,... | collective-permute-start | bytes 1572872 | tf_op jit(solution)/shard_map/ppermute | solution.py:29
  79.2 1.5 collective-permute-start.6
  83.5 1.4 collective-permute-start.21
  84.8 7.3 %collective-permute-done.4.refs_1_ = f32[4,256,128]{2,1,0:T(8,128)} collective-permute-done((f32[4,256,128]{2,1,0:T(8,128)S(1)}, f32[4,256,128]{2,1,0:T(8,128)}, u32[]{:S(2)}, u32[]{:S(2)}) %collective-permute-start.4) | collective-permute-done | bytes 524320 | tf_op jit(solution)/shard_map/ppermute | solution.py:29
  92.2 22.3 %collective-permute-done.5.refs_2_ = f32[4,256,128]{2,1,0:T(8,128)} collective-permute-done((f32[4,256,128]{2,1,0:T(8,128)S(1)}, f32[4,256,128]{2,1,0:T(8,128)}, u32[]{:S(2)}, u32[]{:S(2)}) %collective-permute-start.5) | collective-permute-done | bytes 524320 | tf_op jit(solution)/shard_map/ppermute | solution.py:29
  118.2 10.8 %partial_product.2 = (f32[256,512]{1,0:T(8,128)S(1)}, f32[256,512]{1,0:T(8,128)S(1)}, f32[256,512]{1,0:T(8,128)S(1)}, f32[256,512]{1,0:T(8,128)S(1)}) custom-call(s32[15]{0:T(128)S(1)} %concatenate.12.meta, f32[1024,2048]{1,0:T(8,128)} %tile_ref.3, f32[4,256,128]{2,1,0:T(8,128)S(1)} %pad_maximum_fusion.1.refs_0_, ...), custom_call_target="tpu_custom_call" | custom-call | flops 6442450944 | bytes 14680064 | tf_op jit(solution)/shard_map/partial_product/pallas_call | solution.py:119
  131.8 7.4 %partial_product.3 = (f32[256,512]{1,0:T(8,128)S(1)}, f32[256,512]{1,0:T(8,128)S(1)}, f32[256,512]{1,0:T(8,128)S(1)}, f32[256,512]{1,0:T(8,128)S(1)}) custom-call(s32[15]{0:T(128)S(1)} %concatenate.13.meta, f32[1024,2048]{1,0:T(8,128)} %tile_ref.3, f32[4,256,128]{2,1,0:T(8,128)S(1)} %pad_maximum_fusion.2.refs_0_, ...), custom_call_target="tpu_custom_call" | custom-call | flops 6442450944 | bytes 14680064 | tf_op jit(solution)/shard_map/partial_product/pallas_call | solution.py:119
  140.5 1.7 collective-permute-start.11
  145.4 7.5 %collective-permute-done.28 = f32[256,512]{1,0:T(8,128)S(1)} collective-permute-done((f32[256,512]{1,0:T(8,128)S(1)}, f32[256,512]{1,0:T(8,128)S(1)}, u32[]{:S(2)}, u32[]{:S(2)}) %collective-permute-start.28) | collective-permute-done | bytes 524320 | tf_op jit(solution)/shard_map/ppermute | solution.py:183
  152.9 5.5 %collective-permute-start.26 = (f32[256,512]{1,0:T(8,128)S(1)}, f32[256,512]{1,0:T(8,128)S(1)}, u32[]{:S(2)}, u32[]{:S(2)}) collective-permute-start(f32[256,512]{1,0:T(8,128)S(1)} %get-tuple-element.32), channel_id=1, source_target_pairs={{0,16},{16,24},{24,8},{8,0},{1,17},{17,25},{25,9},{9,1},{2,18},{18... | collective-permute-start | bytes 1572872 | tf_op jit(solution)/shard_map/ppermute | solution.py:184
  158.7 6.4 %collective-permute-done.11 = f32[256,512]{1,0:T(8,128)S(1)} collective-permute-done((f32[256,512]{1,0:T(8,128)S(1)}, f32[256,512]{1,0:T(8,128)S(1)}, u32[]{:S(2)}, u32[]{:S(2)}) %collective-permute-start.11) | collective-permute-done | bytes 524320 | tf_op jit(solution)/shard_map/ppermute | solution.py:184
  165.2 10.2 %collective-permute-done.14 = f32[256,512]{1,0:T(8,128)S(1)} collective-permute-done((f32[256,512]{1,0:T(8,128)S(1)}, f32[256,512]{1,0:T(8,128)S(1)}, u32[]{:S(2)}, u32[]{:S(2)}) %collective-permute-start.14) | collective-permute-done | bytes 524320 | tf_op jit(solution)/shard_map/ppermute | solution.py:186
  180.5 6.2 %collective-permute-done.26 = f32[256,512]{1,0:T(8,128)S(1)} collective-permute-done((f32[256,512]{1,0:T(8,128)S(1)}, f32[256,512]{1,0:T(8,128)S(1)}, u32[]{:S(2)}, u32[]{:S(2)}) %collective-permute-start.26) | collective-permute-done | bytes 524320 | tf_op jit(solution)/shard_map/ppermute | solution.py:184
  186.7 15.1 %collective-permute-done.29 = f32[256,512]{1,0:T(8,128)S(1)} collective-permute-done((f32[256,512]{1,0:T(8,128)S(1)}, f32[256,512]{1,0:T(8,128)S(1)}, u32[]{:S(2)}, u32[]{:S(2)}) %collective-permute-start.29) | collective-permute-done | bytes 524320 | tf_op jit(solution)/shard_map/ppermute | solution.py:186
  204.5 3.2 %collective-permute-start.31 = (f32[2,64,512]{2,1,0:T(8,128)S(1)}, f32[2,64,512]{2,1,0:T(8,128)S(1)}, u32[]{:S(2)}, u32[]{:S(2)}) collective-permute-start(f32[2,64,512]{2,1,0:T(8,128)S(1)} %get-tuple-element.45), channel_id=1, source_target_pairs={{0,2},{1,3},{2,0},{3,1},{4,6},{5,7},{6,4},{7,5},{8,10},{9,11},{10,... | collective-permute-start | bytes 786440 | tf_op jit(solution)/shard_map/ppermute | solution.py:29
  208.0 1.4 collective-permute-start.38
  209.4 4.9 %collective-permute-done.33 = f32[2,64,512]{2,1,0:T(8,128)S(1)} collective-permute-done((f32[2,64,512]{2,1,0:T(8,128)S(1)}, f32[2,64,512]{2,1,0:T(8,128)S(1)}, u32[]{:S(2)}, u32[]{:S(2)}) %collective-permute-start.33) | collective-permute-done | bytes 262176 | tf_op jit(solution)/shard_map/ppermute | solution.py:29
  214.3 4.7 %collective-permute-done.32 = f32[2,64,512]{2,1,0:T(8,128)S(1)} collective-permute-done((f32[2,64,512]{2,1,0:T(8,128)S(1)}, f32[2,64,512]{2,1,0:T(8,128)S(1)}, u32[]{:S(2)}, u32[]{:S(2)}) %collective-permute-start.32) | collective-permute-done | bytes 262176 | tf_op jit(solution)/shard_map/ppermute | solution.py:29
  219.2 3.5 %collective-permute-done.39 = f32[1,64,512]{2,1,0:T(8,128)S(1)} collective-permute-done((f32[1,64,512]{2,1,0:T(8,128)S(1)}, f32[1,64,512]{2,1,0:T(8,128)S(1)}, u32[]{:S(2)}, u32[]{:S(2)}) %collective-permute-start.39) | collective-permute-done | bytes 131104 | tf_op jit(solution)/shard_map/ppermute | solution.py:29
  222.7 1.5 collective-permute-done.38
  224.4 2.3 collective-permute-done.34
  227.8 1.9 fusion.3
  232.8 12.7 %collective-permute-done.41 = f32[1,64,512]{2,1,0:T(8,128)S(1)} collective-permute-done((f32[1,64,512]{2,1,0:T(8,128)S(1)}, f32[1,64,512]{2,1,0:T(8,128)S(1)}, u32[]{:S(2)}, u32[]{:S(2)}) %collective-permute-start.41) | collective-permute-done | bytes 131104 | tf_op jit(solution)/shard_map/ppermute | solution.py:29
  (129 shorter events, 42.6 us)
Async XLA Ops:
  2.1 25.4 %collective-permute-start.18 = (f32[256,128]{1,0:T(8,128)S(1)}, f32[256,128]{1,0:T(8,128)S(1)}, u32[]{:S(2)}, u32[]{:S(2)}) collective-permute-start(f32[256,128]{1,0:T(8,128)S(1)} %get-tuple-element.30), channel_id=1, source_target_pairs={{0,6},{1,7},{2,12},{3,13},{4,18},{5,19},{6,24},{7,25},{8,4},{9,5},... | collective-permute-start | bytes 393224 | tf_op jit(solution)/shard_map/ppermute | solution.py:149
  8.1 41.8 %collective-permute-start.17 = (f32[256,128]{1,0:T(8,128)S(1)}, f32[256,128]{1,0:T(8,128)S(1)}, u32[]{:S(2)}, u32[]{:S(2)}) collective-permute-start(f32[256,128]{1,0:T(8,128)S(1)} %get-tuple-element.29), channel_id=1, source_target_pairs={{0,4},{1,5},{2,14},{3,15},{4,16},{5,17},{6,26},{7,27},{8,6},{9,7},... | collective-permute-start | bytes 393224 | tf_op jit(solution)/shard_map/ppermute | solution.py:149
  12.5 39.7 %collective-permute-start.16 = (f32[256,128]{1,0:T(8,128)S(1)}, f32[256,128]{1,0:T(8,128)}, u32[]{:S(2)}, u32[]{:S(2)}) collective-permute-start(f32[256,128]{1,0:T(8,128)S(1)} %get-tuple-element.28), channel_id=1, source_target_pairs={{0,2},{1,3},{2,8},{3,9},{4,22},{5,23},{6,28},{7,29},{8,0},{9,1},{1... | collective-permute-start | bytes 393224 | tf_op jit(solution)/shard_map/ppermute | solution.py:149
  16.0 40.6 %collective-permute-start.15 = (f32[256,128]{1,0:T(8,128)S(1)}, f32[256,128]{1,0:T(8,128)}, u32[]{:S(2)}, u32[]{:S(2)}) collective-permute-start(f32[256,128]{1,0:T(8,128)S(1)} %get-tuple-element.27), channel_id=1, source_target_pairs={{0,0},{1,1},{2,10},{3,11},{4,20},{5,21},{6,30},{7,31},{8,2},{9,3},... | collective-permute-start | bytes 393224 | tf_op jit(solution)/shard_map/ppermute | solution.py:149
  17.3 51.5 %collective-permute-start.3 = (f32[256,128]{1,0:T(8,128)S(1)}, f32[256,128]{1,0:T(8,128)S(1)}, u32[]{:S(2)}, u32[]{:S(2)}) collective-permute-start(f32[256,128]{1,0:T(8,128)S(1)} %get-tuple-element.22), channel_id=1, source_target_pairs={{0,6},{1,7},{2,12},{3,13},{4,18},{5,19},{6,24},{7,25},{8,4},{9,5},... | collective-permute-start | bytes 393224 | tf_op jit(solution)/shard_map/ppermute | solution.py:149
  27.5 43.0 %collective-permute-start.2 = (f32[256,128]{1,0:T(8,128)S(1)}, f32[256,128]{1,0:T(8,128)}, u32[]{:S(2)}, u32[]{:S(2)}) collective-permute-start(f32[256,128]{1,0:T(8,128)S(1)} %get-tuple-element.21), channel_id=1, source_target_pairs={{0,4},{1,5},{2,14},{3,15},{4,16},{5,17},{6,26},{7,27},{8,6},{9,7},... | collective-permute-start | bytes 393224 | tf_op jit(solution)/shard_map/ppermute | solution.py:149
  49.8 24.9 %collective-permute-start.1 = (f32[256,128]{1,0:T(8,128)S(1)}, f32[256,128]{1,0:T(8,128)}, u32[]{:S(2)}, u32[]{:S(2)}) collective-permute-start(f32[256,128]{1,0:T(8,128)S(1)} %get-tuple-element.20), channel_id=1, source_target_pairs={{0,2},{1,3},{2,8},{3,9},{4,22},{5,23},{6,28},{7,29},{8,0},{9,1},{1... | collective-permute-start | bytes 393224 | tf_op jit(solution)/shard_map/ppermute | solution.py:149
  52.2 22.5 %collective-permute-start = (f32[256,128]{1,0:T(8,128)S(1)}, f32[256,128]{1,0:T(8,128)}, u32[]{:S(2)}, u32[]{:S(2)}) collective-permute-start(f32[256,128]{1,0:T(8,128)S(1)} %get-tuple-element.19), channel_id=1, source_target_pairs={{0,0},{1,1},{2,10},{3,11},{4,20},{5,21},{6,30},{7,31},{8,2},{9,3},... | collective-permute-start | bytes 393224 | tf_op jit(solution)/shard_map/ppermute | solution.py:149
  57.6 25.8 %collective-permute-start.19 = (f32[4,256,128]{2,1,0:T(8,128)S(1)}, f32[4,256,128]{2,1,0:T(8,128)}, u32[]{:S(2)}, u32[]{:S(2)}) collective-permute-start(f32[4,256,128]{2,1,0:T(8,128)S(1)} %pad_maximum_fusion.2.refs_0_), channel_id=1, source_target_pairs={{0,2},{1,3},{2,0},{3,1},{4,6},{5,7},{6,4},{7,5},{8,10},{9,11},{10,... | collective-permute-start | bytes 1572872 | tf_op jit(solution)/shard_map/ppermute | solution.py:29
  68.8 16.0 %collective-permute-start.20 = (f32[4,256,128]{2,1,0:T(8,128)S(1)}, f32[4,256,128]{2,1,0:T(8,128)}, u32[]{:S(2)}, u32[]{:S(2)}) collective-permute-start(f32[4,256,128]{2,1,0:T(8,128)S(1)} %pad_maximum_fusion.2.refs_0_), channel_id=1, source_target_pairs={{0,4},{1,5},{2,6},{3,7},{4,0},{5,1},{6,2},{7,3},{8,12},{9,13},{10,... | collective-permute-start | bytes 1572872 | tf_op jit(solution)/shard_map/ppermute | solution.py:29
  75.8 16.4 %collective-permute-start.4 = (f32[4,256,128]{2,1,0:T(8,128)S(1)}, f32[4,256,128]{2,1,0:T(8,128)}, u32[]{:S(2)}, u32[]{:S(2)}) collective-permute-start(f32[4,256,128]{2,1,0:T(8,128)S(1)} %pad_maximum_fusion.1.refs_0_), channel_id=1, source_target_pairs={{0,2},{1,3},{2,0},{3,1},{4,6},{5,7},{6,4},{7,5},{8,10},{9,11},{10,... | collective-permute-start | bytes 1572872 | tf_op jit(solution)/shard_map/ppermute | solution.py:29
  79.2 35.2 %collective-permute-start.5 = (f32[4,256,128]{2,1,0:T(8,128)S(1)}, f32[4,256,128]{2,1,0:T(8,128)}, u32[]{:S(2)}, u32[]{:S(2)}) collective-permute-start(f32[4,256,128]{2,1,0:T(8,128)S(1)} %pad_maximum_fusion.1.refs_0_), channel_id=1, source_target_pairs={{0,4},{1,5},{2,6},{3,7},{4,0},{5,1},{6,2},{7,3},{8,12},{9,13},{10,... | collective-permute-start | bytes 1572872 | tf_op jit(solution)/shard_map/ppermute | solution.py:29
  79.2 35.3 %collective-permute-start.6 = (f32[4,256,128]{2,1,0:T(8,128)S(1)}, f32[4,256,128]{2,1,0:T(8,128)}, u32[]{:S(2)}, u32[]{:S(2)}) collective-permute-start(f32[4,256,128]{2,1,0:T(8,128)S(1)} %pad_maximum_fusion.1.refs_0_), channel_id=1, source_target_pairs={{0,6},{1,7},{2,4},{3,5},{4,2},{5,3},{6,0},{7,1},{8,14},{9,15},{10,... | collective-permute-start | bytes 1572872 | tf_op jit(solution)/shard_map/ppermute | solution.py:29
  83.5 32.8 %collective-permute-start.21 = (f32[4,256,128]{2,1,0:T(8,128)S(1)}, f32[4,256,128]{2,1,0:T(8,128)S(1)}, u32[]{:S(2)}, u32[]{:S(2)}) collective-permute-start(f32[4,256,128]{2,1,0:T(8,128)S(1)} %pad_maximum_fusion.2.refs_0_), channel_id=1, source_target_pairs={{0,6},{1,7},{2,4},{3,5},{4,2},{5,3},{6,0},{7,1},{8,14},{9,15},{10,... | collective-permute-start | bytes 1572872 | tf_op jit(solution)/shard_map/ppermute | solution.py:29
  84.8 31.5 %collective-permute-start.7 = (f32[4,256,128]{2,1,0:T(8,128)S(1)}, f32[4,256,128]{2,1,0:T(8,128)S(1)}, u32[]{:S(2)}, u32[]{:S(2)}) collective-permute-start(f32[4,256,128]{2,1,0:T(8,128)S(1)} %pad_maximum_fusion.1.refs_0_), channel_id=1, source_target_pairs={{0,1},{1,0},{2,3},{3,2},{4,5},{5,4},{6,7},{7,6},{8,9},{9,8},{10,11... | collective-permute-start | bytes 1572872 | tf_op jit(solution)/shard_map/ppermute | solution.py:29
  92.2 24.6 %collective-permute-start.8 = (f32[4,256,128]{2,1,0:T(8,128)}, f32[4,256,128]{2,1,0:T(8,128)S(1)}, u32[]{:S(2)}, u32[]{:S(2)}) collective-permute-start(f32[4,256,128]{2,1,0:T(8,128)} %collective-permute-done.4.refs_1_), channel_id=1, source_target_pairs={{0,1},{1,0},{2,3},{3,2},{4,5},{5,4},{6,7},{7,6},{8,9},{9,8},{10,11... | collective-permute-start | bytes 1572872 | tf_op jit(solution)/shard_map/ppermute | solution.py:29
  116.3 14.6 %collective-permute-start.23 = (f32[4,256,128]{2,1,0:T(8,128)}, f32[4,256,128]{2,1,0:T(8,128)S(1)}, u32[]{:S(2)}, u32[]{:S(2)}) collective-permute-start(f32[4,256,128]{2,1,0:T(8,128)} %collective-permute-done.19.refs_1_), channel_id=1, source_target_pairs={{0,1},{1,0},{2,3},{3,2},{4,5},{5,4},{6,7},{7,6},{8,9},{9,8},{10,11... | collective-permute-start | bytes 1572872 | tf_op jit(solution)/shard_map/ppermute | solution.py:29
  116.8 14.2 %collective-permute-start.24 = (f32[4,256,128]{2,1,0:T(8,128)}, f32[4,256,128]{2,1,0:T(8,128)S(1)}, u32[]{:S(2)}, u32[]{:S(2)}) collective-permute-start(f32[4,256,128]{2,1,0:T(8,128)} %collective-permute-done.20.refs_2_), channel_id=1, source_target_pairs={{0,1},{1,0},{2,3},{3,2},{4,5},{5,4},{6,7},{7,6},{8,9},{9,8},{10,11... | collective-permute-start | bytes 1572872 | tf_op jit(solution)/shard_map/ppermute | solution.py:29
  116.9 14.1 %collective-permute-start.25 = (f32[4,256,128]{2,1,0:T(8,128)S(1)}, f32[4,256,128]{2,1,0:T(8,128)S(1)}, u32[]{:S(2)}, u32[]{:S(2)}) collective-permute-start(f32[4,256,128]{2,1,0:T(8,128)S(1)} %collective-permute-done.21.refs_3_), channel_id=1, source_target_pairs={{0,1},{1,0},{2,3},{3,2},{4,5},{5,4},{6,7},{7,6},{8,9},{9,8},{10,11... | collective-permute-start | bytes 1572872 | tf_op jit(solution)/shard_map/ppermute | solution.py:29
  130.3 28.2 %collective-permute-start.12 = (f32[256,512]{1,0:T(8,128)S(1)}, f32[256,512]{1,0:T(8,128)S(1)}, u32[]{:S(2)}, u32[]{:S(2)}) collective-permute-start(f32[256,512]{1,0:T(8,128)S(1)} %get-tuple-element.25), channel_id=1, source_target_pairs={{8,16},{16,8},{9,17},{17,9},{10,18},{18,10},{11,19},{19,11},{12,20... | collective-permute-start | bytes 1572872 | tf_op jit(solution)/shard_map/ppermute | solution.py:185
  140.5 24.6 %collective-permute-start.11 = (f32[256,512]{1,0:T(8,128)S(1)}, f32[256,512]{1,0:T(8,128)S(1)}, u32[]{:S(2)}, u32[]{:S(2)}) collective-permute-start(f32[256,512]{1,0:T(8,128)S(1)} %get-tuple-element.24), channel_id=1, source_target_pairs={{0,16},{16,24},{24,8},{8,0},{1,17},{17,25},{25,9},{9,1},{2,18},{18... | collective-permute-start | bytes 1572872 | tf_op jit(solution)/shard_map/ppermute | solution.py:184
  142.3 33.1 %collective-permute-start.14 = (f32[256,512]{1,0:T(8,128)S(1)}, f32[256,512]{1,0:T(8,128)S(1)}, u32[]{:S(2)}, u32[]{:S(2)}) collective-permute-start(f32[256,512]{1,0:T(8,128)S(1)} %add.180), channel_id=1, source_target_pairs={{8,24},{16,0},{0,8},{24,16},{9,25},{17,1},{1,9},{25,17},{10,26},{1... | collective-permute-start | bytes 1572872 | tf_op jit(solution)/shard_map/ppermute | solution.py:186
  144.7 35.8 %collective-permute-start.27 = (f32[256,512]{1,0:T(8,128)S(1)}, f32[256,512]{1,0:T(8,128)S(1)}, u32[]{:S(2)}, u32[]{:S(2)}) collective-permute-start(f32[256,512]{1,0:T(8,128)S(1)} %get-tuple-element.33), channel_id=1, source_target_pairs={{8,16},{16,8},{9,17},{17,9},{10,18},{18,10},{11,19},{19,11},{12,20... | collective-permute-start | bytes 1572872 | tf_op jit(solution)/shard_map/ppermute | solution.py:185
  152.9 33.8 %collective-permute-start.26 = (f32[256,512]{1,0:T(8,128)S(1)}, f32[256,512]{1,0:T(8,128)S(1)}, u32[]{:S(2)}, u32[]{:S(2)}) collective-permute-start(f32[256,512]{1,0:T(8,128)S(1)} %get-tuple-element.32), channel_id=1, source_target_pairs={{0,16},{16,24},{24,8},{8,0},{1,17},{17,25},{25,9},{9,1},{2,18},{18... | collective-permute-start | bytes 1572872 | tf_op jit(solution)/shard_map/ppermute | solution.py:184
  158.5 43.3 %collective-permute-start.29 = (f32[256,512]{1,0:T(8,128)S(1)}, f32[256,512]{1,0:T(8,128)S(1)}, u32[]{:S(2)}, u32[]{:S(2)}) collective-permute-start(f32[256,512]{1,0:T(8,128)S(1)} %add.184), channel_id=1, source_target_pairs={{8,24},{16,0},{0,8},{24,16},{9,25},{17,1},{1,9},{25,17},{10,26},{1... | collective-permute-start | bytes 1572872 | tf_op jit(solution)/shard_map/ppermute | solution.py:186
  179.3 24.6 %collective-permute-start.30 = (f32[2,4,64,512]{3,2,1,0:T(8,128)S(1)}, f32[2,4,64,512]{3,2,1,0:T(8,128)S(1)}, u32[]{:S(2)}, u32[]{:S(2)}) collective-permute-start(f32[2,4,64,512]{3,2,1,0:T(8,128)S(1)} %fusion.5), channel_id=1, source_target_pairs={{0,1},{1,0},{2,3},{3,2},{4,5},{5,4},{6,7},{7,6},{8,9},{9,8},{10,11... | collective-permute-start | bytes 3145736 | tf_op jit(solution)/shard_map/ppermute | solution.py:29
  204.2 14.8 %collective-permute-start.32 = (f32[2,64,512]{2,1,0:T(8,128)S(1)}, f32[2,64,512]{2,1,0:T(8,128)S(1)}, u32[]{:S(2)}, u32[]{:S(2)}) collective-permute-start(f32[2,64,512]{2,1,0:T(8,128)S(1)} %get-tuple-element.47), channel_id=1, source_target_pairs={{0,4},{1,5},{2,6},{3,7},{4,0},{5,1},{6,2},{7,3},{8,12},{9,13},{10,... | collective-permute-start | bytes 786440 | tf_op jit(solution)/shard_map/ppermute | solution.py:29
  204.5 14.5 %collective-permute-start.31 = (f32[2,64,512]{2,1,0:T(8,128)S(1)}, f32[2,64,512]{2,1,0:T(8,128)S(1)}, u32[]{:S(2)}, u32[]{:S(2)}) collective-permute-start(f32[2,64,512]{2,1,0:T(8,128)S(1)} %get-tuple-element.45), channel_id=1, source_target_pairs={{0,2},{1,3},{2,0},{3,1},{4,6},{5,7},{6,4},{7,5},{8,10},{9,11},{10,... | collective-permute-start | bytes 786440 | tf_op jit(solution)/shard_map/ppermute | solution.py:29
  207.9 14.9 %collective-permute-start.39 = (f32[1,64,512]{2,1,0:T(8,128)S(1)}, f32[1,64,512]{2,1,0:T(8,128)S(1)}, u32[]{:S(2)}, u32[]{:S(2)}) collective-permute-start(f32[1,64,512]{2,1,0:T(8,128)S(1)} %get-tuple-element.49), channel_id=1, source_target_pairs={{0,6},{1,7},{2,4},{3,5},{4,2},{5,3},{6,0},{7,1},{8,14},{9,15},{10,... | collective-permute-start | bytes 393224 | tf_op jit(solution)/shard_map/ppermute | solution.py:29
  208.0 16.2 %collective-permute-start.38 = (f32[1,64,512]{2,1,0:T(8,128)S(1)}, f32[1,64,512]{2,1,0:T(8,128)S(1)}, u32[]{:S(2)}, u32[]{:S(2)}) collective-permute-start(f32[1,64,512]{2,1,0:T(8,128)S(1)} %get-tuple-element.50), channel_id=1, source_target_pairs={{0,4},{1,5},{2,6},{3,7},{4,0},{5,1},{6,2},{7,3},{8,12},{9,13},{10,... | collective-permute-start | bytes 393224 | tf_op jit(solution)/shard_map/ppermute | solution.py:29
  226.7 18.8 %collective-permute-start.35 = (f32[2,64,512]{2,1,0:T(8,128)S(1)}, f32[2,64,512]{2,1,0:T(8,128)S(1)}, u32[]{:S(2)}, u32[]{:S(2)}) collective-permute-start(f32[2,64,512]{2,1,0:T(8,128)S(1)} %add.199), channel_id=1, source_target_pairs={{0,16},{8,24},{16,0},{24,8},{1,17},{9,25},{17,1},{25,9},{2,18},{10... | collective-permute-start | bytes 786440 | tf_op jit(solution)/shard_map/ppermute | solution.py:29
  230.7 14.8 %collective-permute-start.41 = (f32[1,64,512]{2,1,0:T(8,128)S(1)}, f32[1,64,512]{2,1,0:T(8,128)S(1)}, u32[]{:S(2)}, u32[]{:S(2)}) collective-permute-start(f32[1,64,512]{2,1,0:T(8,128)S(1)} %add.207), channel_id=1, source_target_pairs={{0,16},{8,24},{16,0},{24,8},{1,17},{9,25},{17,1},{25,9},{2,18},{10... | collective-permute-start | bytes 393224 | tf_op jit(solution)/shard_map/ppermute | solution.py:29
  (18 other events, 396.9 us)

commit v3 on v2

--- a/solution.py
+++ b/solution.py
@@ -2,7 +2,6 @@
 
 import jax
 import jax.numpy as jnp
-import numpy as np
 from jax import lax
 from jax.experimental import pallas as pl
 from jax.experimental.pallas import tpu as pltpu
@@ -27,43 +26,6 @@
 
 def flip(value, axis, bit):
     return lax.ppermute(value, axis, [(i, i ^ bit) for i in range(lax.axis_size(axis))])
-
-
-def spread_kernel(meta, factor_ref, *out_refs):
-    nsuper = factor_ref.shape[0]
-    count = len(out_refs) // nsuper
-    width = out_refs[0].shape[1]
-    for number in range(nsuper):
-        for r in range(count):
-            start = pl.multiple_of((meta[0] ^ r) * width, width)
-            out_refs[number * count + r][...] = factor_ref[number, :, pl.ds(start, width)]
-
-
-def spread(meta, factor, count):
-    nsuper, unit_rows, columns = factor.shape
-    width = columns // count
-    if width % LANES:
-        pieces = []
-        for number in range(nsuper):
-            for r in range(count):
-                start = (meta[0] ^ r) * width
-                pieces.append(lax.dynamic_slice_in_dim(factor[number], start, width, 1))
-        return pieces
-    return pl.pallas_call(
-        spread_kernel,
-        grid_spec=pltpu.PrefetchScalarGridSpec(
-            num_scalar_prefetch=1,
-            grid=(1,),
-            in_specs=[pl.BlockSpec(factor.shape, lambda i, m: (0, 0, 0))],
-            out_specs=[pl.BlockSpec((unit_rows, width), lambda i, m: (0, 0))] * (nsuper * count),
-        ),
-        out_shape=[jax.ShapeDtypeStruct((unit_rows, width), factor.dtype)] * (nsuper * count),
-        compiler_params=pltpu.CompilerParams(vmem_limit_bytes=VMEM_LIMIT),
-        cost_estimate=pl.CostEstimate(
-            flops=0, bytes_accessed=2 * factor.size * 4, transcendentals=0
-        ),
-        name="spread",
-    )(meta, factor)
 
 
 def partial_kernel(places, ratio, count, meta, tile_ref, *refs):
@@ -85,7 +47,7 @@
             column = owner // ratio
             lane = pl.multiple_of(column * width, width)
             for r in range(ref.shape[0]):
-                unit = (owner % ratio) * count + (column ^ meta[1] ^ r)
+                unit = (owner % ratio) * count + r
                 rows = pl.ds(pl.multiple_of(unit * unit_rows, unit_rows), unit_rows)
                 high, low = halves(ref[r])
                 right_high[rows, pl.ds(lane, width)] = high
@@ -136,18 +98,10 @@
     )(meta, tiles, *pieces)
 
 
-def to_plane(sends, count, ratio):
-    pcol_count = count * ratio
-    received = []
-    for r, piece in enumerate(sends):
-        perm = []
-        for z in range(count):
-            for c in range(count):
-                for k in range(ratio):
-                    source = z * pcol_count + c * ratio + k
-                    perm.append((source, c * pcol_count + (c ^ z ^ r) * ratio + k))
-        received.append(lax.ppermute(piece, BOTH, perm))
-    return jnp.stack(received)
+def to_plane(pieces, count, ratio):
+    groups = [[c * ratio + k for c in range(count)] for k in range(ratio)]
+    spread = lax.all_to_all(pieces, "pcol", 0, 0, axis_index_groups=groups)
+    return lax.all_to_all(spread, "prow", 0, 0)
 
 
 def gather_plane(own, pcol_count):
@@ -162,13 +116,8 @@
 def gather_whole(own, count, ratio):
     _, unit_rows, width = own.shape
     gathered = lax.all_gather(own, "pcol", axis=0)
-    column = np.arange(count)[None, None, :]
-    owner = np.broadcast_to(
-        column * ratio + np.arange(ratio)[:, None, None], (ratio, count, count)
-    )
-    part = jnp.asarray(column ^ np.arange(count)[None, :, None]) ^ lax.axis_index("prow")
-    part = jnp.broadcast_to(part, owner.shape)
-    rows = jnp.transpose(gathered[owner, part], (0, 1, 3, 2, 4))
+    split = gathered.reshape(count, ratio, count, unit_rows, width)
+    rows = jnp.transpose(split, (1, 2, 3, 0, 4))
     return rows.reshape(ratio * count * unit_rows, count * width)
 
 
@@ -268,13 +217,12 @@
         for number in range(nsuper)
     ]
 
-    target = ((pcol_index // ratio) ^ z).astype(jnp.int32)
-    sends = spread(target[None], factor, count)
     local = jnp.where(keep, factor, 0.0)
+    cut = jnp.swapaxes(factor.reshape(nsuper, unit_rows, count, width), 1, 2)
 
     partials = []
     for number in range(nsuper):
-        own = to_plane(sends[number * count : (number + 1) * count], count, ratio)
+        own = to_plane(cut[number], count, ratio)
         if width % LANES:
             pieces, places = [gather_whole(own, count, ratio)], [None]
         else:

time: 247 us -> 231 us (0.935)
  starting transfers between devices: 86.6 us -> 54 us
  blocking collectives: 0 us -> 23.9 us
  Pallas kernels: 18.3 us -> 12.8 us
  other arithmetic: 10.9 us -> 6.28 us
  waiting for transfers between devices: 110 us -> 114 us
    ppermute x8 -> x0, starting transfers between devices: 45.7 us -> none  [to_plane(): received.append(lax.ppermute(piece, BOTH, perm))]
    all_to_all x0 -> x2, blocking collectives: none -> 23.9 us  [to_plane(): spread = lax.all_to_all(pieces, 'pcol', 0, 0, axis_index_groups=groups)]
    all_to_all x0 -> x2, waiting for transfers between devices: none -> 19 us  [to_plane(): return lax.all_to_all(spread, 'prow', 0, 0)]
    ppermute x26, waiting for transfers between devices: 60.3 us -> 51.9 us  [flip(): lax.ppermute(value, axis, [(i, i ^ bit) for i in range(lax.axis_size(axis...]
    all_to_all x0 -> x2, starting transfers between devices: none -> 8.34 us  [to_plane(): return lax.all_to_all(spread, 'prow', 0, 0)]
    pallas_call x2, Pallas kernels: 18.2 us -> 12.8 us  [partial_product(): pl.pallas_call(functools.partial(partial_kernel, places, ratio, count), g...]
    ppermute x2, starting transfers between devices: 2.65 us -> 7.65 us  [sum_over_four(): near = lax.ppermute(slots[0], 'prow', [(0, 1), (3, 2)])]
    ppermute x8 -> x0, waiting for transfers between devices: 4.69 us -> none  [to_plane(): received.append(lax.ppermute(piece, BOTH, perm))]
  transfers between devices with their start and end apart: 42 -> 36, of which waited for: 16 -> 19; matrix products, arithmetic and copies ran while one was open for 11% -> 8% of each run, Pallas kernels for 7% -> 6%
where the time goes in v3:
time: 231 us; the launch traced here: 230 us
  waiting for transfers between devices  114 us (49%)
  starting transfers between devices  54 us (23%)
  blocking collectives  23.9 us (10%)
  Pallas kernels  12.8 us (6%)
  matrix products  9.52 us (4%)
  local copies, waits for them, and re-layouts  8.82 us (4%)
  other arithmetic  6.28 us (3%)
    ppermute x26, waiting for transfers between devices, flip(): lax.ppermute(value, axis, [(i, i ^ bit) for i in range(lax.axis_size(axis...  51.9 us
    ppermute x26, starting transfers between devices, flip(): lax.ppermute(value, axis, [(i, i ^ bit) for i in range(lax.axis_size(axis...  29.1 us
    ppermute x2, waiting for transfers between devices, sum_over_four(): lax.ppermute(slots[2] + near, 'prow', [(1, 3), (2, 0), (0, 1), (3, 2)])  27.9 us
    all_to_all x2, blocking collectives, to_plane(): spread = lax.all_to_all(pieces, 'pcol', 0, 0, axis_index_groups=groups)  23.9 us
    all_to_all x2, waiting for transfers between devices, to_plane(): return lax.all_to_all(spread, 'prow', 0, 0)  19 us
    pallas_call x2, Pallas kernels, partial_product(): pl.pallas_call(functools.partial(partial_kernel, places, ratio, count), g...  12.8 us
    dot_general x9, matrix products, product(): jnp.dot(left_part, right_part, precision=lax.Precision.HIGH, preferred_el...  9.52 us
    ppermute x2, waiting for transfers between devices, sum_over_four(): total = lax.ppermute(slots[1], 'prow', [(0, 2), (2, 3), (3, 1), (1, 0)])  9.25 us
  transfers between devices with their start and end apart: 36, of which 19 were waited for; matrix products, arithmetic and copies ran while one was open for 8% of the time, Pallas kernels for 6%

profile of v3, /device:TPU:0, one launch (start us, length us, event | category | flops | bytes accessed | tf_op | source)
XLA Modules:
  0.0 230.3 jit_solution(10316666852837715838)
XLA Ops:
  0.6 1.6 copy.18
  2.7 13.6 %all_to_all.20 = f32[4,256,128]{2,1,0:T(8,128)} all-to-all(f32[4,256,128]{2,1,0:T(8,128)S(1)} %get-tuple-element.33), channel_id=1, replica_groups={{0,2,4,6},{1,3,5,7},{8,10,12,14},{9,11,13,15},{16,18,20,22},{17,19,21,2..., dimensions={0} | all-to-all | bytes 1048576 | tf_op jit(solution)/shard_map/all_to_all | solution.py:103
  16.3 10.3 %all_to_all.21 = f32[4,256,128]{2,1,0:T(8,128)} all-to-all(f32[4,256,128]{2,1,0:T(8,128)S(1)} %get-tuple-element.32), channel_id=1, replica_groups={{0,2,4,6},{1,3,5,7},{8,10,12,14},{9,11,13,15},{16,18,20,22},{17,19,21,2..., dimensions={0} | all-to-all | bytes 1048576 | tf_op jit(solution)/shard_map/all_to_all | solution.py:103
  26.7 4.9 %all-to-all-start.3 = ((f32[4,256,128]{2,1,0:T(8,128)}), f32[4,256,128]{2,1,0:T(8,128)S(1)}, u32[]{:S(2)}, u32[]{:S(2)}) async-start(f32[4,256,128]{2,1,0:T(8,128)} %all_to_all.20), calls=%async_computation.3 | async-start | bytes 1048576 | tf_op jit(solution)/shard_map/all_to_all | solution.py:104
  31.8 11.4 %all-to-all-done.3.refs_0_ = f32[4,256,128]{2,1,0:T(8,128)S(1)} async-done(((f32[4,256,128]{2,1,0:T(8,128)}), f32[4,256,128]{2,1,0:T(8,128)S(1)}, u32[]{:S(2)}, u32[]{:S(2)}) %all-to-all-start.3) | async-done | bytes 524320 | tf_op jit(solution)/shard_map/all_to_all | solution.py:104
  43.2 3.5 %all-to-all-start.1 = ((f32[4,256,128]{2,1,0:T(8,128)}), f32[4,256,128]{2,1,0:T(8,128)S(1)}, u32[]{:S(2)}, u32[]{:S(2)}) async-start(f32[4,256,128]{2,1,0:T(8,128)} %all_to_all.21), calls=%async_computation.1 | async-start | bytes 1048576 | tf_op jit(solution)/shard_map/all_to_all | solution.py:104
  51.4 7.6 %all-to-all-done.1.refs_0_ = f32[4,256,128]{2,1,0:T(8,128)S(1)} async-done(((f32[4,256,128]{2,1,0:T(8,128)}), f32[4,256,128]{2,1,0:T(8,128)S(1)}, u32[]{:S(2)}, u32[]{:S(2)}) %all-to-all-start.1) | async-done | bytes 524320 | tf_op jit(solution)/shard_map/all_to_all | solution.py:104
  60.5 2.0 collective-permute-start.2
  65.4 10.1 %collective-permute-done.refs_1_ = f32[4,256,128]{2,1,0:T(8,128)} collective-permute-done((f32[4,256,128]{2,1,0:T(8,128)S(1)}, f32[4,256,128]{2,1,0:T(8,128)}, u32[]{:S(2)}, u32[]{:S(2)}) %collective-permute-start) | collective-permute-done | bytes 524320 | tf_op jit(solution)/shard_map/ppermute | solution.py:28
  76.2 11.3 %collective-permute-done.2.refs_3_ = f32[4,256,128]{2,1,0:T(8,128)} collective-permute-done((f32[4,256,128]{2,1,0:T(8,128)S(1)}, f32[4,256,128]{2,1,0:T(8,128)}, u32[]{:S(2)}, u32[]{:S(2)}) %collective-permute-start.2) | collective-permute-done | bytes 524320 | tf_op jit(solution)/shard_map/ppermute | solution.py:28
  89.9 5.5 %collective-permute-done.13.refs_3_ = f32[4,256,128]{2,1,0:T(8,128)S(1)} collective-permute-done((f32[4,256,128]{2,1,0:T(8,128)S(1)}, f32[4,256,128]{2,1,0:T(8,128)S(1)}, u32[]{:S(2)}, u32[]{:S(2)}) %collective-permute-start.13) | collective-permute-done | bytes 524320 | tf_op jit(solution)/shard_map/ppermute | solution.py:28
  97.2 7.6 %partial_product.2 = (f32[256,512]{1,0:T(8,128)S(1)}, f32[256,512]{1,0:T(8,128)S(1)}, f32[256,512]{1,0:T(8,128)S(1)}, f32[256,512]{1,0:T(8,128)S(1)}) custom-call(s32[15]{0:T(128)S(1)} %concatenate.12.meta, f32[1024,2048]{1,0:T(8,128)} %tile_ref.3, f32[4,256,128]{2,1,0:T(8,128)S(1)} %all-to-all-done.1.refs_0_, f32[4,256,128]{2,1,0:T(8,128)} %collective-permute-done.refs_1_, ...), custom_call_target="tpu_custom_call" | custom-call | flops 6442450944 | bytes 14680064 | tf_op jit(solution)/shard_map/partial_product/pallas_call | solution.py:81
  104.7 3.8 %collective-permute-start.9 = (f32[256,512]{1,0:T(8,128)S(1)}, f32[256,512]{1,0:T(8,128)S(1)}, u32[]{:S(2)}, u32[]{:S(2)}) collective-permute-start(f32[256,512]{1,0:T(8,128)S(1)} %get-tuple-element.13), channel_id=1, source_target_pairs={{0,8},{24,16},{1,9},{25,17},{2,10},{26,18},{3,11},{27,19},{4,12},{... | collective-permute-start | bytes 1572872 | tf_op jit(solution)/shard_map/ppermute | solution.py:132
  110.0 5.3 %partial_product.3 = (f32[256,512]{1,0:T(8,128)S(1)}, f32[256,512]{1,0:T(8,128)S(1)}, f32[256,512]{1,0:T(8,128)S(1)}, f32[256,512]{1,0:T(8,128)S(1)}) custom-call(s32[15]{0:T(128)S(1)} %concatenate.13.meta, f32[1024,2048]{1,0:T(8,128)} %tile_ref.3, f32[4,256,128]{2,1,0:T(8,128)S(1)} %all-to-all-done.3.refs_0_, ...), custom_call_target="tpu_custom_call" | custom-call | flops 6442450944 | bytes 14680064 | tf_op jit(solution)/shard_map/partial_product/pallas_call | solution.py:81
  115.3 3.9 %collective-permute-start.20 = (f32[256,512]{1,0:T(8,128)S(1)}, f32[256,512]{1,0:T(8,128)S(1)}, u32[]{:S(2)}, u32[]{:S(2)}) collective-permute-start(f32[256,512]{1,0:T(8,128)S(1)} %get-tuple-element.17), channel_id=1, source_target_pairs={{0,8},{24,16},{1,9},{25,17},{2,10},{26,18},{3,11},{27,19},{4,12},{... | collective-permute-start | bytes 1572872 | tf_op jit(solution)/shard_map/ppermute | solution.py:132
  119.9 2.5 %collective-permute-start.10 = (f32[256,512]{1,0:T(8,128)S(1)}, f32[256,512]{1,0:T(8,128)S(1)}, u32[]{:S(2)}, u32[]{:S(2)}) collective-permute-start(f32[256,512]{1,0:T(8,128)S(1)} %add.180), channel_id=1, source_target_pairs={{8,24},{16,0},{0,8},{24,16},{9,25},{17,1},{1,9},{25,17},{10,26},{1... | collective-permute-start | bytes 1572872 | tf_op jit(solution)/shard_map/ppermute | solution.py:135
  124.3 5.3 %collective-permute-done.20 = f32[256,512]{1,0:T(8,128)S(1)} collective-permute-done((f32[256,512]{1,0:T(8,128)S(1)}, f32[256,512]{1,0:T(8,128)S(1)}, u32[]{:S(2)}, u32[]{:S(2)}) %collective-permute-start.20) | collective-permute-done | bytes 524320 | tf_op jit(solution)/shard_map/ppermute | solution.py:132
  129.6 4.7 %collective-permute-start.18 = (f32[256,512]{1,0:T(8,128)S(1)}, f32[256,512]{1,0:T(8,128)S(1)}, u32[]{:S(2)}, u32[]{:S(2)}) collective-permute-start(f32[256,512]{1,0:T(8,128)S(1)} %get-tuple-element.16), channel_id=1, source_target_pairs={{0,16},{16,24},{24,8},{8,0},{1,17},{17,25},{25,9},{9,1},{2,18},{18... | collective-permute-start | bytes 1572872 | tf_op jit(solution)/shard_map/ppermute | solution.py:133
  134.6 6.9 %collective-permute-done.7 = f32[256,512]{1,0:T(8,128)S(1)} collective-permute-done((f32[256,512]{1,0:T(8,128)S(1)}, f32[256,512]{1,0:T(8,128)S(1)}, u32[]{:S(2)}, u32[]{:S(2)}) %collective-permute-start.7) | collective-permute-done | bytes 524320 | tf_op jit(solution)/shard_map/ppermute | solution.py:133
  141.5 10.6 %collective-permute-done.10 = f32[256,512]{1,0:T(8,128)S(1)} collective-permute-done((f32[256,512]{1,0:T(8,128)S(1)}, f32[256,512]{1,0:T(8,128)S(1)}, u32[]{:S(2)}, u32[]{:S(2)}) %collective-permute-start.10) | collective-permute-done | bytes 524320 | tf_op jit(solution)/shard_map/ppermute | solution.py:135
  156.0 4.0 %collective-permute-start.22 = (f32[2,4,64,512]{3,2,1,0:T(8,128)S(1)}, f32[2,4,64,512]{3,2,1,0:T(8,128)S(1)}, u32[]{:S(2)}, u32[]{:S(2)}) collective-permute-start(f32[2,4,64,512]{3,2,1,0:T(8,128)S(1)} %fusion.5), channel_id=1, source_target_pairs={{0,1},{1,0},{2,3},{3,2},{4,5},{5,4},{6,7},{7,6},{8,9},{9,8},{10,11... | collective-permute-start | bytes 3145736 | tf_op jit(solution)/shard_map/ppermute | solution.py:28
  161.0 2.3 %collective-permute-done.18 = f32[256,512]{1,0:T(8,128)S(1)} collective-permute-done((f32[256,512]{1,0:T(8,128)S(1)}, f32[256,512]{1,0:T(8,128)S(1)}, u32[]{:S(2)}, u32[]{:S(2)}) %collective-permute-start.18) | collective-permute-done | bytes 524320 | tf_op jit(solution)/shard_map/ppermute | solution.py:133
  163.4 17.3 %collective-permute-done.21 = f32[256,512]{1,0:T(8,128)S(1)} collective-permute-done((f32[256,512]{1,0:T(8,128)S(1)}, f32[256,512]{1,0:T(8,128)S(1)}, u32[]{:S(2)}, u32[]{:S(2)}) %collective-permute-start.21) | collective-permute-done | bytes 524320 | tf_op jit(solution)/shard_map/ppermute | solution.py:135
  183.4 2.2 collective-permute-start.25
  185.6 4.5 %collective-permute-start.24 = (f32[2,64,512]{2,1,0:T(8,128)S(1)}, f32[2,64,512]{2,1,0:T(8,128)S(1)}, u32[]{:S(2)}, u32[]{:S(2)}) collective-permute-start(f32[2,64,512]{2,1,0:T(8,128)S(1)} %get-tuple-element.31), channel_id=1, source_target_pairs={{0,4},{1,5},{2,6},{3,7},{4,0},{5,1},{6,2},{7,3},{8,12},{9,13},{10,... | collective-permute-start | bytes 786440 | tf_op jit(solution)/shard_map/ppermute | solution.py:28
  191.8 2.0 collective-permute-start.30
  193.8 4.9 %collective-permute-start.29 = (f32[1,64,512]{2,1,0:T(8,128)S(1)}, f32[1,64,512]{2,1,0:T(8,128)S(1)}, u32[]{:S(2)}, u32[]{:S(2)}) collective-permute-start(f32[1,64,512]{2,1,0:T(8,128)S(1)} %get-tuple-element.34), channel_id=1, source_target_pairs={{0,2},{1,3},{2,0},{3,1},{4,6},{5,7},{6,4},{7,5},{8,10},{9,11},{10,... | collective-permute-start | bytes 393224 | tf_op jit(solution)/shard_map/ppermute | solution.py:28
  201.6 4.1 %collective-permute-done.30 = f32[1,64,512]{2,1,0:T(8,128)S(1)} collective-permute-done((f32[1,64,512]{2,1,0:T(8,128)S(1)}, f32[1,64,512]{2,1,0:T(8,128)S(1)}, u32[]{:S(2)}, u32[]{:S(2)}) %collective-permute-start.30) | collective-permute-done | bytes 131104 | tf_op jit(solution)/shard_map/ppermute | solution.py:28
  207.0 2.5 %collective-permute-done.26 = f32[2,64,512]{2,1,0:T(8,128)S(1)} collective-permute-done((f32[2,64,512]{2,1,0:T(8,128)S(1)}, f32[2,64,512]{2,1,0:T(8,128)S(1)}, u32[]{:S(2)}, u32[]{:S(2)}) %collective-permute-start.26) | collective-permute-done | bytes 262176 | tf_op jit(solution)/shard_map/ppermute | solution.py:28
  210.1 1.9 fusion.3
  212.8 1.8 collective-permute-start.33
  215.6 13.2 %collective-permute-done.33 = f32[1,64,512]{2,1,0:T(8,128)S(1)} collective-permute-done((f32[1,64,512]{2,1,0:T(8,128)S(1)}, f32[1,64,512]{2,1,0:T(8,128)S(1)}, u32[]{:S(2)}, u32[]{:S(2)}) %collective-permute-start.33) | collective-permute-done | bytes 131104 | tf_op jit(solution)/shard_map/ppermute | solution.py:28
  (115 shorter events, 36.2 us)
Async XLA Ops:
  26.7 16.6 %all-to-all-start.3 = ((f32[4,256,128]{2,1,0:T(8,128)}), f32[4,256,128]{2,1,0:T(8,128)S(1)}, u32[]{:S(2)}, u32[]{:S(2)}) async-start(f32[4,256,128]{2,1,0:T(8,128)} %all_to_all.20), calls=%async_computation.3 | async-start | bytes 1048576 | tf_op jit(solution)/shard_map/all_to_all | solution.py:104
  43.2 15.7 %all-to-all-start.1 = ((f32[4,256,128]{2,1,0:T(8,128)}), f32[4,256,128]{2,1,0:T(8,128)S(1)}, u32[]{:S(2)}, u32[]{:S(2)}) async-start(f32[4,256,128]{2,1,0:T(8,128)} %all_to_all.21), calls=%async_computation.1 | async-start | bytes 1048576 | tf_op jit(solution)/shard_map/all_to_all | solution.py:104
  49.8 14.7 %collective-permute-start.11 = (f32[4,256,128]{2,1,0:T(8,128)S(1)}, f32[4,256,128]{2,1,0:T(8,128)S(1)}, u32[]{:S(2)}, u32[]{:S(2)}) collective-permute-start(f32[4,256,128]{2,1,0:T(8,128)S(1)} %all-to-all-done.3.refs_0_), channel_id=1, source_target_pairs={{0,2},{1,3},{2,0},{3,1},{4,6},{5,7},{6,4},{7,5},{8,10},{9,11},{10,... | collective-permute-start | bytes 1572872 | tf_op jit(solution)/shard_map/ppermute | solution.py:28
  50.8 14.6 %collective-permute-start.12 = (f32[4,256,128]{2,1,0:T(8,128)S(1)}, f32[4,256,128]{2,1,0:T(8,128)S(1)}, u32[]{:S(2)}, u32[]{:S(2)}) collective-permute-start(f32[4,256,128]{2,1,0:T(8,128)S(1)} %all-to-all-done.3.refs_0_), channel_id=1, source_target_pairs={{0,4},{1,5},{2,6},{3,7},{4,0},{5,1},{6,2},{7,3},{8,12},{9,13},{10,... | collective-permute-start | bytes 1572872 | tf_op jit(solution)/shard_map/ppermute | solution.py:28
  59.0 16.5 %collective-permute-start = (f32[4,256,128]{2,1,0:T(8,128)S(1)}, f32[4,256,128]{2,1,0:T(8,128)}, u32[]{:S(2)}, u32[]{:S(2)}) collective-permute-start(f32[4,256,128]{2,1,0:T(8,128)S(1)} %all-to-all-done.1.refs_0_), channel_id=1, source_target_pairs={{0,2},{1,3},{2,0},{3,1},{4,6},{5,7},{6,4},{7,5},{8,10},{9,11},{10,... | collective-permute-start | bytes 1572872 | tf_op jit(solution)/shard_map/ppermute | solution.py:28
  59.9 16.2 %collective-permute-start.1 = (f32[4,256,128]{2,1,0:T(8,128)S(1)}, f32[4,256,128]{2,1,0:T(8,128)}, u32[]{:S(2)}, u32[]{:S(2)}) collective-permute-start(f32[4,256,128]{2,1,0:T(8,128)S(1)} %all-to-all-done.1.refs_0_), channel_id=1, source_target_pairs={{0,4},{1,5},{2,6},{3,7},{4,0},{5,1},{6,2},{7,3},{8,12},{9,13},{10,... | collective-permute-start | bytes 1572872 | tf_op jit(solution)/shard_map/ppermute | solution.py:28
  60.5 26.9 %collective-permute-start.2 = (f32[4,256,128]{2,1,0:T(8,128)S(1)}, f32[4,256,128]{2,1,0:T(8,128)}, u32[]{:S(2)}, u32[]{:S(2)}) collective-permute-start(f32[4,256,128]{2,1,0:T(8,128)S(1)} %all-to-all-done.1.refs_0_), channel_id=1, source_target_pairs={{0,6},{1,7},{2,4},{3,5},{4,2},{5,3},{6,0},{7,1},{8,14},{9,15},{10,... | collective-permute-start | bytes 1572872 | tf_op jit(solution)/shard_map/ppermute | solution.py:28
  64.5 30.9 %collective-permute-start.13 = (f32[4,256,128]{2,1,0:T(8,128)S(1)}, f32[4,256,128]{2,1,0:T(8,128)S(1)}, u32[]{:S(2)}, u32[]{:S(2)}) collective-permute-start(f32[4,256,128]{2,1,0:T(8,128)S(1)} %all-to-all-done.3.refs_0_), channel_id=1, source_target_pairs={{0,6},{1,7},{2,4},{3,5},{4,2},{5,3},{6,0},{7,1},{8,14},{9,15},{10,... | collective-permute-start | bytes 1572872 | tf_op jit(solution)/shard_map/ppermute | solution.py:28
  65.4 29.9 %collective-permute-start.3 = (f32[4,256,128]{2,1,0:T(8,128)S(1)}, f32[4,256,128]{2,1,0:T(8,128)S(1)}, u32[]{:S(2)}, u32[]{:S(2)}) collective-permute-start(f32[4,256,128]{2,1,0:T(8,128)S(1)} %all-to-all-done.1.refs_0_), channel_id=1, source_target_pairs={{0,1},{1,0},{2,3},{3,2},{4,5},{5,4},{6,7},{7,6},{8,9},{9,8},{10,11... | collective-permute-start | bytes 1572872 | tf_op jit(solution)/shard_map/ppermute | solution.py:28
  75.5 20.3 %collective-permute-start.4 = (f32[4,256,128]{2,1,0:T(8,128)}, f32[4,256,128]{2,1,0:T(8,128)S(1)}, u32[]{:S(2)}, u32[]{:S(2)}) collective-permute-start(f32[4,256,128]{2,1,0:T(8,128)} %collective-permute-done.refs_1_), channel_id=1, source_target_pairs={{0,1},{1,0},{2,3},{3,2},{4,5},{5,4},{6,7},{7,6},{8,9},{9,8},{10,11... | collective-permute-start | bytes 1572872 | tf_op jit(solution)/shard_map/ppermute | solution.py:28
  76.2 19.8 %collective-permute-start.5 = (f32[4,256,128]{2,1,0:T(8,128)}, f32[4,256,128]{2,1,0:T(8,128)S(1)}, u32[]{:S(2)}, u32[]{:S(2)}) collective-permute-start(f32[4,256,128]{2,1,0:T(8,128)} %collective-permute-done.1.refs_2_), channel_id=1, source_target_pairs={{0,1},{1,0},{2,3},{3,2},{4,5},{5,4},{6,7},{7,6},{8,9},{9,8},{10,11... | collective-permute-start | bytes 1572872 | tf_op jit(solution)/shard_map/ppermute | solution.py:28
  95.3 13.2 %collective-permute-start.14 = (f32[4,256,128]{2,1,0:T(8,128)S(1)}, f32[4,256,128]{2,1,0:T(8,128)S(1)}, u32[]{:S(2)}, u32[]{:S(2)}) collective-permute-start(f32[4,256,128]{2,1,0:T(8,128)S(1)} %all-to-all-done.3.refs_0_), channel_id=1, source_target_pairs={{0,1},{1,0},{2,3},{3,2},{4,5},{5,4},{6,7},{7,6},{8,9},{9,8},{10,11... | collective-permute-start | bytes 1572872 | tf_op jit(solution)/shard_map/ppermute | solution.py:28
  95.3 13.9 %collective-permute-start.15 = (f32[4,256,128]{2,1,0:T(8,128)S(1)}, f32[4,256,128]{2,1,0:T(8,128)S(1)}, u32[]{:S(2)}, u32[]{:S(2)}) collective-permute-start(f32[4,256,128]{2,1,0:T(8,128)S(1)} %collective-permute-done.11.refs_1_), channel_id=1, source_target_pairs={{0,1},{1,0},{2,3},{3,2},{4,5},{5,4},{6,7},{7,6},{8,9},{9,8},{10,11... | collective-permute-start | bytes 1572872 | tf_op jit(solution)/shard_map/ppermute | solution.py:28
  95.9 13.4 %collective-permute-start.16 = (f32[4,256,128]{2,1,0:T(8,128)S(1)}, f32[4,256,128]{2,1,0:T(8,128)S(1)}, u32[]{:S(2)}, u32[]{:S(2)}) collective-permute-start(f32[4,256,128]{2,1,0:T(8,128)S(1)} %collective-permute-done.12.refs_2_), channel_id=1, source_target_pairs={{0,1},{1,0},{2,3},{3,2},{4,5},{5,4},{6,7},{7,6},{8,9},{9,8},{10,11... | collective-permute-start | bytes 1572872 | tf_op jit(solution)/shard_map/ppermute | solution.py:28
  95.9 13.3 %collective-permute-start.17 = (f32[4,256,128]{2,1,0:T(8,128)S(1)}, f32[4,256,128]{2,1,0:T(8,128)S(1)}, u32[]{:S(2)}, u32[]{:S(2)}) collective-permute-start(f32[4,256,128]{2,1,0:T(8,128)S(1)} %collective-permute-done.13.refs_3_), channel_id=1, source_target_pairs={{0,1},{1,0},{2,3},{3,2},{4,5},{5,4},{6,7},{7,6},{8,9},{9,8},{10,11... | collective-permute-start | bytes 1572872 | tf_op jit(solution)/shard_map/ppermute | solution.py:28
  104.7 15.1 %collective-permute-start.9 = (f32[256,512]{1,0:T(8,128)S(1)}, f32[256,512]{1,0:T(8,128)S(1)}, u32[]{:S(2)}, u32[]{:S(2)}) collective-permute-start(f32[256,512]{1,0:T(8,128)S(1)} %get-tuple-element.13), channel_id=1, source_target_pairs={{0,8},{24,16},{1,9},{25,17},{2,10},{26,18},{3,11},{27,19},{4,12},{... | collective-permute-start | bytes 1572872 | tf_op jit(solution)/shard_map/ppermute | solution.py:132
  108.5 25.8 %collective-permute-start.8 = (f32[256,512]{1,0:T(8,128)S(1)}, f32[256,512]{1,0:T(8,128)S(1)}, u32[]{:S(2)}, u32[]{:S(2)}) collective-permute-start(f32[256,512]{1,0:T(8,128)S(1)} %get-tuple-element.13), channel_id=1, source_target_pairs={{8,16},{16,8},{9,17},{17,9},{10,18},{18,10},{11,19},{19,11},{12,20... | collective-permute-start | bytes 1572872 | tf_op jit(solution)/shard_map/ppermute | solution.py:134
  115.3 14.2 %collective-permute-start.20 = (f32[256,512]{1,0:T(8,128)S(1)}, f32[256,512]{1,0:T(8,128)S(1)}, u32[]{:S(2)}, u32[]{:S(2)}) collective-permute-start(f32[256,512]{1,0:T(8,128)S(1)} %get-tuple-element.17), channel_id=1, source_target_pairs={{0,8},{24,16},{1,9},{25,17},{2,10},{26,18},{3,11},{27,19},{4,12},{... | collective-permute-start | bytes 1572872 | tf_op jit(solution)/shard_map/ppermute | solution.py:132
  119.2 22.3 %collective-permute-start.7 = (f32[256,512]{1,0:T(8,128)S(1)}, f32[256,512]{1,0:T(8,128)S(1)}, u32[]{:S(2)}, u32[]{:S(2)}) collective-permute-start(f32[256,512]{1,0:T(8,128)S(1)} %get-tuple-element.12), channel_id=1, source_target_pairs={{0,16},{16,24},{24,8},{8,0},{1,17},{17,25},{25,9},{9,1},{2,18},{18... | collective-permute-start | bytes 1572872 | tf_op jit(solution)/shard_map/ppermute | solution.py:133
  119.9 32.2 %collective-permute-start.10 = (f32[256,512]{1,0:T(8,128)S(1)}, f32[256,512]{1,0:T(8,128)S(1)}, u32[]{:S(2)}, u32[]{:S(2)}) collective-permute-start(f32[256,512]{1,0:T(8,128)S(1)} %add.180), channel_id=1, source_target_pairs={{8,24},{16,0},{0,8},{24,16},{9,25},{17,1},{1,9},{25,17},{10,26},{1... | collective-permute-start | bytes 1572872 | tf_op jit(solution)/shard_map/ppermute | solution.py:135
  123.6 37.4 %collective-permute-start.19 = (f32[256,512]{1,0:T(8,128)S(1)}, f32[256,512]{1,0:T(8,128)S(1)}, u32[]{:S(2)}, u32[]{:S(2)}) collective-permute-start(f32[256,512]{1,0:T(8,128)S(1)} %get-tuple-element.17), channel_id=1, source_target_pairs={{8,16},{16,8},{9,17},{17,9},{10,18},{18,10},{11,19},{19,11},{12,20... | collective-permute-start | bytes 1572872 | tf_op jit(solution)/shard_map/ppermute | solution.py:134
  129.6 33.8 %collective-permute-start.18 = (f32[256,512]{1,0:T(8,128)S(1)}, f32[256,512]{1,0:T(8,128)S(1)}, u32[]{:S(2)}, u32[]{:S(2)}) collective-permute-start(f32[256,512]{1,0:T(8,128)S(1)} %get-tuple-element.16), channel_id=1, source_target_pairs={{0,16},{16,24},{24,8},{8,0},{1,17},{17,25},{25,9},{9,1},{2,18},{18... | collective-permute-start | bytes 1572872 | tf_op jit(solution)/shard_map/ppermute | solution.py:133
  134.3 46.4 %collective-permute-start.21 = (f32[256,512]{1,0:T(8,128)S(1)}, f32[256,512]{1,0:T(8,128)S(1)}, u32[]{:S(2)}, u32[]{:S(2)}) collective-permute-start(f32[256,512]{1,0:T(8,128)S(1)} %add.184), channel_id=1, source_target_pairs={{8,24},{16,0},{0,8},{24,16},{9,25},{17,1},{1,9},{25,17},{10,26},{1... | collective-permute-start | bytes 1572872 | tf_op jit(solution)/shard_map/ppermute | solution.py:135
  156.0 27.1 %collective-permute-start.22 = (f32[2,4,64,512]{3,2,1,0:T(8,128)S(1)}, f32[2,4,64,512]{3,2,1,0:T(8,128)S(1)}, u32[]{:S(2)}, u32[]{:S(2)}) collective-permute-start(f32[2,4,64,512]{3,2,1,0:T(8,128)S(1)} %fusion.5), channel_id=1, source_target_pairs={{0,1},{1,0},{2,3},{3,2},{4,5},{5,4},{6,7},{7,6},{8,9},{9,8},{10,11... | collective-permute-start | bytes 3145736 | tf_op jit(solution)/shard_map/ppermute | solution.py:28
  183.4 10.4 %collective-permute-start.25 = (f32[2,64,512]{2,1,0:T(8,128)S(1)}, f32[2,64,512]{2,1,0:T(8,128)S(1)}, u32[]{:S(2)}, u32[]{:S(2)}) collective-permute-start(f32[2,64,512]{2,1,0:T(8,128)S(1)} %get-tuple-element.30), channel_id=1, source_target_pairs={{0,6},{1,7},{2,4},{3,5},{4,2},{5,3},{6,0},{7,1},{8,14},{9,15},{10,... | collective-permute-start | bytes 786440 | tf_op jit(solution)/shard_map/ppermute | solution.py:28
  185.6 14.7 %collective-permute-start.24 = (f32[2,64,512]{2,1,0:T(8,128)S(1)}, f32[2,64,512]{2,1,0:T(8,128)S(1)}, u32[]{:S(2)}, u32[]{:S(2)}) collective-permute-start(f32[2,64,512]{2,1,0:T(8,128)S(1)} %get-tuple-element.31), channel_id=1, source_target_pairs={{0,4},{1,5},{2,6},{3,7},{4,0},{5,1},{6,2},{7,3},{8,12},{9,13},{10,... | collective-permute-start | bytes 786440 | tf_op jit(solution)/shard_map/ppermute | solution.py:28
  190.1 11.4 %collective-permute-start.23 = (f32[2,64,512]{2,1,0:T(8,128)S(1)}, f32[2,64,512]{2,1,0:T(8,128)S(1)}, u32[]{:S(2)}, u32[]{:S(2)}) collective-permute-start(f32[2,64,512]{2,1,0:T(8,128)S(1)} %get-tuple-element.29), channel_id=1, source_target_pairs={{0,2},{1,3},{2,0},{3,1},{4,6},{5,7},{6,4},{7,5},{8,10},{9,11},{10,... | collective-permute-start | bytes 786440 | tf_op jit(solution)/shard_map/ppermute | solution.py:28
  190.2 11.4 %collective-permute-start.31 = (f32[1,64,512]{2,1,0:T(8,128)S(1)}, f32[1,64,512]{2,1,0:T(8,128)S(1)}, u32[]{:S(2)}, u32[]{:S(2)}) collective-permute-start(f32[1,64,512]{2,1,0:T(8,128)S(1)} %get-tuple-element.35), channel_id=1, source_target_pairs={{0,6},{1,7},{2,4},{3,5},{4,2},{5,3},{6,0},{7,1},{8,14},{9,15},{10,... | collective-permute-start | bytes 393224 | tf_op jit(solution)/shard_map/ppermute | solution.py:28
  191.8 14.0 %collective-permute-start.30 = (f32[1,64,512]{2,1,0:T(8,128)S(1)}, f32[1,64,512]{2,1,0:T(8,128)S(1)}, u32[]{:S(2)}, u32[]{:S(2)}) collective-permute-start(f32[1,64,512]{2,1,0:T(8,128)S(1)} %get-tuple-element.36), channel_id=1, source_target_pairs={{0,4},{1,5},{2,6},{3,7},{4,0},{5,1},{6,2},{7,3},{8,12},{9,13},{10,... | collective-permute-start | bytes 393224 | tf_op jit(solution)/shard_map/ppermute | solution.py:28
  193.8 13.1 %collective-permute-start.29 = (f32[1,64,512]{2,1,0:T(8,128)S(1)}, f32[1,64,512]{2,1,0:T(8,128)S(1)}, u32[]{:S(2)}, u32[]{:S(2)}) collective-permute-start(f32[1,64,512]{2,1,0:T(8,128)S(1)} %get-tuple-element.34), channel_id=1, source_target_pairs={{0,2},{1,3},{2,0},{3,1},{4,6},{5,7},{6,4},{7,5},{8,10},{9,11},{10,... | collective-permute-start | bytes 393224 | tf_op jit(solution)/shard_map/ppermute | solution.py:28
  209.5 19.3 %collective-permute-start.27 = (f32[2,64,512]{2,1,0:T(8,128)S(1)}, f32[2,64,512]{2,1,0:T(8,128)S(1)}, u32[]{:S(2)}, u32[]{:S(2)}) collective-permute-start(f32[2,64,512]{2,1,0:T(8,128)S(1)} %add.199), channel_id=1, source_target_pairs={{0,16},{8,24},{16,0},{24,8},{1,17},{9,25},{17,1},{25,9},{2,18},{10... | collective-permute-start | bytes 786440 | tf_op jit(solution)/shard_map/ppermute | solution.py:28
  212.8 16.0 %collective-permute-start.33 = (f32[1,64,512]{2,1,0:T(8,128)S(1)}, f32[1,64,512]{2,1,0:T(8,128)S(1)}, u32[]{:S(2)}, u32[]{:S(2)}) collective-permute-start(f32[1,64,512]{2,1,0:T(8,128)S(1)} %add.207), channel_id=1, source_target_pairs={{0,16},{8,24},{16,0},{24,8},{1,17},{9,25},{17,1},{25,9},{2,18},{10... | collective-permute-start | bytes 393224 | tf_op jit(solution)/shard_map/ppermute | solution.py:28
  (10 other events, 202.9 us)

commit v4 on v3

v4 whole, which is shorter than its diff:
```python
import functools

import jax
import jax.numpy as jnp
from jax import lax
from jax.experimental import pallas as pl
from jax.experimental.pallas import tpu as pltpu
from jax.sharding import PartitionSpec as P

BOTH = ("prow", "pcol")
VMEM_LIMIT = 48 * 1024 * 1024
LANES = 128


def product(left_part, right_part):
    return jnp.dot(
        left_part, right_part, precision=lax.Precision.HIGH, preferred_element_type=jnp.float32
    )


def halves(value):
    high = value.astype(jnp.bfloat16)
    low = (value - high.astype(jnp.float32)).astype(jnp.bfloat16)
    return high, low


def flip(value, axis, bit):
    return lax.ppermute(value, axis, [(i, i ^ bit) for i in range(lax.axis_size(axis))])


def nothing_kernel(*refs):
    del refs


def after(value, *others):
    anywhere = pl.BlockSpec(memory_space=pl.ANY)
    return pl.pallas_call(
        nothing_kernel,
        in_specs=[anywhere] * (1 + len(others)),
        out_specs=anywhere,
        out_shape=jax.ShapeDtypeStruct(value.shape, value.dtype),
        input_output_aliases={0: 0},
        cost_estimate=pl.CostEstimate(flops=0, bytes_accessed=0, transcendentals=0),
        name="after",
    )(value, *others)


def cut_kernel(place, factor_ref, *out_refs):
    width = out_refs[0].shape[1]
    for o, out_ref in enumerate(out_refs):
        start = pl.multiple_of((place[2] ^ o) * width, width)
        out_ref[...] = factor_ref[0, :, pl.ds(start, width)]


def cut(place, factor, number, count):
    _, unit_rows, columns = factor.shape
    width = columns // count
    return pl.pallas_call(
        cut_kernel,
        grid_spec=pltpu.PrefetchScalarGridSpec(
            num_scalar_prefetch=1,
            grid=(1,),
            in_specs=[pl.BlockSpec((1, unit_rows, columns), lambda i, m: (number, 0, 0))],
            out_specs=[pl.BlockSpec((unit_rows, width), lambda i, m: (0, 0))] * count,
        ),
        out_shape=[jax.ShapeDtypeStruct((unit_rows, width), factor.dtype)] * count,
        compiler_params=pltpu.CompilerParams(vmem_limit_bytes=VMEM_LIMIT),
        cost_estimate=pl.CostEstimate(
            flops=0, bytes_accessed=8 * unit_rows * columns, transcendentals=0
        ),
        name="cut",
    )(place, factor)


def arrange_kernel(place, *refs):
    out_ref = refs[-1]
    for o, piece_ref in enumerate(refs[:-1]):
        out_ref[place[2] ^ o] = piece_ref[...]


def arrange(place, pieces):
    shape = pieces[0].shape
    count = len(pieces)
    return pl.pallas_call(
        arrange_kernel,
        grid_spec=pltpu.PrefetchScalarGridSpec(
            num_scalar_prefetch=1,
            grid=(1,),
            in_specs=[pl.BlockSpec(shape, lambda i, m: (0, 0))] * count,
            out_specs=pl.BlockSpec((count,) + shape, lambda i, m: (0, 0, 0)),
        ),
        out_shape=jax.ShapeDtypeStruct((count,) + shape, pieces[0].dtype),
        compiler_params=pltpu.CompilerParams(vmem_limit_bytes=VMEM_LIMIT),
        cost_estimate=pl.CostEstimate(
            flops=0, bytes_accessed=8 * count * shape[0] * shape[1], transcendentals=0
        ),
        name="arrange",
    )(place, *pieces)


def partial_kernel(offsets, ratio, count, number, place, slots, ancestors, tile_ref, *refs):
    piece_refs = refs[: len(offsets)]
    out_refs = refs[len(offsets) : -2]
    right_high, right_low = refs[-2:]
    chunk_rows, columns = out_refs[0].shape
    blocks = tile_ref.shape[1] // columns
    step = pl.program_id(0)

    def listed(block):
        found = ancestors[number, 0] == block
        for i in range(1, ancestors.shape[1]):
            found = found | (ancestors[number, i] == block)
        return found

    @pl.when(step == 0)
    def _assemble():
        for ref, offset in zip(piece_refs, offsets):
            if offset is None:
                right_high[...], right_low[...] = halves(ref[...])
                continue
            unit_rows, width = ref.shape[1:]
            owner = place[0] ^ offset
            lane = pl.multiple_of(owner // ratio * width, width)
            for r in range(ref.shape[0]):
                unit = owner % ratio * count + r
                rows = pl.ds(pl.multiple_of(unit * unit_rows, unit_rows), unit_rows)
                high, low = halves(ref[r])
                right_high[rows, pl.ds(lane, width)] = high
                right_low[rows, pl.ds(lane, width)] = low

    def multiply(out_ref):
        out_ref[...] = jnp.zeros_like(out_ref)
        chunk = place[0] * count + slots[place[1], step]

        @pl.when(listed(chunk * chunk_rows // columns))
        def _chunk():
            def add(block, carry):
                @pl.when(listed(place[1] * blocks + block))
                def _block():
                    span = pl.ds(pl.multiple_of(block * columns, columns), columns)
                    high, low = halves(tile_ref[:, span])
                    right = right_high[span, :]
                    dot = functools.partial(jnp.dot, preferred_element_type=jnp.float32)
                    out_ref[...] += dot(high, right) + (
                        dot(high, right_low[span, :]) + dot(low, right)
                    )

                return carry

            lax.fori_loop(0, blocks, add, 0)

    for index, out_ref in enumerate(out_refs):
        pl.when(step == index)(functools.partial(multiply, out_ref))


def partial_product(place, slots, ancestors, tiles, pieces, offsets, ratio, columns, number):
    rows, cols = tiles.shape
    count = slots.shape[0]
    chunk = rows // count
    whole = [
        pl.BlockSpec(piece.shape, functools.partial(lambda n, i, *m: (0,) * n, piece.ndim))
        for piece in pieces
    ]
    return pl.pallas_call(
        functools.partial(partial_kernel, offsets, ratio, count, number),
        grid_spec=pltpu.PrefetchScalarGridSpec(
            num_scalar_prefetch=3,
            grid=(count,),
            in_specs=[pl.BlockSpec((chunk, cols), lambda i, p, s, a: (s[p[1], i], 0))] + whole,
            out_specs=[pl.BlockSpec((chunk, columns), lambda i, *m: (0, 0))] * count,
            scratch_shapes=[pltpu.VMEM((cols, columns), jnp.bfloat16)] * 2,
        ),
        out_shape=[jax.ShapeDtypeStruct((chunk, columns), jnp.float32)] * count,
        compiler_params=pltpu.CompilerParams(vmem_limit_bytes=VMEM_LIMIT),
        cost_estimate=pl.CostEstimate(
            flops=6 * rows * cols * columns,
            bytes_accessed=4 * (rows * cols + cols * columns + rows * columns),
            transcendentals=0,
        ),
        name="partial_product",
    )(place, slots, ancestors, tiles, *pieces)


def to_plane(place, pieces, ratio):
    received = [pieces[0]]
    for o in range(1, len(pieces)):
        received.append(flip(pieces[o], "pcol", o * ratio))
    return arrange(place, received)


def to_plane_whole(pieces, count, ratio):
    groups = [[c * ratio + k for c in range(count)] for k in range(ratio)]
    return lax.all_to_all(pieces, "pcol", 0, 0, axis_index_groups=groups)


def gather_plane(own, pcol_count):
    found = {0: own}
    for offset in range(2, pcol_count, 2):
        found[offset] = flip(own, "pcol", offset)
    for offset in range(0, pcol_count, 2):
        found[offset + 1] = flip(found[offset], "pcol", 1)
    return found


def gather_whole(own, count, ratio):
    _, unit_rows, width = own.shape
    gathered = lax.all_gather(own, "pcol", axis=0)
    split = gathered.reshape(count, ratio, count, unit_rows, width)
    rows = jnp.transpose(split, (1, 2, 3, 0, 4))
    return rows.reshape(ratio * count * unit_rows, count * width)


FOUR_SLOTS = ((3, 2, 1, 0), (2, 0, 3, 1), (1, 3, 0, 2), (0, 1, 2, 3))


def slots_of(count):
    return FOUR_SLOTS if count == len(FOUR_SLOTS) else (tuple(range(count)),) * count


def sum_over_four(slots, first):
    near = lax.ppermute(slots[0], "prow", [(0, 1), (3, 2)])
    total = lax.ppermute(slots[1], "prow", [(0, 2), (2, 3), (3, 1), (1, 0)])
    middle = lax.ppermute(slots[0], "prow", [(1, 2), (2, 1)])
    last = lax.ppermute(slots[2] + near, "prow", [(1, 3), (2, 0), (0, 1), (3, 2)])
    mine = after(slots[3], *first) if first else slots[3]
    return ((mine + total) + middle) + last


def sum_over_line(slots, z, first):
    count = len(slots)
    if count == len(FOUR_SLOTS):
        return sum_over_four(slots, first)
    chunks = jnp.stack(slots)

    def chunk(index):
        return lax.dynamic_index_in_dim(chunks, jnp.clip(index, 0, count - 1), 0, keepdims=False)

    up = down = None
    for t in range(1, count):
        up_send, down_send = chunk(z + count - t), chunk(z + t - count)
        if up is not None:
            up_send, down_send = up_send + up, down_send + down
        up = lax.ppermute(up_send, "prow", [(i, i + 1) for i in range(min(t, count - 1))])
        down = lax.ppermute(
            down_send, "prow", [(i, i - 1) for i in range(max(count - t, 1), count)]
        )
    mine = chunk(z)
    return mine if up is None else mine + up + down


def sum_plane(matrices, pcol_count, pcol_index):
    number, rows, columns = matrices.shape
    if pcol_count == 1:
        return matrices
    paired = matrices.reshape(number, pcol_count // 2, 2, rows // pcol_count, columns)
    core, chip = pcol_index % 2, pcol_index // 2
    send = lax.dynamic_index_in_dim(paired, 1 - core, 2, keepdims=False)
    mine = lax.dynamic_index_in_dim(paired, core, 2, keepdims=False) + flip(send, "pcol", 1)
    total = lax.dynamic_index_in_dim(mine, chip, 1, keepdims=False)
    for o in range(1, pcol_count // 2):
        send = lax.dynamic_index_in_dim(mine, chip ^ o, 1, keepdims=False)
        total = total + flip(send, "pcol", 2 * o)
    return total


def sum_planes(matrices, count):
    bit = 1
    while bit < count:
        matrices = matrices + flip(matrices, "prow", bit)
        bit *= 2
    return matrices


def body(inverse_tiles, factor, link_factor, diag_inverse, ancestors):
    row_count, col_count = inverse_tiles.shape
    nsuper, unit_rows, columns = factor.shape
    count = lax.axis_size("prow")
    pcol_count = lax.axis_size("pcol")
    ratio = col_count // row_count
    z = lax.axis_index("prow")
    pcol_index = lax.axis_index("pcol")
    slice_rows = columns // pcol_count
    slice_start = pcol_index * slice_rows
    width = columns // count

    place = jnp.stack([pcol_index, z, pcol_index // ratio]).astype(jnp.int32)
    slots = jnp.asarray(slots_of(count), jnp.int32)
    own_block = (pcol_index * count + z) * unit_rows // columns
    keep = jnp.any(ancestors == own_block, axis=1)[:, None, None]
    local = jnp.where(keep, factor, 0.0)

    partials = []
    received, gathered = None, None
    for number in range(nsuper):
        if width % LANES:
            pieces = jnp.swapaxes(factor[number].reshape(unit_rows, count, width), 0, 1)
            received = to_plane_whole(pieces, count, ratio)
            own = lax.all_to_all(received, "prow", 0, 0)
            pieces, offsets = [gather_whole(own, count, ratio)], [None]
        else:
            start = place if received is None else after(place, received)
            received = to_plane(place, cut(start, factor, number, count), ratio)
            own = lax.all_to_all(received, "prow", 0, 0)
            if gathered is not None:
                own = after(own, *gathered)
            found = gather_plane(own, pcol_count)
            gathered = [found[o] for o in range(2, pcol_count, 2)]
            offsets, pieces = list(found.keys()), list(found.values())
        partials.append(
            partial_product(
                place, slots, ancestors, inverse_tiles, pieces, offsets, ratio, columns, number
            )
        )

    def own_rows(matrices):
        return lax.dynamic_slice_in_dim(matrices, slice_start, slice_rows, -2)

    offdiag_list, sums, bases, ready, before = [], [], [], [], []
    for number in range(nsuper):
        summed = sum_over_line(partials[number], z, before)
        part = product(local[number].T, summed)
        if number == 0:
            result = -jnp.where(keep[number], summed, 0.0)
            base = diag_inverse[0]
        else:
            result = -jnp.where(keep[number], summed + link_rows, 0.0)
            part = part + rest
            base = diag_inverse[number] + product(link_block.T, base_link)
        offdiag_list.append(result)
        ready.append(part)
        bases.append(own_rows(base))
        if number + 1 < nsuper:
            link_block = link_factor[number]
            cross_part = product(result.T, local[number + 1])
            link_part = cross_part + product(part, link_block)
            rest = product(cross_part.T, link_block) + product(link_block.T, link_part)
            base_link = product(base, link_block)
            link_rows = product(result, link_block)
            bases.append(own_rows(base_link))
            ready.append(link_part)
            group = sum_plane(jnp.stack(ready), pcol_count, pcol_index)
            before = [group, rest, link_rows]
            sums.append(sum_planes(group, count))
            ready = []
    sums.append(sum_planes(sum_plane(jnp.stack(ready), pcol_count, pcol_index), count))
    totals = jnp.concatenate(sums) + jnp.stack(bases)
    return (jnp.stack(offdiag_list), totals[0::2], -totals[1::2])


def solution(mesh):
    in_specs = (P("pcol", "prow"), P(None, ("pcol", "prow"), None), P(), P(), P())
    out_specs = (P(None, ("pcol", "prow"), None), P(None, "pcol", None), P(None, "pcol", None))
    return jax.shard_map(body, mesh=mesh, in_specs=in_specs, out_specs=out_specs, check_vma=False)
```

time: 231 us -> 226 us (0.978)
  waiting for transfers between devices: 114 us -> 89.2 us
  other arithmetic: 6.28 us -> 18.2 us
  Pallas kernels: 12.8 us -> 24.5 us
  blocking collectives: 23.9 us -> 18 us
  local copies, waits for them, and re-layouts: 8.82 us -> 13.8 us
  starting transfers between devices: 54 us -> 49.5 us
    all_to_all x2 -> x1, waiting for transfers between devices: 19 us -> 0.01 us  [body(): own = lax.all_to_all(received, 'prow', 0, 0)]
    ppermute x2, waiting for transfers between devices: 27.9 us -> 11.8 us  [sum_over_four(): lax.ppermute(slots[2] + near, 'prow', [(1, 3), (2, 0), (0, 1), (3, 2)])]
    ppermute x26 -> x32, waiting for transfers between devices: 51.9 us -> 63.9 us  [flip(): lax.ppermute(value, axis, [(i, i ^ bit) for i in range(lax.axis_size(axis...]
    pallas_call x2 -> x9, Pallas kernels: 12.8 us -> 24.5 us  [the longest x2 21.3 us: partial_product(): pl.pallas_call(functools.partial(partial_kernel, offsets, ratio, count, n...]
    ppermute x2, waiting for transfers between devices: 9.25 us -> 0.01 us  [sum_over_four(): total = lax.ppermute(slots[1], 'prow', [(0, 2), (2, 3), (3, 1), (1, 0)])]
    ppermute x2, waiting for transfers between devices: 5.75 us -> 13.5 us  [sum_over_four(): near = lax.ppermute(slots[0], 'prow', [(0, 1), (3, 2)])]
    all_to_all x2 -> x1, blocking collectives: 23.9 us -> 18 us  [body(): own = lax.all_to_all(received, 'prow', 0, 0)]
    another operation x2 -> x3, other arithmetic: 1.91 us -> 7.46 us  [body(): return (jnp.stack(offdiag_list), totals[0::2], -totals[1::2])]
  transfers between devices with their start and end apart: 36 -> 41, of which waited for: 19 -> 18; matrix products, arithmetic and copies ran while one was open for 8% -> 13% of each run, Pallas kernels for 6% -> 10%
where the time goes in v4:
time: 226 us
  waiting for transfers between devices  89.2 us (39%)
  starting transfers between devices  49.5 us (22%)
  Pallas kernels  24.5 us (11%)
  other arithmetic  18.2 us (8%)
  blocking collectives  18 us (8%)
  local copies, waits for them, and re-layouts  13.8 us (6%)
  matrix products  11.7 us (5%)
    ppermute x32, waiting for transfers between devices, flip(): lax.ppermute(value, axis, [(i, i ^ bit) for i in range(lax.axis_size(axis...  63.9 us
    ppermute x32, starting transfers between devices, flip(): lax.ppermute(value, axis, [(i, i ^ bit) for i in range(lax.axis_size(axis...  27.6 us
    pallas_call x2, Pallas kernels, partial_product(): pl.pallas_call(functools.partial(partial_kernel, offsets, ratio, count, n...  21.3 us
    all_to_all x1, blocking collectives, body(): own = lax.all_to_all(received, 'prow', 0, 0)  18 us
    ppermute x2, waiting for transfers between devices, sum_over_four(): near = lax.ppermute(slots[0], 'prow', [(0, 1), (3, 2)])  13.5 us
    ppermute x2, waiting for transfers between devices, sum_over_four(): lax.ppermute(slots[2] + near, 'prow', [(1, 3), (2, 0), (0, 1), (3, 2)])  11.8 us
    dot_general x9, matrix products, product(): jnp.dot(left_part, right_part, precision=lax.Precision.HIGH, preferred_el...  11.7 us
    ppermute x2, starting transfers between devices, sum_over_four(): total = lax.ppermute(slots[1], 'prow', [(0, 2), (2, 3), (3, 1), (1, 0)])  8.52 us
  transfers between devices with their start and end apart: 41, of which 18 were waited for; matrix products, arithmetic and copies ran while one was open for 13% of the time, Pallas kernels for 10%

profile of v4, /device:TPU:0, one launch (start us, length us, event | category | flops | bytes accessed | tf_op | source)
XLA Modules:
  0.0 226.1 jit_solution(5807814699141696494)
XLA Ops:
  2.7 3.0 %collective-permute-start = (f32[256,128]{1,0:T(8,128)S(1)}, f32[256,128]{1,0:T(8,128)S(1)}, u32[]{:S(2)}, u32[]{:S(2)}) collective-permute-start(f32[256,128]{1,0:T(8,128)S(1)} %get-tuple-element.20), channel_id=1, source_target_pairs={{0,2},{1,3},{2,0},{3,1},{4,6},{5,7},{6,4},{7,5},{8,10},{9,11},{10,... | collective-permute-start | bytes 393224 | tf_op jit(solution)/shard_map/ppermute | solution.py:28
  7.2 2.4 %collective-permute-done.refs_1_ = f32[256,128]{1,0:T(8,128)S(1)} collective-permute-done((f32[256,128]{1,0:T(8,128)S(1)}, f32[256,128]{1,0:T(8,128)S(1)}, u32[]{:S(2)}, u32[]{:S(2)}) %collective-permute-start) | collective-permute-done | bytes 131104 | tf_op jit(solution)/shard_map/ppermute | solution.py:28
  9.6 3.9 %collective-permute-done.1.refs_2_ = f32[256,128]{1,0:T(8,128)S(1)} collective-permute-done((f32[256,128]{1,0:T(8,128)S(1)}, f32[256,128]{1,0:T(8,128)S(1)}, u32[]{:S(2)}, u32[]{:S(2)}) %collective-permute-start.1) | collective-permute-done | bytes 131104 | tf_op jit(solution)/shard_map/ppermute | solution.py:28
  14.0 18.0 %all_to_all.10.refs_0_ = f32[4,256,128]{2,1,0:T(8,128)} all-to-all(f32[4,256,128]{2,1,0:T(8,128)S(1)} %arrange.2.refs_1_), channel_id=1, replica_groups=mesh['prow'=4,'pcol'=8] {'prow'}, dimensions={0} | all-to-all | bytes 1048576 | tf_op jit(solution)/shard_map/all_to_all | solution.py:303
  39.0 8.1 %collective-permute-done.3.refs_1_ = f32[4,256,128]{2,1,0:T(8,128)S(1)} collective-permute-done((f32[4,256,128]{2,1,0:T(8,128)}, f32[4,256,128]{2,1,0:T(8,128)S(1)}, u32[]{:S(2)}, u32[]{:S(2)}) %collective-permute-start.3) | collective-permute-done | bytes 524320 | tf_op jit(solution)/shard_map/ppermute | solution.py:28
  47.1 10.3 %collective-permute-done.4.refs_2_ = f32[4,256,128]{2,1,0:T(8,128)} collective-permute-done((f32[4,256,128]{2,1,0:T(8,128)}, f32[4,256,128]{2,1,0:T(8,128)}, u32[]{:S(2)}, u32[]{:S(2)}) %collective-permute-start.4) | collective-permute-done | bytes 524320 | tf_op jit(solution)/shard_map/ppermute | solution.py:28
  59.0 4.6 %collective-permute-done.15.refs_2_ = f32[256,128]{1,0:T(8,128)S(1)} collective-permute-done((f32[256,128]{1,0:T(8,128)S(1)}, f32[256,128]{1,0:T(8,128)S(1)}, u32[]{:S(2)}, u32[]{:S(2)}) %collective-permute-start.15) | collective-permute-done | bytes 131104 | tf_op jit(solution)/shard_map/ppermute | solution.py:28
  63.6 2.2 collective-permute-start.16
  65.9 3.6 %collective-permute-done.16.refs_3_ = f32[256,128]{1,0:T(8,128)S(1)} collective-permute-done((f32[256,128]{1,0:T(8,128)S(1)}, f32[256,128]{1,0:T(8,128)S(1)}, u32[]{:S(2)}, u32[]{:S(2)}) %collective-permute-start.16) | collective-permute-done | bytes 131104 | tf_op jit(solution)/shard_map/ppermute | solution.py:28
  70.9 3.5 %all-to-all-start.1 = ((f32[4,256,128]{2,1,0:T(8,128)}), f32[4,256,128]{2,1,0:T(8,128)S(1)}, u32[]{:S(2)}, u32[]{:S(2)}) async-start(f32[4,256,128]{2,1,0:T(8,128)} %arrange.3), calls=%async_computation.1 | async-start | bytes 1048576 | tf_op jit(solution)/shard_map/all_to_all | solution.py:303
  74.4 10.3 %partial_product.2 = (f32[256,512]{1,0:T(8,128)}, f32[256,512]{1,0:T(8,128)S(1)}, f32[256,512]{1,0:T(8,128)S(1)}, f32[256,512]{1,0:T(8,128)S(1)}) custom-call(s32[3]{0:T(128)S(1)} %pad_add_fusion.place, s32[4,4]{1,0:T(4,128)S(1)} %copy-done.15, s32[2,8]{1,0:T(2,128)S(1)} %copy-done.13, f32[1024,2048]{1,0:T(8,128)} %tile_ref.3, ...), custom_call_target="tpu_custom_call" | custom-call | flops 6442450944 | bytes 14680064 | tf_op jit(solution)/shard_map/partial_product/pallas_call | solution.py:164
  87.1 3.1 %collective-permute-start.12 = (f32[256,512]{1,0:T(8,128)}, f32[256,512]{1,0:T(8,128)}, u32[]{:S(2)}, u32[]{:S(2)}) collective-permute-start(f32[256,512]{1,0:T(8,128)} %get-tuple-element.25), channel_id=1, source_target_pairs={{0,8},{24,16},{1,9},{25,17},{2,10},{26,18},{3,11},{27,19},{4,12},{... | collective-permute-start | bytes 1572872 | tf_op jit(solution)/shard_map/ppermute | solution.py:221
  91.2 2.7 %collective-permute-start.18 = (f32[4,256,128]{2,1,0:T(8,128)}, f32[4,256,128]{2,1,0:T(8,128)}, u32[]{:S(2)}, u32[]{:S(2)}) collective-permute-start(f32[4,256,128]{2,1,0:T(8,128)} %after.4.refs_0_), channel_id=1, source_target_pairs={{0,4},{1,5},{2,6},{3,7},{4,0},{5,1},{6,2},{7,3},{8,12},{9,13},{10,... | collective-permute-start | bytes 1572872 | tf_op jit(solution)/shard_map/ppermute | solution.py:28
  96.0 2.8 %collective-permute-done.12 = f32[256,512]{1,0:T(8,128)} collective-permute-done((f32[256,512]{1,0:T(8,128)}, f32[256,512]{1,0:T(8,128)}, u32[]{:S(2)}, u32[]{:S(2)}) %collective-permute-start.12) | collective-permute-done | bytes 524320 | tf_op jit(solution)/shard_map/ppermute | solution.py:221
  98.7 8.5 %collective-permute-start.10 = (f32[256,512]{1,0:T(8,128)}, f32[256,512]{1,0:T(8,128)}, u32[]{:S(2)}, u32[]{:S(2)}) collective-permute-start(f32[256,512]{1,0:T(8,128)} %copy-done.14), channel_id=1, source_target_pairs={{0,16},{16,24},{24,8},{8,0},{1,17},{17,25},{25,9},{9,1},{2,18},{18... | collective-permute-start | bytes 1572872 | tf_op jit(solution)/shard_map/ppermute | solution.py:222
  110.2 5.0 %collective-permute-done.18.refs_2_ = f32[4,256,128]{2,1,0:T(8,128)} collective-permute-done((f32[4,256,128]{2,1,0:T(8,128)}, f32[4,256,128]{2,1,0:T(8,128)}, u32[]{:S(2)}, u32[]{:S(2)}) %collective-permute-start.18) | collective-permute-done | bytes 524320 | tf_op jit(solution)/shard_map/ppermute | solution.py:28
  116.3 11.8 %collective-permute-done.13 = f32[256,512]{1,0:T(8,128)} collective-permute-done((f32[256,512]{1,0:T(8,128)}, f32[256,512]{1,0:T(8,128)}, u32[]{:S(2)}, u32[]{:S(2)}) %collective-permute-start.13) | collective-permute-done | bytes 524320 | tf_op jit(solution)/shard_map/ppermute | solution.py:224
  128.1 3.0 %fusion.15 = (f32[1,256,512]{2,1,0:T(8,128)}, f32[256,512]{1,0:T(8,128)S(1)}) fusion(pred[]{:T(512)} %bitcast, f32[256,512]{1,0:T(8,128)} %collective-permute-done.13, f32[256,512]{1,0:T(8,128)} %collective-permute-done.11, f32[256,512]{1,0:T(8,128)S(1)} %copy-done.11, f32[256,512]{1,0:T(8,128)} %collective-permute-done.10), kind=kLoop, calls=%fused_computation.36 | loop fusion | flops 655360 | bytes 3145729 | tf_op jit(solution)/shard_map/stack | solution.py:347
  137.3 11.1 %partial_product.3 = (f32[256,512]{1,0:T(8,128)S(1)}, f32[256,512]{1,0:T(8,128)S(1)}, f32[256,512]{1,0:T(8,128)S(1)}, f32[256,512]{1,0:T(8,128)S(1)}) custom-call(s32[3]{0:T(128)S(1)} %pad_add_fusion.place, s32[4,4]{1,0:T(4,128)S(1)} %copy-done.15, s32[2,8]{1,0:T(2,128)S(1)} %copy-done.13, f32[1024,2048]{1,0:T(8,128)} %tile_ref.3, ...), custom_call_target="tpu_custom_call" | custom-call | flops 6442450944 | bytes 14680064 | tf_op jit(solution)/shard_map/partial_product/pallas_call | solution.py:164
  152.2 10.7 %collective-permute-done.30 = f32[256,512]{1,0:T(8,128)S(1)} collective-permute-done((f32[256,512]{1,0:T(8,128)S(1)}, f32[256,512]{1,0:T(8,128)S(1)}, u32[]{:S(2)}, u32[]{:S(2)}) %collective-permute-start.30) | collective-permute-done | bytes 524320 | tf_op jit(solution)/shard_map/ppermute | solution.py:221
  163.7 2.5 %collective-permute-start.31 = (f32[256,512]{1,0:T(8,128)}, f32[256,512]{1,0:T(8,128)}, u32[]{:S(2)}, u32[]{:S(2)}) collective-permute-start(f32[256,512]{1,0:T(8,128)} %add.142), channel_id=1, source_target_pairs={{8,24},{16,0},{0,8},{24,16},{9,25},{17,1},{1,9},{25,17},{10,26},{1... | collective-permute-start | bytes 1572872 | tf_op jit(solution)/shard_map/ppermute | solution.py:224
  169.9 2.0 fusion.refs_2_
  172.0 7.2 %collective-permute-done.27 = f32[2,64,512]{2,1,0:T(8,128)S(1)} collective-permute-done((f32[2,64,512]{2,1,0:T(8,128)S(1)}, f32[2,64,512]{2,1,0:T(8,128)S(1)}, u32[]{:S(2)}, u32[]{:S(2)}) %collective-permute-start.27) | collective-permute-done | bytes 262176 | tf_op jit(solution)/shard_map/ppermute | solution.py:28
  179.1 2.1 fusion.7.refs_3_
  181.2 3.3 %collective-permute-done.26 = f32[2,64,512]{2,1,0:T(8,128)S(1)} collective-permute-done((f32[2,64,512]{2,1,0:T(8,128)S(1)}, f32[2,64,512]{2,1,0:T(8,128)S(1)}, u32[]{:S(2)}, u32[]{:S(2)}) %collective-permute-start.26) | collective-permute-done | bytes 262176 | tf_op jit(solution)/shard_map/ppermute | solution.py:28
  184.6 3.0 %collective-permute-done.25 = f32[2,64,512]{2,1,0:T(8,128)S(1)} collective-permute-done((f32[2,64,512]{2,1,0:T(8,128)S(1)}, f32[2,64,512]{2,1,0:T(8,128)S(1)}, u32[]{:S(2)}, u32[]{:S(2)}) %collective-permute-start.25) | collective-permute-done | bytes 262176 | tf_op jit(solution)/shard_map/ppermute | solution.py:28
  188.4 3.4 %negate_bitcast_fusion = (f32[1,256,512]{2,1,0:T(8,128)}, f32[256,512]{1,0:T(8,128)S(1)}) fusion(f32[256,512]{1,0:T(8,128)S(1)} %copy-done.26, pred[]{:T(512)} %bitcast.5, f32[256,512]{1,0:T(8,128)} %collective-permute-done.31, f32[256,512]{1,0:T(8,128)} %collective-permute-done.29, f32[256,512]{1,0:T(8,128)} %after.5, f32[256,512]{1,0:T(8,128)} %collective-permute-done.28), kind=kLoop, calls=%fused_computation.30 | loop fusion | flops 786432 | bytes 3670017 | tf_op jit(solution)/shard_map/stack | solution.py:347
  202.3 2.1 collective-permute-done.32
  211.6 3.1 %collective-permute-done.38 = f32[1,64,512]{2,1,0:T(8,128)S(1)} collective-permute-done((f32[1,64,512]{2,1,0:T(8,128)S(1)}, f32[1,64,512]{2,1,0:T(8,128)S(1)}, u32[]{:S(2)}, u32[]{:S(2)}) %collective-permute-start.38) | collective-permute-done | bytes 131104 | tf_op jit(solution)/shard_map/ppermute | solution.py:28
  214.7 2.2 collective-permute-start.39
  218.0 2.6 %collective-permute-done.33 = f32[2,64,512]{2,1,0:T(8,128)S(1)} collective-permute-done((f32[2,64,512]{2,1,0:T(8,128)S(1)}, f32[2,64,512]{2,1,0:T(8,128)S(1)}, u32[]{:S(2)}, u32[]{:S(2)}) %collective-permute-start.33) | collective-permute-done | bytes 262176 | tf_op jit(solution)/shard_map/ppermute | solution.py:28
  220.6 4.0 %collective-permute-done.39 = f32[1,64,512]{2,1,0:T(8,128)S(1)} collective-permute-done((f32[1,64,512]{2,1,0:T(8,128)S(1)}, f32[1,64,512]{2,1,0:T(8,128)S(1)}, u32[]{:S(2)}, u32[]{:S(2)}) %collective-permute-start.39) | collective-permute-done | bytes 131104 | tf_op jit(solution)/shard_map/ppermute | solution.py:28
  (162 shorter events, 59.0 us)
Async XLA Ops:
  32.0 15.1 %collective-permute-start.3 = (f32[4,256,128]{2,1,0:T(8,128)}, f32[4,256,128]{2,1,0:T(8,128)S(1)}, u32[]{:S(2)}, u32[]{:S(2)}) collective-permute-start(f32[4,256,128]{2,1,0:T(8,128)} %all_to_all.10.refs_0_), channel_id=1, source_target_pairs={{0,2},{1,3},{2,0},{3,1},{4,6},{5,7},{6,4},{7,5},{8,10},{9,11},{10,... | collective-permute-start | bytes 1572872 | tf_op jit(solution)/shard_map/ppermute | solution.py:28
  33.7 23.7 %collective-permute-start.4 = (f32[4,256,128]{2,1,0:T(8,128)}, f32[4,256,128]{2,1,0:T(8,128)}, u32[]{:S(2)}, u32[]{:S(2)}) collective-permute-start(f32[4,256,128]{2,1,0:T(8,128)} %all_to_all.10.refs_0_), channel_id=1, source_target_pairs={{0,4},{1,5},{2,6},{3,7},{4,0},{5,1},{6,2},{7,3},{8,12},{9,13},{10,... | collective-permute-start | bytes 1572872 | tf_op jit(solution)/shard_map/ppermute | solution.py:28
  34.2 23.2 %collective-permute-start.5 = (f32[4,256,128]{2,1,0:T(8,128)}, f32[4,256,128]{2,1,0:T(8,128)}, u32[]{:S(2)}, u32[]{:S(2)}) collective-permute-start(f32[4,256,128]{2,1,0:T(8,128)} %all_to_all.10.refs_0_), channel_id=1, source_target_pairs={{0,6},{1,7},{2,4},{3,5},{4,2},{5,3},{6,0},{7,1},{8,14},{9,15},{10,... | collective-permute-start | bytes 1572872 | tf_op jit(solution)/shard_map/ppermute | solution.py:28
  37.3 21.4 %collective-permute-start.14 = (f32[256,128]{1,0:T(8,128)S(1)}, f32[256,128]{1,0:T(8,128)S(1)}, u32[]{:S(2)}, u32[]{:S(2)}) collective-permute-start(f32[256,128]{1,0:T(8,128)S(1)} %get-tuple-element.28), channel_id=1, source_target_pairs={{0,2},{1,3},{2,0},{3,1},{4,6},{5,7},{6,4},{7,5},{8,10},{9,11},{10,... | collective-permute-start | bytes 393224 | tf_op jit(solution)/shard_map/ppermute | solution.py:28
  39.0 35.3 %collective-permute-start.6 = (f32[4,256,128]{2,1,0:T(8,128)}, f32[4,256,128]{2,1,0:T(8,128)}, u32[]{:S(2)}, u32[]{:S(2)}) collective-permute-start(f32[4,256,128]{2,1,0:T(8,128)} %all_to_all.10.refs_0_), channel_id=1, source_target_pairs={{0,1},{1,0},{2,3},{3,2},{4,5},{5,4},{6,7},{7,6},{8,9},{9,8},{10,11... | collective-permute-start | bytes 1572872 | tf_op jit(solution)/shard_map/ppermute | solution.py:28
  47.1 27.3 %collective-permute-start.7 = (f32[4,256,128]{2,1,0:T(8,128)S(1)}, f32[4,256,128]{2,1,0:T(8,128)}, u32[]{:S(2)}, u32[]{:S(2)}) collective-permute-start(f32[4,256,128]{2,1,0:T(8,128)S(1)} %collective-permute-done.3.refs_1_), channel_id=1, source_target_pairs={{0,1},{1,0},{2,3},{3,2},{4,5},{5,4},{6,7},{7,6},{8,9},{9,8},{10,11... | collective-permute-start | bytes 1572872 | tf_op jit(solution)/shard_map/ppermute | solution.py:28
  57.4 17.0 %collective-permute-start.8 = (f32[4,256,128]{2,1,0:T(8,128)}, f32[4,256,128]{2,1,0:T(8,128)}, u32[]{:S(2)}, u32[]{:S(2)}) collective-permute-start(f32[4,256,128]{2,1,0:T(8,128)} %collective-permute-done.4.refs_2_), channel_id=1, source_target_pairs={{0,1},{1,0},{2,3},{3,2},{4,5},{5,4},{6,7},{7,6},{8,9},{9,8},{10,11... | collective-permute-start | bytes 1572872 | tf_op jit(solution)/shard_map/ppermute | solution.py:28
  57.4 17.0 %collective-permute-start.9 = (f32[4,256,128]{2,1,0:T(8,128)}, f32[4,256,128]{2,1,0:T(8,128)}, u32[]{:S(2)}, u32[]{:S(2)}) collective-permute-start(f32[4,256,128]{2,1,0:T(8,128)} %collective-permute-done.5.refs_3_), channel_id=1, source_target_pairs={{0,1},{1,0},{2,3},{3,2},{4,5},{5,4},{6,7},{7,6},{8,9},{9,8},{10,11... | collective-permute-start | bytes 1572872 | tf_op jit(solution)/shard_map/ppermute | solution.py:28
  70.9 19.4 %all-to-all-start.1 = ((f32[4,256,128]{2,1,0:T(8,128)}), f32[4,256,128]{2,1,0:T(8,128)S(1)}, u32[]{:S(2)}, u32[]{:S(2)}) async-start(f32[4,256,128]{2,1,0:T(8,128)} %arrange.3), calls=%async_computation.1 | async-start | bytes 1048576 | tf_op jit(solution)/shard_map/all_to_all | solution.py:303
  87.1 11.6 %collective-permute-start.12 = (f32[256,512]{1,0:T(8,128)}, f32[256,512]{1,0:T(8,128)}, u32[]{:S(2)}, u32[]{:S(2)}) collective-permute-start(f32[256,512]{1,0:T(8,128)} %get-tuple-element.25), channel_id=1, source_target_pairs={{0,8},{24,16},{1,9},{25,17},{2,10},{26,18},{3,11},{27,19},{4,12},{... | collective-permute-start | bytes 1572872 | tf_op jit(solution)/shard_map/ppermute | solution.py:221
  91.0 18.2 %collective-permute-start.17 = (f32[4,256,128]{2,1,0:T(8,128)}, f32[4,256,128]{2,1,0:T(8,128)}, u32[]{:S(2)}, u32[]{:S(2)}) collective-permute-start(f32[4,256,128]{2,1,0:T(8,128)} %after.4.refs_0_), channel_id=1, source_target_pairs={{0,2},{1,3},{2,0},{3,1},{4,6},{5,7},{6,4},{7,5},{8,10},{9,11},{10,... | collective-permute-start | bytes 1572872 | tf_op jit(solution)/shard_map/ppermute | solution.py:28
  91.2 24.1 %collective-permute-start.18 = (f32[4,256,128]{2,1,0:T(8,128)}, f32[4,256,128]{2,1,0:T(8,128)}, u32[]{:S(2)}, u32[]{:S(2)}) collective-permute-start(f32[4,256,128]{2,1,0:T(8,128)} %after.4.refs_0_), channel_id=1, source_target_pairs={{0,4},{1,5},{2,6},{3,7},{4,0},{5,1},{6,2},{7,3},{8,12},{9,13},{10,... | collective-permute-start | bytes 1572872 | tf_op jit(solution)/shard_map/ppermute | solution.py:28
  93.9 21.4 %collective-permute-start.19 = (f32[4,256,128]{2,1,0:T(8,128)}, f32[4,256,128]{2,1,0:T(8,128)}, u32[]{:S(2)}, u32[]{:S(2)}) collective-permute-start(f32[4,256,128]{2,1,0:T(8,128)} %after.4.refs_0_), channel_id=1, source_target_pairs={{0,6},{1,7},{2,4},{3,5},{4,2},{5,3},{6,0},{7,1},{8,14},{9,15},{10,... | collective-permute-start | bytes 1572872 | tf_op jit(solution)/shard_map/ppermute | solution.py:28
  94.5 21.2 %collective-permute-start.11 = (f32[256,512]{1,0:T(8,128)}, f32[256,512]{1,0:T(8,128)}, u32[]{:S(2)}, u32[]{:S(2)}) collective-permute-start(f32[256,512]{1,0:T(8,128)} %get-tuple-element.25), channel_id=1, source_target_pairs={{8,16},{16,8},{9,17},{17,9},{10,18},{18,10},{11,19},{19,11},{12,20... | collective-permute-start | bytes 1572872 | tf_op jit(solution)/shard_map/ppermute | solution.py:223
  98.7 17.1 %collective-permute-start.10 = (f32[256,512]{1,0:T(8,128)}, f32[256,512]{1,0:T(8,128)}, u32[]{:S(2)}, u32[]{:S(2)}) collective-permute-start(f32[256,512]{1,0:T(8,128)} %copy-done.14), channel_id=1, source_target_pairs={{0,16},{16,24},{24,8},{8,0},{1,17},{17,25},{25,9},{9,1},{2,18},{18... | collective-permute-start | bytes 1572872 | tf_op jit(solution)/shard_map/ppermute | solution.py:222
  109.2 18.9 %collective-permute-start.13 = (f32[256,512]{1,0:T(8,128)}, f32[256,512]{1,0:T(8,128)}, u32[]{:S(2)}, u32[]{:S(2)}) collective-permute-start(f32[256,512]{1,0:T(8,128)} %add.125), channel_id=1, source_target_pairs={{8,24},{16,0},{0,8},{24,16},{9,25},{17,1},{1,9},{25,17},{10,26},{1... | collective-permute-start | bytes 1572872 | tf_op jit(solution)/shard_map/ppermute | solution.py:224
  115.2 21.2 %collective-permute-start.20 = (f32[4,256,128]{2,1,0:T(8,128)S(1)}, f32[4,256,128]{2,1,0:T(8,128)S(1)}, u32[]{:S(2)}, u32[]{:S(2)}) collective-permute-start(f32[4,256,128]{2,1,0:T(8,128)S(1)} %copy-done.5), channel_id=1, source_target_pairs={{0,1},{1,0},{2,3},{3,2},{4,5},{5,4},{6,7},{7,6},{8,9},{9,8},{10,11... | collective-permute-start | bytes 1572872 | tf_op jit(solution)/shard_map/ppermute | solution.py:28
  115.3 21.2 %collective-permute-start.21 = (f32[4,256,128]{2,1,0:T(8,128)}, f32[4,256,128]{2,1,0:T(8,128)S(1)}, u32[]{:S(2)}, u32[]{:S(2)}) collective-permute-start(f32[4,256,128]{2,1,0:T(8,128)} %collective-permute-done.17.refs_1_), channel_id=1, source_target_pairs={{0,1},{1,0},{2,3},{3,2},{4,5},{5,4},{6,7},{7,6},{8,9},{9,8},{10,11... | collective-permute-start | bytes 1572872 | tf_op jit(solution)/shard_map/ppermute | solution.py:28
  115.8 20.7 %collective-permute-start.22 = (f32[4,256,128]{2,1,0:T(8,128)}, f32[4,256,128]{2,1,0:T(8,128)S(1)}, u32[]{:S(2)}, u32[]{:S(2)}) collective-permute-start(f32[4,256,128]{2,1,0:T(8,128)} %collective-permute-done.18.refs_2_), channel_id=1, source_target_pairs={{0,1},{1,0},{2,3},{3,2},{4,5},{5,4},{6,7},{7,6},{8,9},{9,8},{10,11... | collective-permute-start | bytes 1572872 | tf_op jit(solution)/shard_map/ppermute | solution.py:28
  115.8 20.7 %collective-permute-start.23 = (f32[4,256,128]{2,1,0:T(8,128)}, f32[4,256,128]{2,1,0:T(8,128)S(1)}, u32[]{:S(2)}, u32[]{:S(2)}) collective-permute-start(f32[4,256,128]{2,1,0:T(8,128)} %collective-permute-done.19.refs_3_), channel_id=1, source_target_pairs={{0,1},{1,0},{2,3},{3,2},{4,5},{5,4},{6,7},{7,6},{8,9},{9,8},{10,11... | collective-permute-start | bytes 1572872 | tf_op jit(solution)/shard_map/ppermute | solution.py:28
  136.5 30.8 %collective-permute-start.24 = (f32[2,4,64,512]{3,2,0,1:T(8,128)}, f32[2,4,64,512]{3,2,0,1:T(8,128)}, u32[]{:S(2)}, u32[]{:S(2)}) collective-permute-start(f32[2,4,64,512]{3,2,0,1:T(8,128)} %bitcast.85), channel_id=1, source_target_pairs={{0,1},{1,0},{2,3},{3,2},{4,5},{5,4},{6,7},{7,6},{8,9},{9,8},{10,11... | collective-permute-start | bytes 3145736 | tf_op jit(solution)/shard_map/ppermute | solution.py:28
  149.2 13.7 %collective-permute-start.30 = (f32[256,512]{1,0:T(8,128)S(1)}, f32[256,512]{1,0:T(8,128)S(1)}, u32[]{:S(2)}, u32[]{:S(2)}) collective-permute-start(f32[256,512]{1,0:T(8,128)S(1)} %get-tuple-element.33), channel_id=1, source_target_pairs={{0,8},{24,16},{1,9},{25,17},{2,10},{26,18},{3,11},{27,19},{4,12},{... | collective-permute-start | bytes 1572872 | tf_op jit(solution)/shard_map/ppermute | solution.py:221
  150.6 37.8 %collective-permute-start.29 = (f32[256,512]{1,0:T(8,128)S(1)}, f32[256,512]{1,0:T(8,128)}, u32[]{:S(2)}, u32[]{:S(2)}) collective-permute-start(f32[256,512]{1,0:T(8,128)S(1)} %get-tuple-element.33), channel_id=1, source_target_pairs={{8,16},{16,8},{9,17},{17,9},{10,18},{18,10},{11,19},{19,11},{12,20... | collective-permute-start | bytes 1572872 | tf_op jit(solution)/shard_map/ppermute | solution.py:223
  152.1 36.2 %collective-permute-start.28 = (f32[256,512]{1,0:T(8,128)S(1)}, f32[256,512]{1,0:T(8,128)}, u32[]{:S(2)}, u32[]{:S(2)}) collective-permute-start(f32[256,512]{1,0:T(8,128)S(1)} %get-tuple-element.32), channel_id=1, source_target_pairs={{0,16},{16,24},{24,8},{8,0},{1,17},{17,25},{25,9},{9,1},{2,18},{18... | collective-permute-start | bytes 1572872 | tf_op jit(solution)/shard_map/ppermute | solution.py:222
  163.7 24.6 %collective-permute-start.31 = (f32[256,512]{1,0:T(8,128)}, f32[256,512]{1,0:T(8,128)}, u32[]{:S(2)}, u32[]{:S(2)}) collective-permute-start(f32[256,512]{1,0:T(8,128)} %add.142), channel_id=1, source_target_pairs={{8,24},{16,0},{0,8},{24,16},{9,25},{17,1},{1,9},{25,17},{10,26},{1... | collective-permute-start | bytes 1572872 | tf_op jit(solution)/shard_map/ppermute | solution.py:224
  168.9 10.2 %collective-permute-start.27 = (f32[2,64,512]{2,1,0:T(8,128)S(1)}, f32[2,64,512]{2,1,0:T(8,128)S(1)}, u32[]{:S(2)}, u32[]{:S(2)}) collective-permute-start(f32[2,64,512]{2,1,0:T(8,128)S(1)} %get-tuple-element.44), channel_id=1, source_target_pairs={{0,6},{1,7},{2,4},{3,5},{4,2},{5,3},{6,0},{7,1},{8,14},{9,15},{10,... | collective-permute-start | bytes 786440 | tf_op jit(solution)/shard_map/ppermute | solution.py:28
  171.9 12.6 %collective-permute-start.26 = (f32[2,64,512]{2,1,0:T(8,128)S(1)}, f32[2,64,512]{2,1,0:T(8,128)S(1)}, u32[]{:S(2)}, u32[]{:S(2)}) collective-permute-start(f32[2,64,512]{2,1,0:T(8,128)S(1)} %get-tuple-element.45), channel_id=1, source_target_pairs={{0,4},{1,5},{2,6},{3,7},{4,0},{5,1},{6,2},{7,3},{8,12},{9,13},{10,... | collective-permute-start | bytes 786440 | tf_op jit(solution)/shard_map/ppermute | solution.py:28
  179.1 8.4 %collective-permute-start.25 = (f32[2,64,512]{2,1,0:T(8,128)S(1)}, f32[2,64,512]{2,1,0:T(8,128)S(1)}, u32[]{:S(2)}, u32[]{:S(2)}) collective-permute-start(f32[2,64,512]{2,1,0:T(8,128)S(1)} %get-tuple-element.43), channel_id=1, source_target_pairs={{0,2},{1,3},{2,0},{3,1},{4,6},{5,7},{6,4},{7,5},{8,10},{9,11},{10,... | collective-permute-start | bytes 786440 | tf_op jit(solution)/shard_map/ppermute | solution.py:28
  196.4 8.0 %collective-permute-start.32 = (f32[2,64,512]{2,1,0:T(8,128)S(1)}, f32[2,64,512]{2,1,0:T(8,128)}, u32[]{:S(2)}, u32[]{:S(2)}) collective-permute-start(f32[2,64,512]{2,1,0:T(8,128)S(1)} %copy-done.28), channel_id=1, source_target_pairs={{0,8},{8,0},{16,24},{24,16},{1,9},{9,1},{17,25},{25,17},{2,10},{10... | collective-permute-start | bytes 786440 | tf_op jit(solution)/shard_map/ppermute | solution.py:28
  197.3 9.5 %collective-permute-start.37 = (f32[1,64,512]{2,1,0:T(8,128)}, f32[1,64,512]{2,1,0:T(8,128)}, u32[]{:S(2)}, u32[]{:S(2)}) collective-permute-start(f32[1,64,512]{2,1,0:T(8,128)} %get-tuple-element.47), channel_id=1, source_target_pairs={{0,6},{1,7},{2,4},{3,5},{4,2},{5,3},{6,0},{7,1},{8,14},{9,15},{10,... | collective-permute-start | bytes 393224 | tf_op jit(solution)/shard_map/ppermute | solution.py:28
  205.4 15.2 %collective-permute-start.33 = (f32[2,64,512]{2,1,0:T(8,128)S(1)}, f32[2,64,512]{2,1,0:T(8,128)S(1)}, u32[]{:S(2)}, u32[]{:S(2)}) collective-permute-start(f32[2,64,512]{2,1,0:T(8,128)S(1)} %add.145), channel_id=1, source_target_pairs={{0,16},{8,24},{16,0},{24,8},{1,17},{9,25},{17,1},{25,9},{2,18},{10... | collective-permute-start | bytes 786440 | tf_op jit(solution)/shard_map/ppermute | solution.py:28
  214.7 9.9 %collective-permute-start.39 = (f32[1,64,512]{2,1,0:T(8,128)S(1)}, f32[1,64,512]{2,1,0:T(8,128)S(1)}, u32[]{:S(2)}, u32[]{:S(2)}) collective-permute-start(f32[1,64,512]{2,1,0:T(8,128)S(1)} %add.152), channel_id=1, source_target_pairs={{0,16},{8,24},{16,0},{24,8},{1,17},{9,25},{17,1},{25,9},{2,18},{10... | collective-permute-start | bytes 393224 | tf_op jit(solution)/shard_map/ppermute | solution.py:28
  (41 other events, 544.7 us)

commit v5 on v4

v5 whole, which is shorter than its diff:
```python
import functools

import jax
import jax.numpy as jnp
from jax import lax
from jax.experimental import pallas as pl
from jax.experimental.pallas import tpu as pltpu
from jax.sharding import PartitionSpec as P

BOTH = ("prow", "pcol")
VMEM_LIMIT = 28 * 1024 * 1024
LANES = 128


def product(left_part, right_part):
    return jnp.dot(
        left_part, right_part, precision=lax.Precision.HIGH, preferred_element_type=jnp.float32
    )


def halves(value):
    high = value.astype(jnp.bfloat16)
    low = (value - high.astype(jnp.float32)).astype(jnp.bfloat16)
    return high, low


def flip(value, axis, bit):
    return lax.ppermute(value, axis, [(i, i ^ bit) for i in range(lax.axis_size(axis))])


def run(kernel, scalars, arrays, specs, waits, outs, out_specs, grid=(1,), scratch=(), name=None):
    def corner(array):
        block = (1,) * (array.ndim - 2) + (8, LANES)
        return pl.BlockSpec(block, lambda *_: (0,) * array.ndim)

    def body(*refs):
        first = len(scalars) + len(arrays)
        kernel(*refs[:first], *refs[first + len(waits) :])

    return pl.pallas_call(
        body,
        grid_spec=pltpu.PrefetchScalarGridSpec(
            num_scalar_prefetch=len(scalars),
            grid=grid,
            in_specs=list(specs) + [corner(array) for array in waits],
            out_specs=out_specs,
            scratch_shapes=list(scratch),
        ),
        out_shape=outs,
        compiler_params=pltpu.CompilerParams(vmem_limit_bytes=VMEM_LIMIT),
        cost_estimate=pl.CostEstimate(flops=0, bytes_accessed=0, transcendentals=0),
        name=name,
    )(*scalars, *arrays, *waits)


def whole(array):
    return pl.BlockSpec(array.shape, lambda *_: (0,) * array.ndim)


def cut_kernel(place, factor_ref, *out_refs):
    width = out_refs[0].shape[1]
    for o, out_ref in enumerate(out_refs):
        start = pl.multiple_of((place[2] ^ o) * width, width)
        out_ref[...] = factor_ref[0, :, pl.ds(start, width)]


def cut(place, factor, number, count, waits):
    _, unit_rows, columns = factor.shape
    piece = jax.ShapeDtypeStruct((unit_rows, columns // count), factor.dtype)
    spec = pl.BlockSpec((1, unit_rows, columns), lambda *_: (number, 0, 0))
    return run(
        cut_kernel, [place], [factor], [spec], waits, [piece] * count, [whole(piece)] * count,
        name="cut",
    )


def turn_kernel(place, *refs):
    count = len(refs) // 2
    for shift in range(count):

        @pl.when((place[1] ^ place[2]) == shift)
        def _copy(shift=shift):
            for o in range(count):
                refs[count + o][...] = refs[o ^ shift][...]


def turn(place, pieces):
    count = len(pieces)
    piece = jax.ShapeDtypeStruct(pieces[0].shape, pieces[0].dtype)
    specs = [whole(piece)] * count
    return run(turn_kernel, [place], pieces, specs, [], [piece] * count, specs, name="turn")


def arrange_kernel(place, *refs):
    out_ref = refs[-1]
    for o, piece_ref in enumerate(refs[:-1]):
        out_ref[place[1] ^ o] = piece_ref[...]


def arrange(place, pieces, waits):
    out = jax.ShapeDtypeStruct((len(pieces),) + pieces[0].shape, pieces[0].dtype)
    specs = [whole(piece) for piece in pieces]
    return run(arrange_kernel, [place], pieces, specs, waits, out, whole(out), name="arrange")


def add_kernel(*refs):
    total = refs[0][...]
    for ref in refs[1:-1]:
        total = total + ref[...]
    refs[-1][...] = total


def add_up(arrays, waits):
    out = jax.ShapeDtypeStruct(arrays[0].shape, arrays[0].dtype)
    specs = [whole(array) for array in arrays]
    return run(add_kernel, [], arrays, specs, waits, out, whole(out), name="add_up")


def partial_kernel(ratio, count, number, place, slots, ancestors, tile_ref, right_ref, *refs):
    out_refs, (right_high, right_low) = refs[:-2], refs[-2:]
    chunk_rows, columns = out_refs[0].shape
    blocks = tile_ref.shape[1] // columns
    step = pl.program_id(0)

    def listed(block):
        found = ancestors[number, 0] == block
        for i in range(1, ancestors.shape[1]):
            found = found | (ancestors[number, i] == block)
        return found

    @pl.when(step == 0)
    def _assemble():
        if len(right_ref.shape) == 2:
            right_high[...], right_low[...] = halves(right_ref[...])
            return
        _, _, unit_rows, width = right_ref.shape
        for owner in range(right_ref.shape[0]):
            lanes = pl.ds(owner // ratio * width, width)
            rows = pl.ds(owner % ratio * count * unit_rows, count * unit_rows)
            high, low = halves(right_ref[owner].reshape(count * unit_rows, width))
            right_high[rows, lanes] = high
            right_low[rows, lanes] = low

    def multiply(out_ref):
        out_ref[...] = jnp.zeros_like(out_ref)
        chunk = place[0] * count + slots[place[1], step]

        @pl.when(listed(chunk * chunk_rows // columns))
        def _chunk():
            def add(block, carry):
                @pl.when(listed(place[1] * blocks + block))
                def _block():
                    span = pl.ds(pl.multiple_of(block * columns, columns), columns)
                    high, low = halves(tile_ref[:, span])
                    right = right_high[span, :]
                    dot = functools.partial(jnp.dot, preferred_element_type=jnp.float32)
                    out_ref[...] += dot(high, right) + (
                        dot(high, right_low[span, :]) + dot(low, right)
                    )

                return carry

            lax.fori_loop(0, blocks, add, 0)

    for index, out_ref in enumerate(out_refs):
        pl.when(step == index)(functools.partial(multiply, out_ref))


def partial_product(place, slots, ancestors, tiles, right, ratio, columns, number):
    rows, cols = tiles.shape
    count = slots.shape[0]
    out = jax.ShapeDtypeStruct((rows // count, columns), jnp.float32)
    tile = pl.BlockSpec((rows // count, cols), lambda i, p, s, a: (s[p[1], i], 0))
    return run(
        functools.partial(partial_kernel, ratio, count, number),
        [place, slots, ancestors],
        [tiles, right],
        [tile, whole(right)],
        [],
        [out] * count,
        [whole(out)] * count,
        grid=(count,),
        scratch=[pltpu.VMEM((cols, columns), jnp.bfloat16)] * 2,
        name="partial_product",
    )


def to_column(pieces, ratio):
    return [pieces[0]] + [flip(pieces[o], "pcol", o * ratio) for o in range(1, len(pieces))]


def to_plane(pieces):
    return [pieces[0]] + [flip(pieces[o], "prow", o) for o in range(1, len(pieces))]


def to_plane_whole(factor, count, ratio):
    pieces = jnp.swapaxes(factor.reshape(factor.shape[0], count, -1), 0, 1)
    groups = [[c * ratio + k for c in range(count)] for k in range(ratio)]
    spread = lax.all_to_all(pieces, "pcol", 0, 0, axis_index_groups=groups)
    return lax.all_to_all(spread, "prow", 0, 0)


def in_rows(gathered, count, ratio):
    _, _, unit_rows, width = gathered.shape
    split = gathered.reshape(count, ratio, count, unit_rows, width)
    rows = jnp.transpose(split, (1, 2, 3, 0, 4))
    return rows.reshape(ratio * count * unit_rows, count * width)


FOUR_SLOTS = ((3, 2, 1, 0), (2, 0, 3, 1), (1, 3, 0, 2), (0, 1, 2, 3))


def slots_of(count):
    return FOUR_SLOTS if count == len(FOUR_SLOTS) else (tuple(range(count)),) * count


def sum_over_four(slots, first):
    near = lax.ppermute(slots[0], "prow", [(0, 1), (3, 2)])
    total = lax.ppermute(slots[1], "prow", [(0, 2), (2, 3), (3, 1), (1, 0)])
    middle = lax.ppermute(slots[0], "prow", [(1, 2), (2, 1)])
    last = lax.ppermute(slots[2] + near, "prow", [(1, 3), (2, 0), (0, 1), (3, 2)])
    return add_up([slots[3], total, middle, last], first)


def sum_over_line(slots, z, first):
    count = len(slots)
    if count == len(FOUR_SLOTS):
        return sum_over_four(slots, first)
    chunks = jnp.stack(slots)

    def chunk(index):
        return lax.dynamic_index_in_dim(chunks, jnp.clip(index, 0, count - 1), 0, keepdims=False)

    up = down = None
    for t in range(1, count):
        up_send, down_send = chunk(z + count - t), chunk(z + t - count)
        if up is not None:
            up_send, down_send = up_send + up, down_send + down
        up = lax.ppermute(up_send, "prow", [(i, i + 1) for i in range(min(t, count - 1))])
        down = lax.ppermute(
            down_send, "prow", [(i, i - 1) for i in range(max(count - t, 1), count)]
        )
    mine = chunk(z)
    return mine if up is None else mine + up + down


def sum_plane(matrices, pcol_count, pcol_index):
    number, rows, columns = matrices.shape
    if pcol_count == 1:
        return matrices
    paired = matrices.reshape(number, pcol_count // 2, 2, rows // pcol_count, columns)
    core, chip = pcol_index % 2, pcol_index // 2
    send = lax.dynamic_index_in_dim(paired, 1 - core, 2, keepdims=False)
    mine = lax.dynamic_index_in_dim(paired, core, 2, keepdims=False) + flip(send, "pcol", 1)
    total = lax.dynamic_index_in_dim(mine, chip, 1, keepdims=False)
    for o in range(1, pcol_count // 2):
        send = lax.dynamic_index_in_dim(mine, chip ^ o, 1, keepdims=False)
        total = total + flip(send, "pcol", 2 * o)
    return total


def sum_planes(matrices, count):
    bit = 1
    while bit < count:
        matrices = matrices + flip(matrices, "prow", bit)
        bit *= 2
    return matrices


def body(inverse_tiles, factor, link_factor, diag_inverse, ancestors):
    row_count, col_count = inverse_tiles.shape
    nsuper, unit_rows, columns = factor.shape
    count = lax.axis_size("prow")
    pcol_count = lax.axis_size("pcol")
    ratio = col_count // row_count
    z = lax.axis_index("prow")
    pcol_index = lax.axis_index("pcol")
    slice_rows = columns // pcol_count
    slice_start = pcol_index * slice_rows
    width = columns // count

    place = jnp.stack([pcol_index, z, pcol_index // ratio]).astype(jnp.int32)
    slots = jnp.asarray(slots_of(count), jnp.int32)
    own_block = (pcol_index * count + z) * unit_rows // columns
    keep = jnp.any(ancestors == own_block, axis=1)[:, None, None]
    local = jnp.where(keep, factor, 0.0)

    partials = []
    moved, gathered = [], []
    for number in range(nsuper):
        if width % LANES:
            own = to_plane_whole(factor[number], count, ratio)
            right = in_rows(lax.all_gather(own, "pcol", axis=0), count, ratio)
        else:
            sent = to_column(cut(place, factor, number, count, moved), ratio)
            moved = sent[1:]
            own = arrange(place, to_plane(turn(place, sent)), gathered)
            right = lax.all_gather(own, "pcol", axis=0)
            gathered = [right]
        partials.append(
            partial_product(
                place, slots, ancestors, inverse_tiles, right, ratio, columns, number
            )
        )

    def own_rows(matrices):
        return lax.dynamic_slice_in_dim(matrices, slice_start, slice_rows, -2)

    offdiag_list, sums, bases, ready, before = [], [], [], [], []
    for number in range(nsuper):
        before = before + [later[0] for later in partials[number + 1 : number + 2]]
        summed = sum_over_line(partials[number], z, before)
        part = product(local[number].T, summed)
        if number == 0:
            result = -jnp.where(keep[number], summed, 0.0)
            base = diag_inverse[0]
        else:
            result = -jnp.where(keep[number], summed + link_rows, 0.0)
            part = part + rest
            base = diag_inverse[number] + product(link_block.T, base_link)
        offdiag_list.append(result)
        ready.append(part)
        bases.append(own_rows(base))
        if number + 1 < nsuper:
            link_block = link_factor[number]
            cross_part = product(result.T, local[number + 1])
            link_part = cross_part + product(part, link_block)
            rest = product(cross_part.T, link_block) + product(link_block.T, link_part)
            base_link = product(base, link_block)
            link_rows = product(result, link_block)
            bases.append(own_rows(base_link))
            ready.append(link_part)
            group = sum_plane(jnp.stack(ready), pcol_count, pcol_index)
            before = [group, rest, link_rows]
            sums.append(sum_planes(group, count))
            ready = []
    sums.append(sum_planes(sum_plane(jnp.stack(ready), pcol_count, pcol_index), count))
    totals = jnp.concatenate(sums) + jnp.stack(bases)
    return (jnp.stack(offdiag_list), totals[0::2], -totals[1::2])


def solution(mesh):
    in_specs = (P("pcol", "prow"), P(None, ("pcol", "prow"), None), P(), P(), P())
    out_specs = (P(None, ("pcol", "prow"), None), P(None, "pcol", None), P(None, "pcol", None))
    return jax.shard_map(body, mesh=mesh, in_specs=in_specs, out_specs=out_specs, check_vma=False)
```

time: 226 us -> 220 us (0.973)
  blocking collectives: 18 us -> 0 us
  between operations: 1.18 us -> 14.5 us
  other arithmetic: 18.2 us -> 8.67 us
  waiting for transfers between devices: 89.2 us -> 98.1 us
  local copies, waits for them, and re-layouts: 13.8 us -> 21.5 us
  starting transfers between devices: 49.5 us -> 43.1 us
  matrix products: 11.7 us -> 8.89 us
    all_to_all x1 -> x0, blocking collectives: 18 us -> none  [body(): own = lax.all_to_all(received, 'prow', 0, 0)]
    all_gather x0 -> x2, waiting for transfers between devices: none -> 16.8 us  [body(): right = lax.all_gather(own, 'pcol', axis=0)]
    ppermute x32 -> x24, waiting for transfers between devices: 63.9 us -> 54.3 us  [flip(): lax.ppermute(value, axis, [(i, i ^ bit) for i in range(lax.axis_size(axis...]
    unnamed x65 -> x44, local copies, waits for them, and re-layouts: 8.17 us -> 17.1 us
    ppermute x2, starting transfers between devices: 8.52 us -> 2.86 us  [sum_over_four(): total = lax.ppermute(slots[1], 'prow', [(0, 2), (2, 3), (3, 1), (1, 0)])]
    another operation x3, other arithmetic: 7.46 us -> 2.37 us  [body(): return (jnp.stack(offdiag_list), totals[0::2], -totals[1::2])]
    all_to_all x1 -> x0, starting transfers between devices: 3.47 us -> none  [body(): own = lax.all_to_all(received, 'prow', 0, 0)]
    dot_general x9, matrix products: 11.7 us -> 8.89 us  [product(): jnp.dot(left_part, right_part, precision=lax.Precision.HIGH, preferred_el...]
  transfers between devices with their start and end apart: 41 -> 34, of which waited for: 18 -> 20; matrix products, arithmetic and copies ran while one was open for 13% -> 7% of each run, Pallas kernels for 10% -> 9%
where the time goes in v5:
time: 220 us; the launch traced here: 221 us
  waiting for transfers between devices  98.1 us (45%)
  starting transfers between devices  43.1 us (20%)
  Pallas kernels  25.8 us (12%)
  local copies, waits for them, and re-layouts  21.5 us (10%)
  between operations  14.5 us (7%)
  matrix products  8.89 us (4%)
  other arithmetic  8.67 us (4%)
    ppermute x24, waiting for transfers between devices, flip(): lax.ppermute(value, axis, [(i, i ^ bit) for i in range(lax.axis_size(axis...  54.3 us
    ppermute x24, starting transfers between devices, flip(): lax.ppermute(value, axis, [(i, i ^ bit) for i in range(lax.axis_size(axis...  30.3 us
    pallas_call x10, Pallas kernels, run(): pl.pallas_call(body, grid_spec=pltpu.PrefetchScalarGridSpec(num_scalar_pr...  25.8 us
    unnamed x44, local copies, waits for them, and re-layouts  17.1 us
    all_gather x2, waiting for transfers between devices, body(): right = lax.all_gather(own, 'pcol', axis=0)  16.8 us
    ppermute x2, waiting for transfers between devices, sum_over_four(): near = lax.ppermute(slots[0], 'prow', [(0, 1), (3, 2)])  14.6 us
    ppermute x2, waiting for transfers between devices, sum_over_four(): lax.ppermute(slots[2] + near, 'prow', [(1, 3), (2, 0), (0, 1), (3, 2)])  12.4 us
    dot_general x9, matrix products, product(): jnp.dot(left_part, right_part, precision=lax.Precision.HIGH, preferred_el...  8.89 us
  transfers between devices with their start and end apart: 34, of which 20 were waited for; matrix products, arithmetic and copies ran while one was open for 7% of the time, Pallas kernels for 9%

profile of v5, /device:TPU:0, one launch (start us, length us, event | category | flops | bytes accessed | tf_op | source)
XLA Modules:
  0.0 220.6 jit_solution(18104751301560384281)
XLA Ops:
  9.2 3.0 %collective-permute-start = (f32[256,128]{1,0:T(8,128)S(1)}, f32[256,128]{1,0:T(8,128)S(1)}, u32[]{:S(2)}, u32[]{:S(2)}) collective-permute-start(f32[256,128]{1,0:T(8,128)S(1)} %get-tuple-element.28), channel_id=1, source_target_pairs={{0,2},{1,3},{2,0},{3,1},{4,6},{5,7},{6,4},{7,5},{8,10},{9,11},{10,... | collective-permute-start | bytes 393224 | tf_op jit(solution)/shard_map/ppermute | solution.py:28
  13.8 2.4 %collective-permute-done.refs_2_ = f32[256,128]{1,0:T(8,128)S(1)} collective-permute-done((f32[256,128]{1,0:T(8,128)S(1)}, f32[256,128]{1,0:T(8,128)S(1)}, u32[]{:S(2)}, u32[]{:S(2)}) %collective-permute-start) | collective-permute-done | bytes 131104 | tf_op jit(solution)/shard_map/ppermute | solution.py:28
  16.2 3.9 %collective-permute-done.1.refs_3_ = f32[256,128]{1,0:T(8,128)S(1)} collective-permute-done((f32[256,128]{1,0:T(8,128)S(1)}, f32[256,128]{1,0:T(8,128)S(1)}, u32[]{:S(2)}, u32[]{:S(2)}) %collective-permute-start.1) | collective-permute-done | bytes 131104 | tf_op jit(solution)/shard_map/ppermute | solution.py:28
  22.3 2.6 %collective-permute-start.4 = (f32[256,128]{1,0:T(8,128)S(1)}, f32[256,128]{1,0:T(8,128)S(1)}, u32[]{:S(2)}, u32[]{:S(2)}) collective-permute-start(f32[256,128]{1,0:T(8,128)S(1)} %get-tuple-element.33), channel_id=1, source_target_pairs={{0,16},{8,24},{16,0},{24,8},{1,17},{9,25},{17,1},{25,9},{2,18},{10... | collective-permute-start | bytes 393224 | tf_op jit(solution)/shard_map/ppermute | solution.py:28
  25.1 1.8 collective-permute-done.3.refs_2_
  26.8 7.0 %collective-permute-done.4.refs_3_ = f32[256,128]{1,0:T(8,128)S(1)} collective-permute-done((f32[256,128]{1,0:T(8,128)S(1)}, f32[256,128]{1,0:T(8,128)S(1)}, u32[]{:S(2)}, u32[]{:S(2)}) %collective-permute-start.4) | collective-permute-done | bytes 131104 | tf_op jit(solution)/shard_map/ppermute | solution.py:28
  36.0 1.8 collective-permute-start.10
  44.7 2.4 %collective-permute-start.13 = (f32[256,128]{1,0:T(8,128)S(1)}, f32[256,128]{1,0:T(8,128)S(1)}, u32[]{:S(2)}, u32[]{:S(2)}) collective-permute-start(f32[256,128]{1,0:T(8,128)S(1)} %get-tuple-element.44), channel_id=1, source_target_pairs={{0,8},{8,0},{16,24},{24,16},{1,9},{9,1},{17,25},{25,17},{2,10},{10... | collective-permute-start | bytes 393224 | tf_op jit(solution)/shard_map/ppermute | solution.py:28
  50.3 7.0 %collective-permute-done.14.refs_3_ = f32[256,128]{1,0:T(8,128)S(1)} collective-permute-done((f32[256,128]{1,0:T(8,128)S(1)}, f32[256,128]{1,0:T(8,128)S(1)}, u32[]{:S(2)}, u32[]{:S(2)}) %collective-permute-start.14) | collective-permute-done | bytes 131104 | tf_op jit(solution)/shard_map/ppermute | solution.py:28
  57.4 14.6 %all-gather.5.cloned.1.call-done = f32[32,256,128]{2,1,0:T(8,128)} async-done(((f32[4,256,128]{2,1,0:T(8,128)}), f32[32,256,128]{2,1,0:T(8,128)}) %all-gather.5.cloned.1.call-update) | async-done | bytes 4194320 | tf_op jit(solution)/shard_map/all_gather | solution.py:298
  72.0 2.2 copy-done.3
  75.6 3.4 %copy-done.1 = f32[1024,2048]{1,0:T(8,128)S(1)} copy-done((f32[1024,2048]{1,0:T(8,128)S(1)}, f32[1024,2048]{1,0:T(8,128)}, u32[]{:S(2)}) %copy-start.1) | copy-done | bytes 8388632
  79.0 2.2 copy-done.4
  81.2 10.0 %partial_product.2 = (f32[256,512]{1,0:T(8,128)}, f32[256,512]{1,0:T(8,128)}, f32[256,512]{1,0:T(8,128)S(1)}, f32[256,512]{1,0:T(8,128)S(1)}) custom-call(s32[3]{0:T(128)S(1)} %pad_add_fusion.refs_0_, s32[4,4]{1,0:T(4,128)S(1)} %copy-done.11, s32[2,8]{1,0:T(2,128)S(1)} %copy-done.10, f32[1024,2048]{1,0:T(8,128)S(1)} %copy-done.1, f32[8,4,256,128]{3,2,1,0:T(8,128)S(1)} %bitcast.89), custom_call_target="tpu_custom_call" | custom-call | tf_op jit(solution)/shard_map/partial_product/pallas_call | solution.py:40
  95.1 10.1 %collective-permute-done.8 = f32[256,512]{1,0:T(8,128)S(1)} collective-permute-done((f32[256,512]{1,0:T(8,128)}, f32[256,512]{1,0:T(8,128)S(1)}, u32[]{:S(2)}, u32[]{:S(2)}) %collective-permute-start.8) | collective-permute-done | bytes 524320 | tf_op jit(solution)/shard_map/ppermute | solution.py:218
  106.1 2.4 %collective-permute-start.9 = (f32[256,512]{1,0:T(8,128)}, f32[256,512]{1,0:T(8,128)}, u32[]{:S(2)}, u32[]{:S(2)}) collective-permute-start(f32[256,512]{1,0:T(8,128)} %add.105), channel_id=1, source_target_pairs={{8,24},{16,0},{0,8},{24,16},{9,25},{17,1},{1,9},{25,17},{10,26},{1... | collective-permute-start | bytes 1572872 | tf_op jit(solution)/shard_map/ppermute | solution.py:221
  110.3 2.2 all-gather.7.cloned.1.call-done
  112.5 3.4 %copy-done.2 = f32[1024,2048]{1,0:T(8,128)S(1)} copy-done((f32[1024,2048]{1,0:T(8,128)S(1)}, f32[1024,2048]{1,0:T(8,128)}, u32[]{:S(2)}) %copy-start.2) | copy-done | bytes 8388632
  115.8 2.2 copy-done.7
  118.0 9.0 %partial_product.3 = (f32[256,512]{1,0:T(8,128)S(1)}, f32[256,512]{1,0:T(8,128)S(1)}, f32[256,512]{1,0:T(8,128)S(1)}, f32[256,512]{1,0:T(8,128)S(1)}) custom-call(s32[3]{0:T(128)S(1)} %pad_add_fusion.refs_0_, s32[4,4]{1,0:T(4,128)S(1)} %copy-done.11, s32[2,8]{1,0:T(2,128)S(1)} %copy-done.10, f32[1024,2048]{1,0:T(8,128)S(1)} %copy-done.2, ...), custom_call_target="tpu_custom_call" | custom-call | tf_op jit(solution)/shard_map/partial_product/pallas_call | solution.py:40
  135.0 1.9 fusion.28
  140.4 1.8 collective-permute-start.16
  147.4 4.6 %collective-permute-done.18 = f32[256,512]{1,0:T(8,128)S(1)} collective-permute-done((f32[256,512]{1,0:T(8,128)S(1)}, f32[256,512]{1,0:T(8,128)S(1)}, u32[]{:S(2)}, u32[]{:S(2)}) %collective-permute-start.18) | collective-permute-done | bytes 524320 | tf_op jit(solution)/shard_map/ppermute | solution.py:218
  152.1 2.5 %collective-permute-start.19 = (f32[256,512]{1,0:T(8,128)S(1)}, f32[256,512]{1,0:T(8,128)S(1)}, u32[]{:S(2)}, u32[]{:S(2)}) collective-permute-start(f32[256,512]{1,0:T(8,128)S(1)} %add.106), channel_id=1, source_target_pairs={{8,24},{16,0},{0,8},{24,16},{9,25},{17,1},{1,9},{25,17},{10,26},{1... | collective-permute-start | bytes 1572872 | tf_op jit(solution)/shard_map/ppermute | solution.py:221
  158.2 9.7 %collective-permute-done.22 = f32[2,64,512]{2,1,0:T(8,128)S(1)} collective-permute-done((f32[2,64,512]{2,1,0:T(8,128)S(1)}, f32[2,64,512]{2,1,0:T(8,128)S(1)}, u32[]{:S(2)}, u32[]{:S(2)}) %collective-permute-start.22) | collective-permute-done | bytes 262176 | tf_op jit(solution)/shard_map/ppermute | solution.py:28
  168.0 12.4 %collective-permute-done.19.refs_3_ = f32[256,512]{1,0:T(8,128)S(1)} collective-permute-done((f32[256,512]{1,0:T(8,128)S(1)}, f32[256,512]{1,0:T(8,128)S(1)}, u32[]{:S(2)}, u32[]{:S(2)}) %collective-permute-start.19) | collective-permute-done | bytes 524320 | tf_op jit(solution)/shard_map/ppermute | solution.py:221
  184.5 2.0 collective-permute-start.28
  188.6 3.6 %collective-permute-done.24 = f32[2,64,512]{2,1,0:T(8,128)S(1)} collective-permute-done((f32[2,64,512]{2,1,0:T(8,128)S(1)}, f32[2,64,512]{2,1,0:T(8,128)S(1)}, u32[]{:S(2)}, u32[]{:S(2)}) %collective-permute-start.24) | collective-permute-done | bytes 262176 | tf_op jit(solution)/shard_map/ppermute | solution.py:28
  195.0 6.2 %collective-permute-done.30 = f32[1,64,512]{2,1,0:T(8,128)S(1)} collective-permute-done((f32[1,64,512]{2,1,0:T(8,128)S(1)}, f32[1,64,512]{2,1,0:T(8,128)S(1)}, u32[]{:S(2)}, u32[]{:S(2)}) %collective-permute-start.30) | collective-permute-done | bytes 131104 | tf_op jit(solution)/shard_map/ppermute | solution.py:28
  201.3 3.3 %collective-permute-start.31 = (f32[1,64,512]{2,1,0:T(8,128)S(1)}, f32[1,64,512]{2,1,0:T(8,128)S(1)}, u32[]{:S(2)}, u32[]{:S(2)}) collective-permute-start(f32[1,64,512]{2,1,0:T(8,128)S(1)} %add.128), channel_id=1, source_target_pairs={{0,16},{8,24},{16,0},{24,8},{1,17},{9,25},{17,1},{25,9},{2,18},{10... | collective-permute-start | bytes 393224 | tf_op jit(solution)/shard_map/ppermute | solution.py:28
  205.6 4.0 %collective-permute-done.25 = f32[2,64,512]{2,1,0:T(8,128)S(1)} collective-permute-done((f32[2,64,512]{2,1,0:T(8,128)S(1)}, f32[2,64,512]{2,1,0:T(8,128)S(1)}, u32[]{:S(2)}, u32[]{:S(2)}) %collective-permute-start.25) | collective-permute-done | bytes 262176 | tf_op jit(solution)/shard_map/ppermute | solution.py:28
  209.7 2.7 %collective-permute-done.31 = f32[1,64,512]{2,1,0:T(8,128)S(1)} collective-permute-done((f32[1,64,512]{2,1,0:T(8,128)S(1)}, f32[1,64,512]{2,1,0:T(8,128)S(1)}, u32[]{:S(2)}, u32[]{:S(2)}) %collective-permute-start.31) | collective-permute-done | bytes 131104 | tf_op jit(solution)/shard_map/ppermute | solution.py:28
  (129 shorter events, 58.2 us)
Async XLA Ops:
  7.2 64.8 %all-gather.5.cloned.1.call-start = ((), (), s32[]{:S(2)}) async-start(), calls=%async_computation | async-start | bytes 4718592 | tf_op jit(solution)/shard_map/all_gather | solution.py:298
  9.2 6.9 %collective-permute-start = (f32[256,128]{1,0:T(8,128)S(1)}, f32[256,128]{1,0:T(8,128)S(1)}, u32[]{:S(2)}, u32[]{:S(2)}) collective-permute-start(f32[256,128]{1,0:T(8,128)S(1)} %get-tuple-element.28), channel_id=1, source_target_pairs={{0,2},{1,3},{2,0},{3,1},{4,6},{5,7},{6,4},{7,5},{8,10},{9,11},{10,... | collective-permute-start | bytes 393224 | tf_op jit(solution)/shard_map/ppermute | solution.py:28
  12.2 7.8 %collective-permute-start.1 = (f32[256,128]{1,0:T(8,128)S(1)}, f32[256,128]{1,0:T(8,128)S(1)}, u32[]{:S(2)}, u32[]{:S(2)}) collective-permute-start(f32[256,128]{1,0:T(8,128)S(1)} %get-tuple-element.29), channel_id=1, source_target_pairs={{0,4},{1,5},{2,6},{3,7},{4,0},{5,1},{6,2},{7,3},{8,12},{9,13},{10,... | collective-permute-start | bytes 393224 | tf_op jit(solution)/shard_map/ppermute | solution.py:28
  13.8 6.3 %collective-permute-start.2 = (f32[256,128]{1,0:T(8,128)S(1)}, f32[256,128]{1,0:T(8,128)S(1)}, u32[]{:S(2)}, u32[]{:S(2)}) collective-permute-start(f32[256,128]{1,0:T(8,128)S(1)} %get-tuple-element.30), channel_id=1, source_target_pairs={{0,6},{1,7},{2,4},{3,5},{4,2},{5,3},{6,0},{7,1},{8,14},{9,15},{10,... | collective-permute-start | bytes 393224 | tf_op jit(solution)/shard_map/ppermute | solution.py:28
  20.6 6.2 %collective-permute-start.3 = (f32[256,128]{1,0:T(8,128)S(1)}, f32[256,128]{1,0:T(8,128)S(1)}, u32[]{:S(2)}, u32[]{:S(2)}) collective-permute-start(f32[256,128]{1,0:T(8,128)S(1)} %get-tuple-element.32), channel_id=1, source_target_pairs={{0,8},{8,0},{16,24},{24,16},{1,9},{9,1},{17,25},{25,17},{2,10},{10... | collective-permute-start | bytes 393224 | tf_op jit(solution)/shard_map/ppermute | solution.py:28
  22.3 11.6 %collective-permute-start.4 = (f32[256,128]{1,0:T(8,128)S(1)}, f32[256,128]{1,0:T(8,128)S(1)}, u32[]{:S(2)}, u32[]{:S(2)}) collective-permute-start(f32[256,128]{1,0:T(8,128)S(1)} %get-tuple-element.33), channel_id=1, source_target_pairs={{0,16},{8,24},{16,0},{24,8},{1,17},{9,25},{17,1},{25,9},{2,18},{10... | collective-permute-start | bytes 393224 | tf_op jit(solution)/shard_map/ppermute | solution.py:28
  24.9 9.0 %collective-permute-start.5 = (f32[256,128]{1,0:T(8,128)S(1)}, f32[256,128]{1,0:T(8,128)S(1)}, u32[]{:S(2)}, u32[]{:S(2)}) collective-permute-start(f32[256,128]{1,0:T(8,128)S(1)} %get-tuple-element.34), channel_id=1, source_target_pairs={{0,24},{8,16},{16,8},{24,0},{1,25},{9,17},{17,9},{25,1},{2,26},{10... | collective-permute-start | bytes 393224 | tf_op jit(solution)/shard_map/ppermute | solution.py:28
  35.3 77.2 %all-gather.7.cloned.1.call-start = ((), (), s32[]{:S(2)}) async-start(), calls=%async_computation.1 | async-start | bytes 4718592 | tf_op jit(solution)/shard_map/all_gather | solution.py:298
  36.0 5.0 %collective-permute-start.10 = (f32[256,128]{1,0:T(8,128)S(1)}, f32[256,128]{1,0:T(8,128)S(1)}, u32[]{:S(2)}, u32[]{:S(2)}) collective-permute-start(f32[256,128]{1,0:T(8,128)S(1)} %get-tuple-element.40), channel_id=1, source_target_pairs={{0,2},{1,3},{2,0},{3,1},{4,6},{5,7},{6,4},{7,5},{8,10},{9,11},{10,... | collective-permute-start | bytes 393224 | tf_op jit(solution)/shard_map/ppermute | solution.py:28
  38.2 5.9 %collective-permute-start.12 = (f32[256,128]{1,0:T(8,128)S(1)}, f32[256,128]{1,0:T(8,128)S(1)}, u32[]{:S(2)}, u32[]{:S(2)}) collective-permute-start(f32[256,128]{1,0:T(8,128)S(1)} %get-tuple-element.42), channel_id=1, source_target_pairs={{0,6},{1,7},{2,4},{3,5},{4,2},{5,3},{6,0},{7,1},{8,14},{9,15},{10,... | collective-permute-start | bytes 393224 | tf_op jit(solution)/shard_map/ppermute | solution.py:28
  44.7 5.6 %collective-permute-start.13 = (f32[256,128]{1,0:T(8,128)S(1)}, f32[256,128]{1,0:T(8,128)S(1)}, u32[]{:S(2)}, u32[]{:S(2)}) collective-permute-start(f32[256,128]{1,0:T(8,128)S(1)} %get-tuple-element.44), channel_id=1, source_target_pairs={{0,8},{8,0},{16,24},{24,16},{1,9},{9,1},{17,25},{25,17},{2,10},{10... | collective-permute-start | bytes 393224 | tf_op jit(solution)/shard_map/ppermute | solution.py:28
  47.1 10.2 %collective-permute-start.14 = (f32[256,128]{1,0:T(8,128)S(1)}, f32[256,128]{1,0:T(8,128)S(1)}, u32[]{:S(2)}, u32[]{:S(2)}) collective-permute-start(f32[256,128]{1,0:T(8,128)S(1)} %get-tuple-element.45), channel_id=1, source_target_pairs={{0,16},{8,24},{16,0},{24,8},{1,17},{9,25},{17,1},{25,9},{2,18},{10... | collective-permute-start | bytes 393224 | tf_op jit(solution)/shard_map/ppermute | solution.py:28
  48.0 9.4 %collective-permute-start.15 = (f32[256,128]{1,0:T(8,128)S(1)}, f32[256,128]{1,0:T(8,128)S(1)}, u32[]{:S(2)}, u32[]{:S(2)}) collective-permute-start(f32[256,128]{1,0:T(8,128)S(1)} %get-tuple-element.46), channel_id=1, source_target_pairs={{0,24},{8,16},{16,8},{24,0},{1,25},{9,17},{17,9},{25,1},{2,26},{10... | collective-permute-start | bytes 393224 | tf_op jit(solution)/shard_map/ppermute | solution.py:28
  91.2 14.0 %collective-permute-start.8 = (f32[256,512]{1,0:T(8,128)}, f32[256,512]{1,0:T(8,128)S(1)}, u32[]{:S(2)}, u32[]{:S(2)}) collective-permute-start(f32[256,512]{1,0:T(8,128)} %get-tuple-element.37), channel_id=1, source_target_pairs={{0,8},{24,16},{1,9},{25,17},{2,10},{26,18},{3,11},{27,19},{4,12},{... | collective-permute-start | bytes 1572872 | tf_op jit(solution)/shard_map/ppermute | solution.py:218
  92.5 35.4 %collective-permute-start.7 = (f32[256,512]{1,0:T(8,128)}, f32[256,512]{1,0:T(8,128)}, u32[]{:S(2)}, u32[]{:S(2)}) collective-permute-start(f32[256,512]{1,0:T(8,128)} %get-tuple-element.37), channel_id=1, source_target_pairs={{8,16},{16,8},{9,17},{17,9},{10,18},{18,10},{11,19},{19,11},{12,20... | collective-permute-start | bytes 1572872 | tf_op jit(solution)/shard_map/ppermute | solution.py:220
  94.0 33.9 %collective-permute-start.6 = (f32[256,512]{1,0:T(8,128)}, f32[256,512]{1,0:T(8,128)}, u32[]{:S(2)}, u32[]{:S(2)}) collective-permute-start(f32[256,512]{1,0:T(8,128)} %get-tuple-element.36), channel_id=1, source_target_pairs={{0,16},{16,24},{24,8},{8,0},{1,17},{17,25},{25,9},{9,1},{2,18},{18... | collective-permute-start | bytes 1572872 | tf_op jit(solution)/shard_map/ppermute | solution.py:219
  106.1 21.8 %collective-permute-start.9 = (f32[256,512]{1,0:T(8,128)}, f32[256,512]{1,0:T(8,128)}, u32[]{:S(2)}, u32[]{:S(2)}) collective-permute-start(f32[256,512]{1,0:T(8,128)} %add.105), channel_id=1, source_target_pairs={{8,24},{16,0},{0,8},{24,16},{9,25},{17,1},{1,9},{25,17},{10,26},{1... | collective-permute-start | bytes 1572872 | tf_op jit(solution)/shard_map/ppermute | solution.py:221
  135.0 8.2 %collective-permute-start.20 = (f32[2,4,64,512]{3,2,0,1:T(8,128)}, f32[2,4,64,512]{3,2,0,1:T(8,128)}, u32[]{:S(2)}, u32[]{:S(2)}) collective-permute-start(f32[2,4,64,512]{3,2,0,1:T(8,128)} %bitcast.87), channel_id=1, source_target_pairs={{0,1},{1,0},{2,3},{3,2},{4,5},{5,4},{6,7},{7,6},{8,9},{9,8},{10,11... | collective-permute-start | bytes 3145736 | tf_op jit(solution)/shard_map/ppermute | solution.py:28
  138.2 13.7 %collective-permute-start.18 = (f32[256,512]{1,0:T(8,128)S(1)}, f32[256,512]{1,0:T(8,128)S(1)}, u32[]{:S(2)}, u32[]{:S(2)}) collective-permute-start(f32[256,512]{1,0:T(8,128)S(1)} %get-tuple-element.47.refs_4_), channel_id=1, source_target_pairs={{0,8},{24,16},{1,9},{25,17},{2,10},{26,18},{3,11},{27,19},{4,12},{... | collective-permute-start | bytes 1572872 | tf_op jit(solution)/shard_map/ppermute | solution.py:218
  139.7 28.3 %collective-permute-start.17 = (f32[256,512]{1,0:T(8,128)S(1)}, f32[256,512]{1,0:T(8,128)S(1)}, u32[]{:S(2)}, u32[]{:S(2)}) collective-permute-start(f32[256,512]{1,0:T(8,128)S(1)} %get-tuple-element.47.refs_4_), channel_id=1, source_target_pairs={{8,16},{16,8},{9,17},{17,9},{10,18},{18,10},{11,19},{19,11},{12,20... | collective-permute-start | bytes 1572872 | tf_op jit(solution)/shard_map/ppermute | solution.py:220
  140.4 27.6 %collective-permute-start.16 = (f32[256,512]{1,0:T(8,128)S(1)}, f32[256,512]{1,0:T(8,128)S(1)}, u32[]{:S(2)}, u32[]{:S(2)}) collective-permute-start(f32[256,512]{1,0:T(8,128)S(1)} %copy-done.13), channel_id=1, source_target_pairs={{0,16},{16,24},{24,8},{8,0},{1,17},{17,25},{25,9},{9,1},{2,18},{18... | collective-permute-start | bytes 1572872 | tf_op jit(solution)/shard_map/ppermute | solution.py:219
  144.8 10.4 %collective-permute-start.21 = (f32[2,64,512]{2,1,0:T(8,128)S(1)}, f32[2,64,512]{2,1,0:T(8,128)S(1)}, u32[]{:S(2)}, u32[]{:S(2)}) collective-permute-start(f32[2,64,512]{2,1,0:T(8,128)S(1)} %get-tuple-element.55), channel_id=1, source_target_pairs={{0,2},{1,3},{2,0},{3,1},{4,6},{5,7},{6,4},{7,5},{8,10},{9,11},{10,... | collective-permute-start | bytes 786440 | tf_op jit(solution)/shard_map/ppermute | solution.py:28
  152.1 28.3 %collective-permute-start.19 = (f32[256,512]{1,0:T(8,128)S(1)}, f32[256,512]{1,0:T(8,128)S(1)}, u32[]{:S(2)}, u32[]{:S(2)}) collective-permute-start(f32[256,512]{1,0:T(8,128)S(1)} %add.106), channel_id=1, source_target_pairs={{8,24},{16,0},{0,8},{24,16},{9,25},{17,1},{1,9},{25,17},{10,26},{1... | collective-permute-start | bytes 1572872 | tf_op jit(solution)/shard_map/ppermute | solution.py:221
  154.6 13.3 %collective-permute-start.22 = (f32[2,64,512]{2,1,0:T(8,128)S(1)}, f32[2,64,512]{2,1,0:T(8,128)S(1)}, u32[]{:S(2)}, u32[]{:S(2)}) collective-permute-start(f32[2,64,512]{2,1,0:T(8,128)S(1)} %get-tuple-element.57), channel_id=1, source_target_pairs={{0,4},{1,5},{2,6},{3,7},{4,0},{5,1},{6,2},{7,3},{8,12},{9,13},{10,... | collective-permute-start | bytes 786440 | tf_op jit(solution)/shard_map/ppermute | solution.py:28
  155.3 12.6 %collective-permute-start.23 = (f32[2,64,512]{2,1,0:T(8,128)S(1)}, f32[2,64,512]{2,1,0:T(8,128)S(1)}, u32[]{:S(2)}, u32[]{:S(2)}) collective-permute-start(f32[2,64,512]{2,1,0:T(8,128)S(1)} %get-tuple-element.56), channel_id=1, source_target_pairs={{0,6},{1,7},{2,4},{3,5},{4,2},{5,3},{6,0},{7,1},{8,14},{9,15},{10,... | collective-permute-start | bytes 786440 | tf_op jit(solution)/shard_map/ppermute | solution.py:28
  183.5 8.8 %collective-permute-start.24 = (f32[2,64,512]{2,1,0:T(8,128)S(1)}, f32[2,64,512]{2,1,0:T(8,128)S(1)}, u32[]{:S(2)}, u32[]{:S(2)}) collective-permute-start(f32[2,64,512]{2,1,0:T(8,128)S(1)} %fusion.17.refs_4_), channel_id=1, source_target_pairs={{0,8},{8,0},{16,24},{24,16},{1,9},{9,1},{17,25},{25,17},{2,10},{10... | collective-permute-start | bytes 786440 | tf_op jit(solution)/shard_map/ppermute | solution.py:28
  184.4 8.6 %collective-permute-start.27 = (f32[1,64,512]{2,1,0:T(8,128)S(1)}, f32[1,64,512]{2,1,0:T(8,128)S(1)}, u32[]{:S(2)}, u32[]{:S(2)}) collective-permute-start(f32[1,64,512]{2,1,0:T(8,128)S(1)} %get-tuple-element.58), channel_id=1, source_target_pairs={{0,2},{1,3},{2,0},{3,1},{4,6},{5,7},{6,4},{7,5},{8,10},{9,11},{10,... | collective-permute-start | bytes 393224 | tf_op jit(solution)/shard_map/ppermute | solution.py:28
  184.5 8.5 %collective-permute-start.28 = (f32[1,64,512]{2,1,0:T(8,128)S(1)}, f32[1,64,512]{2,1,0:T(8,128)S(1)}, u32[]{:S(2)}, u32[]{:S(2)}) collective-permute-start(f32[1,64,512]{2,1,0:T(8,128)S(1)} %get-tuple-element.60), channel_id=1, source_target_pairs={{0,4},{1,5},{2,6},{3,7},{4,0},{5,1},{6,2},{7,3},{8,12},{9,13},{10,... | collective-permute-start | bytes 393224 | tf_op jit(solution)/shard_map/ppermute | solution.py:28
  186.5 6.5 %collective-permute-start.29 = (f32[1,64,512]{2,1,0:T(8,128)S(1)}, f32[1,64,512]{2,1,0:T(8,128)S(1)}, u32[]{:S(2)}, u32[]{:S(2)}) collective-permute-start(f32[1,64,512]{2,1,0:T(8,128)S(1)} %get-tuple-element.59), channel_id=1, source_target_pairs={{0,6},{1,7},{2,4},{3,5},{4,2},{5,3},{6,0},{7,1},{8,14},{9,15},{10,... | collective-permute-start | bytes 393224 | tf_op jit(solution)/shard_map/ppermute | solution.py:28
  192.3 17.3 %collective-permute-start.25 = (f32[2,64,512]{2,1,0:T(8,128)S(1)}, f32[2,64,512]{2,1,0:T(8,128)S(1)}, u32[]{:S(2)}, u32[]{:S(2)}) collective-permute-start(f32[2,64,512]{2,1,0:T(8,128)S(1)} %add.121), channel_id=1, source_target_pairs={{0,16},{8,24},{16,0},{24,8},{1,17},{9,25},{17,1},{25,9},{2,18},{10... | collective-permute-start | bytes 786440 | tf_op jit(solution)/shard_map/ppermute | solution.py:28
  193.0 8.2 %collective-permute-start.30 = (f32[1,64,512]{2,1,0:T(8,128)S(1)}, f32[1,64,512]{2,1,0:T(8,128)S(1)}, u32[]{:S(2)}, u32[]{:S(2)}) collective-permute-start(f32[1,64,512]{2,1,0:T(8,128)S(1)} %fusion.24), channel_id=1, source_target_pairs={{0,8},{8,0},{16,24},{24,16},{1,9},{9,1},{17,25},{25,17},{2,10},{10... | collective-permute-start | bytes 393224 | tf_op jit(solution)/shard_map/ppermute | solution.py:28
  201.3 11.1 %collective-permute-start.31 = (f32[1,64,512]{2,1,0:T(8,128)S(1)}, f32[1,64,512]{2,1,0:T(8,128)S(1)}, u32[]{:S(2)}, u32[]{:S(2)}) collective-permute-start(f32[1,64,512]{2,1,0:T(8,128)S(1)} %add.128), channel_id=1, source_target_pairs={{0,16},{8,24},{16,0},{24,8},{1,17},{9,25},{17,1},{25,9},{2,18},{10... | collective-permute-start | bytes 393224 | tf_op jit(solution)/shard_map/ppermute | solution.py:28
  (24 other events, 224.7 us)
Sparse Core Ops, SparseCore 0:
  35.4 36.5 all-gather.4
  75.7 36.7 all-gather.6

commit v6 on v5

v6 whole, which is shorter than its diff:
```python
import functools

import jax
import jax.numpy as jnp
from jax import lax
from jax.experimental import pallas as pl
from jax.experimental.pallas import tpu as pltpu
from jax.sharding import PartitionSpec as P

BOTH = ("prow", "pcol")
VMEM_LIMIT = 28 * 1024 * 1024
LANES = 128


def halves(value):
    high = value.astype(jnp.bfloat16)
    low = (value - high.astype(jnp.float32)).astype(jnp.bfloat16)
    return high, low


def flip(value, axis, bit):
    return lax.ppermute(value, axis, [(i, i ^ bit) for i in range(lax.axis_size(axis))])


def run(
    kernel, scalars, arrays, specs, waits, outs, out_specs, grid=(1,), scratch=(), alias=None, name=None
):
    def corner(array):
        block = (1,) * (array.ndim - 2) + (8, LANES)
        return pl.BlockSpec(block, lambda *_: (0,) * array.ndim)

    def body(*refs):
        first = len(scalars) + len(arrays)
        kernel(*refs[:first], *refs[first + len(waits) :])

    return pl.pallas_call(
        body,
        grid_spec=pltpu.PrefetchScalarGridSpec(
            num_scalar_prefetch=len(scalars),
            grid=grid,
            in_specs=list(specs) + [corner(array) for array in waits],
            out_specs=out_specs,
            scratch_shapes=list(scratch),
        ),
        out_shape=outs,
        input_output_aliases=alias or {},
        compiler_params=pltpu.CompilerParams(vmem_limit_bytes=VMEM_LIMIT),
        cost_estimate=pl.CostEstimate(flops=0, bytes_accessed=0, transcendentals=0),
        name=name,
    )(*scalars, *arrays, *waits)


def whole(array):
    return pl.BlockSpec(array.shape, lambda *_: (0,) * array.ndim)


def cut_kernel(place, factor_ref, *out_refs):
    width = out_refs[0].shape[1]
    for o, out_ref in enumerate(out_refs):
        start = pl.multiple_of((place[2] ^ o) * width, width)
        out_ref[...] = factor_ref[0, :, pl.ds(start, width)]


def cut(place, factor, number, count, waits):
    _, unit_rows, columns = factor.shape
    piece = jax.ShapeDtypeStruct((unit_rows, columns // count), factor.dtype)
    spec = pl.BlockSpec((1, unit_rows, columns), lambda *_: (number, 0, 0))
    return run(
        cut_kernel, [place], [factor], [spec], waits, [piece] * count, [whole(piece)] * count,
        name="cut",
    )


def turn_kernel(place, *refs):
    count = len(refs) // 2
    for shift in range(count):

        @pl.when((place[1] ^ place[2]) == shift)
        def _copy(shift=shift):
            for o in range(count):
                refs[count + o][...] = refs[o ^ shift][...]


def turn(place, pieces):
    count = len(pieces)
    piece = jax.ShapeDtypeStruct(pieces[0].shape, pieces[0].dtype)
    specs = [whole(piece)] * count
    return run(turn_kernel, [place], pieces, specs, [], [piece] * count, specs, name="turn")


def arrange_kernel(place, *refs):
    out_ref = refs[-1]
    for o, piece_ref in enumerate(refs[:-1]):
        out_ref[place[1] ^ o] = piece_ref[...]


def arrange(place, pieces, waits):
    out = jax.ShapeDtypeStruct((len(pieces),) + pieces[0].shape, pieces[0].dtype)
    specs = [whole(piece) for piece in pieces]
    return run(arrange_kernel, [place], pieces, specs, waits, out, whole(out), name="arrange")


def add_kernel(*refs):
    total = refs[0][...]
    for ref in refs[1:-1]:
        total = total + ref[...]
    refs[-1][...] = total


def add_up(arrays, waits):
    out = jax.ShapeDtypeStruct(arrays[0].shape, arrays[0].dtype)
    specs = [whole(array) for array in arrays]
    return run(add_kernel, [], arrays, specs, waits, out, whole(out), name="add_up")


def is_listed(ancestors, number, block):
    found = ancestors[number, 0] == block
    for i in range(1, ancestors.shape[1]):
        found = found | (ancestors[number, i] == block)
    return found


def partial_kernel(offsets, ratio, count, number, place, slots, ancestors, tile_ref, *refs):
    piece_refs = refs[: len(offsets)]
    out_refs = refs[len(offsets) : -2]
    right_high, right_low = refs[-2:]
    chunk_rows, columns = out_refs[0].shape
    blocks = tile_ref.shape[1] // columns
    step = pl.program_id(0)

    def listed(block):
        return is_listed(ancestors, number, block)

    @pl.when(step == 0)
    def _assemble():
        for ref, offset in zip(piece_refs, offsets):
            if offset is None:
                right_high[...], right_low[...] = halves(ref[...])
                continue
            parts, unit_rows, width = ref.shape
            owner = place[0] ^ offset
            lanes = pl.ds(pl.multiple_of(owner // ratio * width, width), width)
            first = owner % ratio * (parts * unit_rows)
            rows = pl.ds(pl.multiple_of(first, parts * unit_rows), parts * unit_rows)
            high, low = halves(ref[...].reshape(parts * unit_rows, width))
            right_high[rows, lanes] = high
            right_low[rows, lanes] = low

    def multiply(out_ref):
        out_ref[...] = jnp.zeros_like(out_ref)
        chunk = place[0] * count + slots[place[1], step]

        @pl.when(listed(chunk * chunk_rows // columns))
        def _chunk():
            def add(block, carry):
                @pl.when(listed(place[1] * blocks + block))
                def _block():
                    span = pl.ds(pl.multiple_of(block * columns, columns), columns)
                    high, low = halves(tile_ref[:, span])
                    right = right_high[span, :]
                    dot = functools.partial(jnp.dot, preferred_element_type=jnp.float32)
                    out_ref[...] += dot(high, right) + (
                        dot(high, right_low[span, :]) + dot(low, right)
                    )

                return carry

            lax.fori_loop(0, blocks, add, 0)

    for index, out_ref in enumerate(out_refs):
        pl.when(step == index)(functools.partial(multiply, out_ref))


def partial_product(place, slots, ancestors, tiles, pieces, offsets, ratio, columns, number, waits):
    rows, cols = tiles.shape
    count = slots.shape[0]
    out = jax.ShapeDtypeStruct((rows // count, columns), jnp.float32)
    tile = pl.BlockSpec((rows // count, cols), lambda i, p, s, a: (s[p[1], i], 0))
    return run(
        functools.partial(partial_kernel, offsets, ratio, count, number),
        [place, slots, ancestors],
        [tiles] + pieces,
        [tile] + [whole(piece) for piece in pieces],
        waits,
        [out] * count,
        [whole(out)] * count,
        grid=(count,),
        scratch=[pltpu.VMEM((cols, columns), jnp.bfloat16)] * 2,
        name="partial_product",
    )


def dot(left, right, side=1):
    def one(a, b):
        return lax.dot_general(
            a, b, (((side,), (0,)), ((), ())), preferred_element_type=jnp.float32
        )

    left_high, left_low = halves(left)
    right_high, right_low = halves(right)
    return one(left_high, right_high) + (one(left_high, right_low) + one(left_low, right_high))


def part_by_core(place, matrix_ref, index, keep_ref, send_ref):
    _, chips, rows, _ = keep_ref.shape
    core = place[0] % 2
    for chip in range(chips):
        for ref, side in ((keep_ref, core), (send_ref, 1 - core)):
            first = pl.multiple_of((chip * 2 + side) * rows, rows)
            ref[index, chip] = matrix_ref[pl.ds(first, rows), :]


def finish_kernel(number, last, first, block, place, ancestors, *refs):
    refs = list(refs)
    sums, factor_ref = [refs.pop(0) for _ in range(4)], refs.pop(0)
    if not first:
        old_rest, old_rows, _ = (refs.pop(0) for _ in range(3))
    if not last:
        link_ref, next_ref = refs.pop(0), refs.pop(0)
    offdiag_ref, keep_ref, send_ref = (refs.pop(0) for _ in range(3))
    if not last:
        rest_ref, rows_ref = refs.pop(0), refs.pop(0)
    part_ref = refs.pop(0)
    offdiag_ref[...] = jnp.zeros_like(offdiag_ref)
    part_ref[...] = jnp.zeros_like(part_ref) if first else old_rest[...]

    own = block(place)

    @pl.when(is_listed(ancestors, number, own))
    def _own():
        summed = ((sums[0][...] + sums[1][...]) + sums[2][...]) + sums[3][...]
        part_ref[...] += dot(factor_ref[0], summed, 0)
        offdiag_ref[0] = -(summed if first else summed + old_rows[...])

    part_by_core(place, part_ref, 0, keep_ref, send_ref)
    if last:
        return
    link = link_ref[0]
    rest_ref[...] = jnp.zeros_like(rest_ref)
    rows_ref[...] = dot(offdiag_ref[0], link)

    @pl.when(is_listed(ancestors, number + 1, own))
    def _cross():
        rest_ref[...] = dot(offdiag_ref[0], next_ref[0], 0)

    cross = rest_ref[...]
    part_ref[...] = cross + dot(part_ref[...], link)
    part_by_core(place, part_ref, 1, keep_ref, send_ref)
    rest_ref[...] = dot(cross, link, 0) + dot(link, part_ref[...], 0)


def finish(number, block, place, ancestors, sums, factor, before, link_factor, chips, waits):
    nsuper, unit_rows, columns = factor.shape
    first, last = number == 0, number + 1 == nsuper
    slab = (1, unit_rows, columns)
    arrays, specs = list(sums), [whole(array) for array in sums]
    arrays.append(factor)
    specs.append(pl.BlockSpec(slab, lambda *_: (number, 0, 0)))
    alias = {}
    if not first:
        alias = {2 + len(arrays) + 2: 0}
        arrays += before
        specs += [whole(before[0]), whole(before[1])]
        specs.append(pl.BlockSpec((1, 8, LANES), lambda *_: (0, 0, 0)))
    if not last:
        arrays += [link_factor, factor]
        specs.append(pl.BlockSpec((1, columns, columns), lambda *_: (number, 0, 0)))
        specs.append(pl.BlockSpec(slab, lambda *_: (number + 1, 0, 0)))
    shape = jax.ShapeDtypeStruct
    groups = shape((1 if last else 2, chips, columns // (2 * chips), columns), jnp.float32)
    outs = [shape(factor.shape, jnp.float32), groups, groups]
    out_specs = [pl.BlockSpec(slab, lambda *_: (number, 0, 0)), whole(groups), whole(groups)]
    if not last:
        more = [shape((columns, columns), jnp.float32), shape((unit_rows, columns), jnp.float32)]
        outs += more
        out_specs += [whole(array) for array in more]
    return run(
        functools.partial(finish_kernel, number, last, first, block),
        [place, ancestors],
        arrays,
        specs,
        waits,
        outs,
        out_specs,
        scratch=[pltpu.VMEM((columns, columns), jnp.float32)],
        alias=alias,
        name="finish",
    )


def fold_kernel(place, keep_ref, received_ref, *out_refs):
    chip = place[0] // 2
    for o, out_ref in enumerate(out_refs):
        out_ref[...] = keep_ref[:, chip ^ o] + received_ref[:, chip ^ o]


def fold(place, keep, received):
    number, chips, rows, columns = keep.shape
    out = jax.ShapeDtypeStruct((number, rows, columns), jnp.float32)
    specs = [whole(keep)] * 2
    outs = [out] * chips
    return run(
        fold_kernel, [place], [keep, received], specs, [], outs, [whole(out)] * chips, name="fold"
    )


def bases_kernel(nsuper, place, diag_ref, link_ref, *refs):
    diag_out, link_out, base_ref, next_ref = refs
    rows = diag_out.shape[1]
    mine = pl.ds(pl.multiple_of(place[0] * rows, rows), rows)
    base_ref[...] = diag_ref[0]
    diag_out[0] = base_ref[mine, :]
    for number in range(1, nsuper):
        link = link_ref[number - 1]
        next_ref[...] = dot(base_ref[...], link)
        link_out[number - 1] = next_ref[mine, :]
        base_ref[...] = diag_ref[number] + dot(link, next_ref[...], 0)
        diag_out[number] = base_ref[mine, :]


def bases_of(place, diag_inverse, link_factor, rows, waits):
    nsuper, columns, _ = diag_inverse.shape
    outs = [
        jax.ShapeDtypeStruct((nsuper, rows, columns), jnp.float32),
        jax.ShapeDtypeStruct((nsuper - 1, rows, columns), jnp.float32),
    ]
    return run(
        functools.partial(bases_kernel, nsuper),
        [place],
        [diag_inverse, link_factor],
        [whole(diag_inverse), whole(link_factor)],
        waits,
        outs,
        [whole(out) for out in outs],
        scratch=[pltpu.VMEM((columns, columns), jnp.float32)] * 2,
        name="bases",
    )


def outputs_kernel(*refs):
    diag_base, link_base, *sums, diag_out, link_out = refs
    at = 0
    for left, right in zip(sums[::2], sums[1::2]):
        for index in range(left.shape[0]):
            total = left[index] + right[index]
            if at % 2 == 0:
                diag_out[at // 2] = total + diag_base[at // 2]
            else:
                link_out[at // 2] = -(total + link_base[at // 2])
            at += 1


def outputs(bases, sums):
    arrays = list(bases) + sums
    specs = [whole(array) for array in arrays]
    outs = [jax.ShapeDtypeStruct(base.shape, jnp.float32) for base in bases]
    return run(outputs_kernel, [], arrays, specs, [], outs, specs[:2], name="outputs")


def to_column(pieces, ratio):
    return [pieces[0]] + [flip(pieces[o], "pcol", o * ratio) for o in range(1, len(pieces))]


def to_plane(pieces):
    return [pieces[0]] + [flip(pieces[o], "prow", o) for o in range(1, len(pieces))]


def to_plane_whole(factor, count, ratio):
    pieces = jnp.swapaxes(factor.reshape(factor.shape[0], count, -1), 0, 1)
    groups = [[c * ratio + k for c in range(count)] for k in range(ratio)]
    spread = lax.all_to_all(pieces, "pcol", 0, 0, axis_index_groups=groups)
    return lax.all_to_all(spread, "prow", 0, 0)


def gather_plane(own, pcol_count):
    found = {0: own}
    for offset in range(2, pcol_count, 2):
        found[offset] = flip(own, "pcol", offset)
    for offset in range(0, pcol_count, 2):
        found[offset + 1] = flip(found[offset], "pcol", 1)
    return found


def in_rows(gathered, count, ratio):
    _, _, unit_rows, width = gathered.shape
    split = gathered.reshape(count, ratio, count, unit_rows, width)
    rows = jnp.transpose(split, (1, 2, 3, 0, 4))
    return rows.reshape(ratio * count * unit_rows, count * width)


FOUR_SLOTS = ((3, 2, 1, 0), (2, 0, 3, 1), (1, 3, 0, 2), (0, 1, 2, 3))


def slots_of(count):
    return FOUR_SLOTS if count == len(FOUR_SLOTS) else (tuple(range(count)),) * count


def sum_over_four(slots):
    near = lax.ppermute(slots[0], "prow", [(0, 1), (3, 2)])
    total = lax.ppermute(slots[1], "prow", [(0, 2), (2, 3), (3, 1), (1, 0)])
    middle = lax.ppermute(slots[0], "prow", [(1, 2), (2, 1)])
    both = add_up([slots[2], near], [])
    last = lax.ppermute(both, "prow", [(1, 3), (2, 0), (0, 1), (3, 2)])
    return [slots[3], total, middle, last]


def sum_over_line(slots, z):
    count = len(slots)
    if count == len(FOUR_SLOTS):
        return sum_over_four(slots)
    chunks = jnp.stack(slots)

    def chunk(index):
        return lax.dynamic_index_in_dim(chunks, jnp.clip(index, 0, count - 1), 0, keepdims=False)

    up = down = None
    for t in range(1, count):
        up_send, down_send = chunk(z + count - t), chunk(z + t - count)
        if up is not None:
            up_send, down_send = up_send + up, down_send + down
        up = lax.ppermute(up_send, "prow", [(i, i + 1) for i in range(min(t, count - 1))])
        down = lax.ppermute(
            down_send, "prow", [(i, i - 1) for i in range(max(count - t, 1), count)]
        )
    mine = chunk(z)
    none = jnp.zeros_like(mine)
    return [mine, none if up is None else up, none if down is None else down, none]


def sum_plane(place, keep, send):
    pieces = fold(place, keep, flip(send, "pcol", 1))
    return [pieces[0]] + [flip(pieces[o], "pcol", 2 * o) for o in range(1, len(pieces))]


def sum_planes(pieces, count, waits):
    bit = 1
    while True:
        total = add_up(pieces, waits)
        if bit >= count:
            return [total, jnp.zeros_like(total)]
        pieces, waits = [total, flip(total, "prow", bit)], []
        bit *= 2
        if bit >= count:
            return pieces


def body(inverse_tiles, factor, link_factor, diag_inverse, ancestors):
    row_count, col_count = inverse_tiles.shape
    nsuper, unit_rows, columns = factor.shape
    count = lax.axis_size("prow")
    pcol_count = lax.axis_size("pcol")
    ratio = col_count // row_count
    z = lax.axis_index("prow")
    pcol_index = lax.axis_index("pcol")
    width = columns // count
    place = jnp.stack([pcol_index, z, pcol_index // ratio]).astype(jnp.int32)
    slots = jnp.asarray(slots_of(count), jnp.int32)

    def own_block(place):
        return (place[0] * count + place[1]) * unit_rows // columns

    firsts = []
    moved, gathered = [], []
    for number in range(nsuper):
        if width % LANES:
            own = to_plane_whole(factor[number], count, ratio)
            right = in_rows(lax.all_gather(own, "pcol", axis=0), count, ratio)
            firsts.append((own, [None], [right]))
        else:
            sent = to_column(cut(place, factor, number, count, moved), ratio)
            moved = sent[1:]
            own = arrange(place, to_plane(turn(place, sent)), gathered)
            found = gather_plane(own, pcol_count)
            gathered = [found[o] for o in range(2, pcol_count, 2)]
            firsts.append((own, list(found.keys()), list(found.values())))
    bases = bases_of(place, diag_inverse, link_factor, columns // pcol_count, [firsts[0][0]])
    partials = []
    for number, (_, offsets, pieces) in enumerate(firsts):
        waits = [later[0] for later in firsts[number + 1 : number + 2]] + [bases[0]]
        partials.append(
            partial_product(
                place, slots, ancestors, inverse_tiles, pieces, offsets, ratio, columns, number,
                waits,
            )
        )

    sums, before, pending = [], [], None
    for number in range(nsuper):
        waits = [later[0] for later in partials[number + 1 : number + 2]]
        rows = sum_over_line(partials[number], z)
        offdiag, keep, send, *link = finish(
            number, own_block, place, ancestors, rows, factor, before, link_factor,
            pcol_count // 2, waits + (pending[1:] if pending else []),
        )
        if pending:
            sums += sum_planes(pending, count, [keep])
        before = link + [offdiag]
        pending = sum_plane(place, keep, send)
    sums += sum_planes(pending, count, [])
    return (offdiag, *outputs(bases, sums))


def solution(mesh):
    in_specs = (P("pcol", "prow"), P(None, ("pcol", "prow"), None), P(), P(), P())
    out_specs = (P(None, ("pcol", "prow"), None), P(None, "pcol", None), P(None, "pcol", None))
    return jax.shard_map(body, mesh=mesh, in_specs=in_specs, out_specs=out_specs, check_vma=False)
```

time: 220 us -> 225 us (1.023)
  waiting for transfers between devices: 98.1 us -> 142 us
  local copies, waits for them, and re-layouts: 21.5 us -> 5.44 us
  between operations: 14.5 us -> 0.99 us
  matrix products: 8.89 us -> 0 us
  other arithmetic: 8.67 us -> 0.08 us
  starting transfers between devices: 43.1 us -> 47.6 us
    ppermute x24 -> x38, waiting for transfers between devices: 54.3 us -> 79.1 us  [flip(): lax.ppermute(value, axis, [(i, i ^ bit) for i in range(lax.axis_size(axis...]
    ppermute x2, waiting for transfers between devices: 12.4 us -> 35.2 us  [sum_over_four(): last = lax.ppermute(both, 'prow', [(1, 3), (2, 0), (0, 1), (3, 2)])]
    all_gather x2 -> x0, waiting for transfers between devices: 16.8 us -> none  [body(): right = lax.all_gather(own, 'pcol', axis=0)]
    ppermute x2, waiting for transfers between devices: 0.01 us -> 16.5 us  [sum_over_four(): total = lax.ppermute(slots[1], 'prow', [(0, 2), (2, 3), (3, 1), (1, 0)])]
    unnamed x44 -> x18, local copies, waits for them, and re-layouts: 17.1 us -> 5.44 us
    dot_general x9 -> x0, matrix products: 8.89 us -> none  [product(): jnp.dot(left_part, right_part, precision=lax.Precision.HIGH, preferred_el...]
    ppermute x24 -> x38, starting transfers between devices: 30.3 us -> 38.4 us  [flip(): lax.ppermute(value, axis, [(i, i ^ bit) for i in range(lax.axis_size(axis...]
    another operation x5 -> x0, other arithmetic: 3.74 us -> none  [the longest x3 2.37 us: body(): return (jnp.stack(offdiag_list), totals[0::2], -totals[1::2])]
  transfers between devices with their start and end apart: 34 -> 46, of which waited for: 20 -> 21; matrix products, arithmetic and copies ran while one was open for 7% -> 0% of each run, Pallas kernels for 9% -> 8%
where the time goes in v6:
time: 225 us; the launch traced here: 224 us
  waiting for transfers between devices  142 us (63%)
  starting transfers between devices  47.6 us (21%)
  Pallas kernels  28 us (12%)
  local copies, waits for them, and re-layouts  5.44 us (2%)
    ppermute x38, waiting for transfers between devices, flip(): lax.ppermute(value, axis, [(i, i ^ bit) for i in range(lax.axis_size(axis...  79.1 us
    ppermute x38, starting transfers between devices, flip(): lax.ppermute(value, axis, [(i, i ^ bit) for i in range(lax.axis_size(axis...  38.4 us
    ppermute x2, waiting for transfers between devices, sum_over_four(): last = lax.ppermute(both, 'prow', [(1, 3), (2, 0), (0, 1), (3, 2)])  35.2 us
    pallas_call x20, Pallas kernels, run(): pl.pallas_call(body, grid_spec=pltpu.PrefetchScalarGridSpec(num_scalar_pr...  28 us
    ppermute x2, waiting for transfers between devices, sum_over_four(): total = lax.ppermute(slots[1], 'prow', [(0, 2), (2, 3), (3, 1), (1, 0)])  16.5 us
    ppermute x2, waiting for transfers between devices, sum_over_four(): near = lax.ppermute(slots[0], 'prow', [(0, 1), (3, 2)])  11.4 us
    unnamed x18, local copies, waits for them, and re-layouts  5.44 us
  transfers between devices with their start and end apart: 46, of which 21 were waited for; matrix products, arithmetic and copies ran while one was open for 0% of the time, Pallas kernels for 8%

profile of v6, /device:TPU:0, one launch (start us, length us, event | category | flops | bytes accessed | tf_op | source)
XLA Modules:
  0.0 224.3 jit_solution(11144261420549788529)
XLA Ops:
  2.7 3.0 %collective-permute-start = (f32[256,128]{1,0:T(8,128)S(1)}, f32[256,128]{1,0:T(8,128)S(1)}, u32[]{:S(2)}, u32[]{:S(2)}) collective-permute-start(f32[256,128]{1,0:T(8,128)S(1)} %get-tuple-element.47), channel_id=1, source_target_pairs={{0,2},{1,3},{2,0},{3,1},{4,6},{5,7},{6,4},{7,5},{8,10},{9,11},{10,... | collective-permute-start | bytes 393224 | tf_op jit(solution)/shard_map/ppermute | solution.py:22
  7.3 2.4 %collective-permute-done.refs_2_ = f32[256,128]{1,0:T(8,128)S(1)} collective-permute-done((f32[256,128]{1,0:T(8,128)S(1)}, f32[256,128]{1,0:T(8,128)S(1)}, u32[]{:S(2)}, u32[]{:S(2)}) %collective-permute-start) | collective-permute-done | bytes 131104 | tf_op jit(solution)/shard_map/ppermute | solution.py:22
  9.7 3.9 %collective-permute-done.1.refs_3_ = f32[256,128]{1,0:T(8,128)S(1)} collective-permute-done((f32[256,128]{1,0:T(8,128)S(1)}, f32[256,128]{1,0:T(8,128)S(1)}, u32[]{:S(2)}, u32[]{:S(2)}) %collective-permute-start.1) | collective-permute-done | bytes 131104 | tf_op jit(solution)/shard_map/ppermute | solution.py:22
  14.1 2.7 %collective-permute-start.10 = (f32[256,128]{1,0:T(8,128)S(1)}, f32[256,128]{1,0:T(8,128)S(1)}, u32[]{:S(2)}, u32[]{:S(2)}) collective-permute-start(f32[256,128]{1,0:T(8,128)S(1)} %get-tuple-element.61), channel_id=1, source_target_pairs={{0,16},{8,24},{16,0},{24,8},{1,17},{9,25},{17,1},{25,9},{2,18},{10... | collective-permute-start | bytes 393224 | tf_op jit(solution)/shard_map/ppermute | solution.py:22
  18.4 7.5 %collective-permute-done.10.refs_3_ = f32[256,128]{1,0:T(8,128)S(1)} collective-permute-done((f32[256,128]{1,0:T(8,128)S(1)}, f32[256,128]{1,0:T(8,128)S(1)}, u32[]{:S(2)}, u32[]{:S(2)}) %collective-permute-start.10) | collective-permute-done | bytes 131104 | tf_op jit(solution)/shard_map/ppermute | solution.py:22
  34.3 18.5 %collective-permute-done.3.refs_2_ = f32[256,128]{1,0:T(8,128)S(1)} collective-permute-done((f32[256,128]{1,0:T(8,128)S(1)}, f32[256,128]{1,0:T(8,128)S(1)}, u32[]{:S(2)}, u32[]{:S(2)}) %collective-permute-start.3) | collective-permute-done | bytes 131104 | tf_op jit(solution)/shard_map/ppermute | solution.py:22
  54.5 4.2 %collective-permute-done.5.refs_4_ = f32[256,128]{1,0:T(8,128)S(1)} collective-permute-done((f32[256,128]{1,0:T(8,128)S(1)}, f32[256,128]{1,0:T(8,128)S(1)}, u32[]{:S(2)}, u32[]{:S(2)}) %collective-permute-start.5) | collective-permute-done | bytes 131104 | tf_op jit(solution)/shard_map/ppermute | solution.py:22
  59.3 4.1 %collective-permute-start.6 = (f32[256,128]{1,0:T(8,128)S(1)}, f32[256,128]{1,0:T(8,128)S(1)}, u32[]{:S(2)}, u32[]{:S(2)}) collective-permute-start(f32[256,128]{1,0:T(8,128)S(1)} %get-tuple-element.55), channel_id=1, source_target_pairs={{0,8},{8,0},{16,24},{24,16},{1,9},{9,1},{17,25},{25,17},{2,10},{10... | collective-permute-start | bytes 393224 | tf_op jit(solution)/shard_map/ppermute | solution.py:22
  63.3 2.0 collective-permute-start.7
  65.3 2.0 collective-permute-done.6.refs_2_
  67.4 3.7 %collective-permute-start.8 = (f32[256,128]{1,0:T(8,128)S(1)}, f32[256,128]{1,0:T(8,128)S(1)}, u32[]{:S(2)}, u32[]{:S(2)}) collective-permute-start(f32[256,128]{1,0:T(8,128)S(1)} %get-tuple-element.57), channel_id=1, source_target_pairs={{0,24},{8,16},{16,8},{24,0},{1,25},{9,17},{17,9},{25,1},{2,26},{10... | collective-permute-start | bytes 393224 | tf_op jit(solution)/shard_map/ppermute | solution.py:22
  71.0 4.1 %collective-permute-done.7.refs_3_ = f32[256,128]{1,0:T(8,128)S(1)} collective-permute-done((f32[256,128]{1,0:T(8,128)S(1)}, f32[256,128]{1,0:T(8,128)S(1)}, u32[]{:S(2)}, u32[]{:S(2)}) %collective-permute-start.7) | collective-permute-done | bytes 131104 | tf_op jit(solution)/shard_map/ppermute | solution.py:22
  81.2 2.5 %bases.1 = (f32[2,64,512]{2,1,0:T(8,128)S(1)}, f32[1,64,512]{2,1,0:T(8,128)S(1)}) custom-call(s32[3]{0:T(128)S(1)} %pad_add_fusion.refs_0_, f32[2,512,512]{2,1,0:T(8,128)S(1)} %copy-done.6, f32[1,512,512]{2,1,0:T(8,128)S(1)} %copy-done.4, f32[4,256,128]{2,1,0:T(8,128)S(1)} %arrange.2.refs_3_.refs_4_), custom_call_target="tpu_custom_call" | custom-call | tf_op jit(solution)/shard_map/bases/pallas_call | solution.py:36
  85.7 9.2 %partial_product.3 = (f32[256,512]{1,0:T(8,128)S(1)}, f32[256,512]{1,0:T(8,128)S(1)}, f32[256,512]{1,0:T(8,128)S(1)}, f32[256,512]{1,0:T(8,128)S(1)}) custom-call(s32[3]{0:T(128)S(1)} %pad_add_fusion.refs_0_, s32[4,4]{1,0:T(4,128)S(1)} %copy-done.8, s32[2,8]{1,0:T(2,128)S(1)} %copy-done.7, f32[1024,2048]{1,0:T(8,128)S(1)} %copy-done, ...), custom_call_target="tpu_custom_call" | custom-call | tf_op jit(solution)/shard_map/partial_product/pallas_call | solution.py:36
  97.0 11.6 %collective-permute-done.16.refs_6_ = f32[4,256,128]{2,1,0:T(8,128)S(1)} collective-permute-done((f32[4,256,128]{2,1,0:T(8,128)S(1)}, f32[4,256,128]{2,1,0:T(8,128)S(1)}, u32[]{:S(2)}, u32[]{:S(2)}) %collective-permute-start.16) | collective-permute-done | bytes 524320 | tf_op jit(solution)/shard_map/ppermute | solution.py:22
  110.0 2.3 %collective-permute-start.30 = (f32[256,512]{1,0:T(8,128)S(1)}, f32[256,512]{1,0:T(8,128)S(1)}, u32[]{:S(2)}, u32[]{:S(2)}) collective-permute-start(f32[256,512]{1,0:T(8,128)S(1)} %get-tuple-element.69), channel_id=1, source_target_pairs={{0,16},{16,24},{24,8},{8,0},{1,17},{17,25},{25,9},{9,1},{2,18},{18... | collective-permute-start | bytes 1572872 | tf_op jit(solution)/shard_map/ppermute | solution.py:400
  112.3 3.1 %partial_product.2 = (f32[256,512]{1,0:T(8,128)S(1)}, f32[256,512]{1,0:T(8,128)S(1)}, f32[256,512]{1,0:T(8,128)S(1)}, f32[256,512]{1,0:T(8,128)S(1)}) custom-call(s32[3]{0:T(128)S(1)} %pad_add_fusion.refs_0_, s32[4,4]{1,0:T(4,128)S(1)} %copy-done.8, s32[2,8]{1,0:T(2,128)S(1)} %copy-done.7, f32[1024,2048]{1,0:T(8,128)S(1)} %copy-done, ...), custom_call_target="tpu_custom_call" | custom-call | tf_op jit(solution)/shard_map/partial_product/pallas_call | solution.py:36
  115.5 9.2 %collective-permute-done.30.refs_3_ = f32[256,512]{1,0:T(8,128)S(1)} collective-permute-done((f32[256,512]{1,0:T(8,128)S(1)}, f32[256,512]{1,0:T(8,128)S(1)}, u32[]{:S(2)}, u32[]{:S(2)}) %collective-permute-start.30) | collective-permute-done | bytes 524320 | tf_op jit(solution)/shard_map/ppermute | solution.py:400
  124.7 18.9 %collective-permute-done.33.refs_5_ = f32[256,512]{1,0:T(8,128)S(1)} collective-permute-done((f32[256,512]{1,0:T(8,128)S(1)}, f32[256,512]{1,0:T(8,128)S(1)}, u32[]{:S(2)}, u32[]{:S(2)}) %collective-permute-start.33) | collective-permute-done | bytes 524320 | tf_op jit(solution)/shard_map/ppermute | solution.py:403
  143.6 5.1 %finish.2 = (f32[2,256,512]{2,1,0:T(8,128)}, f32[2,4,64,512]{3,2,1,0:T(8,128)S(1)}, f32[2,4,64,512]{3,2,1,0:T(8,128)S(1)}, f32[512,512]{1,0:T(8,128)S(1)}, f32[256,512]{1,0:T(8,128)S(1)}) custom-call(s32[3]{0:T(128)S(1)} %pad_add_fusion.refs_0_, s32[2,8]{1,0:T(2,128)S(1)} %copy-done.7, f32[256,512]{1,0:T(8,128)S(1)} %get-tuple-element.68.refs_2_, ...), custom_call_target="tpu_custom_call" | custom-call | tf_op jit(solution)/shard_map/finish/pallas_call | solution.py:36
  151.0 11.4 %collective-permute-done.24.refs_1_ = f32[256,512]{1,0:T(8,128)S(1)} collective-permute-done((f32[256,512]{1,0:T(8,128)S(1)}, f32[256,512]{1,0:T(8,128)S(1)}, u32[]{:S(2)}, u32[]{:S(2)}) %collective-permute-start.24) | collective-permute-done | bytes 524320 | tf_op jit(solution)/shard_map/ppermute | solution.py:399
  162.4 2.5 %collective-permute-start.25 = (f32[256,512]{1,0:T(8,128)S(1)}, f32[256,512]{1,0:T(8,128)S(1)}, u32[]{:S(2)}, u32[]{:S(2)}) collective-permute-start(f32[256,512]{1,0:T(8,128)S(1)} %add_up.6), channel_id=1, source_target_pairs={{8,24},{16,0},{0,8},{24,16},{9,25},{17,1},{1,9},{25,17},{10,26},{1... | collective-permute-start | bytes 1572872 | tf_op jit(solution)/shard_map/ppermute | solution.py:403
  166.4 7.3 %collective-permute-done.22.refs_3_ = f32[256,512]{1,0:T(8,128)S(1)} collective-permute-done((f32[256,512]{1,0:T(8,128)S(1)}, f32[256,512]{1,0:T(8,128)S(1)}, u32[]{:S(2)}, u32[]{:S(2)}) %collective-permute-start.22) | collective-permute-done | bytes 524320 | tf_op jit(solution)/shard_map/ppermute | solution.py:400
  173.7 16.3 %collective-permute-done.25.refs_5_ = f32[256,512]{1,0:T(8,128)S(1)} collective-permute-done((f32[256,512]{1,0:T(8,128)S(1)}, f32[256,512]{1,0:T(8,128)S(1)}, u32[]{:S(2)}, u32[]{:S(2)}) %collective-permute-start.25) | collective-permute-done | bytes 524320 | tf_op jit(solution)/shard_map/ppermute | solution.py:403
  190.0 2.1 finish.3
  192.3 1.8 collective-permute-done.40.refs_2_
  195.8 2.5 %collective-permute-start.43 = (f32[1,64,512]{2,1,0:T(8,128)S(1)}, f32[1,64,512]{2,1,0:T(8,128)S(1)}, u32[]{:S(2)}, u32[]{:S(2)}) collective-permute-start(f32[1,64,512]{2,1,0:T(8,128)S(1)} %get-tuple-element.88), channel_id=1, source_target_pairs={{0,6},{1,7},{2,4},{3,5},{4,2},{5,3},{6,0},{7,1},{8,14},{9,15},{10,... | collective-permute-start | bytes 393224 | tf_op jit(solution)/shard_map/ppermute | solution.py:22
  198.2 2.8 %collective-permute-done.38.refs_1_ = f32[2,64,512]{2,1,0:T(8,128)S(1)} collective-permute-done((f32[2,64,512]{2,1,0:T(8,128)S(1)}, f32[2,64,512]{2,1,0:T(8,128)S(1)}, u32[]{:S(2)}, u32[]{:S(2)}) %collective-permute-start.38) | collective-permute-done | bytes 262176 | tf_op jit(solution)/shard_map/ppermute | solution.py:22
  201.1 2.4 %collective-permute-done.43.refs_3_ = f32[1,64,512]{2,1,0:T(8,128)S(1)} collective-permute-done((f32[1,64,512]{2,1,0:T(8,128)S(1)}, f32[1,64,512]{2,1,0:T(8,128)S(1)}, u32[]{:S(2)}, u32[]{:S(2)}) %collective-permute-start.43) | collective-permute-done | bytes 131104 | tf_op jit(solution)/shard_map/ppermute | solution.py:22
  203.9 2.6 %collective-permute-start.39 = (f32[2,64,512]{2,1,0:T(8,128)S(1)}, f32[2,64,512]{2,1,0:T(8,128)S(1)}, u32[]{:S(2)}, u32[]{:S(2)}) collective-permute-start(f32[2,64,512]{2,1,0:T(8,128)S(1)} %add_up.9.refs_2_), channel_id=1, source_target_pairs={{0,16},{8,24},{16,0},{24,8},{1,17},{9,25},{17,1},{25,9},{2,18},{10... | collective-permute-start | bytes 786440 | tf_op jit(solution)/shard_map/ppermute | solution.py:22
  206.6 4.1 %collective-permute-done.44.refs_1_ = f32[1,64,512]{2,1,0:T(8,128)S(1)} collective-permute-done((f32[1,64,512]{2,1,0:T(8,128)S(1)}, f32[1,64,512]{2,1,0:T(8,128)S(1)}, u32[]{:S(2)}, u32[]{:S(2)}) %collective-permute-start.44) | collective-permute-done | bytes 131104 | tf_op jit(solution)/shard_map/ppermute | solution.py:22
  211.4 10.5 %collective-permute-done.39.refs_3_ = f32[2,64,512]{2,1,0:T(8,128)S(1)} collective-permute-done((f32[2,64,512]{2,1,0:T(8,128)S(1)}, f32[2,64,512]{2,1,0:T(8,128)S(1)}, u32[]{:S(2)}, u32[]{:S(2)}) %collective-permute-start.39) | collective-permute-done | bytes 262176 | tf_op jit(solution)/shard_map/ppermute | solution.py:22
  (99 shorter events, 37.2 us)
Async XLA Ops:
  14.1 11.7 %collective-permute-start.10 = (f32[256,128]{1,0:T(8,128)S(1)}, f32[256,128]{1,0:T(8,128)S(1)}, u32[]{:S(2)}, u32[]{:S(2)}) collective-permute-start(f32[256,128]{1,0:T(8,128)S(1)} %get-tuple-element.61), channel_id=1, source_target_pairs={{0,16},{8,24},{16,0},{24,8},{1,17},{9,25},{17,1},{25,9},{2,18},{10... | collective-permute-start | bytes 393224 | tf_op jit(solution)/shard_map/ppermute | solution.py:22
  16.8 9.0 %collective-permute-start.11 = (f32[256,128]{1,0:T(8,128)S(1)}, f32[256,128]{1,0:T(8,128)S(1)}, u32[]{:S(2)}, u32[]{:S(2)}) collective-permute-start(f32[256,128]{1,0:T(8,128)S(1)} %get-tuple-element.62), channel_id=1, source_target_pairs={{0,24},{8,16},{16,8},{24,0},{1,25},{9,17},{17,9},{25,1},{2,26},{10... | collective-permute-start | bytes 393224 | tf_op jit(solution)/shard_map/ppermute | solution.py:22
  26.6 48.5 %collective-permute-start.12 = (f32[4,256,128]{2,1,0:T(8,128)S(1)}, f32[4,256,128]{2,1,0:T(8,128)S(1)}, u32[]{:S(2)}, u32[]{:S(2)}) collective-permute-start(f32[4,256,128]{2,1,0:T(8,128)S(1)} %arrange.2.refs_3_.refs_4_), channel_id=1, source_target_pairs={{0,2},{1,3},{2,0},{3,1},{4,6},{5,7},{6,4},{7,5},{8,10},{9,11},{10,... | collective-permute-start | bytes 1572872 | tf_op jit(solution)/shard_map/ppermute | solution.py:22
  28.4 47.3 %collective-permute-start.13 = (f32[4,256,128]{2,1,0:T(8,128)S(1)}, f32[4,256,128]{2,1,0:T(8,128)S(1)}, u32[]{:S(2)}, u32[]{:S(2)}) collective-permute-start(f32[4,256,128]{2,1,0:T(8,128)S(1)} %arrange.2.refs_3_.refs_4_), channel_id=1, source_target_pairs={{0,4},{1,5},{2,6},{3,7},{4,0},{5,1},{6,2},{7,3},{8,12},{9,13},{10,... | collective-permute-start | bytes 1572872 | tf_op jit(solution)/shard_map/ppermute | solution.py:22
  28.9 46.9 %collective-permute-start.14 = (f32[4,256,128]{2,1,0:T(8,128)S(1)}, f32[4,256,128]{2,1,0:T(8,128)S(1)}, u32[]{:S(2)}, u32[]{:S(2)}) collective-permute-start(f32[4,256,128]{2,1,0:T(8,128)S(1)} %arrange.2.refs_3_.refs_4_), channel_id=1, source_target_pairs={{0,6},{1,7},{2,4},{3,5},{4,2},{5,3},{6,0},{7,1},{8,14},{9,15},{10,... | collective-permute-start | bytes 1572872 | tf_op jit(solution)/shard_map/ppermute | solution.py:22
  32.0 20.7 %collective-permute-start.3 = (f32[256,128]{1,0:T(8,128)S(1)}, f32[256,128]{1,0:T(8,128)S(1)}, u32[]{:S(2)}, u32[]{:S(2)}) collective-permute-start(f32[256,128]{1,0:T(8,128)S(1)} %get-tuple-element.51), channel_id=1, source_target_pairs={{0,2},{1,3},{2,0},{3,1},{4,6},{5,7},{6,4},{7,5},{8,10},{9,11},{10,... | collective-permute-start | bytes 393224 | tf_op jit(solution)/shard_map/ppermute | solution.py:22
  33.8 20.7 %collective-permute-start.4 = (f32[256,128]{1,0:T(8,128)S(1)}, f32[256,128]{1,0:T(8,128)S(1)}, u32[]{:S(2)}, u32[]{:S(2)}) collective-permute-start(f32[256,128]{1,0:T(8,128)S(1)} %get-tuple-element.52), channel_id=1, source_target_pairs={{0,4},{1,5},{2,6},{3,7},{4,0},{5,1},{6,2},{7,3},{8,12},{9,13},{10,... | collective-permute-start | bytes 393224 | tf_op jit(solution)/shard_map/ppermute | solution.py:22
  63.3 11.8 %collective-permute-start.7 = (f32[256,128]{1,0:T(8,128)S(1)}, f32[256,128]{1,0:T(8,128)S(1)}, u32[]{:S(2)}, u32[]{:S(2)}) collective-permute-start(f32[256,128]{1,0:T(8,128)S(1)} %get-tuple-element.56), channel_id=1, source_target_pairs={{0,16},{8,24},{16,0},{24,8},{1,17},{9,25},{17,1},{25,9},{2,18},{10... | collective-permute-start | bytes 393224 | tf_op jit(solution)/shard_map/ppermute | solution.py:22
  67.4 8.8 %collective-permute-start.8 = (f32[256,128]{1,0:T(8,128)S(1)}, f32[256,128]{1,0:T(8,128)S(1)}, u32[]{:S(2)}, u32[]{:S(2)}) collective-permute-start(f32[256,128]{1,0:T(8,128)S(1)} %get-tuple-element.57), channel_id=1, source_target_pairs={{0,24},{8,16},{16,8},{24,0},{1,25},{9,17},{17,9},{25,1},{2,26},{10... | collective-permute-start | bytes 393224 | tf_op jit(solution)/shard_map/ppermute | solution.py:22
  75.1 9.2 %collective-permute-start.27 = (f32[4,256,128]{2,1,0:T(8,128)S(1)}, f32[4,256,128]{2,1,0:T(8,128)S(1)}, u32[]{:S(2)}, u32[]{:S(2)}) collective-permute-start(f32[4,256,128]{2,1,0:T(8,128)S(1)} %collective-permute-done.12.refs_5_), channel_id=1, source_target_pairs={{0,1},{1,0},{2,3},{3,2},{4,5},{5,4},{6,7},{7,6},{8,9},{9,8},{10,11... | collective-permute-start | bytes 1572872 | tf_op jit(solution)/shard_map/ppermute | solution.py:22
  75.6 10.1 %collective-permute-start.28 = (f32[4,256,128]{2,1,0:T(8,128)S(1)}, f32[4,256,128]{2,1,0:T(8,128)S(1)}, u32[]{:S(2)}, u32[]{:S(2)}) collective-permute-start(f32[4,256,128]{2,1,0:T(8,128)S(1)} %collective-permute-done.13.refs_6_), channel_id=1, source_target_pairs={{0,1},{1,0},{2,3},{3,2},{4,5},{5,4},{6,7},{7,6},{8,9},{9,8},{10,11... | collective-permute-start | bytes 1572872 | tf_op jit(solution)/shard_map/ppermute | solution.py:22
  75.7 10.0 %collective-permute-start.29 = (f32[4,256,128]{2,1,0:T(8,128)S(1)}, f32[4,256,128]{2,1,0:T(8,128)S(1)}, u32[]{:S(2)}, u32[]{:S(2)}) collective-permute-start(f32[4,256,128]{2,1,0:T(8,128)S(1)} %collective-permute-done.14.refs_7_), channel_id=1, source_target_pairs={{0,1},{1,0},{2,3},{3,2},{4,5},{5,4},{6,7},{7,6},{8,9},{9,8},{10,11... | collective-permute-start | bytes 1572872 | tf_op jit(solution)/shard_map/ppermute | solution.py:22
  76.7 19.8 %collective-permute-start.15 = (f32[4,256,128]{2,1,0:T(8,128)S(1)}, f32[4,256,128]{2,1,0:T(8,128)S(1)}, u32[]{:S(2)}, u32[]{:S(2)}) collective-permute-start(f32[4,256,128]{2,1,0:T(8,128)S(1)} %arrange.3.refs_4_.refs_12_), channel_id=1, source_target_pairs={{0,2},{1,3},{2,0},{3,1},{4,6},{5,7},{6,4},{7,5},{8,10},{9,11},{10,... | collective-permute-start | bytes 1572872 | tf_op jit(solution)/shard_map/ppermute | solution.py:22
  83.7 24.9 %collective-permute-start.16 = (f32[4,256,128]{2,1,0:T(8,128)S(1)}, f32[4,256,128]{2,1,0:T(8,128)S(1)}, u32[]{:S(2)}, u32[]{:S(2)}) collective-permute-start(f32[4,256,128]{2,1,0:T(8,128)S(1)} %arrange.3.refs_4_.refs_12_), channel_id=1, source_target_pairs={{0,4},{1,5},{2,6},{3,7},{4,0},{5,1},{6,2},{7,3},{8,12},{9,13},{10,... | collective-permute-start | bytes 1572872 | tf_op jit(solution)/shard_map/ppermute | solution.py:22
  84.3 25.0 %collective-permute-start.17 = (f32[4,256,128]{2,1,0:T(8,128)S(1)}, f32[4,256,128]{2,1,0:T(8,128)S(1)}, u32[]{:S(2)}, u32[]{:S(2)}) collective-permute-start(f32[4,256,128]{2,1,0:T(8,128)S(1)} %arrange.3.refs_4_.refs_12_), channel_id=1, source_target_pairs={{0,6},{1,7},{2,4},{3,5},{4,2},{5,3},{6,0},{7,1},{8,14},{9,15},{10,... | collective-permute-start | bytes 1572872 | tf_op jit(solution)/shard_map/ppermute | solution.py:22
  95.0 14.4 %collective-permute-start.32 = (f32[256,512]{1,0:T(8,128)S(1)}, f32[256,512]{1,0:T(8,128)S(1)}, u32[]{:S(2)}, u32[]{:S(2)}) collective-permute-start(f32[256,512]{1,0:T(8,128)S(1)} %get-tuple-element.70), channel_id=1, source_target_pairs={{0,8},{24,16},{1,9},{25,17},{2,10},{26,18},{3,11},{27,19},{4,12},{... | collective-permute-start | bytes 1572872 | tf_op jit(solution)/shard_map/ppermute | solution.py:399
  96.5 13.5 %collective-permute-start.18 = (f32[4,256,128]{2,1,0:T(8,128)S(1)}, f32[4,256,128]{2,1,0:T(8,128)S(1)}, u32[]{:S(2)}, u32[]{:S(2)}) collective-permute-start(f32[4,256,128]{2,1,0:T(8,128)S(1)} %arrange.3.refs_4_.refs_12_), channel_id=1, source_target_pairs={{0,1},{1,0},{2,3},{3,2},{4,5},{5,4},{6,7},{7,6},{8,9},{9,8},{10,11... | collective-permute-start | bytes 1572872 | tf_op jit(solution)/shard_map/ppermute | solution.py:22
  96.5 15.8 %collective-permute-start.19 = (f32[4,256,128]{2,1,0:T(8,128)S(1)}, f32[4,256,128]{2,1,0:T(8,128)S(1)}, u32[]{:S(2)}, u32[]{:S(2)}) collective-permute-start(f32[4,256,128]{2,1,0:T(8,128)S(1)} %collective-permute-done.15.refs_5_), channel_id=1, source_target_pairs={{0,1},{1,0},{2,3},{3,2},{4,5},{5,4},{6,7},{7,6},{8,9},{9,8},{10,11... | collective-permute-start | bytes 1572872 | tf_op jit(solution)/shard_map/ppermute | solution.py:22
  108.7 16.0 %collective-permute-start.31 = (f32[256,512]{1,0:T(8,128)S(1)}, f32[256,512]{1,0:T(8,128)S(1)}, u32[]{:S(2)}, u32[]{:S(2)}) collective-permute-start(f32[256,512]{1,0:T(8,128)S(1)} %get-tuple-element.70), channel_id=1, source_target_pairs={{8,16},{16,8},{9,17},{17,9},{10,18},{18,10},{11,19},{19,11},{12,20... | collective-permute-start | bytes 1572872 | tf_op jit(solution)/shard_map/ppermute | solution.py:401
  110.0 14.7 %collective-permute-start.30 = (f32[256,512]{1,0:T(8,128)S(1)}, f32[256,512]{1,0:T(8,128)S(1)}, u32[]{:S(2)}, u32[]{:S(2)}) collective-permute-start(f32[256,512]{1,0:T(8,128)S(1)} %get-tuple-element.69), channel_id=1, source_target_pairs={{0,16},{16,24},{24,8},{8,0},{1,17},{17,25},{25,9},{9,1},{2,18},{18... | collective-permute-start | bytes 1572872 | tf_op jit(solution)/shard_map/ppermute | solution.py:400
  112.3 31.3 %collective-permute-start.33 = (f32[256,512]{1,0:T(8,128)S(1)}, f32[256,512]{1,0:T(8,128)S(1)}, u32[]{:S(2)}, u32[]{:S(2)}) collective-permute-start(f32[256,512]{1,0:T(8,128)S(1)} %add_up.7), channel_id=1, source_target_pairs={{8,24},{16,0},{0,8},{24,16},{9,25},{17,1},{1,9},{25,17},{10,26},{1... | collective-permute-start | bytes 1572872 | tf_op jit(solution)/shard_map/ppermute | solution.py:403
  148.7 16.3 %collective-permute-start.34 = (f32[2,4,64,512]{3,2,1,0:T(8,128)S(1)}, f32[2,4,64,512]{3,2,1,0:T(8,128)S(1)}, u32[]{:S(2)}, u32[]{:S(2)}) collective-permute-start(f32[2,4,64,512]{3,2,1,0:T(8,128)S(1)} %get-tuple-element.76), channel_id=1, source_target_pairs={{0,1},{1,0},{2,3},{3,2},{4,5},{5,4},{6,7},{7,6},{8,9},{9,8},{10,11... | collective-permute-start | bytes 3145736 | tf_op jit(solution)/shard_map/ppermute | solution.py:22
  148.8 13.6 %collective-permute-start.24 = (f32[256,512]{1,0:T(8,128)S(1)}, f32[256,512]{1,0:T(8,128)S(1)}, u32[]{:S(2)}, u32[]{:S(2)}) collective-permute-start(f32[256,512]{1,0:T(8,128)S(1)} %get-tuple-element.66.refs_9_), channel_id=1, source_target_pairs={{0,8},{24,16},{1,9},{25,17},{2,10},{26,18},{3,11},{27,19},{4,12},{... | collective-permute-start | bytes 1572872 | tf_op jit(solution)/shard_map/ppermute | solution.py:399
  150.1 23.5 %collective-permute-start.22 = (f32[256,512]{1,0:T(8,128)S(1)}, f32[256,512]{1,0:T(8,128)S(1)}, u32[]{:S(2)}, u32[]{:S(2)}) collective-permute-start(f32[256,512]{1,0:T(8,128)S(1)} %get-tuple-element.65), channel_id=1, source_target_pairs={{0,16},{16,24},{24,8},{8,0},{1,17},{17,25},{25,9},{9,1},{2,18},{18... | collective-permute-start | bytes 1572872 | tf_op jit(solution)/shard_map/ppermute | solution.py:400
  150.3 23.4 %collective-permute-start.23 = (f32[256,512]{1,0:T(8,128)S(1)}, f32[256,512]{1,0:T(8,128)S(1)}, u32[]{:S(2)}, u32[]{:S(2)}) collective-permute-start(f32[256,512]{1,0:T(8,128)S(1)} %get-tuple-element.66.refs_9_), channel_id=1, source_target_pairs={{8,16},{16,8},{9,17},{17,9},{10,18},{18,10},{11,19},{19,11},{12,20... | collective-permute-start | bytes 1572872 | tf_op jit(solution)/shard_map/ppermute | solution.py:401
  162.4 27.6 %collective-permute-start.25 = (f32[256,512]{1,0:T(8,128)S(1)}, f32[256,512]{1,0:T(8,128)S(1)}, u32[]{:S(2)}, u32[]{:S(2)}) collective-permute-start(f32[256,512]{1,0:T(8,128)S(1)} %add_up.6), channel_id=1, source_target_pairs={{8,24},{16,0},{0,8},{24,16},{9,25},{17,1},{1,9},{25,17},{10,26},{1... | collective-permute-start | bytes 1572872 | tf_op jit(solution)/shard_map/ppermute | solution.py:403
  165.6 24.4 %collective-permute-start.35 = (f32[2,64,512]{2,1,0:T(8,128)S(1)}, f32[2,64,512]{2,1,0:T(8,128)S(1)}, u32[]{:S(2)}, u32[]{:S(2)}) collective-permute-start(f32[2,64,512]{2,1,0:T(8,128)S(1)} %get-tuple-element.77), channel_id=1, source_target_pairs={{0,2},{1,3},{2,0},{3,1},{4,6},{5,7},{6,4},{7,5},{8,10},{9,11},{10,... | collective-permute-start | bytes 786440 | tf_op jit(solution)/shard_map/ppermute | solution.py:22
  165.7 24.3 %collective-permute-start.36 = (f32[2,64,512]{2,1,0:T(8,128)S(1)}, f32[2,64,512]{2,1,0:T(8,128)S(1)}, u32[]{:S(2)}, u32[]{:S(2)}) collective-permute-start(f32[2,64,512]{2,1,0:T(8,128)S(1)} %get-tuple-element.78), channel_id=1, source_target_pairs={{0,4},{1,5},{2,6},{3,7},{4,0},{5,1},{6,2},{7,3},{8,12},{9,13},{10,... | collective-permute-start | bytes 786440 | tf_op jit(solution)/shard_map/ppermute | solution.py:22
  173.6 16.4 %collective-permute-start.37 = (f32[2,64,512]{2,1,0:T(8,128)S(1)}, f32[2,64,512]{2,1,0:T(8,128)S(1)}, u32[]{:S(2)}, u32[]{:S(2)}) collective-permute-start(f32[2,64,512]{2,1,0:T(8,128)S(1)} %get-tuple-element.79), channel_id=1, source_target_pairs={{0,6},{1,7},{2,4},{3,5},{4,2},{5,3},{6,0},{7,1},{8,14},{9,15},{10,... | collective-permute-start | bytes 786440 | tf_op jit(solution)/shard_map/ppermute | solution.py:22
  192.2 8.8 %collective-permute-start.38 = (f32[2,64,512]{2,1,0:T(8,128)S(1)}, f32[2,64,512]{2,1,0:T(8,128)S(1)}, u32[]{:S(2)}, u32[]{:S(2)}) collective-permute-start(f32[2,64,512]{2,1,0:T(8,128)S(1)} %add_up.8.refs_0_), channel_id=1, source_target_pairs={{0,8},{8,0},{16,24},{24,16},{1,9},{9,1},{17,25},{25,17},{2,10},{10... | collective-permute-start | bytes 786440 | tf_op jit(solution)/shard_map/ppermute | solution.py:22
  203.9 18.0 %collective-permute-start.39 = (f32[2,64,512]{2,1,0:T(8,128)S(1)}, f32[2,64,512]{2,1,0:T(8,128)S(1)}, u32[]{:S(2)}, u32[]{:S(2)}) collective-permute-start(f32[2,64,512]{2,1,0:T(8,128)S(1)} %add_up.9.refs_2_), channel_id=1, source_target_pairs={{0,16},{8,24},{16,0},{24,8},{1,17},{9,25},{17,1},{25,9},{2,18},{10... | collective-permute-start | bytes 786440 | tf_op jit(solution)/shard_map/ppermute | solution.py:22
  210.6 12.8 %collective-permute-start.45 = (f32[1,64,512]{2,1,0:T(8,128)S(1)}, f32[1,64,512]{2,1,0:T(8,128)S(1)}, u32[]{:S(2)}, u32[]{:S(2)}) collective-permute-start(f32[1,64,512]{2,1,0:T(8,128)S(1)} %add_up.11.refs_4_), channel_id=1, source_target_pairs={{0,16},{8,24},{16,0},{24,8},{1,17},{9,25},{17,1},{25,9},{2,18},{10... | collective-permute-start | bytes 393224 | tf_op jit(solution)/shard_map/ppermute | solution.py:22
  (23 other events, 444.6 us)

commit v7 on v6

--- a/solution.py
+++ b/solution.py
@@ -55,20 +55,18 @@
 
 
 def cut_kernel(place, factor_ref, *out_refs):
-    width = out_refs[0].shape[1]
+    width = out_refs[0].shape[2]
     for o, out_ref in enumerate(out_refs):
         start = pl.multiple_of((place[2] ^ o) * width, width)
-        out_ref[...] = factor_ref[0, :, pl.ds(start, width)]
-
-
-def cut(place, factor, number, count, waits):
-    _, unit_rows, columns = factor.shape
-    piece = jax.ShapeDtypeStruct((unit_rows, columns // count), factor.dtype)
-    spec = pl.BlockSpec((1, unit_rows, columns), lambda *_: (number, 0, 0))
-    return run(
-        cut_kernel, [place], [factor], [spec], waits, [piece] * count, [whole(piece)] * count,
-        name="cut",
-    )
+        out_ref[...] = factor_ref[:, :, pl.ds(start, width)]
+
+
+def cut(place, factor, count):
+    nsuper, unit_rows, columns = factor.shape
+    piece = jax.ShapeDtypeStruct((nsuper, unit_rows, columns // count), factor.dtype)
+    outs = [piece] * count
+    specs = [whole(piece)] * count
+    return run(cut_kernel, [place], [factor], [whole(factor)], [], outs, specs, name="cut")
 
 
 def turn_kernel(place, *refs):
@@ -78,14 +76,18 @@
         @pl.when((place[1] ^ place[2]) == shift)
         def _copy(shift=shift):
             for o in range(count):
-                refs[count + o][...] = refs[o ^ shift][...]
-
-
-def turn(place, pieces):
+                refs[count + o][...] = refs[o ^ shift][0]
+
+
+def turn(place, pieces, number, waits):
     count = len(pieces)
-    piece = jax.ShapeDtypeStruct(pieces[0].shape, pieces[0].dtype)
-    specs = [whole(piece)] * count
-    return run(turn_kernel, [place], pieces, specs, [], [piece] * count, specs, name="turn")
+    _, unit_rows, width = pieces[0].shape
+    piece = jax.ShapeDtypeStruct((unit_rows, width), pieces[0].dtype)
+    spec = pl.BlockSpec((1, unit_rows, width), lambda *_: (number, 0, 0))
+    return run(
+        turn_kernel, [place], pieces, [spec] * count, waits, [piece] * count,
+        [whole(piece)] * count, name="turn",
+    )
 
 
 def arrange_kernel(place, *refs):
@@ -98,6 +100,17 @@
     out = jax.ShapeDtypeStruct((len(pieces),) + pieces[0].shape, pieces[0].dtype)
     specs = [whole(piece) for piece in pieces]
     return run(arrange_kernel, [place], pieces, specs, waits, out, whole(out), name="arrange")
+
+
+def pack_kernel(*refs):
+    for index, ref in enumerate(refs[:-1]):
+        refs[-1][index] = ref[...]
+
+
+def pack(pieces, waits):
+    out = jax.ShapeDtypeStruct((len(pieces),) + pieces[0].shape, pieces[0].dtype)
+    specs = [whole(piece) for piece in pieces]
+    return run(pack_kernel, [], pieces, specs, waits, out, whole(out), name="pack")
 
 
 def add_kernel(*refs):
@@ -120,9 +133,8 @@
     return found
 
 
-def partial_kernel(offsets, ratio, count, number, place, slots, ancestors, tile_ref, *refs):
-    piece_refs = refs[: len(offsets)]
-    out_refs = refs[len(offsets) : -2]
+def partial_kernel(sides, ratio, count, number, place, slots, ancestors, tile_ref, *refs):
+    piece_refs, out_refs = refs[:sides], refs[sides:-2]
     right_high, right_low = refs[-2:]
     chunk_rows, columns = out_refs[0].shape
     blocks = tile_ref.shape[1] // columns
@@ -133,18 +145,19 @@
 
     @pl.when(step == 0)
     def _assemble():
-        for ref, offset in zip(piece_refs, offsets):
-            if offset is None:
-                right_high[...], right_low[...] = halves(ref[...])
-                continue
-            parts, unit_rows, width = ref.shape
-            owner = place[0] ^ offset
-            lanes = pl.ds(pl.multiple_of(owner // ratio * width, width), width)
-            first = owner % ratio * (parts * unit_rows)
-            rows = pl.ds(pl.multiple_of(first, parts * unit_rows), parts * unit_rows)
-            high, low = halves(ref[...].reshape(parts * unit_rows, width))
-            right_high[rows, lanes] = high
-            right_low[rows, lanes] = low
+        if len(piece_refs) == 1:
+            right_high[...], right_low[...] = halves(piece_refs[0][...])
+            return
+        for side, ref in enumerate(piece_refs):
+            chips, parts, unit_rows, width = ref.shape
+            for o in range(chips):
+                owner = place[0] ^ (2 * o + side)
+                lanes = pl.ds(pl.multiple_of(owner // ratio * width, width), width)
+                first = owner % ratio * (parts * unit_rows)
+                rows = pl.ds(pl.multiple_of(first, parts * unit_rows), parts * unit_rows)
+                high, low = halves(ref[o].reshape(parts * unit_rows, width))
+                right_high[rows, lanes] = high
+                right_low[rows, lanes] = low
 
     def multiply(out_ref):
         out_ref[...] = jnp.zeros_like(out_ref)
@@ -171,13 +184,13 @@
         pl.when(step == index)(functools.partial(multiply, out_ref))
 
 
-def partial_product(place, slots, ancestors, tiles, pieces, offsets, ratio, columns, number, waits):
+def partial_product(place, slots, ancestors, tiles, pieces, ratio, columns, number, waits):
     rows, cols = tiles.shape
     count = slots.shape[0]
     out = jax.ShapeDtypeStruct((rows // count, columns), jnp.float32)
     tile = pl.BlockSpec((rows // count, cols), lambda i, p, s, a: (s[p[1], i], 0))
     return run(
-        functools.partial(partial_kernel, offsets, ratio, count, number),
+        functools.partial(partial_kernel, len(pieces), ratio, count, number),
         [place, slots, ancestors],
         [tiles] + pieces,
         [tile] + [whole(piece) for piece in pieces],
@@ -219,7 +232,7 @@
         link_ref, next_ref = refs.pop(0), refs.pop(0)
     offdiag_ref, keep_ref, send_ref = (refs.pop(0) for _ in range(3))
     if not last:
-        rest_ref, rows_ref = refs.pop(0), refs.pop(0)
+        cross_ref, kept_ref = refs.pop(0), refs.pop(0)
     part_ref = refs.pop(0)
     offdiag_ref[...] = jnp.zeros_like(offdiag_ref)
     part_ref[...] = jnp.zeros_like(part_ref) if first else old_rest[...]
@@ -235,18 +248,33 @@
     part_by_core(place, part_ref, 0, keep_ref, send_ref)
     if last:
         return
-    link = link_ref[0]
-    rest_ref[...] = jnp.zeros_like(rest_ref)
-    rows_ref[...] = dot(offdiag_ref[0], link)
+    cross_ref[...] = jnp.zeros_like(cross_ref)
 
     @pl.when(is_listed(ancestors, number + 1, own))
     def _cross():
-        rest_ref[...] = dot(offdiag_ref[0], next_ref[0], 0)
-
-    cross = rest_ref[...]
-    part_ref[...] = cross + dot(part_ref[...], link)
-    part_by_core(place, part_ref, 1, keep_ref, send_ref)
-    rest_ref[...] = dot(cross, link, 0) + dot(link, part_ref[...], 0)
+        cross_ref[...] = dot(offdiag_ref[0], next_ref[0], 0)
+
+    kept_ref[...] = cross_ref[...] + dot(part_ref[...], link_ref[0])
+    part_by_core(place, kept_ref, 1, keep_ref, send_ref)
+
+
+def rest_kernel(link_ref, cross_ref, part_ref, offdiag_ref, rest_ref, rows_ref):
+    link = link_ref[0]
+    rest_ref[...] = dot(cross_ref[...], link, 0) + dot(link, part_ref[...], 0)
+    rows_ref[...] = dot(offdiag_ref[0], link)
+
+
+def rest_of(link_factor, cross, link_part, offdiag, number):
+    _, unit_rows, columns = offdiag.shape
+    link = pl.BlockSpec((1, columns, columns), lambda *_: (number, 0, 0))
+    rows = pl.BlockSpec((1, unit_rows, columns), lambda *_: (number, 0, 0))
+    outs = [cross, jax.ShapeDtypeStruct((unit_rows, columns), jnp.float32)]
+    outs = [jax.ShapeDtypeStruct(out.shape, jnp.float32) for out in outs]
+    return run(
+        rest_kernel, [], [link_factor, cross, link_part, offdiag],
+        [link, whole(cross), whole(link_part), rows], [], outs, [whole(out) for out in outs],
+        name="rest",
+    )
 
 
 def finish(number, block, place, ancestors, sums, factor, before, link_factor, chips, waits):
@@ -271,7 +299,7 @@
     outs = [shape(factor.shape, jnp.float32), groups, groups]
     out_specs = [pl.BlockSpec(slab, lambda *_: (number, 0, 0)), whole(groups), whole(groups)]
     if not last:
-        more = [shape((columns, columns), jnp.float32), shape((unit_rows, columns), jnp.float32)]
+        more = [shape((columns, columns), jnp.float32)] * 2
         outs += more
         out_specs += [whole(array) for array in more]
     return run(
@@ -294,13 +322,32 @@
         out_ref[...] = keep_ref[:, chip ^ o] + received_ref[:, chip ^ o]
 
 
-def fold(place, keep, received):
+def fold(place, keep, received, waits):
     number, chips, rows, columns = keep.shape
     out = jax.ShapeDtypeStruct((number, rows, columns), jnp.float32)
     specs = [whole(keep)] * 2
     outs = [out] * chips
     return run(
-        fold_kernel, [place], [keep, received], specs, [], outs, [whole(out)] * chips, name="fold"
+        fold_kernel, [place], [keep, received], specs, waits, outs, [whole(out)] * chips,
+        name="fold",
+    )
+
+
+def fold_pair_kernel(place, *refs):
+    *piece_refs, kept_ref, other_ref = refs
+    mine = place[1] % 2
+    for out_ref, index in ((kept_ref, mine), (other_ref, 1 - mine)):
+        total = piece_refs[0][index]
+        for ref in piece_refs[1:]:
+            total = total + ref[index]
+        out_ref[...] = total
+
+
+def fold_pair(place, pieces):
+    out = jax.ShapeDtypeStruct(pieces[0].shape[1:], jnp.float32)
+    specs = [whole(piece) for piece in pieces]
+    return run(
+        fold_pair_kernel, [place], pieces, specs, [], [out] * 2, [whole(out)] * 2, name="fold_pair"
     )
 
 
@@ -337,24 +384,26 @@
     )
 
 
-def outputs_kernel(*refs):
+def outputs_kernel(place, *refs):
     diag_base, link_base, *sums, diag_out, link_out = refs
-    at = 0
-    for left, right in zip(sums[::2], sums[1::2]):
-        for index in range(left.shape[0]):
-            total = left[index] + right[index]
-            if at % 2 == 0:
-                diag_out[at // 2] = total + diag_base[at // 2]
-            else:
-                link_out[at // 2] = -(total + link_base[at // 2])
-            at += 1
-
-
-def outputs(bases, sums):
+    steps = link_out.shape[0]
+    for number in range(steps):
+        pair = sums[2 * number : 2 * number + 2]
+
+        def put(diag, link, number=number):
+            diag_out[number] = diag[...] + diag_base[number]
+            link_out[number] = -(link[...] + link_base[number])
+
+        pl.when(place[1] % 2 == 0)(functools.partial(put, *pair))
+        pl.when(place[1] % 2 == 1)(functools.partial(put, *pair[::-1]))
+    diag_out[steps] = sums[-2][0] + sums[-1][0] + diag_base[steps]
+
+
+def outputs(place, bases, sums):
     arrays = list(bases) + sums
     specs = [whole(array) for array in arrays]
     outs = [jax.ShapeDtypeStruct(base.shape, jnp.float32) for base in bases]
-    return run(outputs_kernel, [], arrays, specs, [], outs, specs[:2], name="outputs")
+    return run(outputs_kernel, [place], arrays, specs, [], outs, specs[:2], name="outputs")
 
 
 def to_column(pieces, ratio):
@@ -373,12 +422,7 @@
 
 
 def gather_plane(own, pcol_count):
-    found = {0: own}
-    for offset in range(2, pcol_count, 2):
-        found[offset] = flip(own, "pcol", offset)
-    for offset in range(0, pcol_count, 2):
-        found[offset + 1] = flip(found[offset], "pcol", 1)
-    return found
+    return [own] + [flip(own, "pcol", offset) for offset in range(2, pcol_count, 2)]
 
 
 def in_rows(gathered, count, ratio):
@@ -401,7 +445,7 @@
     middle = lax.ppermute(slots[0], "prow", [(1, 2), (2, 1)])
     both = add_up([slots[2], near], [])
     last = lax.ppermute(both, "prow", [(1, 3), (2, 0), (0, 1), (3, 2)])
-    return [slots[3], total, middle, last]
+    return [slots[3], total, middle, last, near]
 
 
 def sum_over_line(slots, z):
@@ -424,24 +468,39 @@
         )
     mine = chunk(z)
     none = jnp.zeros_like(mine)
-    return [mine, none if up is None else up, none if down is None else down, none]
-
-
-def sum_plane(place, keep, send):
-    pieces = fold(place, keep, flip(send, "pcol", 1))
+    return [mine, none if up is None else up, none if down is None else down, none, mine]
+
+
+def sum_plane(place, keep, send, waits):
+    pieces = fold(place, keep, flip(send, "pcol", 1), waits)
     return [pieces[0]] + [flip(pieces[o], "pcol", 2 * o) for o in range(1, len(pieces))]
 
 
-def sum_planes(pieces, count, waits):
+def sum_planes(pieces, count):
     bit = 1
+    while True:
+        total = add_up(pieces, [])
+        if bit >= count:
+            return [total, jnp.zeros_like(total)]
+        pieces = [total, flip(total, "prow", bit)]
+        bit *= 2
+        if bit >= count:
+            return pieces
+
+
+def sum_pair_near(place, pieces):
+    kept, other = fold_pair(place, pieces)
+    return [kept, flip(other, "prow", 1)]
+
+
+def sum_pair_far(pieces, count, waits):
+    bit = 2
     while True:
         total = add_up(pieces, waits)
         if bit >= count:
-            return [total, jnp.zeros_like(total)]
+            return [total, flip(total, "prow", 1)]
         pieces, waits = [total, flip(total, "prow", bit)], []
         bit *= 2
-        if bit >= count:
-            return pieces
 
 
 def body(inverse_tiles, factor, link_factor, diag_inverse, ancestors):
@@ -459,45 +518,52 @@
     def own_block(place):
         return (place[0] * count + place[1]) * unit_rows // columns
 
-    firsts = []
-    moved, gathered = [], []
+    received = []
+    if width % LANES == 0:
+        sent = to_column(cut(place, factor, count), ratio)
+        for number in range(nsuper):
+            waits = received[-1][1:] if received else []
+            received.append(to_plane(turn(place, sent, number, waits)))
+    rows, firsts, gathered = [], [], []
     for number in range(nsuper):
-        if width % LANES:
+        if received:
+            own = arrange(place, received[number], gathered)
+            found = gather_plane(own, pcol_count)
+            gathered = found[1:]
+            waits = [piece for later in received[number + 1 : number + 2] for piece in later[1:]]
+            packed = pack(found, waits + (rows[-1][1:4] if rows else []))
+            pieces = [packed, flip(packed, "pcol", 1)]
+        else:
             own = to_plane_whole(factor[number], count, ratio)
-            right = in_rows(lax.all_gather(own, "pcol", axis=0), count, ratio)
-            firsts.append((own, [None], [right]))
-        else:
-            sent = to_column(cut(place, factor, number, count, moved), ratio)
-            moved = sent[1:]
-            own = arrange(place, to_plane(turn(place, sent)), gathered)
-            found = gather_plane(own, pcol_count)
-            gathered = [found[o] for o in range(2, pcol_count, 2)]
-            firsts.append((own, list(found.keys()), list(found.values())))
-    bases = bases_of(place, diag_inverse, link_factor, columns // pcol_count, [firsts[0][0]])
-    partials = []
-    for number, (_, offsets, pieces) in enumerate(firsts):
-        waits = [later[0] for later in firsts[number + 1 : number + 2]] + [bases[0]]
-        partials.append(
-            partial_product(
-                place, slots, ancestors, inverse_tiles, pieces, offsets, ratio, columns, number,
-                waits,
-            )
+            pieces = [in_rows(lax.all_gather(own, "pcol", axis=0), count, ratio)]
+        if number == 0:
+            bases = bases_of(place, diag_inverse, link_factor, columns // pcol_count, [own])
+        partial = partial_product(
+            place, slots, ancestors, inverse_tiles, pieces, ratio, columns, number, [bases[0]]
         )
+        firsts.append(partial[0])
+        *early, last_row, near = sum_over_line(partial, z)
+        rows.append([*early, near, last_row])
 
     sums, before, pending = [], [], None
     for number in range(nsuper):
-        waits = [later[0] for later in partials[number + 1 : number + 2]]
-        rows = sum_over_line(partials[number], z)
+        last = number + 1 == nsuper
+        waits = [] if last else [firsts[number + 1], rows[number + 1][3]]
         offdiag, keep, send, *link = finish(
-            number, own_block, place, ancestors, rows, factor, before, link_factor,
-            pcol_count // 2, waits + (pending[1:] if pending else []),
+            number, own_block, place, ancestors, rows[number][:3] + rows[number][4:], factor, before,
+            link_factor, pcol_count // 2, waits + (pending if pending else []),
         )
         if pending:
-            sums += sum_planes(pending, count, [keep])
-        before = link + [offdiag]
-        pending = sum_plane(place, keep, send)
-    sums += sum_planes(pending, count, [])
-    return (offdiag, *outputs(bases, sums))
+            sums += sum_pair_far(pending, count, [keep])
+        waits = []
+        if not last:
+            rest = rest_of(link_factor, *link, offdiag, number)
+            before = [*rest, offdiag]
+            waits = [rest[0], rows[number + 1][1]]
+        group = sum_plane(place, keep, send, waits)
+        pending = None if last else sum_pair_near(place, group)
+    sums += sum_planes(group, count)
+    return (offdiag, *outputs(place, bases, sums))
 
 
 def solution(mesh):

time: 225 us -> 200 us (0.89)
  waiting for transfers between devices: 142 us -> 113 us
  starting transfers between devices: 47.6 us -> 58 us
  local copies, waits for them, and re-layouts: 5.44 us -> 1.27 us
    ppermute x2, waiting for transfers between devices: 35.2 us -> 10.6 us  [sum_over_four(): last = lax.ppermute(both, 'prow', [(1, 3), (2, 0), (0, 1), (3, 2)])]
    ppermute x2, starting transfers between devices: 2.78 us -> 9.73 us  [sum_over_four(): near = lax.ppermute(slots[0], 'prow', [(0, 1), (3, 2)])]
    ppermute x2, starting transfers between devices: 2.54 us -> 9.47 us  [sum_over_four(): last = lax.ppermute(both, 'prow', [(1, 3), (2, 0), (0, 1), (3, 2)])]
    ppermute x38 -> x30, starting transfers between devices: 38.4 us -> 33 us  [flip(): lax.ppermute(value, axis, [(i, i ^ bit) for i in range(lax.axis_size(axis...]
    unnamed x18, local copies, waits for them, and re-layouts: 5.44 us -> 1.27 us
    ppermute x38 -> x30, waiting for transfers between devices: 79.1 us -> 77.2 us  [flip(): lax.ppermute(value, axis, [(i, i ^ bit) for i in range(lax.axis_size(axis...]
    pallas_call x20 -> x23, Pallas kernels: 28 us -> 26.4 us  [run(): pl.pallas_call(body, grid_spec=pltpu.PrefetchScalarGridSpec(num_scalar_pr...]
  transfers between devices with their start and end apart: 46 -> 38, of which waited for: 21 -> 24; matrix products, arithmetic and copies ran while one was open for 0% -> 0% of each run, Pallas kernels for 8% -> 8%
where the time goes in v7:
time: 200 us
  waiting for transfers between devices  113 us (56%)
  starting transfers between devices  58 us (29%)
  Pallas kernels  26.4 us (13%)
    ppermute x30, waiting for transfers between devices, flip(): lax.ppermute(value, axis, [(i, i ^ bit) for i in range(lax.axis_size(axis...  77.2 us
    ppermute x30, starting transfers between devices, flip(): lax.ppermute(value, axis, [(i, i ^ bit) for i in range(lax.axis_size(axis...  33 us
    pallas_call x23, Pallas kernels, run(): pl.pallas_call(body, grid_spec=pltpu.PrefetchScalarGridSpec(num_scalar_pr...  26.4 us
    ppermute x2, waiting for transfers between devices, sum_over_four(): total = lax.ppermute(slots[1], 'prow', [(0, 2), (2, 3), (3, 1), (1, 0)])  15.5 us
    ppermute x2, waiting for transfers between devices, sum_over_four(): last = lax.ppermute(both, 'prow', [(1, 3), (2, 0), (0, 1), (3, 2)])  10.6 us
    ppermute x2, starting transfers between devices, sum_over_four(): near = lax.ppermute(slots[0], 'prow', [(0, 1), (3, 2)])  9.73 us
    ppermute x2, waiting for transfers between devices, sum_over_four(): near = lax.ppermute(slots[0], 'prow', [(0, 1), (3, 2)])  9.73 us
    ppermute x2, starting transfers between devices, sum_over_four(): last = lax.ppermute(both, 'prow', [(1, 3), (2, 0), (0, 1), (3, 2)])  9.47 us
  transfers between devices with their start and end apart: 38, of which 24 were waited for; matrix products, arithmetic and copies ran while one was open for 0% of the time, Pallas kernels for 8%

profile of v7, /device:TPU:0, one launch (start us, length us, event | category | flops | bytes accessed | tf_op | source)
XLA Modules:
  0.0 199.8 jit_solution(4960696893390169957)
XLA Ops:
  2.6 3.0 %collective-permute-start = (f32[2,256,128]{2,1,0:T(8,128)S(1)}, f32[2,256,128]{2,1,0:T(8,128)S(1)}, u32[]{:S(2)}, u32[]{:S(2)}) collective-permute-start(f32[2,256,128]{2,1,0:T(8,128)S(1)} %get-tuple-element.48), channel_id=1, source_target_pairs={{0,2},{1,3},{2,0},{3,1},{4,6},{5,7},{6,4},{7,5},{8,10},{9,11},{10,... | collective-permute-start | bytes 786440 | tf_op jit(solution)/shard_map/ppermute | solution.py:22
  7.2 5.6 %collective-permute-done.refs_2_ = f32[2,256,128]{2,1,0:T(8,128)S(1)} collective-permute-done((f32[2,256,128]{2,1,0:T(8,128)S(1)}, f32[2,256,128]{2,1,0:T(8,128)S(1)}, u32[]{:S(2)}, u32[]{:S(2)}) %collective-permute-start) | collective-permute-done | bytes 262176 | tf_op jit(solution)/shard_map/ppermute | solution.py:22
  12.8 6.2 %collective-permute-done.1.refs_3_ = f32[2,256,128]{2,1,0:T(8,128)S(1)} collective-permute-done((f32[2,256,128]{2,1,0:T(8,128)S(1)}, f32[2,256,128]{2,1,0:T(8,128)S(1)}, u32[]{:S(2)}, u32[]{:S(2)}) %collective-permute-start.1) | collective-permute-done | bytes 262176 | tf_op jit(solution)/shard_map/ppermute | solution.py:22
  21.3 2.6 %collective-permute-start.4 = (f32[256,128]{1,0:T(8,128)S(1)}, f32[256,128]{1,0:T(8,128)S(1)}, u32[]{:S(2)}, u32[]{:S(2)}) collective-permute-start(f32[256,128]{1,0:T(8,128)S(1)} %get-tuple-element.52), channel_id=1, source_target_pairs={{0,16},{8,24},{16,0},{24,8},{1,17},{9,25},{17,1},{25,9},{2,18},{10... | collective-permute-start | bytes 393224 | tf_op jit(solution)/shard_map/ppermute | solution.py:22
  26.1 7.0 %collective-permute-done.4.refs_6_.refs_3_ = f32[256,128]{1,0:T(8,128)S(1)} collective-permute-done((f32[256,128]{1,0:T(8,128)S(1)}, f32[256,128]{1,0:T(8,128)S(1)}, u32[]{:S(2)}, u32[]{:S(2)}) %collective-permute-start.4) | collective-permute-done | bytes 131104 | tf_op jit(solution)/shard_map/ppermute | solution.py:22
  34.2 2.4 %collective-permute-start.11 = (f32[4,256,128]{2,1,0:T(8,128)S(1)}, f32[4,256,128]{2,1,0:T(8,128)S(1)}, u32[]{:S(2)}, u32[]{:S(2)}) collective-permute-start(f32[4,256,128]{2,1,0:T(8,128)S(1)} %arrange.2.refs_0_.refs_3_), channel_id=1, source_target_pairs={{0,6},{1,7},{2,4},{3,5},{4,2},{5,3},{6,0},{7,1},{8,14},{9,15},{10,... | collective-permute-start | bytes 1572872 | tf_op jit(solution)/shard_map/ppermute | solution.py:22
  43.1 3.3 %collective-permute-start.8 = (f32[256,128]{1,0:T(8,128)S(1)}, f32[256,128]{1,0:T(8,128)S(1)}, u32[]{:S(2)}, u32[]{:S(2)}) collective-permute-start(f32[256,128]{1,0:T(8,128)S(1)} %get-tuple-element.57), channel_id=1, source_target_pairs={{0,24},{8,16},{16,8},{24,0},{1,25},{9,17},{17,9},{25,1},{2,26},{10... | collective-permute-start | bytes 393224 | tf_op jit(solution)/shard_map/ppermute | solution.py:22
  46.3 4.2 %collective-permute-done.7.refs_3_.refs_5_ = f32[256,128]{1,0:T(8,128)S(1)} collective-permute-done((f32[256,128]{1,0:T(8,128)S(1)}, f32[256,128]{1,0:T(8,128)S(1)}, u32[]{:S(2)}, u32[]{:S(2)}) %collective-permute-start.7) | collective-permute-done | bytes 131104 | tf_op jit(solution)/shard_map/ppermute | solution.py:22
  50.5 4.3 %collective-permute-done.10.refs_6_.refs_2_ = f32[4,256,128]{2,1,0:T(8,128)S(1)} collective-permute-done((f32[4,256,128]{2,1,0:T(8,128)S(1)}, f32[4,256,128]{2,1,0:T(8,128)S(1)}, u32[]{:S(2)}, u32[]{:S(2)}) %collective-permute-start.10) | collective-permute-done | bytes 524320 | tf_op jit(solution)/shard_map/ppermute | solution.py:22
  58.6 2.5 %bases.1 = (f32[2,64,512]{2,1,0:T(8,128)S(1)}, f32[1,64,512]{2,1,0:T(8,128)S(1)}) custom-call(s32[3]{0:T(128)S(1)} %pad_add_fusion.refs_0_, f32[2,512,512]{2,1,0:T(8,128)S(1)} %copy-done.4, f32[1,512,512]{2,1,0:T(8,128)S(1)} %copy-done.2, f32[4,256,128]{2,1,0:T(8,128)S(1)} %arrange.2.refs_0_.refs_3_), custom_call_target="tpu_custom_call" | custom-call | tf_op jit(solution)/shard_map/bases/pallas_call | solution.py:36
  63.1 4.3 %partial_product.2 = (f32[256,512]{1,0:T(8,128)S(1)}, f32[256,512]{1,0:T(8,128)S(1)}, f32[256,512]{1,0:T(8,128)S(1)}, f32[256,512]{1,0:T(8,128)S(1)}) custom-call(s32[3]{0:T(128)S(1)} %pad_add_fusion.refs_0_, s32[4,4]{1,0:T(4,128)S(1)} %copy-done.6, s32[2,8]{1,0:T(2,128)S(1)} %copy-done.5, f32[1024,2048]{1,0:T(8,128)S(1)} %bitcast.4, ...), custom_call_target="tpu_custom_call" | custom-call | tf_op jit(solution)/shard_map/partial_product/pallas_call | solution.py:36
  67.4 5.0 %collective-permute-start.18 = (f32[256,512]{1,0:T(8,128)S(1)}, f32[256,512]{1,0:T(8,128)S(1)}, u32[]{:S(2)}, u32[]{:S(2)}) collective-permute-start(f32[256,512]{1,0:T(8,128)S(1)} %get-tuple-element.61), channel_id=1, source_target_pairs={{0,8},{24,16},{1,9},{25,17},{2,10},{26,18},{3,11},{27,19},{4,12},{... | collective-permute-start | bytes 1572872 | tf_op jit(solution)/shard_map/ppermute | solution.py:443
  74.4 12.0 %collective-permute-done.13.refs_2_ = f32[4,256,128]{2,1,0:T(8,128)S(1)} collective-permute-done((f32[4,256,128]{2,1,0:T(8,128)S(1)}, f32[4,256,128]{2,1,0:T(8,128)S(1)}, u32[]{:S(2)}, u32[]{:S(2)}) %collective-permute-start.13) | collective-permute-done | bytes 524320 | tf_op jit(solution)/shard_map/ppermute | solution.py:22
  86.4 8.2 %collective-permute-done.16.refs_4_.refs_3_ = f32[256,512]{1,0:T(8,128)S(1)} collective-permute-done((f32[256,512]{1,0:T(8,128)S(1)}, f32[256,512]{1,0:T(8,128)S(1)}, u32[]{:S(2)}, u32[]{:S(2)}) %collective-permute-start.16) | collective-permute-done | bytes 524320 | tf_op jit(solution)/shard_map/ppermute | solution.py:444
  94.9 7.6 %collective-permute-start.24 = (f32[256,512]{1,0:T(8,128)S(1)}, f32[256,512]{1,0:T(8,128)S(1)}, u32[]{:S(2)}, u32[]{:S(2)}) collective-permute-start(f32[256,512]{1,0:T(8,128)S(1)} %add_up.7), channel_id=1, source_target_pairs={{8,24},{16,0},{0,8},{24,16},{9,25},{17,1},{1,9},{25,17},{10,26},{1... | collective-permute-start | bytes 1572872 | tf_op jit(solution)/shard_map/ppermute | solution.py:447
  102.6 4.3 %partial_product.3 = (f32[256,512]{1,0:T(8,128)S(1)}, f32[256,512]{1,0:T(8,128)S(1)}, f32[256,512]{1,0:T(8,128)S(1)}, f32[256,512]{1,0:T(8,128)S(1)}) custom-call(s32[3]{0:T(128)S(1)} %pad_add_fusion.refs_0_, s32[4,4]{1,0:T(4,128)S(1)} %copy-done.6, s32[2,8]{1,0:T(2,128)S(1)} %copy-done.5, f32[1024,2048]{1,0:T(8,128)S(1)} %bitcast.4, ...), custom_call_target="tpu_custom_call" | custom-call | tf_op jit(solution)/shard_map/partial_product/pallas_call | solution.py:36
  106.9 4.8 %collective-permute-start.22 = (f32[256,512]{1,0:T(8,128)S(1)}, f32[256,512]{1,0:T(8,128)S(1)}, u32[]{:S(2)}, u32[]{:S(2)}) collective-permute-start(f32[256,512]{1,0:T(8,128)S(1)} %get-tuple-element.64.refs_9_), channel_id=1, source_target_pairs={{0,8},{24,16},{1,9},{25,17},{2,10},{26,18},{3,11},{27,19},{4,12},{... | collective-permute-start | bytes 1572872 | tf_op jit(solution)/shard_map/ppermute | solution.py:443
  111.6 4.3 %collective-permute-done.24.refs_5_ = f32[256,512]{1,0:T(8,128)S(1)} collective-permute-done((f32[256,512]{1,0:T(8,128)S(1)}, f32[256,512]{1,0:T(8,128)S(1)}, u32[]{:S(2)}, u32[]{:S(2)}) %collective-permute-start.24) | collective-permute-done | bytes 524320 | tf_op jit(solution)/shard_map/ppermute | solution.py:447
  115.9 9.7 %collective-permute-done.22.refs_1_.refs_10_ = f32[256,512]{1,0:T(8,128)S(1)} collective-permute-done((f32[256,512]{1,0:T(8,128)S(1)}, f32[256,512]{1,0:T(8,128)S(1)}, u32[]{:S(2)}, u32[]{:S(2)}) %collective-permute-start.22) | collective-permute-done | bytes 524320 | tf_op jit(solution)/shard_map/ppermute | solution.py:443
  125.6 3.4 %finish.2 = (f32[2,256,512]{2,1,0:T(8,128)}, f32[2,4,64,512]{3,2,1,0:T(8,128)S(1)}, f32[2,4,64,512]{3,2,1,0:T(8,128)S(1)}, f32[512,512]{1,0:T(8,128)S(1)}, f32[512,512]{1,0:T(8,128)S(1)}) custom-call(s32[3]{0:T(128)S(1)} %pad_add_fusion.refs_0_, s32[2,8]{1,0:T(2,128)S(1)} %copy-done.5, f32[256,512]{1,0:T(8,128)S(1)} %get-tuple-element.66.refs_2_, ...), custom_call_target="tpu_custom_call" | custom-call | tf_op jit(solution)/shard_map/finish/pallas_call | solution.py:36
  129.0 3.0 %collective-permute-start.20 = (f32[256,512]{1,0:T(8,128)S(1)}, f32[256,512]{1,0:T(8,128)S(1)}, u32[]{:S(2)}, u32[]{:S(2)}) collective-permute-start(f32[256,512]{1,0:T(8,128)S(1)} %get-tuple-element.63), channel_id=1, source_target_pairs={{0,16},{16,24},{24,8},{8,0},{1,17},{17,25},{25,9},{9,1},{2,18},{18... | collective-permute-start | bytes 1572872 | tf_op jit(solution)/shard_map/ppermute | solution.py:444
  137.1 7.3 %collective-permute-done.20.refs_4_.refs_3_ = f32[256,512]{1,0:T(8,128)S(1)} collective-permute-done((f32[256,512]{1,0:T(8,128)S(1)}, f32[256,512]{1,0:T(8,128)S(1)}, u32[]{:S(2)}, u32[]{:S(2)}) %collective-permute-start.20) | collective-permute-done | bytes 524320 | tf_op jit(solution)/shard_map/ppermute | solution.py:444
  148.5 5.7 %collective-permute-done.26.refs_2_ = f32[2,64,512]{2,1,0:T(8,128)S(1)} collective-permute-done((f32[2,64,512]{2,1,0:T(8,128)S(1)}, f32[2,64,512]{2,1,0:T(8,128)S(1)}, u32[]{:S(2)}, u32[]{:S(2)}) %collective-permute-start.26) | collective-permute-done | bytes 262176 | tf_op jit(solution)/shard_map/ppermute | solution.py:22
  154.3 5.0 %collective-permute-done.27.refs_3_ = f32[2,64,512]{2,1,0:T(8,128)S(1)} collective-permute-done((f32[2,64,512]{2,1,0:T(8,128)S(1)}, f32[2,64,512]{2,1,0:T(8,128)S(1)}, u32[]{:S(2)}, u32[]{:S(2)}) %collective-permute-start.27) | collective-permute-done | bytes 262176 | tf_op jit(solution)/shard_map/ppermute | solution.py:22
  162.4 6.4 %collective-permute-done.23.refs_5_ = f32[256,512]{1,0:T(8,128)S(1)} collective-permute-done((f32[256,512]{1,0:T(8,128)S(1)}, f32[256,512]{1,0:T(8,128)S(1)}, u32[]{:S(2)}, u32[]{:S(2)}) %collective-permute-start.23) | collective-permute-done | bytes 524320 | tf_op jit(solution)/shard_map/ppermute | solution.py:447
  168.7 2.7 %collective-permute-done.29.refs_11_.refs_1_ = f32[64,512]{1,0:T(8,128)S(1)} collective-permute-done((f32[64,512]{1,0:T(8,128)S(1)}, f32[64,512]{1,0:T(8,128)S(1)}, u32[]{:S(2)}, u32[]{:S(2)}) %collective-permute-start.29) | collective-permute-done | bytes 131104 | tf_op jit(solution)/shard_map/ppermute | solution.py:22
  171.5 2.9 %finish.3 = (f32[2,256,512]{2,1,0:T(8,128)}, f32[1,4,64,512]{3,2,1,0:T(8,128)S(1)}, f32[1,4,64,512]{3,2,1,0:T(8,128)S(1)}) custom-call(s32[3]{0:T(128)S(1)} %pad_add_fusion.refs_0_, s32[2,8]{1,0:T(2,128)S(1)} %copy-done.5, f32[256,512]{1,0:T(8,128)S(1)} %get-tuple-element.62.refs_2_, ...), custom_call_target="tpu_custom_call", output_to_operand_aliasing={{0}: (9, {})} | custom-call | tf_op jit(solution)/shard_map/finish/pallas_call | solution.py:36
  180.5 2.7 %collective-permute-done.33.refs_1_ = f32[1,64,512]{2,1,0:T(8,128)S(1)} collective-permute-done((f32[1,64,512]{2,1,0:T(8,128)S(1)}, f32[1,64,512]{2,1,0:T(8,128)S(1)}, u32[]{:S(2)}, u32[]{:S(2)}) %collective-permute-start.33) | collective-permute-done | bytes 131104 | tf_op jit(solution)/shard_map/ppermute | solution.py:22
  183.2 2.9 %collective-permute-done.34.refs_2_ = f32[1,64,512]{2,1,0:T(8,128)S(1)} collective-permute-done((f32[1,64,512]{2,1,0:T(8,128)S(1)}, f32[1,64,512]{2,1,0:T(8,128)S(1)}, u32[]{:S(2)}, u32[]{:S(2)}) %collective-permute-start.34) | collective-permute-done | bytes 131104 | tf_op jit(solution)/shard_map/ppermute | solution.py:22
  188.3 3.5 %collective-permute-done.36.refs_1_ = f32[1,64,512]{2,1,0:T(8,128)S(1)} collective-permute-done((f32[1,64,512]{2,1,0:T(8,128)S(1)}, f32[1,64,512]{2,1,0:T(8,128)S(1)}, u32[]{:S(2)}, u32[]{:S(2)}) %collective-permute-start.36) | collective-permute-done | bytes 131104 | tf_op jit(solution)/shard_map/ppermute | solution.py:22
  192.0 3.3 %collective-permute-done.31.refs_4_ = f32[64,512]{1,0:T(8,128)S(1)} collective-permute-done((f32[64,512]{1,0:T(8,128)S(1)}, f32[64,512]{1,0:T(8,128)S(1)}, u32[]{:S(2)}, u32[]{:S(2)}) %collective-permute-start.31) | collective-permute-done | bytes 131104 | tf_op jit(solution)/shard_map/ppermute | solution.py:22
  195.3 3.1 %collective-permute-done.37.refs_6_ = f32[1,64,512]{2,1,0:T(8,128)S(1)} collective-permute-done((f32[1,64,512]{2,1,0:T(8,128)S(1)}, f32[1,64,512]{2,1,0:T(8,128)S(1)}, u32[]{:S(2)}, u32[]{:S(2)}) %collective-permute-start.37) | collective-permute-done | bytes 131104 | tf_op jit(solution)/shard_map/ppermute | solution.py:22
  (87 shorter events, 45.8 us)
Async XLA Ops:
  2.6 10.1 %collective-permute-start = (f32[2,256,128]{2,1,0:T(8,128)S(1)}, f32[2,256,128]{2,1,0:T(8,128)S(1)}, u32[]{:S(2)}, u32[]{:S(2)}) collective-permute-start(f32[2,256,128]{2,1,0:T(8,128)S(1)} %get-tuple-element.48), channel_id=1, source_target_pairs={{0,2},{1,3},{2,0},{3,1},{4,6},{5,7},{6,4},{7,5},{8,10},{9,11},{10,... | collective-permute-start | bytes 786440 | tf_op jit(solution)/shard_map/ppermute | solution.py:22
  5.6 13.4 %collective-permute-start.1 = (f32[2,256,128]{2,1,0:T(8,128)S(1)}, f32[2,256,128]{2,1,0:T(8,128)S(1)}, u32[]{:S(2)}, u32[]{:S(2)}) collective-permute-start(f32[2,256,128]{2,1,0:T(8,128)S(1)} %get-tuple-element.49), channel_id=1, source_target_pairs={{0,4},{1,5},{2,6},{3,7},{4,0},{5,1},{6,2},{7,3},{8,12},{9,13},{10,... | collective-permute-start | bytes 786440 | tf_op jit(solution)/shard_map/ppermute | solution.py:22
  7.2 11.9 %collective-permute-start.2 = (f32[2,256,128]{2,1,0:T(8,128)S(1)}, f32[2,256,128]{2,1,0:T(8,128)S(1)}, u32[]{:S(2)}, u32[]{:S(2)}) collective-permute-start(f32[2,256,128]{2,1,0:T(8,128)S(1)} %get-tuple-element.50), channel_id=1, source_target_pairs={{0,6},{1,7},{2,4},{3,5},{4,2},{5,3},{6,0},{7,1},{8,14},{9,15},{10,... | collective-permute-start | bytes 786440 | tf_op jit(solution)/shard_map/ppermute | solution.py:22
  21.3 11.8 %collective-permute-start.4 = (f32[256,128]{1,0:T(8,128)S(1)}, f32[256,128]{1,0:T(8,128)S(1)}, u32[]{:S(2)}, u32[]{:S(2)}) collective-permute-start(f32[256,128]{1,0:T(8,128)S(1)} %get-tuple-element.52), channel_id=1, source_target_pairs={{0,16},{8,24},{16,0},{24,8},{1,17},{9,25},{17,1},{25,9},{2,18},{10... | collective-permute-start | bytes 393224 | tf_op jit(solution)/shard_map/ppermute | solution.py:22
  23.9 9.2 %collective-permute-start.5 = (f32[256,128]{1,0:T(8,128)S(1)}, f32[256,128]{1,0:T(8,128)S(1)}, u32[]{:S(2)}, u32[]{:S(2)}) collective-permute-start(f32[256,128]{1,0:T(8,128)S(1)} %get-tuple-element.53), channel_id=1, source_target_pairs={{0,24},{8,16},{16,8},{24,0},{1,25},{9,17},{17,9},{25,1},{2,26},{10... | collective-permute-start | bytes 393224 | tf_op jit(solution)/shard_map/ppermute | solution.py:22
  33.7 21.1 %collective-permute-start.10 = (f32[4,256,128]{2,1,0:T(8,128)S(1)}, f32[4,256,128]{2,1,0:T(8,128)S(1)}, u32[]{:S(2)}, u32[]{:S(2)}) collective-permute-start(f32[4,256,128]{2,1,0:T(8,128)S(1)} %arrange.2.refs_0_.refs_3_), channel_id=1, source_target_pairs={{0,4},{1,5},{2,6},{3,7},{4,0},{5,1},{6,2},{7,3},{8,12},{9,13},{10,... | collective-permute-start | bytes 1572872 | tf_op jit(solution)/shard_map/ppermute | solution.py:22
  34.2 20.6 %collective-permute-start.11 = (f32[4,256,128]{2,1,0:T(8,128)S(1)}, f32[4,256,128]{2,1,0:T(8,128)S(1)}, u32[]{:S(2)}, u32[]{:S(2)}) collective-permute-start(f32[4,256,128]{2,1,0:T(8,128)S(1)} %arrange.2.refs_0_.refs_3_), channel_id=1, source_target_pairs={{0,6},{1,7},{2,4},{3,5},{4,2},{5,3},{6,0},{7,1},{8,14},{9,15},{10,... | collective-permute-start | bytes 1572872 | tf_op jit(solution)/shard_map/ppermute | solution.py:22
  36.7 19.4 %collective-permute-start.9 = (f32[4,256,128]{2,1,0:T(8,128)S(1)}, f32[4,256,128]{2,1,0:T(8,128)S(1)}, u32[]{:S(2)}, u32[]{:S(2)}) collective-permute-start(f32[4,256,128]{2,1,0:T(8,128)S(1)} %arrange.2.refs_0_.refs_3_), channel_id=1, source_target_pairs={{0,2},{1,3},{2,0},{3,1},{4,6},{5,7},{6,4},{7,5},{8,10},{9,11},{10,... | collective-permute-start | bytes 1572872 | tf_op jit(solution)/shard_map/ppermute | solution.py:22
  39.9 10.7 %collective-permute-start.7 = (f32[256,128]{1,0:T(8,128)S(1)}, f32[256,128]{1,0:T(8,128)S(1)}, u32[]{:S(2)}, u32[]{:S(2)}) collective-permute-start(f32[256,128]{1,0:T(8,128)S(1)} %get-tuple-element.56), channel_id=1, source_target_pairs={{0,16},{8,24},{16,0},{24,8},{1,17},{9,25},{17,1},{25,9},{2,18},{10... | collective-permute-start | bytes 393224 | tf_op jit(solution)/shard_map/ppermute | solution.py:22
  43.1 7.5 %collective-permute-start.8 = (f32[256,128]{1,0:T(8,128)S(1)}, f32[256,128]{1,0:T(8,128)S(1)}, u32[]{:S(2)}, u32[]{:S(2)}) collective-permute-start(f32[256,128]{1,0:T(8,128)S(1)} %get-tuple-element.57), channel_id=1, source_target_pairs={{0,24},{8,16},{16,8},{24,0},{1,25},{9,17},{17,9},{25,1},{2,26},{10... | collective-permute-start | bytes 393224 | tf_op jit(solution)/shard_map/ppermute | solution.py:22
  56.2 6.8 %collective-permute-start.15 = (f32[4,4,256,128]{3,2,1,0:T(8,128)S(1)}, f32[4,4,256,128]{3,2,1,0:T(8,128)S(1)}, u32[]{:S(2)}, u32[]{:S(2)}) collective-permute-start(f32[4,4,256,128]{3,2,1,0:T(8,128)S(1)} %pack.2.refs_4_), channel_id=1, source_target_pairs={{0,1},{1,0},{2,3},{3,2},{4,5},{5,4},{6,7},{7,6},{8,9},{9,8},{10,11... | collective-permute-start | bytes 6291464 | tf_op jit(solution)/shard_map/ppermute | solution.py:22
  56.9 16.9 %collective-permute-start.12 = (f32[4,256,128]{2,1,0:T(8,128)S(1)}, f32[4,256,128]{2,1,0:T(8,128)S(1)}, u32[]{:S(2)}, u32[]{:S(2)}) collective-permute-start(f32[4,256,128]{2,1,0:T(8,128)S(1)} %arrange.3.refs_0_), channel_id=1, source_target_pairs={{0,2},{1,3},{2,0},{3,1},{4,6},{5,7},{6,4},{7,5},{8,10},{9,11},{10,... | collective-permute-start | bytes 1572872 | tf_op jit(solution)/shard_map/ppermute | solution.py:22
  61.0 25.4 %collective-permute-start.13 = (f32[4,256,128]{2,1,0:T(8,128)S(1)}, f32[4,256,128]{2,1,0:T(8,128)S(1)}, u32[]{:S(2)}, u32[]{:S(2)}) collective-permute-start(f32[4,256,128]{2,1,0:T(8,128)S(1)} %arrange.3.refs_0_), channel_id=1, source_target_pairs={{0,4},{1,5},{2,6},{3,7},{4,0},{5,1},{6,2},{7,3},{8,12},{9,13},{10,... | collective-permute-start | bytes 1572872 | tf_op jit(solution)/shard_map/ppermute | solution.py:22
  61.5 24.9 %collective-permute-start.14 = (f32[4,256,128]{2,1,0:T(8,128)S(1)}, f32[4,256,128]{2,1,0:T(8,128)S(1)}, u32[]{:S(2)}, u32[]{:S(2)}) collective-permute-start(f32[4,256,128]{2,1,0:T(8,128)S(1)} %arrange.3.refs_0_), channel_id=1, source_target_pairs={{0,6},{1,7},{2,4},{3,5},{4,2},{5,3},{6,0},{7,1},{8,14},{9,15},{10,... | collective-permute-start | bytes 1572872 | tf_op jit(solution)/shard_map/ppermute | solution.py:22
  67.4 19.0 %collective-permute-start.18 = (f32[256,512]{1,0:T(8,128)S(1)}, f32[256,512]{1,0:T(8,128)S(1)}, u32[]{:S(2)}, u32[]{:S(2)}) collective-permute-start(f32[256,512]{1,0:T(8,128)S(1)} %get-tuple-element.61), channel_id=1, source_target_pairs={{0,8},{24,16},{1,9},{25,17},{2,10},{26,18},{3,11},{27,19},{4,12},{... | collective-permute-start | bytes 1572872 | tf_op jit(solution)/shard_map/ppermute | solution.py:443
  72.4 22.2 %collective-permute-start.16 = (f32[256,512]{1,0:T(8,128)S(1)}, f32[256,512]{1,0:T(8,128)S(1)}, u32[]{:S(2)}, u32[]{:S(2)}) collective-permute-start(f32[256,512]{1,0:T(8,128)S(1)} %get-tuple-element.60), channel_id=1, source_target_pairs={{0,16},{16,24},{24,8},{8,0},{1,17},{17,25},{25,9},{9,1},{2,18},{18... | collective-permute-start | bytes 1572872 | tf_op jit(solution)/shard_map/ppermute | solution.py:444
  73.8 20.9 %collective-permute-start.17 = (f32[256,512]{1,0:T(8,128)S(1)}, f32[256,512]{1,0:T(8,128)S(1)}, u32[]{:S(2)}, u32[]{:S(2)}) collective-permute-start(f32[256,512]{1,0:T(8,128)S(1)} %get-tuple-element.61), channel_id=1, source_target_pairs={{8,16},{16,8},{9,17},{17,9},{10,18},{18,10},{11,19},{19,11},{12,20... | collective-permute-start | bytes 1572872 | tf_op jit(solution)/shard_map/ppermute | solution.py:445
  94.8 7.8 %collective-permute-start.19 = (f32[4,4,256,128]{3,2,1,0:T(8,128)S(1)}, f32[4,4,256,128]{3,2,1,0:T(8,128)S(1)}, u32[]{:S(2)}, u32[]{:S(2)}) collective-permute-start(f32[4,4,256,128]{3,2,1,0:T(8,128)S(1)} %pack.3.refs_4_), channel_id=1, source_target_pairs={{0,1},{1,0},{2,3},{3,2},{4,5},{5,4},{6,7},{7,6},{8,9},{9,8},{10,11... | collective-permute-start | bytes 6291464 | tf_op jit(solution)/shard_map/ppermute | solution.py:22
  94.9 21.0 %collective-permute-start.24 = (f32[256,512]{1,0:T(8,128)S(1)}, f32[256,512]{1,0:T(8,128)S(1)}, u32[]{:S(2)}, u32[]{:S(2)}) collective-permute-start(f32[256,512]{1,0:T(8,128)S(1)} %add_up.7), channel_id=1, source_target_pairs={{8,24},{16,0},{0,8},{24,16},{9,25},{17,1},{1,9},{25,17},{10,26},{1... | collective-permute-start | bytes 1572872 | tf_op jit(solution)/shard_map/ppermute | solution.py:447
  106.9 18.8 %collective-permute-start.22 = (f32[256,512]{1,0:T(8,128)S(1)}, f32[256,512]{1,0:T(8,128)S(1)}, u32[]{:S(2)}, u32[]{:S(2)}) collective-permute-start(f32[256,512]{1,0:T(8,128)S(1)} %get-tuple-element.64.refs_9_), channel_id=1, source_target_pairs={{0,8},{24,16},{1,9},{25,17},{2,10},{26,18},{3,11},{27,19},{4,12},{... | collective-permute-start | bytes 1572872 | tf_op jit(solution)/shard_map/ppermute | solution.py:443
  129.0 15.3 %collective-permute-start.25 = (f32[2,4,64,512]{3,2,1,0:T(8,128)S(1)}, f32[2,4,64,512]{3,2,1,0:T(8,128)S(1)}, u32[]{:S(2)}, u32[]{:S(2)}) collective-permute-start(f32[2,4,64,512]{3,2,1,0:T(8,128)S(1)} %get-tuple-element.74), channel_id=1, source_target_pairs={{0,1},{1,0},{2,3},{3,2},{4,5},{5,4},{6,7},{7,6},{8,9},{9,8},{10,11... | collective-permute-start | bytes 3145736 | tf_op jit(solution)/shard_map/ppermute | solution.py:22
  129.0 15.3 %collective-permute-start.20 = (f32[256,512]{1,0:T(8,128)S(1)}, f32[256,512]{1,0:T(8,128)S(1)}, u32[]{:S(2)}, u32[]{:S(2)}) collective-permute-start(f32[256,512]{1,0:T(8,128)S(1)} %get-tuple-element.63), channel_id=1, source_target_pairs={{0,16},{16,24},{24,8},{8,0},{1,17},{17,25},{25,9},{9,1},{2,18},{18... | collective-permute-start | bytes 1572872 | tf_op jit(solution)/shard_map/ppermute | solution.py:444
  132.0 30.4 %collective-permute-start.21 = (f32[256,512]{1,0:T(8,128)S(1)}, f32[256,512]{1,0:T(8,128)S(1)}, u32[]{:S(2)}, u32[]{:S(2)}) collective-permute-start(f32[256,512]{1,0:T(8,128)S(1)} %get-tuple-element.64.refs_9_), channel_id=1, source_target_pairs={{8,16},{16,8},{9,17},{17,9},{10,18},{18,10},{11,19},{19,11},{12,20... | collective-permute-start | bytes 1572872 | tf_op jit(solution)/shard_map/ppermute | solution.py:445
  132.9 35.8 %collective-permute-start.23 = (f32[256,512]{1,0:T(8,128)S(1)}, f32[256,512]{1,0:T(8,128)S(1)}, u32[]{:S(2)}, u32[]{:S(2)}) collective-permute-start(f32[256,512]{1,0:T(8,128)S(1)} %add_up.6), channel_id=1, source_target_pairs={{8,24},{16,0},{0,8},{24,16},{9,25},{17,1},{1,9},{25,17},{10,26},{1... | collective-permute-start | bytes 1572872 | tf_op jit(solution)/shard_map/ppermute | solution.py:447
  145.0 9.3 %collective-permute-start.26 = (f32[2,64,512]{2,1,0:T(8,128)S(1)}, f32[2,64,512]{2,1,0:T(8,128)S(1)}, u32[]{:S(2)}, u32[]{:S(2)}) collective-permute-start(f32[2,64,512]{2,1,0:T(8,128)S(1)} %get-tuple-element.76), channel_id=1, source_target_pairs={{0,2},{1,3},{2,0},{3,1},{4,6},{5,7},{6,4},{7,5},{8,10},{9,11},{10,... | collective-permute-start | bytes 786440 | tf_op jit(solution)/shard_map/ppermute | solution.py:22
  146.2 13.1 %collective-permute-start.27 = (f32[2,64,512]{2,1,0:T(8,128)S(1)}, f32[2,64,512]{2,1,0:T(8,128)S(1)}, u32[]{:S(2)}, u32[]{:S(2)}) collective-permute-start(f32[2,64,512]{2,1,0:T(8,128)S(1)} %get-tuple-element.77), channel_id=1, source_target_pairs={{0,4},{1,5},{2,6},{3,7},{4,0},{5,1},{6,2},{7,3},{8,12},{9,13},{10,... | collective-permute-start | bytes 786440 | tf_op jit(solution)/shard_map/ppermute | solution.py:22
  148.5 10.8 %collective-permute-start.28 = (f32[2,64,512]{2,1,0:T(8,128)S(1)}, f32[2,64,512]{2,1,0:T(8,128)S(1)}, u32[]{:S(2)}, u32[]{:S(2)}) collective-permute-start(f32[2,64,512]{2,1,0:T(8,128)S(1)} %get-tuple-element.78), channel_id=1, source_target_pairs={{0,6},{1,7},{2,4},{3,5},{4,2},{5,3},{6,0},{7,1},{8,14},{9,15},{10,... | collective-permute-start | bytes 786440 | tf_op jit(solution)/shard_map/ppermute | solution.py:22
  159.9 11.5 %collective-permute-start.29 = (f32[64,512]{1,0:T(8,128)S(1)}, f32[64,512]{1,0:T(8,128)S(1)}, u32[]{:S(2)}, u32[]{:S(2)}) collective-permute-start(f32[64,512]{1,0:T(8,128)S(1)} %get-tuple-element.80), channel_id=1, source_target_pairs={{0,8},{8,0},{16,24},{24,16},{1,9},{9,1},{17,25},{25,17},{2,10},{10... | collective-permute-start | bytes 393224 | tf_op jit(solution)/shard_map/ppermute | solution.py:22
  177.7 8.4 %collective-permute-start.34 = (f32[1,64,512]{2,1,0:T(8,128)S(1)}, f32[1,64,512]{2,1,0:T(8,128)S(1)}, u32[]{:S(2)}, u32[]{:S(2)}) collective-permute-start(f32[1,64,512]{2,1,0:T(8,128)S(1)} %get-tuple-element.87), channel_id=1, source_target_pairs={{0,4},{1,5},{2,6},{3,7},{4,0},{5,1},{6,2},{7,3},{8,12},{9,13},{10,... | collective-permute-start | bytes 393224 | tf_op jit(solution)/shard_map/ppermute | solution.py:22
  180.4 7.6 %collective-permute-start.30 = (f32[64,512]{1,0:T(8,128)S(1)}, f32[64,512]{1,0:T(8,128)S(1)}, u32[]{:S(2)}, u32[]{:S(2)}) collective-permute-start(f32[64,512]{1,0:T(8,128)S(1)} %add_up.8.refs_0_), channel_id=1, source_target_pairs={{0,16},{8,24},{16,0},{24,8},{1,17},{9,25},{17,1},{25,9},{2,18},{10... | collective-permute-start | bytes 393224 | tf_op jit(solution)/shard_map/ppermute | solution.py:22
  188.0 7.3 %collective-permute-start.31 = (f32[64,512]{1,0:T(8,128)S(1)}, f32[64,512]{1,0:T(8,128)S(1)}, u32[]{:S(2)}, u32[]{:S(2)}) collective-permute-start(f32[64,512]{1,0:T(8,128)S(1)} %add_up.9.refs_3_), channel_id=1, source_target_pairs={{0,8},{8,0},{16,24},{24,16},{1,9},{9,1},{17,25},{25,17},{2,10},{10... | collective-permute-start | bytes 393224 | tf_op jit(solution)/shard_map/ppermute | solution.py:22
  191.8 6.6 %collective-permute-start.37 = (f32[1,64,512]{2,1,0:T(8,128)S(1)}, f32[1,64,512]{2,1,0:T(8,128)S(1)}, u32[]{:S(2)}, u32[]{:S(2)}) collective-permute-start(f32[1,64,512]{2,1,0:T(8,128)S(1)} %add_up.11.refs_5_), channel_id=1, source_target_pairs={{0,16},{8,24},{16,0},{24,8},{1,17},{9,25},{17,1},{25,9},{2,18},{10... | collective-permute-start | bytes 393224 | tf_op jit(solution)/shard_map/ppermute | solution.py:22
  (15 other events, 187.0 us)

commit v8 on v7

--- a/solution.py
+++ b/solution.py
@@ -524,7 +524,7 @@
         for number in range(nsuper):
             waits = received[-1][1:] if received else []
             received.append(to_plane(turn(place, sent, number, waits)))
-    rows, firsts, gathered = [], [], []
+    rows, gathered = [], []
     for number in range(nsuper):
         if received:
             own = arrange(place, received[number], gathered)
@@ -541,17 +541,16 @@
         partial = partial_product(
             place, slots, ancestors, inverse_tiles, pieces, ratio, columns, number, [bases[0]]
         )
-        firsts.append(partial[0])
         *early, last_row, near = sum_over_line(partial, z)
         rows.append([*early, near, last_row])
 
-    sums, before, pending = [], [], None
+    sums, before, pending = [], [], []
     for number in range(nsuper):
         last = number + 1 == nsuper
-        waits = [] if last else [firsts[number + 1], rows[number + 1][3]]
+        waits = [] if last else rows[number + 1][1:4]
         offdiag, keep, send, *link = finish(
             number, own_block, place, ancestors, rows[number][:3] + rows[number][4:], factor, before,
-            link_factor, pcol_count // 2, waits + (pending if pending else []),
+            link_factor, pcol_count // 2, waits + pending[:1],
         )
         if pending:
             sums += sum_pair_far(pending, count, [keep])
@@ -559,9 +558,9 @@
         if not last:
             rest = rest_of(link_factor, *link, offdiag, number)
             before = [*rest, offdiag]
-            waits = [rest[0], rows[number + 1][1]]
+            waits = [rest[0]]
         group = sum_plane(place, keep, send, waits)
-        pending = None if last else sum_pair_near(place, group)
+        pending = [] if last else sum_pair_near(place, group)
     sums += sum_planes(group, count)
     return (offdiag, *outputs(place, bases, sums))
 

time: 200 us -> 187 us (0.935)
  waiting for transfers between devices: 113 us -> 103 us
  starting transfers between devices: 58 us -> 54.3 us
    ppermute x2, waiting for transfers between devices: 9.73 us -> 20.4 us  [sum_over_four(): near = lax.ppermute(slots[0], 'prow', [(0, 1), (3, 2)])]
    ppermute x2, waiting for transfers between devices: 10.6 us -> 1.1 us  [sum_over_four(): last = lax.ppermute(both, 'prow', [(1, 3), (2, 0), (0, 1), (3, 2)])]
    ppermute x30, waiting for transfers between devices: 77.2 us -> 69.8 us  [flip(): lax.ppermute(value, axis, [(i, i ^ bit) for i in range(lax.axis_size(axis...]
    ppermute x2, starting transfers between devices: 9.73 us -> 3.68 us  [sum_over_four(): near = lax.ppermute(slots[0], 'prow', [(0, 1), (3, 2)])]
    ppermute x2, starting transfers between devices: 4.33 us -> 9 us  [sum_over_four(): total = lax.ppermute(slots[1], 'prow', [(0, 2), (2, 3), (3, 1), (1, 0)])]
    ppermute x2, waiting for transfers between devices: 15.5 us -> 11.4 us  [sum_over_four(): total = lax.ppermute(slots[1], 'prow', [(0, 2), (2, 3), (3, 1), (1, 0)])]
    ppermute x2, starting transfers between devices: 9.47 us -> 6.37 us  [sum_over_four(): last = lax.ppermute(both, 'prow', [(1, 3), (2, 0), (0, 1), (3, 2)])]
  transfers between devices with their start and end apart: 38 -> 38, of which waited for: 24 -> 23; matrix products, arithmetic and copies ran while one was open for 0% -> 0% of each run, Pallas kernels for 8% -> 9%
where the time goes in v8:
time: 187 us; the launch traced here: 186 us
  waiting for transfers between devices  103 us (55%)
  starting transfers between devices  54.3 us (29%)
  Pallas kernels  26.6 us (14%)
    ppermute x30, waiting for transfers between devices, flip(): lax.ppermute(value, axis, [(i, i ^ bit) for i in range(lax.axis_size(axis...  69.8 us
    ppermute x30, starting transfers between devices, flip(): lax.ppermute(value, axis, [(i, i ^ bit) for i in range(lax.axis_size(axis...  33.9 us
    pallas_call x23, Pallas kernels, run(): pl.pallas_call(body, grid_spec=pltpu.PrefetchScalarGridSpec(num_scalar_pr...  26.6 us
    ppermute x2, waiting for transfers between devices, sum_over_four(): near = lax.ppermute(slots[0], 'prow', [(0, 1), (3, 2)])  20.4 us
    ppermute x2, waiting for transfers between devices, sum_over_four(): total = lax.ppermute(slots[1], 'prow', [(0, 2), (2, 3), (3, 1), (1, 0)])  11.4 us
    ppermute x2, starting transfers between devices, sum_over_four(): total = lax.ppermute(slots[1], 'prow', [(0, 2), (2, 3), (3, 1), (1, 0)])  9 us
    ppermute x2, starting transfers between devices, sum_over_four(): last = lax.ppermute(both, 'prow', [(1, 3), (2, 0), (0, 1), (3, 2)])  6.37 us
  transfers between devices with their start and end apart: 38, of which 23 were waited for; matrix products, arithmetic and copies ran while one was open for 0% of the time, Pallas kernels for 9%

profile of v8, /device:TPU:0, one launch (start us, length us, event | category | flops | bytes accessed | tf_op | source)
XLA Modules:
  0.0 185.8 jit_solution(7674339974390869297)
XLA Ops:
  2.6 3.0 %collective-permute-start = (f32[2,256,128]{2,1,0:T(8,128)S(1)}, f32[2,256,128]{2,1,0:T(8,128)S(1)}, u32[]{:S(2)}, u32[]{:S(2)}) collective-permute-start(f32[2,256,128]{2,1,0:T(8,128)S(1)} %get-tuple-element.48), channel_id=1, source_target_pairs={{0,2},{1,3},{2,0},{3,1},{4,6},{5,7},{6,4},{7,5},{8,10},{9,11},{10,... | collective-permute-start | bytes 786440 | tf_op jit(solution)/shard_map/ppermute | solution.py:22
  7.2 5.6 %collective-permute-done.refs_2_ = f32[2,256,128]{2,1,0:T(8,128)S(1)} collective-permute-done((f32[2,256,128]{2,1,0:T(8,128)S(1)}, f32[2,256,128]{2,1,0:T(8,128)S(1)}, u32[]{:S(2)}, u32[]{:S(2)}) %collective-permute-start) | collective-permute-done | bytes 262176 | tf_op jit(solution)/shard_map/ppermute | solution.py:22
  12.8 6.2 %collective-permute-done.1.refs_3_ = f32[2,256,128]{2,1,0:T(8,128)S(1)} collective-permute-done((f32[2,256,128]{2,1,0:T(8,128)S(1)}, f32[2,256,128]{2,1,0:T(8,128)S(1)}, u32[]{:S(2)}, u32[]{:S(2)}) %collective-permute-start.1) | collective-permute-done | bytes 262176 | tf_op jit(solution)/shard_map/ppermute | solution.py:22
  21.3 2.6 %collective-permute-start.4 = (f32[256,128]{1,0:T(8,128)S(1)}, f32[256,128]{1,0:T(8,128)S(1)}, u32[]{:S(2)}, u32[]{:S(2)}) collective-permute-start(f32[256,128]{1,0:T(8,128)S(1)} %get-tuple-element.52), channel_id=1, source_target_pairs={{0,16},{8,24},{16,0},{24,8},{1,17},{9,25},{17,1},{25,9},{2,18},{10... | collective-permute-start | bytes 393224 | tf_op jit(solution)/shard_map/ppermute | solution.py:22
  26.1 7.0 %collective-permute-done.4.refs_6_.refs_3_ = f32[256,128]{1,0:T(8,128)S(1)} collective-permute-done((f32[256,128]{1,0:T(8,128)S(1)}, f32[256,128]{1,0:T(8,128)S(1)}, u32[]{:S(2)}, u32[]{:S(2)}) %collective-permute-start.4) | collective-permute-done | bytes 131104 | tf_op jit(solution)/shard_map/ppermute | solution.py:22
  37.8 2.0 %collective-permute-start.6 = (f32[256,128]{1,0:T(8,128)S(1)}, f32[256,128]{1,0:T(8,128)S(1)}, u32[]{:S(2)}, u32[]{:S(2)}) collective-permute-start(f32[256,128]{1,0:T(8,128)S(1)} %get-tuple-element.55), channel_id=1, source_target_pairs={{0,8},{8,0},{16,24},{24,16},{1,9},{9,1},{17,25},{25,17},{2,10},{10... | collective-permute-start | bytes 393224 | tf_op jit(solution)/shard_map/ppermute | solution.py:22
  41.0 2.1 %collective-permute-done.6.refs_2_.refs_4_ = f32[256,128]{1,0:T(8,128)S(1)} collective-permute-done((f32[256,128]{1,0:T(8,128)S(1)}, f32[256,128]{1,0:T(8,128)S(1)}, u32[]{:S(2)}, u32[]{:S(2)}) %collective-permute-start.6) | collective-permute-done | bytes 131104 | tf_op jit(solution)/shard_map/ppermute | solution.py:22
  43.1 3.3 %collective-permute-start.8 = (f32[256,128]{1,0:T(8,128)S(1)}, f32[256,128]{1,0:T(8,128)S(1)}, u32[]{:S(2)}, u32[]{:S(2)}) collective-permute-start(f32[256,128]{1,0:T(8,128)S(1)} %get-tuple-element.57), channel_id=1, source_target_pairs={{0,24},{8,16},{16,8},{24,0},{1,25},{9,17},{17,9},{25,1},{2,26},{10... | collective-permute-start | bytes 393224 | tf_op jit(solution)/shard_map/ppermute | solution.py:22
  46.3 4.2 %collective-permute-done.7.refs_3_.refs_5_ = f32[256,128]{1,0:T(8,128)S(1)} collective-permute-done((f32[256,128]{1,0:T(8,128)S(1)}, f32[256,128]{1,0:T(8,128)S(1)}, u32[]{:S(2)}, u32[]{:S(2)}) %collective-permute-start.7) | collective-permute-done | bytes 131104 | tf_op jit(solution)/shard_map/ppermute | solution.py:22
  50.5 5.2 %collective-permute-done.10.refs_6_.refs_2_ = f32[4,256,128]{2,1,0:T(8,128)S(1)} collective-permute-done((f32[4,256,128]{2,1,0:T(8,128)S(1)}, f32[4,256,128]{2,1,0:T(8,128)S(1)}, u32[]{:S(2)}, u32[]{:S(2)}) %collective-permute-start.10) | collective-permute-done | bytes 524320 | tf_op jit(solution)/shard_map/ppermute | solution.py:22
  58.3 2.5 %bases.1 = (f32[2,64,512]{2,1,0:T(8,128)S(1)}, f32[1,64,512]{2,1,0:T(8,128)S(1)}) custom-call(s32[3]{0:T(128)S(1)} %pad_add_fusion.refs_0_, f32[2,512,512]{2,1,0:T(8,128)S(1)} %copy-done.4, f32[1,512,512]{2,1,0:T(8,128)S(1)} %copy-done.2, f32[4,256,128]{2,1,0:T(8,128)S(1)} %arrange.2.refs_0_.refs_3_), custom_call_target="tpu_custom_call" | custom-call | tf_op jit(solution)/shard_map/bases/pallas_call | solution.py:36
  62.7 4.3 %partial_product.2 = (f32[256,512]{1,0:T(8,128)S(1)}, f32[256,512]{1,0:T(8,128)S(1)}, f32[256,512]{1,0:T(8,128)S(1)}, f32[256,512]{1,0:T(8,128)S(1)}) custom-call(s32[3]{0:T(128)S(1)} %pad_add_fusion.refs_0_, s32[4,4]{1,0:T(4,128)S(1)} %copy-done.6, s32[2,8]{1,0:T(2,128)S(1)} %copy-done.5, f32[1024,2048]{1,0:T(8,128)S(1)} %bitcast.4, ...), custom_call_target="tpu_custom_call" | custom-call | tf_op jit(solution)/shard_map/partial_product/pallas_call | solution.py:36
  67.0 3.9 %collective-permute-start.16 = (f32[256,512]{1,0:T(8,128)S(1)}, f32[256,512]{1,0:T(8,128)S(1)}, u32[]{:S(2)}, u32[]{:S(2)}) collective-permute-start(f32[256,512]{1,0:T(8,128)S(1)} %get-tuple-element.60), channel_id=1, source_target_pairs={{0,16},{16,24},{24,8},{8,0},{1,17},{17,25},{25,9},{9,1},{2,18},{18... | collective-permute-start | bytes 1572872 | tf_op jit(solution)/shard_map/ppermute | solution.py:444
  70.9 2.4 %collective-permute-start.18 = (f32[256,512]{1,0:T(8,128)S(1)}, f32[256,512]{1,0:T(8,128)S(1)}, u32[]{:S(2)}, u32[]{:S(2)}) collective-permute-start(f32[256,512]{1,0:T(8,128)S(1)} %get-tuple-element.61), channel_id=1, source_target_pairs={{0,8},{24,16},{1,9},{25,17},{2,10},{26,18},{3,11},{27,19},{4,12},{... | collective-permute-start | bytes 1572872 | tf_op jit(solution)/shard_map/ppermute | solution.py:443
  74.0 9.1 %collective-permute-done.13.refs_2_ = f32[4,256,128]{2,1,0:T(8,128)S(1)} collective-permute-done((f32[4,256,128]{2,1,0:T(8,128)S(1)}, f32[4,256,128]{2,1,0:T(8,128)S(1)}, u32[]{:S(2)}, u32[]{:S(2)}) %collective-permute-start.13) | collective-permute-done | bytes 524320 | tf_op jit(solution)/shard_map/ppermute | solution.py:22
  83.3 9.9 %collective-permute-done.18.refs_6_.refs_1_ = f32[256,512]{1,0:T(8,128)S(1)} collective-permute-done((f32[256,512]{1,0:T(8,128)S(1)}, f32[256,512]{1,0:T(8,128)S(1)}, u32[]{:S(2)}, u32[]{:S(2)}) %collective-permute-start.18) | collective-permute-done | bytes 524320 | tf_op jit(solution)/shard_map/ppermute | solution.py:443
  93.5 3.8 %collective-permute-start.24 = (f32[256,512]{1,0:T(8,128)S(1)}, f32[256,512]{1,0:T(8,128)S(1)}, u32[]{:S(2)}, u32[]{:S(2)}) collective-permute-start(f32[256,512]{1,0:T(8,128)S(1)} %add_up.7), channel_id=1, source_target_pairs={{8,24},{16,0},{0,8},{24,16},{9,25},{17,1},{1,9},{25,17},{10,26},{1... | collective-permute-start | bytes 1572872 | tf_op jit(solution)/shard_map/ppermute | solution.py:447
  97.6 4.3 %partial_product.3 = (f32[256,512]{1,0:T(8,128)S(1)}, f32[256,512]{1,0:T(8,128)S(1)}, f32[256,512]{1,0:T(8,128)S(1)}, f32[256,512]{1,0:T(8,128)S(1)}) custom-call(s32[3]{0:T(128)S(1)} %pad_add_fusion.refs_0_, s32[4,4]{1,0:T(4,128)S(1)} %copy-done.6, s32[2,8]{1,0:T(2,128)S(1)} %copy-done.5, f32[1024,2048]{1,0:T(8,128)S(1)} %bitcast.4, ...), custom_call_target="tpu_custom_call" | custom-call | tf_op jit(solution)/shard_map/partial_product/pallas_call | solution.py:36
  101.8 5.1 %collective-permute-start.20 = (f32[256,512]{1,0:T(8,128)S(1)}, f32[256,512]{1,0:T(8,128)S(1)}, u32[]{:S(2)}, u32[]{:S(2)}) collective-permute-start(f32[256,512]{1,0:T(8,128)S(1)} %get-tuple-element.63), channel_id=1, source_target_pairs={{0,16},{16,24},{24,8},{8,0},{1,17},{17,25},{25,9},{9,1},{2,18},{18... | collective-permute-start | bytes 1572872 | tf_op jit(solution)/shard_map/ppermute | solution.py:444
  110.1 11.1 %collective-permute-done.20.refs_9_.refs_3_ = f32[256,512]{1,0:T(8,128)S(1)} collective-permute-done((f32[256,512]{1,0:T(8,128)S(1)}, f32[256,512]{1,0:T(8,128)S(1)}, u32[]{:S(2)}, u32[]{:S(2)}) %collective-permute-start.20) | collective-permute-done | bytes 524320 | tf_op jit(solution)/shard_map/ppermute | solution.py:444
  121.2 10.5 %collective-permute-done.22.refs_1_.refs_11_ = f32[256,512]{1,0:T(8,128)S(1)} collective-permute-done((f32[256,512]{1,0:T(8,128)S(1)}, f32[256,512]{1,0:T(8,128)S(1)}, u32[]{:S(2)}, u32[]{:S(2)}) %collective-permute-start.22) | collective-permute-done | bytes 524320 | tf_op jit(solution)/shard_map/ppermute | solution.py:443
  131.7 3.5 %finish.2 = (f32[2,256,512]{2,1,0:T(8,128)}, f32[2,4,64,512]{3,2,1,0:T(8,128)S(1)}, f32[2,4,64,512]{3,2,1,0:T(8,128)S(1)}, f32[512,512]{1,0:T(8,128)S(1)}, f32[512,512]{1,0:T(8,128)S(1)}) custom-call(s32[3]{0:T(128)S(1)} %pad_add_fusion.refs_0_, s32[2,8]{1,0:T(2,128)S(1)} %copy-done.5, f32[256,512]{1,0:T(8,128)S(1)} %get-tuple-element.66.refs_2_, ...), custom_call_target="tpu_custom_call" | custom-call | tf_op jit(solution)/shard_map/finish/pallas_call | solution.py:36
  135.3 2.5 %collective-permute-start.23 = (f32[256,512]{1,0:T(8,128)S(1)}, f32[256,512]{1,0:T(8,128)S(1)}, u32[]{:S(2)}, u32[]{:S(2)}) collective-permute-start(f32[256,512]{1,0:T(8,128)S(1)} %add_up.6), channel_id=1, source_target_pairs={{8,24},{16,0},{0,8},{24,16},{9,25},{17,1},{1,9},{25,17},{10,26},{1... | collective-permute-start | bytes 1572872 | tf_op jit(solution)/shard_map/ppermute | solution.py:447
  137.9 2.3 %rest.1 = (f32[512,512]{1,0:T(8,128)S(1)}, f32[256,512]{1,0:T(8,128)S(1)}) custom-call(f32[1,512,512]{2,1,0:T(8,128)S(1)} %copy-done.2, f32[512,512]{1,0:T(8,128)S(1)} %get-tuple-element.68.refs_1_, f32[512,512]{1,0:T(8,128)S(1)} %get-tuple-element.69.refs_2_, f32[2,256,512]{2,1,0:T(8,128)S(1)} %copy-done.3), custom_call_target="tpu_custom_call" | custom-call | tf_op jit(solution)/shard_map/rest/pallas_call | solution.py:36
  144.4 5.7 %collective-permute-done.26.refs_2_ = f32[2,64,512]{2,1,0:T(8,128)S(1)} collective-permute-done((f32[2,64,512]{2,1,0:T(8,128)S(1)}, f32[2,64,512]{2,1,0:T(8,128)S(1)}, u32[]{:S(2)}, u32[]{:S(2)}) %collective-permute-start.26) | collective-permute-done | bytes 262176 | tf_op jit(solution)/shard_map/ppermute | solution.py:22
  150.0 5.3 %collective-permute-done.27.refs_3_ = f32[2,64,512]{2,1,0:T(8,128)S(1)} collective-permute-done((f32[2,64,512]{2,1,0:T(8,128)S(1)}, f32[2,64,512]{2,1,0:T(8,128)S(1)}, u32[]{:S(2)}, u32[]{:S(2)}) %collective-permute-start.27) | collective-permute-done | bytes 262176 | tf_op jit(solution)/shard_map/ppermute | solution.py:22
  156.0 2.9 %finish.3 = (f32[2,256,512]{2,1,0:T(8,128)}, f32[1,4,64,512]{3,2,1,0:T(8,128)S(1)}, f32[1,4,64,512]{3,2,1,0:T(8,128)S(1)}) custom-call(s32[3]{0:T(128)S(1)} %pad_add_fusion.refs_0_, s32[2,8]{1,0:T(2,128)S(1)} %copy-done.5, f32[256,512]{1,0:T(8,128)S(1)} %get-tuple-element.62.refs_2_, ...), custom_call_target="tpu_custom_call", output_to_operand_aliasing={{0}: (9, {})} | custom-call | tf_op jit(solution)/shard_map/finish/pallas_call | solution.py:36
  162.8 2.2 %collective-permute-start.35 = (f32[1,64,512]{2,1,0:T(8,128)S(1)}, f32[1,64,512]{2,1,0:T(8,128)S(1)}, u32[]{:S(2)}, u32[]{:S(2)}) collective-permute-start(f32[1,64,512]{2,1,0:T(8,128)S(1)} %get-tuple-element.88), channel_id=1, source_target_pairs={{0,6},{1,7},{2,4},{3,5},{4,2},{5,3},{6,0},{7,1},{8,14},{9,15},{10,... | collective-permute-start | bytes 393224 | tf_op jit(solution)/shard_map/ppermute | solution.py:22
  167.5 3.3 %collective-permute-done.34.refs_2_ = f32[1,64,512]{2,1,0:T(8,128)S(1)} collective-permute-done((f32[1,64,512]{2,1,0:T(8,128)S(1)}, f32[1,64,512]{2,1,0:T(8,128)S(1)}, u32[]{:S(2)}, u32[]{:S(2)}) %collective-permute-start.34) | collective-permute-done | bytes 131104 | tf_op jit(solution)/shard_map/ppermute | solution.py:22
  171.6 2.0 %collective-permute-done.30.refs_1_ = f32[64,512]{1,0:T(8,128)S(1)} collective-permute-done((f32[64,512]{1,0:T(8,128)S(1)}, f32[64,512]{1,0:T(8,128)S(1)}, u32[]{:S(2)}, u32[]{:S(2)}) %collective-permute-start.30) | collective-permute-done | bytes 131104 | tf_op jit(solution)/shard_map/ppermute | solution.py:22
  173.7 2.7 %collective-permute-done.36.refs_1_ = f32[1,64,512]{2,1,0:T(8,128)S(1)} collective-permute-done((f32[1,64,512]{2,1,0:T(8,128)S(1)}, f32[1,64,512]{2,1,0:T(8,128)S(1)}, u32[]{:S(2)}, u32[]{:S(2)}) %collective-permute-start.36) | collective-permute-done | bytes 131104 | tf_op jit(solution)/shard_map/ppermute | solution.py:22
  179.3 5.1 %collective-permute-done.37.refs_6_ = f32[1,64,512]{2,1,0:T(8,128)S(1)} collective-permute-done((f32[1,64,512]{2,1,0:T(8,128)S(1)}, f32[1,64,512]{2,1,0:T(8,128)S(1)}, u32[]{:S(2)}, u32[]{:S(2)}) %collective-permute-start.37) | collective-permute-done | bytes 131104 | tf_op jit(solution)/shard_map/ppermute | solution.py:22
  (87 shorter events, 39.4 us)
Async XLA Ops:
  2.6 10.1 %collective-permute-start = (f32[2,256,128]{2,1,0:T(8,128)S(1)}, f32[2,256,128]{2,1,0:T(8,128)S(1)}, u32[]{:S(2)}, u32[]{:S(2)}) collective-permute-start(f32[2,256,128]{2,1,0:T(8,128)S(1)} %get-tuple-element.48), channel_id=1, source_target_pairs={{0,2},{1,3},{2,0},{3,1},{4,6},{5,7},{6,4},{7,5},{8,10},{9,11},{10,... | collective-permute-start | bytes 786440 | tf_op jit(solution)/shard_map/ppermute | solution.py:22
  5.6 13.4 %collective-permute-start.1 = (f32[2,256,128]{2,1,0:T(8,128)S(1)}, f32[2,256,128]{2,1,0:T(8,128)S(1)}, u32[]{:S(2)}, u32[]{:S(2)}) collective-permute-start(f32[2,256,128]{2,1,0:T(8,128)S(1)} %get-tuple-element.49), channel_id=1, source_target_pairs={{0,4},{1,5},{2,6},{3,7},{4,0},{5,1},{6,2},{7,3},{8,12},{9,13},{10,... | collective-permute-start | bytes 786440 | tf_op jit(solution)/shard_map/ppermute | solution.py:22
  7.2 11.9 %collective-permute-start.2 = (f32[2,256,128]{2,1,0:T(8,128)S(1)}, f32[2,256,128]{2,1,0:T(8,128)S(1)}, u32[]{:S(2)}, u32[]{:S(2)}) collective-permute-start(f32[2,256,128]{2,1,0:T(8,128)S(1)} %get-tuple-element.50), channel_id=1, source_target_pairs={{0,6},{1,7},{2,4},{3,5},{4,2},{5,3},{6,0},{7,1},{8,14},{9,15},{10,... | collective-permute-start | bytes 786440 | tf_op jit(solution)/shard_map/ppermute | solution.py:22
  19.6 6.5 %collective-permute-start.3 = (f32[256,128]{1,0:T(8,128)S(1)}, f32[256,128]{1,0:T(8,128)S(1)}, u32[]{:S(2)}, u32[]{:S(2)}) collective-permute-start(f32[256,128]{1,0:T(8,128)S(1)} %get-tuple-element.51), channel_id=1, source_target_pairs={{0,8},{8,0},{16,24},{24,16},{1,9},{9,1},{17,25},{25,17},{2,10},{10... | collective-permute-start | bytes 393224 | tf_op jit(solution)/shard_map/ppermute | solution.py:22
  21.3 11.8 %collective-permute-start.4 = (f32[256,128]{1,0:T(8,128)S(1)}, f32[256,128]{1,0:T(8,128)S(1)}, u32[]{:S(2)}, u32[]{:S(2)}) collective-permute-start(f32[256,128]{1,0:T(8,128)S(1)} %get-tuple-element.52), channel_id=1, source_target_pairs={{0,16},{8,24},{16,0},{24,8},{1,17},{9,25},{17,1},{25,9},{2,18},{10... | collective-permute-start | bytes 393224 | tf_op jit(solution)/shard_map/ppermute | solution.py:22
  23.9 9.2 %collective-permute-start.5 = (f32[256,128]{1,0:T(8,128)S(1)}, f32[256,128]{1,0:T(8,128)S(1)}, u32[]{:S(2)}, u32[]{:S(2)}) collective-permute-start(f32[256,128]{1,0:T(8,128)S(1)} %get-tuple-element.53), channel_id=1, source_target_pairs={{0,24},{8,16},{16,8},{24,0},{1,25},{9,17},{17,9},{25,1},{2,26},{10... | collective-permute-start | bytes 393224 | tf_op jit(solution)/shard_map/ppermute | solution.py:22
  33.7 16.9 %collective-permute-start.11 = (f32[4,256,128]{2,1,0:T(8,128)S(1)}, f32[4,256,128]{2,1,0:T(8,128)S(1)}, u32[]{:S(2)}, u32[]{:S(2)}) collective-permute-start(f32[4,256,128]{2,1,0:T(8,128)S(1)} %arrange.2.refs_0_.refs_3_), channel_id=1, source_target_pairs={{0,6},{1,7},{2,4},{3,5},{4,2},{5,3},{6,0},{7,1},{8,14},{9,15},{10,... | collective-permute-start | bytes 1572872 | tf_op jit(solution)/shard_map/ppermute | solution.py:22
  35.2 20.5 %collective-permute-start.10 = (f32[4,256,128]{2,1,0:T(8,128)S(1)}, f32[4,256,128]{2,1,0:T(8,128)S(1)}, u32[]{:S(2)}, u32[]{:S(2)}) collective-permute-start(f32[4,256,128]{2,1,0:T(8,128)S(1)} %arrange.2.refs_0_.refs_3_), channel_id=1, source_target_pairs={{0,4},{1,5},{2,6},{3,7},{4,0},{5,1},{6,2},{7,3},{8,12},{9,13},{10,... | collective-permute-start | bytes 1572872 | tf_op jit(solution)/shard_map/ppermute | solution.py:22
  36.7 19.0 %collective-permute-start.9 = (f32[4,256,128]{2,1,0:T(8,128)S(1)}, f32[4,256,128]{2,1,0:T(8,128)S(1)}, u32[]{:S(2)}, u32[]{:S(2)}) collective-permute-start(f32[4,256,128]{2,1,0:T(8,128)S(1)} %arrange.2.refs_0_.refs_3_), channel_id=1, source_target_pairs={{0,2},{1,3},{2,0},{3,1},{4,6},{5,7},{6,4},{7,5},{8,10},{9,11},{10,... | collective-permute-start | bytes 1572872 | tf_op jit(solution)/shard_map/ppermute | solution.py:22
  39.9 10.7 %collective-permute-start.7 = (f32[256,128]{1,0:T(8,128)S(1)}, f32[256,128]{1,0:T(8,128)S(1)}, u32[]{:S(2)}, u32[]{:S(2)}) collective-permute-start(f32[256,128]{1,0:T(8,128)S(1)} %get-tuple-element.56), channel_id=1, source_target_pairs={{0,16},{8,24},{16,0},{24,8},{1,17},{9,25},{17,1},{25,9},{2,18},{10... | collective-permute-start | bytes 393224 | tf_op jit(solution)/shard_map/ppermute | solution.py:22
  43.1 7.5 %collective-permute-start.8 = (f32[256,128]{1,0:T(8,128)S(1)}, f32[256,128]{1,0:T(8,128)S(1)}, u32[]{:S(2)}, u32[]{:S(2)}) collective-permute-start(f32[256,128]{1,0:T(8,128)S(1)} %get-tuple-element.57), channel_id=1, source_target_pairs={{0,24},{8,16},{16,8},{24,0},{1,25},{9,17},{17,9},{25,1},{2,26},{10... | collective-permute-start | bytes 393224 | tf_op jit(solution)/shard_map/ppermute | solution.py:22
  55.9 6.8 %collective-permute-start.15 = (f32[4,4,256,128]{3,2,1,0:T(8,128)S(1)}, f32[4,4,256,128]{3,2,1,0:T(8,128)S(1)}, u32[]{:S(2)}, u32[]{:S(2)}) collective-permute-start(f32[4,4,256,128]{3,2,1,0:T(8,128)S(1)} %pack.2.refs_4_), channel_id=1, source_target_pairs={{0,1},{1,0},{2,3},{3,2},{4,5},{5,4},{6,7},{7,6},{8,9},{9,8},{10,11... | collective-permute-start | bytes 6291464 | tf_op jit(solution)/shard_map/ppermute | solution.py:22
  56.6 16.8 %collective-permute-start.14 = (f32[4,256,128]{2,1,0:T(8,128)S(1)}, f32[4,256,128]{2,1,0:T(8,128)S(1)}, u32[]{:S(2)}, u32[]{:S(2)}) collective-permute-start(f32[4,256,128]{2,1,0:T(8,128)S(1)} %arrange.3.refs_0_), channel_id=1, source_target_pairs={{0,6},{1,7},{2,4},{3,5},{4,2},{5,3},{6,0},{7,1},{8,14},{9,15},{10,... | collective-permute-start | bytes 1572872 | tf_op jit(solution)/shard_map/ppermute | solution.py:22
  60.8 22.3 %collective-permute-start.13 = (f32[4,256,128]{2,1,0:T(8,128)S(1)}, f32[4,256,128]{2,1,0:T(8,128)S(1)}, u32[]{:S(2)}, u32[]{:S(2)}) collective-permute-start(f32[4,256,128]{2,1,0:T(8,128)S(1)} %arrange.3.refs_0_), channel_id=1, source_target_pairs={{0,4},{1,5},{2,6},{3,7},{4,0},{5,1},{6,2},{7,3},{8,12},{9,13},{10,... | collective-permute-start | bytes 1572872 | tf_op jit(solution)/shard_map/ppermute | solution.py:22
  61.5 21.6 %collective-permute-start.12 = (f32[4,256,128]{2,1,0:T(8,128)S(1)}, f32[4,256,128]{2,1,0:T(8,128)S(1)}, u32[]{:S(2)}, u32[]{:S(2)}) collective-permute-start(f32[4,256,128]{2,1,0:T(8,128)S(1)} %arrange.3.refs_0_), channel_id=1, source_target_pairs={{0,2},{1,3},{2,0},{3,1},{4,6},{5,7},{6,4},{7,5},{8,10},{9,11},{10,... | collective-permute-start | bytes 1572872 | tf_op jit(solution)/shard_map/ppermute | solution.py:22
  67.0 16.3 %collective-permute-start.16 = (f32[256,512]{1,0:T(8,128)S(1)}, f32[256,512]{1,0:T(8,128)S(1)}, u32[]{:S(2)}, u32[]{:S(2)}) collective-permute-start(f32[256,512]{1,0:T(8,128)S(1)} %get-tuple-element.60), channel_id=1, source_target_pairs={{0,16},{16,24},{24,8},{8,0},{1,17},{17,25},{25,9},{9,1},{2,18},{18... | collective-permute-start | bytes 1572872 | tf_op jit(solution)/shard_map/ppermute | solution.py:444
  70.9 22.3 %collective-permute-start.18 = (f32[256,512]{1,0:T(8,128)S(1)}, f32[256,512]{1,0:T(8,128)S(1)}, u32[]{:S(2)}, u32[]{:S(2)}) collective-permute-start(f32[256,512]{1,0:T(8,128)S(1)} %get-tuple-element.61), channel_id=1, source_target_pairs={{0,8},{24,16},{1,9},{25,17},{2,10},{26,18},{3,11},{27,19},{4,12},{... | collective-permute-start | bytes 1572872 | tf_op jit(solution)/shard_map/ppermute | solution.py:443
  73.3 19.9 %collective-permute-start.17 = (f32[256,512]{1,0:T(8,128)S(1)}, f32[256,512]{1,0:T(8,128)S(1)}, u32[]{:S(2)}, u32[]{:S(2)}) collective-permute-start(f32[256,512]{1,0:T(8,128)S(1)} %get-tuple-element.61), channel_id=1, source_target_pairs={{8,16},{16,8},{9,17},{17,9},{10,18},{18,10},{11,19},{19,11},{12,20... | collective-permute-start | bytes 1572872 | tf_op jit(solution)/shard_map/ppermute | solution.py:445
  93.5 16.6 %collective-permute-start.24 = (f32[256,512]{1,0:T(8,128)S(1)}, f32[256,512]{1,0:T(8,128)S(1)}, u32[]{:S(2)}, u32[]{:S(2)}) collective-permute-start(f32[256,512]{1,0:T(8,128)S(1)} %add_up.7), channel_id=1, source_target_pairs={{8,24},{16,0},{0,8},{24,16},{9,25},{17,1},{1,9},{25,17},{10,26},{1... | collective-permute-start | bytes 1572872 | tf_op jit(solution)/shard_map/ppermute | solution.py:447
  101.8 19.4 %collective-permute-start.20 = (f32[256,512]{1,0:T(8,128)S(1)}, f32[256,512]{1,0:T(8,128)S(1)}, u32[]{:S(2)}, u32[]{:S(2)}) collective-permute-start(f32[256,512]{1,0:T(8,128)S(1)} %get-tuple-element.63), channel_id=1, source_target_pairs={{0,16},{16,24},{24,8},{8,0},{1,17},{17,25},{25,9},{9,1},{2,18},{18... | collective-permute-start | bytes 1572872 | tf_op jit(solution)/shard_map/ppermute | solution.py:444
  107.0 24.7 %collective-permute-start.22 = (f32[256,512]{1,0:T(8,128)S(1)}, f32[256,512]{1,0:T(8,128)S(1)}, u32[]{:S(2)}, u32[]{:S(2)}) collective-permute-start(f32[256,512]{1,0:T(8,128)S(1)} %get-tuple-element.64), channel_id=1, source_target_pairs={{0,8},{24,16},{1,9},{25,17},{2,10},{26,18},{3,11},{27,19},{4,12},{... | collective-permute-start | bytes 1572872 | tf_op jit(solution)/shard_map/ppermute | solution.py:443
  108.3 23.4 %collective-permute-start.21 = (f32[256,512]{1,0:T(8,128)S(1)}, f32[256,512]{1,0:T(8,128)S(1)}, u32[]{:S(2)}, u32[]{:S(2)}) collective-permute-start(f32[256,512]{1,0:T(8,128)S(1)} %get-tuple-element.64), channel_id=1, source_target_pairs={{8,16},{16,8},{9,17},{17,9},{10,18},{18,10},{11,19},{19,11},{12,20... | collective-permute-start | bytes 1572872 | tf_op jit(solution)/shard_map/ppermute | solution.py:445
  135.3 20.7 %collective-permute-start.23 = (f32[256,512]{1,0:T(8,128)S(1)}, f32[256,512]{1,0:T(8,128)S(1)}, u32[]{:S(2)}, u32[]{:S(2)}) collective-permute-start(f32[256,512]{1,0:T(8,128)S(1)} %add_up.6), channel_id=1, source_target_pairs={{8,24},{16,0},{0,8},{24,16},{9,25},{17,1},{1,9},{25,17},{10,26},{1... | collective-permute-start | bytes 1572872 | tf_op jit(solution)/shard_map/ppermute | solution.py:447
  140.8 9.2 %collective-permute-start.26 = (f32[2,64,512]{2,1,0:T(8,128)S(1)}, f32[2,64,512]{2,1,0:T(8,128)S(1)}, u32[]{:S(2)}, u32[]{:S(2)}) collective-permute-start(f32[2,64,512]{2,1,0:T(8,128)S(1)} %get-tuple-element.76), channel_id=1, source_target_pairs={{0,2},{1,3},{2,0},{3,1},{4,6},{5,7},{6,4},{7,5},{8,10},{9,11},{10,... | collective-permute-start | bytes 786440 | tf_op jit(solution)/shard_map/ppermute | solution.py:22
  141.6 13.8 %collective-permute-start.27 = (f32[2,64,512]{2,1,0:T(8,128)S(1)}, f32[2,64,512]{2,1,0:T(8,128)S(1)}, u32[]{:S(2)}, u32[]{:S(2)}) collective-permute-start(f32[2,64,512]{2,1,0:T(8,128)S(1)} %get-tuple-element.77), channel_id=1, source_target_pairs={{0,4},{1,5},{2,6},{3,7},{4,0},{5,1},{6,2},{7,3},{8,12},{9,13},{10,... | collective-permute-start | bytes 786440 | tf_op jit(solution)/shard_map/ppermute | solution.py:22
  142.4 13.0 %collective-permute-start.28 = (f32[2,64,512]{2,1,0:T(8,128)S(1)}, f32[2,64,512]{2,1,0:T(8,128)S(1)}, u32[]{:S(2)}, u32[]{:S(2)}) collective-permute-start(f32[2,64,512]{2,1,0:T(8,128)S(1)} %get-tuple-element.78), channel_id=1, source_target_pairs={{0,6},{1,7},{2,4},{3,5},{4,2},{5,3},{6,0},{7,1},{8,14},{9,15},{10,... | collective-permute-start | bytes 786440 | tf_op jit(solution)/shard_map/ppermute | solution.py:22
  158.9 6.1 %collective-permute-start.29 = (f32[64,512]{1,0:T(8,128)S(1)}, f32[64,512]{1,0:T(8,128)S(1)}, u32[]{:S(2)}, u32[]{:S(2)}) collective-permute-start(f32[64,512]{1,0:T(8,128)S(1)} %get-tuple-element.82), channel_id=1, source_target_pairs={{0,8},{8,0},{16,24},{24,16},{1,9},{9,1},{17,25},{25,17},{2,10},{10... | collective-permute-start | bytes 393224 | tf_op jit(solution)/shard_map/ppermute | solution.py:22
  161.4 6.1 %collective-permute-start.33 = (f32[1,64,512]{2,1,0:T(8,128)S(1)}, f32[1,64,512]{2,1,0:T(8,128)S(1)}, u32[]{:S(2)}, u32[]{:S(2)}) collective-permute-start(f32[1,64,512]{2,1,0:T(8,128)S(1)} %get-tuple-element.86), channel_id=1, source_target_pairs={{0,2},{1,3},{2,0},{3,1},{4,6},{5,7},{6,4},{7,5},{8,10},{9,11},{10,... | collective-permute-start | bytes 393224 | tf_op jit(solution)/shard_map/ppermute | solution.py:22
  162.8 8.1 %collective-permute-start.34 = (f32[1,64,512]{2,1,0:T(8,128)S(1)}, f32[1,64,512]{2,1,0:T(8,128)S(1)}, u32[]{:S(2)}, u32[]{:S(2)}) collective-permute-start(f32[1,64,512]{2,1,0:T(8,128)S(1)} %get-tuple-element.87), channel_id=1, source_target_pairs={{0,4},{1,5},{2,6},{3,7},{4,0},{5,1},{6,2},{7,3},{8,12},{9,13},{10,... | collective-permute-start | bytes 393224 | tf_op jit(solution)/shard_map/ppermute | solution.py:22
  162.8 8.1 %collective-permute-start.35 = (f32[1,64,512]{2,1,0:T(8,128)S(1)}, f32[1,64,512]{2,1,0:T(8,128)S(1)}, u32[]{:S(2)}, u32[]{:S(2)}) collective-permute-start(f32[1,64,512]{2,1,0:T(8,128)S(1)} %get-tuple-element.88), channel_id=1, source_target_pairs={{0,6},{1,7},{2,4},{3,5},{4,2},{5,3},{6,0},{7,1},{8,14},{9,15},{10,... | collective-permute-start | bytes 393224 | tf_op jit(solution)/shard_map/ppermute | solution.py:22
  165.0 8.6 %collective-permute-start.30 = (f32[64,512]{1,0:T(8,128)S(1)}, f32[64,512]{1,0:T(8,128)S(1)}, u32[]{:S(2)}, u32[]{:S(2)}) collective-permute-start(f32[64,512]{1,0:T(8,128)S(1)} %add_up.8.refs_0_), channel_id=1, source_target_pairs={{0,16},{8,24},{16,0},{24,8},{1,17},{9,25},{17,1},{25,9},{2,18},{10... | collective-permute-start | bytes 393224 | tf_op jit(solution)/shard_map/ppermute | solution.py:22
  176.3 8.1 %collective-permute-start.37 = (f32[1,64,512]{2,1,0:T(8,128)S(1)}, f32[1,64,512]{2,1,0:T(8,128)S(1)}, u32[]{:S(2)}, u32[]{:S(2)}) collective-permute-start(f32[1,64,512]{2,1,0:T(8,128)S(1)} %add_up.11.refs_5_), channel_id=1, source_target_pairs={{0,16},{8,24},{16,0},{24,8},{1,17},{9,25},{17,1},{25,9},{2,18},{10... | collective-permute-start | bytes 393224 | tf_op jit(solution)/shard_map/ppermute | solution.py:22
  (15 other events, 185.7 us)

commit v9 on v8

--- a/solution.py
+++ b/solution.py
@@ -133,11 +133,11 @@
     return found
 
 
-def partial_kernel(sides, ratio, count, number, place, slots, ancestors, tile_ref, *refs):
+def partial_kernel(sides, ratio, count, number, block, group, place, slots, ancestors, tile_ref, *refs):
     piece_refs, out_refs = refs[:sides], refs[sides:-2]
     right_high, right_low = refs[-2:]
     chunk_rows, columns = out_refs[0].shape
-    blocks = tile_ref.shape[1] // columns
+    blocks = tile_ref.shape[1] // block
     step = pl.program_id(0)
 
     def listed(block):
@@ -151,8 +151,9 @@
         for side, ref in enumerate(piece_refs):
             chips, parts, unit_rows, width = ref.shape
             for o in range(chips):
-                owner = place[0] ^ (2 * o + side)
-                lanes = pl.ds(pl.multiple_of(owner // ratio * width, width), width)
+                owner = place[0] ^ (2 * (group + o) + side)
+                lane = owner // ratio % (columns // width) * width
+                lanes = pl.ds(pl.multiple_of(lane, width), width)
                 first = owner % ratio * (parts * unit_rows)
                 rows = pl.ds(pl.multiple_of(first, parts * unit_rows), parts * unit_rows)
                 high, low = halves(ref[o].reshape(parts * unit_rows, width))
@@ -163,12 +164,12 @@
         out_ref[...] = jnp.zeros_like(out_ref)
         chunk = place[0] * count + slots[place[1], step]
 
-        @pl.when(listed(chunk * chunk_rows // columns))
+        @pl.when(listed(chunk * chunk_rows // block))
         def _chunk():
-            def add(block, carry):
-                @pl.when(listed(place[1] * blocks + block))
+            def add(index, carry):
+                @pl.when(listed(place[1] * blocks + index))
                 def _block():
-                    span = pl.ds(pl.multiple_of(block * columns, columns), columns)
+                    span = pl.ds(pl.multiple_of(index * block, block), block)
                     high, low = halves(tile_ref[:, span])
                     right = right_high[span, :]
                     dot = functools.partial(jnp.dot, preferred_element_type=jnp.float32)
@@ -184,13 +185,15 @@
         pl.when(step == index)(functools.partial(multiply, out_ref))
 
 
-def partial_product(place, slots, ancestors, tiles, pieces, ratio, columns, number, waits):
+def partial_product(
+    place, slots, ancestors, tiles, pieces, ratio, columns, number, group, block, waits
+):
     rows, cols = tiles.shape
     count = slots.shape[0]
     out = jax.ShapeDtypeStruct((rows // count, columns), jnp.float32)
     tile = pl.BlockSpec((rows // count, cols), lambda i, p, s, a: (s[p[1], i], 0))
     return run(
-        functools.partial(partial_kernel, len(pieces), ratio, count, number),
+        functools.partial(partial_kernel, len(pieces), ratio, count, number, block, group),
         [place, slots, ancestors],
         [tiles] + pieces,
         [tile] + [whole(piece) for piece in pieces],
@@ -223,9 +226,10 @@
             ref[index, chip] = matrix_ref[pl.ds(first, rows), :]
 
 
-def finish_kernel(number, last, first, block, place, ancestors, *refs):
+def finish_kernel(number, last, first, block, group_count, count, place, ancestors, *refs):
     refs = list(refs)
-    sums, factor_ref = [refs.pop(0) for _ in range(4)], refs.pop(0)
+    sums = [[refs.pop(0) for _ in range(4)] for _ in range(group_count)]
+    factor_ref = refs.pop(0)
     if not first:
         old_rest, old_rows, _ = (refs.pop(0) for _ in range(3))
     if not last:
@@ -233,7 +237,7 @@
     offdiag_ref, keep_ref, send_ref = (refs.pop(0) for _ in range(3))
     if not last:
         cross_ref, kept_ref = refs.pop(0), refs.pop(0)
-    part_ref = refs.pop(0)
+    part_ref, summed_ref = refs
     offdiag_ref[...] = jnp.zeros_like(offdiag_ref)
     part_ref[...] = jnp.zeros_like(part_ref) if first else old_rest[...]
 
@@ -241,7 +245,12 @@
 
     @pl.when(is_listed(ancestors, number, own))
     def _own():
-        summed = ((sums[0][...] + sums[1][...]) + sums[2][...]) + sums[3][...]
+        for group, (one, two, three, four) in enumerate(sums):
+            width = one.shape[1]
+            lane = (place[2] // (count // group_count) ^ group) * width
+            total = ((one[...] + two[...]) + three[...]) + four[...]
+            summed_ref[:, pl.ds(pl.multiple_of(lane, width), width)] = total
+        summed = summed_ref[...]
         part_ref[...] += dot(factor_ref[0], summed, 0)
         offdiag_ref[0] = -(summed if first else summed + old_rows[...])
 
@@ -277,11 +286,12 @@
     )
 
 
-def finish(number, block, place, ancestors, sums, factor, before, link_factor, chips, waits):
+def finish(number, block, place, ancestors, groups, factor, before, link_factor, count, chips, waits):
     nsuper, unit_rows, columns = factor.shape
     first, last = number == 0, number + 1 == nsuper
     slab = (1, unit_rows, columns)
-    arrays, specs = list(sums), [whole(array) for array in sums]
+    arrays = [array for sums in groups for array in sums]
+    specs = [whole(array) for array in arrays]
     arrays.append(factor)
     specs.append(pl.BlockSpec(slab, lambda *_: (number, 0, 0)))
     alias = {}
@@ -295,22 +305,22 @@
         specs.append(pl.BlockSpec((1, columns, columns), lambda *_: (number, 0, 0)))
         specs.append(pl.BlockSpec(slab, lambda *_: (number + 1, 0, 0)))
     shape = jax.ShapeDtypeStruct
-    groups = shape((1 if last else 2, chips, columns // (2 * chips), columns), jnp.float32)
-    outs = [shape(factor.shape, jnp.float32), groups, groups]
-    out_specs = [pl.BlockSpec(slab, lambda *_: (number, 0, 0)), whole(groups), whole(groups)]
+    parts = shape((1 if last else 2, chips, columns // (2 * chips), columns), jnp.float32)
+    outs = [shape(factor.shape, jnp.float32), parts, parts]
+    out_specs = [pl.BlockSpec(slab, lambda *_: (number, 0, 0)), whole(parts), whole(parts)]
     if not last:
         more = [shape((columns, columns), jnp.float32)] * 2
         outs += more
         out_specs += [whole(array) for array in more]
     return run(
-        functools.partial(finish_kernel, number, last, first, block),
+        functools.partial(finish_kernel, number, last, first, block, len(groups), count),
         [place, ancestors],
         arrays,
         specs,
         waits,
         outs,
         out_specs,
-        scratch=[pltpu.VMEM((columns, columns), jnp.float32)],
+        scratch=[pltpu.VMEM((rows, columns), jnp.float32) for rows in (columns, unit_rows)],
         alias=alias,
         name="finish",
     )
@@ -524,33 +534,55 @@
         for number in range(nsuper):
             waits = received[-1][1:] if received else []
             received.append(to_plane(turn(place, sent, number, waits)))
-    rows, gathered = [], []
+    chips = pcol_count // 2
+    waits = received[0][1:2] if received else []
+    bases = bases_of(place, diag_inverse, link_factor, columns // pcol_count, waits)
+    rows, gathered, early = [], [], []
     for number in range(nsuper):
+        rows.append([])
+        group_count = 2 if number == 0 and received and count % 2 == 0 and chips % 2 == 0 else 1
         if received:
             own = arrange(place, received[number], gathered)
             found = gather_plane(own, pcol_count)
             gathered = found[1:]
-            waits = [piece for later in received[number + 1 : number + 2] for piece in later[1:]]
-            packed = pack(found, waits + (rows[-1][1:4] if rows else []))
-            pieces = [packed, flip(packed, "pcol", 1)]
-        else:
-            own = to_plane_whole(factor[number], count, ratio)
-            pieces = [in_rows(lax.all_gather(own, "pcol", axis=0), count, ratio)]
-        if number == 0:
-            bases = bases_of(place, diag_inverse, link_factor, columns // pcol_count, [own])
-        partial = partial_product(
-            place, slots, ancestors, inverse_tiles, pieces, ratio, columns, number, [bases[0]]
-        )
-        *early, last_row, near = sum_over_line(partial, z)
-        rows.append([*early, near, last_row])
+            others = [piece for later in received[number + 1 : number + 2] for piece in later[1:]]
+        for group in range(group_count):
+            waits = []
+            if received:
+                size = chips // group_count
+                if not group:
+                    waits, early = early + others, []
+                if group:
+                    waits = waits + [rows[-1][-1][3]]
+                elif group_count > 1:
+                    waits = waits + found[size : size + 1]
+                packed = pack(found[group * size : (group + 1) * size], waits)
+                pieces = [packed, flip(packed, "pcol", 1)]
+            else:
+                own = to_plane_whole(factor[number], count, ratio)
+                pieces = [in_rows(lax.all_gather(own, "pcol", axis=0), count, ratio)]
+            waits = [bases[0]] if group + 1 == group_count else []
+            if number and not group:
+                waits.append(rows[-2][-1][4])
+            for earlier in rows[-1]:
+                waits += earlier[1:4]
+                early.append(earlier[4])
+            partial = partial_product(
+                place, slots, ancestors, inverse_tiles, pieces, ratio, columns // group_count,
+                number, group * (chips // group_count), columns, waits,
+            )
+            *three, last_row, near = sum_over_line(partial, z)
+            rows[-1].append([*three, near, last_row])
+        early = early + rows[-1][-1][1:4]
 
     sums, before, pending = [], [], []
     for number in range(nsuper):
         last = number + 1 == nsuper
-        waits = [] if last else rows[number + 1][1:4]
+        waits = [] if last else rows[number + 1][0][1:4]
+        groups = [sums_of[:3] + sums_of[4:] for sums_of in rows[number]]
         offdiag, keep, send, *link = finish(
-            number, own_block, place, ancestors, rows[number][:3] + rows[number][4:], factor, before,
-            link_factor, pcol_count // 2, waits + pending[:1],
+            number, own_block, place, ancestors, groups, factor, before, link_factor, count, chips,
+            waits + pending[:1],
         )
         if pending:
             sums += sum_pair_far(pending, count, [keep])

time: 187 us -> 204 us (1.091)
  starting transfers between devices: 54.3 us -> 72.2 us
  local copies, waits for them, and re-layouts: 1.27 us -> 4.64 us
    ppermute x2 -> x3, starting transfers between devices: 6.37 us -> 13.5 us  [sum_over_four(): last = lax.ppermute(both, 'prow', [(1, 3), (2, 0), (0, 1), (3, 2)])]
    ppermute x2 -> x3, starting transfers between devices: 3.68 us -> 10.6 us  [sum_over_four(): near = lax.ppermute(slots[0], 'prow', [(0, 1), (3, 2)])]
    ppermute x2 -> x3, waiting for transfers between devices: 1.1 us -> 7.77 us  [sum_over_four(): last = lax.ppermute(both, 'prow', [(1, 3), (2, 0), (0, 1), (3, 2)])]
    ppermute x30 -> x31, starting transfers between devices: 33.9 us -> 40.5 us  [flip(): lax.ppermute(value, axis, [(i, i ^ bit) for i in range(lax.axis_size(axis...]
    ppermute x2 -> x3, waiting for transfers between devices: 20.4 us -> 14.7 us  [sum_over_four(): near = lax.ppermute(slots[0], 'prow', [(0, 1), (3, 2)])]
    ppermute x2 -> x3, starting transfers between devices: 9 us -> 5.54 us  [sum_over_four(): total = lax.ppermute(slots[1], 'prow', [(0, 2), (2, 3), (3, 1), (1, 0)])]
    unnamed x18, local copies, waits for them, and re-layouts: 1.27 us -> 4.64 us
    ppermute x30 -> x31, waiting for transfers between devices: 69.8 us -> 67.3 us  [flip(): lax.ppermute(value, axis, [(i, i ^ bit) for i in range(lax.axis_size(axis...]
  transfers between devices with their start and end apart: 38 -> 43, of which waited for: 23 -> 25; matrix products, arithmetic and copies ran while one was open for 0% -> 0% of each run, Pallas kernels for 9% -> 6%
where the time goes in v9:
time: 204 us
  waiting for transfers between devices  101 us (50%)
  starting transfers between devices  72.2 us (35%)
  Pallas kernels  25.3 us (12%)
  local copies, waits for them, and re-layouts  4.64 us (2%)
    ppermute x31, waiting for transfers between devices, flip(): lax.ppermute(value, axis, [(i, i ^ bit) for i in range(lax.axis_size(axis...  67.3 us
    ppermute x31, starting transfers between devices, flip(): lax.ppermute(value, axis, [(i, i ^ bit) for i in range(lax.axis_size(axis...  40.5 us
    pallas_call x26, Pallas kernels, run(): pl.pallas_call(body, grid_spec=pltpu.PrefetchScalarGridSpec(num_scalar_pr...  25.3 us
    ppermute x3, waiting for transfers between devices, sum_over_four(): near = lax.ppermute(slots[0], 'prow', [(0, 1), (3, 2)])  14.7 us
    ppermute x3, starting transfers between devices, sum_over_four(): last = lax.ppermute(both, 'prow', [(1, 3), (2, 0), (0, 1), (3, 2)])  13.5 us
    ppermute x3, waiting for transfers between devices, sum_over_four(): total = lax.ppermute(slots[1], 'prow', [(0, 2), (2, 3), (3, 1), (1, 0)])  10.8 us
    ppermute x3, starting transfers between devices, sum_over_four(): near = lax.ppermute(slots[0], 'prow', [(0, 1), (3, 2)])  10.6 us
    ppermute x3, waiting for transfers between devices, sum_over_four(): last = lax.ppermute(both, 'prow', [(1, 3), (2, 0), (0, 1), (3, 2)])  7.77 us
  transfers between devices with their start and end apart: 43, of which 25 were waited for; matrix products, arithmetic and copies ran while one was open for 0% of the time, Pallas kernels for 6%

profile of v9, /device:TPU:0, one launch (start us, length us, event | category | flops | bytes accessed | tf_op | source)
XLA Modules:
  0.0 203.8 jit_solution(6883557011046176216)
XLA Ops:
  2.6 3.0 %collective-permute-start = (f32[2,256,128]{2,1,0:T(8,128)S(1)}, f32[2,256,128]{2,1,0:T(8,128)S(1)}, u32[]{:S(2)}, u32[]{:S(2)}) collective-permute-start(f32[2,256,128]{2,1,0:T(8,128)S(1)} %get-tuple-element.52), channel_id=1, source_target_pairs={{0,2},{1,3},{2,0},{3,1},{4,6},{5,7},{6,4},{7,5},{8,10},{9,11},{10,... | collective-permute-start | bytes 786440 | tf_op jit(solution)/shard_map/ppermute | solution.py:22
  7.2 5.6 %collective-permute-done.refs_2_ = f32[2,256,128]{2,1,0:T(8,128)S(1)} collective-permute-done((f32[2,256,128]{2,1,0:T(8,128)S(1)}, f32[2,256,128]{2,1,0:T(8,128)S(1)}, u32[]{:S(2)}, u32[]{:S(2)}) %collective-permute-start) | collective-permute-done | bytes 262176 | tf_op jit(solution)/shard_map/ppermute | solution.py:22
  12.8 6.2 %collective-permute-done.1.refs_3_ = f32[2,256,128]{2,1,0:T(8,128)S(1)} collective-permute-done((f32[2,256,128]{2,1,0:T(8,128)S(1)}, f32[2,256,128]{2,1,0:T(8,128)S(1)}, u32[]{:S(2)}, u32[]{:S(2)}) %collective-permute-start.1) | collective-permute-done | bytes 262176 | tf_op jit(solution)/shard_map/ppermute | solution.py:22
  21.3 2.6 %collective-permute-start.4 = (f32[256,128]{1,0:T(8,128)S(1)}, f32[256,128]{1,0:T(8,128)S(1)}, u32[]{:S(2)}, u32[]{:S(2)}) collective-permute-start(f32[256,128]{1,0:T(8,128)S(1)} %get-tuple-element.56), channel_id=1, source_target_pairs={{0,16},{8,24},{16,0},{24,8},{1,17},{9,25},{17,1},{25,9},{2,18},{10... | collective-permute-start | bytes 393224 | tf_op jit(solution)/shard_map/ppermute | solution.py:22
  26.1 7.0 %collective-permute-done.4.refs_6_.refs_3_ = f32[256,128]{1,0:T(8,128)S(1)} collective-permute-done((f32[256,128]{1,0:T(8,128)S(1)}, f32[256,128]{1,0:T(8,128)S(1)}, u32[]{:S(2)}, u32[]{:S(2)}) %collective-permute-start.4) | collective-permute-done | bytes 131104 | tf_op jit(solution)/shard_map/ppermute | solution.py:22
  41.9 7.1 %collective-permute-done.7.refs_3_ = f32[256,128]{1,0:T(8,128)S(1)} collective-permute-done((f32[256,128]{1,0:T(8,128)S(1)}, f32[256,128]{1,0:T(8,128)S(1)}, u32[]{:S(2)}, u32[]{:S(2)}) %collective-permute-start.7) | collective-permute-done | bytes 131104 | tf_op jit(solution)/shard_map/ppermute | solution.py:22
  51.9 3.4 %copy-done = f32[1024,2048]{1,0:T(8,128)S(1)} copy-done((f32[1024,2048]{1,0:T(8,128)S(1)}, f32[1024,2048]{1,0:T(8,128)}, u32[]{:S(2)}) %copy-start) | copy-done | bytes 8388632
  57.4 4.8 %collective-permute-start.16 = (f32[256,256]{1,0:T(8,128)S(1)}, f32[256,256]{1,0:T(8,128)S(1)}, u32[]{:S(2)}, u32[]{:S(2)}) collective-permute-start(f32[256,256]{1,0:T(8,128)S(1)} %get-tuple-element.64), channel_id=1, source_target_pairs={{0,8},{24,16},{1,9},{25,17},{2,10},{26,18},{3,11},{27,19},{4,12},{... | collective-permute-start | bytes 786440 | tf_op jit(solution)/shard_map/ppermute | solution.py:453
  62.3 2.2 %collective-permute-done.11.refs_7_.refs_1_ = f32[4,256,128]{2,1,0:T(8,128)S(1)} collective-permute-done((f32[4,256,128]{2,1,0:T(8,128)S(1)}, f32[4,256,128]{2,1,0:T(8,128)S(1)}, u32[]{:S(2)}, u32[]{:S(2)}) %collective-permute-start.11) | collective-permute-done | bytes 524320 | tf_op jit(solution)/shard_map/ppermute | solution.py:22
  67.1 3.3 %collective-permute-start.19 = (f32[256,256]{1,0:T(8,128)S(1)}, f32[256,256]{1,0:T(8,128)S(1)}, u32[]{:S(2)}, u32[]{:S(2)}) collective-permute-start(f32[256,256]{1,0:T(8,128)S(1)} %get-tuple-element.66), channel_id=1, source_target_pairs={{0,16},{16,24},{24,8},{8,0},{1,17},{17,25},{25,9},{9,1},{2,18},{18... | collective-permute-start | bytes 786440 | tf_op jit(solution)/shard_map/ppermute | solution.py:454
  70.5 3.8 %collective-permute-start.14 = (f32[4,256,128]{2,1,0:T(8,128)S(1)}, f32[4,256,128]{2,1,0:T(8,128)S(1)}, u32[]{:S(2)}, u32[]{:S(2)}) collective-permute-start(f32[4,256,128]{2,1,0:T(8,128)S(1)} %arrange.3.refs_0_), channel_id=1, source_target_pairs={{0,6},{1,7},{2,4},{3,5},{4,2},{5,3},{6,0},{7,1},{8,14},{9,15},{10,... | collective-permute-start | bytes 1572872 | tf_op jit(solution)/shard_map/ppermute | solution.py:22
  76.7 2.3 %collective-permute-start.12 = (f32[4,256,128]{2,1,0:T(8,128)S(1)}, f32[4,256,128]{2,1,0:T(8,128)S(1)}, u32[]{:S(2)}, u32[]{:S(2)}) collective-permute-start(f32[4,256,128]{2,1,0:T(8,128)S(1)} %arrange.3.refs_0_), channel_id=1, source_target_pairs={{0,2},{1,3},{2,0},{3,1},{4,6},{5,7},{6,4},{7,5},{8,10},{9,11},{10,... | collective-permute-start | bytes 1572872 | tf_op jit(solution)/shard_map/ppermute | solution.py:22
  78.9 2.5 %bases.1 = (f32[2,64,512]{2,1,0:T(8,128)S(1)}, f32[1,64,512]{2,1,0:T(8,128)S(1)}) custom-call(s32[3]{0:T(128)S(1)} %pad_add_fusion.refs_0_, f32[2,512,512]{2,1,0:T(8,128)S(1)} %copy-done.6, f32[1,512,512]{2,1,0:T(8,128)S(1)} %copy-done.4, f32[256,128]{1,0:T(8,128)S(1)} %collective-permute-done.3.refs_5_.refs_2_.refs_3_), custom_call_target="tpu_custom_call" | custom-call | tf_op jit(solution)/shard_map/bases/pallas_call | solution.py:36
  81.5 3.4 %collective-permute-start.17 = (f32[256,256]{1,0:T(8,128)S(1)}, f32[256,256]{1,0:T(8,128)S(1)}, u32[]{:S(2)}, u32[]{:S(2)}) collective-permute-start(f32[256,256]{1,0:T(8,128)S(1)} %add_up.7), channel_id=1, source_target_pairs={{8,24},{16,0},{0,8},{24,16},{9,25},{17,1},{1,9},{25,17},{10,26},{1... | collective-permute-start | bytes 786440 | tf_op jit(solution)/shard_map/ppermute | solution.py:457
  88.7 2.4 %collective-permute-start.23 = (f32[256,256]{1,0:T(8,128)S(1)}, f32[256,256]{1,0:T(8,128)S(1)}, u32[]{:S(2)}, u32[]{:S(2)}) collective-permute-start(f32[256,256]{1,0:T(8,128)S(1)} %get-tuple-element.68), channel_id=1, source_target_pairs={{0,8},{24,16},{1,9},{25,17},{2,10},{26,18},{3,11},{27,19},{4,12},{... | collective-permute-start | bytes 786440 | tf_op jit(solution)/shard_map/ppermute | solution.py:453
  91.1 6.3 %collective-permute-done.13.refs_2_ = f32[4,256,128]{2,1,0:T(8,128)S(1)} collective-permute-done((f32[4,256,128]{2,1,0:T(8,128)S(1)}, f32[4,256,128]{2,1,0:T(8,128)S(1)}, u32[]{:S(2)}, u32[]{:S(2)}) %collective-permute-start.13) | collective-permute-done | bytes 524320 | tf_op jit(solution)/shard_map/ppermute | solution.py:22
  98.2 3.6 %collective-permute-done.23.refs_7_.refs_1_ = f32[256,256]{1,0:T(8,128)S(1)} collective-permute-done((f32[256,256]{1,0:T(8,128)S(1)}, f32[256,256]{1,0:T(8,128)S(1)}, u32[]{:S(2)}, u32[]{:S(2)}) %collective-permute-start.23) | collective-permute-done | bytes 262176 | tf_op jit(solution)/shard_map/ppermute | solution.py:453
  102.1 5.2 %collective-permute-start.25 = (f32[256,256]{1,0:T(8,128)S(1)}, f32[256,256]{1,0:T(8,128)S(1)}, u32[]{:S(2)}, u32[]{:S(2)}) collective-permute-start(f32[256,256]{1,0:T(8,128)S(1)} %add_up.8), channel_id=1, source_target_pairs={{8,24},{16,0},{0,8},{24,16},{9,25},{17,1},{1,9},{25,17},{10,26},{1... | collective-permute-start | bytes 786440 | tf_op jit(solution)/shard_map/ppermute | solution.py:457
  107.3 7.8 %collective-permute-done.25.refs_7_.refs_9_ = f32[256,256]{1,0:T(8,128)S(1)} collective-permute-done((f32[256,256]{1,0:T(8,128)S(1)}, f32[256,256]{1,0:T(8,128)S(1)}, u32[]{:S(2)}, u32[]{:S(2)}) %collective-permute-start.25) | collective-permute-done | bytes 262176 | tf_op jit(solution)/shard_map/ppermute | solution.py:457
  115.1 4.3 %partial_product.5 = (f32[256,512]{1,0:T(8,128)S(1)}, f32[256,512]{1,0:T(8,128)S(1)}, f32[256,512]{1,0:T(8,128)S(1)}, f32[256,512]{1,0:T(8,128)S(1)}) custom-call(s32[3]{0:T(128)S(1)} %pad_add_fusion.refs_0_, s32[4,4]{1,0:T(4,128)S(1)} %copy-done.8, s32[2,8]{1,0:T(2,128)S(1)} %copy-done.7, f32[1024,2048]{1,0:T(8,128)S(1)} %copy-done.1, ...), custom_call_target="tpu_custom_call" | custom-call | tf_op jit(solution)/shard_map/partial_product/pallas_call | solution.py:36
  120.0 3.4 %collective-permute-start.28 = (f32[256,512]{1,0:T(8,128)S(1)}, f32[256,512]{1,0:T(8,128)S(1)}, u32[]{:S(2)}, u32[]{:S(2)}) collective-permute-start(f32[256,512]{1,0:T(8,128)S(1)} %get-tuple-element.72), channel_id=1, source_target_pairs={{0,8},{24,16},{1,9},{25,17},{2,10},{26,18},{3,11},{27,19},{4,12},{... | collective-permute-start | bytes 1572872 | tf_op jit(solution)/shard_map/ppermute | solution.py:453
  124.1 9.1 %collective-permute-done.26.refs_13_.refs_3_ = f32[256,512]{1,0:T(8,128)S(1)} collective-permute-done((f32[256,512]{1,0:T(8,128)S(1)}, f32[256,512]{1,0:T(8,128)S(1)}, u32[]{:S(2)}, u32[]{:S(2)}) %collective-permute-start.26) | collective-permute-done | bytes 524320 | tf_op jit(solution)/shard_map/ppermute | solution.py:454
  133.2 9.1 %collective-permute-done.28.refs_1_.refs_15_ = f32[256,512]{1,0:T(8,128)S(1)} collective-permute-done((f32[256,512]{1,0:T(8,128)S(1)}, f32[256,512]{1,0:T(8,128)S(1)}, u32[]{:S(2)}, u32[]{:S(2)}) %collective-permute-start.28) | collective-permute-done | bytes 524320 | tf_op jit(solution)/shard_map/ppermute | solution.py:453
  142.3 2.9 %finish.2 = (f32[2,256,512]{2,1,0:T(8,128)}, f32[2,4,64,512]{3,2,1,0:T(8,128)S(1)}, f32[2,4,64,512]{3,2,1,0:T(8,128)S(1)}, f32[512,512]{1,0:T(8,128)S(1)}, f32[512,512]{1,0:T(8,128)S(1)}) custom-call(s32[3]{0:T(128)S(1)} %pad_add_fusion.refs_0_, s32[2,8]{1,0:T(2,128)S(1)} %copy-done.7, f32[256,256]{1,0:T(8,128)S(1)} %get-tuple-element.74.refs_2_, ...), custom_call_target="tpu_custom_call" | custom-call | tf_op jit(solution)/shard_map/finish/pallas_call | solution.py:36
  145.4 4.9 %collective-permute-start.29 = (f32[256,512]{1,0:T(8,128)S(1)}, f32[256,512]{1,0:T(8,128)S(1)}, u32[]{:S(2)}, u32[]{:S(2)}) collective-permute-start(f32[256,512]{1,0:T(8,128)S(1)} %add_up.9), channel_id=1, source_target_pairs={{8,24},{16,0},{0,8},{24,16},{9,25},{17,1},{1,9},{25,17},{10,26},{1... | collective-permute-start | bytes 1572872 | tf_op jit(solution)/shard_map/ppermute | solution.py:457
  150.3 2.3 %rest.1 = (f32[512,512]{1,0:T(8,128)S(1)}, f32[256,512]{1,0:T(8,128)S(1)}) custom-call(f32[1,512,512]{2,1,0:T(8,128)S(1)} %copy-done.4, f32[512,512]{1,0:T(8,128)S(1)} %get-tuple-element.76.refs_1_, f32[512,512]{1,0:T(8,128)S(1)} %get-tuple-element.77.refs_2_, f32[2,256,512]{2,1,0:T(8,128)S(1)} %copy-done.5), custom_call_target="tpu_custom_call" | custom-call | tf_op jit(solution)/shard_map/rest/pallas_call | solution.py:36
  153.3 8.2 %collective-permute-start.32 = (f32[2,64,512]{2,1,0:T(8,128)S(1)}, f32[2,64,512]{2,1,0:T(8,128)S(1)}, u32[]{:S(2)}, u32[]{:S(2)}) collective-permute-start(f32[2,64,512]{2,1,0:T(8,128)S(1)} %get-tuple-element.85), channel_id=1, source_target_pairs={{0,4},{1,5},{2,6},{3,7},{4,0},{5,1},{6,2},{7,3},{8,12},{9,13},{10,... | collective-permute-start | bytes 786440 | tf_op jit(solution)/shard_map/ppermute | solution.py:22
  161.8 11.3 %collective-permute-done.32.refs_3_ = f32[2,64,512]{2,1,0:T(8,128)S(1)} collective-permute-done((f32[2,64,512]{2,1,0:T(8,128)S(1)}, f32[2,64,512]{2,1,0:T(8,128)S(1)}, u32[]{:S(2)}, u32[]{:S(2)}) %collective-permute-start.32) | collective-permute-done | bytes 262176 | tf_op jit(solution)/shard_map/ppermute | solution.py:22
  184.6 2.4 %collective-permute-done.39.refs_2_ = f32[1,64,512]{2,1,0:T(8,128)S(1)} collective-permute-done((f32[1,64,512]{2,1,0:T(8,128)S(1)}, f32[1,64,512]{2,1,0:T(8,128)S(1)}, u32[]{:S(2)}, u32[]{:S(2)}) %collective-permute-start.39) | collective-permute-done | bytes 131104 | tf_op jit(solution)/shard_map/ppermute | solution.py:22
  191.4 3.7 %collective-permute-done.41.refs_1_ = f32[1,64,512]{2,1,0:T(8,128)S(1)} collective-permute-done((f32[1,64,512]{2,1,0:T(8,128)S(1)}, f32[1,64,512]{2,1,0:T(8,128)S(1)}, u32[]{:S(2)}, u32[]{:S(2)}) %collective-permute-start.41) | collective-permute-done | bytes 131104 | tf_op jit(solution)/shard_map/ppermute | solution.py:22
  195.2 2.3 %collective-permute-done.36.refs_4_ = f32[64,512]{1,0:T(8,128)S(1)} collective-permute-done((f32[64,512]{1,0:T(8,128)S(1)}, f32[64,512]{1,0:T(8,128)S(1)}, u32[]{:S(2)}, u32[]{:S(2)}) %collective-permute-start.36) | collective-permute-done | bytes 131104 | tf_op jit(solution)/shard_map/ppermute | solution.py:22
  197.5 4.9 %collective-permute-done.42.refs_6_ = f32[1,64,512]{2,1,0:T(8,128)S(1)} collective-permute-done((f32[1,64,512]{2,1,0:T(8,128)S(1)}, f32[1,64,512]{2,1,0:T(8,128)S(1)}, u32[]{:S(2)}, u32[]{:S(2)}) %collective-permute-start.42) | collective-permute-done | bytes 131104 | tf_op jit(solution)/shard_map/ppermute | solution.py:22
  (99 shorter events, 51.5 us)
Async XLA Ops:
  2.6 10.1 %collective-permute-start = (f32[2,256,128]{2,1,0:T(8,128)S(1)}, f32[2,256,128]{2,1,0:T(8,128)S(1)}, u32[]{:S(2)}, u32[]{:S(2)}) collective-permute-start(f32[2,256,128]{2,1,0:T(8,128)S(1)} %get-tuple-element.52), channel_id=1, source_target_pairs={{0,2},{1,3},{2,0},{3,1},{4,6},{5,7},{6,4},{7,5},{8,10},{9,11},{10,... | collective-permute-start | bytes 786440 | tf_op jit(solution)/shard_map/ppermute | solution.py:22
  5.6 13.4 %collective-permute-start.1 = (f32[2,256,128]{2,1,0:T(8,128)S(1)}, f32[2,256,128]{2,1,0:T(8,128)S(1)}, u32[]{:S(2)}, u32[]{:S(2)}) collective-permute-start(f32[2,256,128]{2,1,0:T(8,128)S(1)} %get-tuple-element.53), channel_id=1, source_target_pairs={{0,4},{1,5},{2,6},{3,7},{4,0},{5,1},{6,2},{7,3},{8,12},{9,13},{10,... | collective-permute-start | bytes 786440 | tf_op jit(solution)/shard_map/ppermute | solution.py:22
  7.2 11.9 %collective-permute-start.2 = (f32[2,256,128]{2,1,0:T(8,128)S(1)}, f32[2,256,128]{2,1,0:T(8,128)S(1)}, u32[]{:S(2)}, u32[]{:S(2)}) collective-permute-start(f32[2,256,128]{2,1,0:T(8,128)S(1)} %get-tuple-element.54), channel_id=1, source_target_pairs={{0,6},{1,7},{2,4},{3,5},{4,2},{5,3},{6,0},{7,1},{8,14},{9,15},{10,... | collective-permute-start | bytes 786440 | tf_op jit(solution)/shard_map/ppermute | solution.py:22
  21.3 11.8 %collective-permute-start.4 = (f32[256,128]{1,0:T(8,128)S(1)}, f32[256,128]{1,0:T(8,128)S(1)}, u32[]{:S(2)}, u32[]{:S(2)}) collective-permute-start(f32[256,128]{1,0:T(8,128)S(1)} %get-tuple-element.56), channel_id=1, source_target_pairs={{0,16},{8,24},{16,0},{24,8},{1,17},{9,25},{17,1},{25,9},{2,18},{10... | collective-permute-start | bytes 393224 | tf_op jit(solution)/shard_map/ppermute | solution.py:22
  23.9 9.2 %collective-permute-start.5 = (f32[256,128]{1,0:T(8,128)S(1)}, f32[256,128]{1,0:T(8,128)S(1)}, u32[]{:S(2)}, u32[]{:S(2)}) collective-permute-start(f32[256,128]{1,0:T(8,128)S(1)} %get-tuple-element.57), channel_id=1, source_target_pairs={{0,24},{8,16},{16,8},{24,0},{1,25},{9,17},{17,9},{25,1},{2,26},{10... | collective-permute-start | bytes 393224 | tf_op jit(solution)/shard_map/ppermute | solution.py:22
  33.7 15.4 %collective-permute-start.10 = (f32[4,256,128]{2,1,0:T(8,128)S(1)}, f32[4,256,128]{2,1,0:T(8,128)S(1)}, u32[]{:S(2)}, u32[]{:S(2)}) collective-permute-start(f32[4,256,128]{2,1,0:T(8,128)S(1)} %arrange.2.refs_0_), channel_id=1, source_target_pairs={{0,4},{1,5},{2,6},{3,7},{4,0},{5,1},{6,2},{7,3},{8,12},{9,13},{10,... | collective-permute-start | bytes 1572872 | tf_op jit(solution)/shard_map/ppermute | solution.py:22
  34.3 14.8 %collective-permute-start.9 = (f32[4,256,128]{2,1,0:T(8,128)S(1)}, f32[4,256,128]{2,1,0:T(8,128)S(1)}, u32[]{:S(2)}, u32[]{:S(2)}) collective-permute-start(f32[4,256,128]{2,1,0:T(8,128)S(1)} %arrange.2.refs_0_), channel_id=1, source_target_pairs={{0,2},{1,3},{2,0},{3,1},{4,6},{5,7},{6,4},{7,5},{8,10},{9,11},{10,... | collective-permute-start | bytes 1572872 | tf_op jit(solution)/shard_map/ppermute | solution.py:22
  38.4 10.6 %collective-permute-start.7 = (f32[256,128]{1,0:T(8,128)S(1)}, f32[256,128]{1,0:T(8,128)S(1)}, u32[]{:S(2)}, u32[]{:S(2)}) collective-permute-start(f32[256,128]{1,0:T(8,128)S(1)} %get-tuple-element.60), channel_id=1, source_target_pairs={{0,16},{8,24},{16,0},{24,8},{1,17},{9,25},{17,1},{25,9},{2,18},{10... | collective-permute-start | bytes 393224 | tf_op jit(solution)/shard_map/ppermute | solution.py:22
  39.5 9.5 %collective-permute-start.8 = (f32[256,128]{1,0:T(8,128)S(1)}, f32[256,128]{1,0:T(8,128)S(1)}, u32[]{:S(2)}, u32[]{:S(2)}) collective-permute-start(f32[256,128]{1,0:T(8,128)S(1)} %get-tuple-element.61), channel_id=1, source_target_pairs={{0,24},{8,16},{16,8},{24,0},{1,25},{9,17},{17,9},{25,1},{2,26},{10... | collective-permute-start | bytes 393224 | tf_op jit(solution)/shard_map/ppermute | solution.py:22
  49.2 15.2 %collective-permute-start.11 = (f32[4,256,128]{2,1,0:T(8,128)S(1)}, f32[4,256,128]{2,1,0:T(8,128)S(1)}, u32[]{:S(2)}, u32[]{:S(2)}) collective-permute-start(f32[4,256,128]{2,1,0:T(8,128)S(1)} %arrange.2.refs_0_), channel_id=1, source_target_pairs={{0,6},{1,7},{2,4},{3,5},{4,2},{5,3},{6,0},{7,1},{8,14},{9,15},{10,... | collective-permute-start | bytes 1572872 | tf_op jit(solution)/shard_map/ppermute | solution.py:22
  57.4 9.0 %collective-permute-start.16 = (f32[256,256]{1,0:T(8,128)S(1)}, f32[256,256]{1,0:T(8,128)S(1)}, u32[]{:S(2)}, u32[]{:S(2)}) collective-permute-start(f32[256,256]{1,0:T(8,128)S(1)} %get-tuple-element.64), channel_id=1, source_target_pairs={{0,8},{24,16},{1,9},{25,17},{2,10},{26,18},{3,11},{27,19},{4,12},{... | collective-permute-start | bytes 786440 | tf_op jit(solution)/shard_map/ppermute | solution.py:453
  66.5 18.4 %collective-permute-start.18 = (f32[2,4,256,128]{3,2,1,0:T(8,128)S(1)}, f32[2,4,256,128]{3,2,1,0:T(8,128)S(1)}, u32[]{:S(2)}, u32[]{:S(2)}) collective-permute-start(f32[2,4,256,128]{3,2,1,0:T(8,128)S(1)} %pack.4.refs_4_), channel_id=1, source_target_pairs={{0,1},{1,0},{2,3},{3,2},{4,5},{5,4},{6,7},{7,6},{8,9},{9,8},{10,11... | collective-permute-start | bytes 3145736 | tf_op jit(solution)/shard_map/ppermute | solution.py:22
  67.1 9.5 %collective-permute-start.19 = (f32[256,256]{1,0:T(8,128)S(1)}, f32[256,256]{1,0:T(8,128)S(1)}, u32[]{:S(2)}, u32[]{:S(2)}) collective-permute-start(f32[256,256]{1,0:T(8,128)S(1)} %get-tuple-element.66), channel_id=1, source_target_pairs={{0,16},{16,24},{24,8},{8,0},{1,17},{17,25},{25,9},{9,1},{2,18},{18... | collective-permute-start | bytes 786440 | tf_op jit(solution)/shard_map/ppermute | solution.py:454
  70.5 18.2 %collective-permute-start.14 = (f32[4,256,128]{2,1,0:T(8,128)S(1)}, f32[4,256,128]{2,1,0:T(8,128)S(1)}, u32[]{:S(2)}, u32[]{:S(2)}) collective-permute-start(f32[4,256,128]{2,1,0:T(8,128)S(1)} %arrange.3.refs_0_), channel_id=1, source_target_pairs={{0,6},{1,7},{2,4},{3,5},{4,2},{5,3},{6,0},{7,1},{8,14},{9,15},{10,... | collective-permute-start | bytes 1572872 | tf_op jit(solution)/shard_map/ppermute | solution.py:22
  74.3 23.1 %collective-permute-start.13 = (f32[4,256,128]{2,1,0:T(8,128)S(1)}, f32[4,256,128]{2,1,0:T(8,128)S(1)}, u32[]{:S(2)}, u32[]{:S(2)}) collective-permute-start(f32[4,256,128]{2,1,0:T(8,128)S(1)} %arrange.3.refs_0_), channel_id=1, source_target_pairs={{0,4},{1,5},{2,6},{3,7},{4,0},{5,1},{6,2},{7,3},{8,12},{9,13},{10,... | collective-permute-start | bytes 1572872 | tf_op jit(solution)/shard_map/ppermute | solution.py:22
  76.7 21.5 %collective-permute-start.12 = (f32[4,256,128]{2,1,0:T(8,128)S(1)}, f32[4,256,128]{2,1,0:T(8,128)S(1)}, u32[]{:S(2)}, u32[]{:S(2)}) collective-permute-start(f32[4,256,128]{2,1,0:T(8,128)S(1)} %arrange.3.refs_0_), channel_id=1, source_target_pairs={{0,2},{1,3},{2,0},{3,1},{4,6},{5,7},{6,4},{7,5},{8,10},{9,11},{10,... | collective-permute-start | bytes 1572872 | tf_op jit(solution)/shard_map/ppermute | solution.py:22
  81.5 16.7 %collective-permute-start.17 = (f32[256,256]{1,0:T(8,128)S(1)}, f32[256,256]{1,0:T(8,128)S(1)}, u32[]{:S(2)}, u32[]{:S(2)}) collective-permute-start(f32[256,256]{1,0:T(8,128)S(1)} %add_up.7), channel_id=1, source_target_pairs={{8,24},{16,0},{0,8},{24,16},{9,25},{17,1},{1,9},{25,17},{10,26},{1... | collective-permute-start | bytes 786440 | tf_op jit(solution)/shard_map/ppermute | solution.py:457
  87.1 11.1 %collective-permute-start.21 = (f32[256,256]{1,0:T(8,128)S(1)}, f32[256,256]{1,0:T(8,128)S(1)}, u32[]{:S(2)}, u32[]{:S(2)}) collective-permute-start(f32[256,256]{1,0:T(8,128)S(1)} %get-tuple-element.67), channel_id=1, source_target_pairs={{0,16},{16,24},{24,8},{8,0},{1,17},{17,25},{25,9},{9,1},{2,18},{18... | collective-permute-start | bytes 786440 | tf_op jit(solution)/shard_map/ppermute | solution.py:454
  88.7 13.2 %collective-permute-start.23 = (f32[256,256]{1,0:T(8,128)S(1)}, f32[256,256]{1,0:T(8,128)S(1)}, u32[]{:S(2)}, u32[]{:S(2)}) collective-permute-start(f32[256,256]{1,0:T(8,128)S(1)} %get-tuple-element.68), channel_id=1, source_target_pairs={{0,8},{24,16},{1,9},{25,17},{2,10},{26,18},{3,11},{27,19},{4,12},{... | collective-permute-start | bytes 786440 | tf_op jit(solution)/shard_map/ppermute | solution.py:453
  102.0 13.1 %collective-permute-start.24 = (f32[4,4,256,128]{3,2,1,0:T(8,128)S(1)}, f32[4,4,256,128]{3,2,1,0:T(8,128)S(1)}, u32[]{:S(2)}, u32[]{:S(2)}) collective-permute-start(f32[4,4,256,128]{3,2,1,0:T(8,128)S(1)} %pack.5.refs_4_), channel_id=1, source_target_pairs={{0,1},{1,0},{2,3},{3,2},{4,5},{5,4},{6,7},{7,6},{8,9},{9,8},{10,11... | collective-permute-start | bytes 6291464 | tf_op jit(solution)/shard_map/ppermute | solution.py:22
  102.1 13.0 %collective-permute-start.25 = (f32[256,256]{1,0:T(8,128)S(1)}, f32[256,256]{1,0:T(8,128)S(1)}, u32[]{:S(2)}, u32[]{:S(2)}) collective-permute-start(f32[256,256]{1,0:T(8,128)S(1)} %add_up.8), channel_id=1, source_target_pairs={{8,24},{16,0},{0,8},{24,16},{9,25},{17,1},{1,9},{25,17},{10,26},{1... | collective-permute-start | bytes 786440 | tf_op jit(solution)/shard_map/ppermute | solution.py:457
  119.4 13.8 %collective-permute-start.26 = (f32[256,512]{1,0:T(8,128)S(1)}, f32[256,512]{1,0:T(8,128)S(1)}, u32[]{:S(2)}, u32[]{:S(2)}) collective-permute-start(f32[256,512]{1,0:T(8,128)S(1)} %get-tuple-element.71), channel_id=1, source_target_pairs={{0,16},{16,24},{24,8},{8,0},{1,17},{17,25},{25,9},{9,1},{2,18},{18... | collective-permute-start | bytes 1572872 | tf_op jit(solution)/shard_map/ppermute | solution.py:454
  120.0 22.3 %collective-permute-start.28 = (f32[256,512]{1,0:T(8,128)S(1)}, f32[256,512]{1,0:T(8,128)S(1)}, u32[]{:S(2)}, u32[]{:S(2)}) collective-permute-start(f32[256,512]{1,0:T(8,128)S(1)} %get-tuple-element.72), channel_id=1, source_target_pairs={{0,8},{24,16},{1,9},{25,17},{2,10},{26,18},{3,11},{27,19},{4,12},{... | collective-permute-start | bytes 1572872 | tf_op jit(solution)/shard_map/ppermute | solution.py:453
  123.4 18.9 %collective-permute-start.27 = (f32[256,512]{1,0:T(8,128)S(1)}, f32[256,512]{1,0:T(8,128)S(1)}, u32[]{:S(2)}, u32[]{:S(2)}) collective-permute-start(f32[256,512]{1,0:T(8,128)S(1)} %get-tuple-element.72), channel_id=1, source_target_pairs={{8,16},{16,8},{9,17},{17,9},{10,18},{18,10},{11,19},{19,11},{12,20... | collective-permute-start | bytes 1572872 | tf_op jit(solution)/shard_map/ppermute | solution.py:455
  145.3 7.3 %collective-permute-start.30 = (f32[2,4,64,512]{3,2,1,0:T(8,128)S(1)}, f32[2,4,64,512]{3,2,1,0:T(8,128)S(1)}, u32[]{:S(2)}, u32[]{:S(2)}) collective-permute-start(f32[2,4,64,512]{3,2,1,0:T(8,128)S(1)} %get-tuple-element.82), channel_id=1, source_target_pairs={{0,1},{1,0},{2,3},{3,2},{4,5},{5,4},{6,7},{7,6},{8,9},{9,8},{10,11... | collective-permute-start | bytes 3145736 | tf_op jit(solution)/shard_map/ppermute | solution.py:22
  145.4 28.3 %collective-permute-start.29 = (f32[256,512]{1,0:T(8,128)S(1)}, f32[256,512]{1,0:T(8,128)S(1)}, u32[]{:S(2)}, u32[]{:S(2)}) collective-permute-start(f32[256,512]{1,0:T(8,128)S(1)} %add_up.9), channel_id=1, source_target_pairs={{8,24},{16,0},{0,8},{24,16},{9,25},{17,1},{1,9},{25,17},{10,26},{1... | collective-permute-start | bytes 1572872 | tf_op jit(solution)/shard_map/ppermute | solution.py:457
  153.3 8.5 %collective-permute-start.31 = (f32[2,64,512]{2,1,0:T(8,128)S(1)}, f32[2,64,512]{2,1,0:T(8,128)S(1)}, u32[]{:S(2)}, u32[]{:S(2)}) collective-permute-start(f32[2,64,512]{2,1,0:T(8,128)S(1)} %get-tuple-element.84), channel_id=1, source_target_pairs={{0,2},{1,3},{2,0},{3,1},{4,6},{5,7},{6,4},{7,5},{8,10},{9,11},{10,... | collective-permute-start | bytes 786440 | tf_op jit(solution)/shard_map/ppermute | solution.py:22
  153.3 19.7 %collective-permute-start.32 = (f32[2,64,512]{2,1,0:T(8,128)S(1)}, f32[2,64,512]{2,1,0:T(8,128)S(1)}, u32[]{:S(2)}, u32[]{:S(2)}) collective-permute-start(f32[2,64,512]{2,1,0:T(8,128)S(1)} %get-tuple-element.85), channel_id=1, source_target_pairs={{0,4},{1,5},{2,6},{3,7},{4,0},{5,1},{6,2},{7,3},{8,12},{9,13},{10,... | collective-permute-start | bytes 786440 | tf_op jit(solution)/shard_map/ppermute | solution.py:22
  161.5 11.5 %collective-permute-start.33 = (f32[2,64,512]{2,1,0:T(8,128)S(1)}, f32[2,64,512]{2,1,0:T(8,128)S(1)}, u32[]{:S(2)}, u32[]{:S(2)}) collective-permute-start(f32[2,64,512]{2,1,0:T(8,128)S(1)} %get-tuple-element.86), channel_id=1, source_target_pairs={{0,6},{1,7},{2,4},{3,5},{4,2},{5,3},{6,0},{7,1},{8,14},{9,15},{10,... | collective-permute-start | bytes 786440 | tf_op jit(solution)/shard_map/ppermute | solution.py:22
  181.3 7.4 %collective-permute-start.40 = (f32[1,64,512]{2,1,0:T(8,128)S(1)}, f32[1,64,512]{2,1,0:T(8,128)S(1)}, u32[]{:S(2)}, u32[]{:S(2)}) collective-permute-start(f32[1,64,512]{2,1,0:T(8,128)S(1)} %get-tuple-element.96), channel_id=1, source_target_pairs={{0,6},{1,7},{2,4},{3,5},{4,2},{5,3},{6,0},{7,1},{8,14},{9,15},{10,... | collective-permute-start | bytes 393224 | tf_op jit(solution)/shard_map/ppermute | solution.py:22
  182.5 8.8 %collective-permute-start.35 = (f32[64,512]{1,0:T(8,128)S(1)}, f32[64,512]{1,0:T(8,128)S(1)}, u32[]{:S(2)}, u32[]{:S(2)}) collective-permute-start(f32[64,512]{1,0:T(8,128)S(1)} %add_up.10.refs_0_), channel_id=1, source_target_pairs={{0,16},{8,24},{16,0},{24,8},{1,17},{9,25},{17,1},{25,9},{2,18},{10... | collective-permute-start | bytes 393224 | tf_op jit(solution)/shard_map/ppermute | solution.py:22
  195.1 7.3 %collective-permute-start.42 = (f32[1,64,512]{2,1,0:T(8,128)S(1)}, f32[1,64,512]{2,1,0:T(8,128)S(1)}, u32[]{:S(2)}, u32[]{:S(2)}) collective-permute-start(f32[1,64,512]{2,1,0:T(8,128)S(1)} %add_up.13.refs_5_), channel_id=1, source_target_pairs={{0,16},{8,24},{16,0},{24,8},{1,17},{9,25},{17,1},{25,9},{2,18},{10... | collective-permute-start | bytes 393224 | tf_op jit(solution)/shard_map/ppermute | solution.py:22
  (20 other events, 212.1 us)

commit v10 on v8

--- a/solution.py
+++ b/solution.py
@@ -8,7 +8,7 @@
 from jax.sharding import PartitionSpec as P
 
 BOTH = ("prow", "pcol")
-VMEM_LIMIT = 28 * 1024 * 1024
+VMEM_LIMIT = 32 * 1024 * 1024
 LANES = 128
 
 
@@ -55,18 +55,19 @@
 
 
 def cut_kernel(place, factor_ref, *out_refs):
-    width = out_refs[0].shape[2]
+    width = out_refs[0].shape[1]
     for o, out_ref in enumerate(out_refs):
         start = pl.multiple_of((place[2] ^ o) * width, width)
-        out_ref[...] = factor_ref[:, :, pl.ds(start, width)]
-
-
-def cut(place, factor, count):
-    nsuper, unit_rows, columns = factor.shape
-    piece = jax.ShapeDtypeStruct((nsuper, unit_rows, columns // count), factor.dtype)
+        out_ref[...] = factor_ref[0, :, pl.ds(start, width)]
+
+
+def cut(place, factor, number, count, waits):
+    _, unit_rows, columns = factor.shape
+    piece = jax.ShapeDtypeStruct((unit_rows, columns // count), factor.dtype)
+    spec = pl.BlockSpec((1, unit_rows, columns), lambda *_: (number, 0, 0))
     outs = [piece] * count
     specs = [whole(piece)] * count
-    return run(cut_kernel, [place], [factor], [whole(factor)], [], outs, specs, name="cut")
+    return run(cut_kernel, [place], [factor], [spec], waits, outs, specs, name="cut")
 
 
 def turn_kernel(place, *refs):
@@ -76,18 +77,14 @@
         @pl.when((place[1] ^ place[2]) == shift)
         def _copy(shift=shift):
             for o in range(count):
-                refs[count + o][...] = refs[o ^ shift][0]
-
-
-def turn(place, pieces, number, waits):
+                refs[count + o][...] = refs[o ^ shift][...]
+
+
+def turn(place, pieces, waits):
     count = len(pieces)
-    _, unit_rows, width = pieces[0].shape
-    piece = jax.ShapeDtypeStruct((unit_rows, width), pieces[0].dtype)
-    spec = pl.BlockSpec((1, unit_rows, width), lambda *_: (number, 0, 0))
-    return run(
-        turn_kernel, [place], pieces, [spec] * count, waits, [piece] * count,
-        [whole(piece)] * count, name="turn",
-    )
+    piece = jax.ShapeDtypeStruct(pieces[0].shape, pieces[0].dtype)
+    specs = [whole(piece)] * count
+    return run(turn_kernel, [place], pieces, specs, waits, [piece] * count, specs, name="turn")
 
 
 def arrange_kernel(place, *refs):
@@ -134,8 +131,7 @@
 
 
 def partial_kernel(sides, ratio, count, number, place, slots, ancestors, tile_ref, *refs):
-    piece_refs, out_refs = refs[:sides], refs[sides:-2]
-    right_high, right_low = refs[-2:]
+    piece_refs, out_refs, right_ref = refs[:sides], refs[sides:-1], refs[-1]
     chunk_rows, columns = out_refs[0].shape
     blocks = tile_ref.shape[1] // columns
     step = pl.program_id(0)
@@ -145,19 +141,23 @@
 
     @pl.when(step == 0)
     def _assemble():
+        def put(first, lanes, value):
+            high, low = halves(value)
+            for index in range(value.shape[0] // columns):
+                part = slice(index * columns, (index + 1) * columns)
+                for turn, side in enumerate((high, low, high)):
+                    right_ref[first + index, pl.ds(turn * columns, columns), lanes] = side[part]
+
         if len(piece_refs) == 1:
-            right_high[...], right_low[...] = halves(piece_refs[0][...])
+            put(0, slice(None), piece_refs[0][...])
             return
         for side, ref in enumerate(piece_refs):
             chips, parts, unit_rows, width = ref.shape
+            span = parts * unit_rows
             for o in range(chips):
                 owner = place[0] ^ (2 * o + side)
                 lanes = pl.ds(pl.multiple_of(owner // ratio * width, width), width)
-                first = owner % ratio * (parts * unit_rows)
-                rows = pl.ds(pl.multiple_of(first, parts * unit_rows), parts * unit_rows)
-                high, low = halves(ref[o].reshape(parts * unit_rows, width))
-                right_high[rows, lanes] = high
-                right_low[rows, lanes] = low
+                put(owner % ratio * (span // columns), lanes, ref[o].reshape(span, width))
 
     def multiply(out_ref):
         out_ref[...] = jnp.zeros_like(out_ref)
@@ -170,10 +170,9 @@
                 def _block():
                     span = pl.ds(pl.multiple_of(block * columns, columns), columns)
                     high, low = halves(tile_ref[:, span])
-                    right = right_high[span, :]
-                    dot = functools.partial(jnp.dot, preferred_element_type=jnp.float32)
-                    out_ref[...] += dot(high, right) + (
-                        dot(high, right_low[span, :]) + dot(low, right)
+                    left = jnp.concatenate([high, high, low], axis=1)
+                    out_ref[...] += jnp.dot(
+                        left, right_ref[block], preferred_element_type=jnp.float32
                     )
 
                 return carry
@@ -198,7 +197,7 @@
         [out] * count,
         [whole(out)] * count,
         grid=(count,),
-        scratch=[pltpu.VMEM((cols, columns), jnp.bfloat16)] * 2,
+        scratch=[pltpu.VMEM((cols // columns, 3 * columns, columns), jnp.bfloat16)],
         name="partial_product",
     )
 
@@ -518,15 +517,19 @@
     def own_block(place):
         return (place[0] * count + place[1]) * unit_rows // columns
 
-    received = []
+    sent, turned, received, waits = [], [], [], []
     if width % LANES == 0:
-        sent = to_column(cut(place, factor, count), ratio)
         for number in range(nsuper):
+            sent.append(to_column(cut(place, factor, number, count, waits), ratio))
             waits = received[-1][1:] if received else []
-            received.append(to_plane(turn(place, sent, number, waits)))
-    rows, gathered = [], []
+            turned.append(turn(place, sent[number], waits))
+            waits = [turned[0][0]]
+            received.append(to_plane(turned[number]))
+    bases = bases_of(place, diag_inverse, link_factor, columns // pcol_count, [piece[0] for piece in turned[:1]])
+    rows, gathered = [], [bases[0]]
     for number in range(nsuper):
         if received:
+            gathered += [piece for later in sent[number + 1 : number + 2] for piece in later[1:]]
             own = arrange(place, received[number], gathered)
             found = gather_plane(own, pcol_count)
             gathered = found[1:]
@@ -536,8 +539,6 @@
         else:
             own = to_plane_whole(factor[number], count, ratio)
             pieces = [in_rows(lax.all_gather(own, "pcol", axis=0), count, ratio)]
-        if number == 0:
-            bases = bases_of(place, diag_inverse, link_factor, columns // pcol_count, [own])
         partial = partial_product(
             place, slots, ancestors, inverse_tiles, pieces, ratio, columns, number, [bases[0]]
         )

time: 187 us -> 180 us (0.963)
  waiting for transfers between devices: 103 us -> 80.8 us
  starting transfers between devices: 54.3 us -> 60.8 us
  Pallas kernels: 26.6 us -> 31.2 us
  local copies, waits for them, and re-layouts: 1.27 us -> 5.3 us
    ppermute x30 -> x33, waiting for transfers between devices: 69.8 us -> 52.8 us  [flip(): lax.ppermute(value, axis, [(i, i ^ bit) for i in range(lax.axis_size(axis...]
    ppermute x30 -> x33, starting transfers between devices: 33.9 us -> 40.5 us  [flip(): lax.ppermute(value, axis, [(i, i ^ bit) for i in range(lax.axis_size(axis...]
    ppermute x2, waiting for transfers between devices: 20.4 us -> 14.9 us  [sum_over_four(): near = lax.ppermute(slots[0], 'prow', [(0, 1), (3, 2)])]
    pallas_call x23 -> x24, Pallas kernels: 26.6 us -> 31.2 us  [run(): pl.pallas_call(body, grid_spec=pltpu.PrefetchScalarGridSpec(num_scalar_pr...]
    ppermute x2, starting transfers between devices: 9 us -> 4.57 us  [sum_over_four(): total = lax.ppermute(slots[1], 'prow', [(0, 2), (2, 3), (3, 1), (1, 0)])]
    unnamed x18 -> x22, local copies, waits for them, and re-layouts: 1.27 us -> 5.3 us
    ppermute x2, starting transfers between devices: 6.37 us -> 9.01 us  [sum_over_four(): last = lax.ppermute(both, 'prow', [(1, 3), (2, 0), (0, 1), (3, 2)])]
  transfers between devices with their start and end apart: 38 -> 41, of which waited for: 23 -> 20; matrix products, arithmetic and copies ran while one was open for 0% -> 0% of each run, Pallas kernels for 9% -> 12%
where the time goes in v10:
time: 180 us; the launch traced here: 179 us
  waiting for transfers between devices  80.8 us (45%)
  starting transfers between devices  60.8 us (34%)
  Pallas kernels  31.2 us (17%)
  local copies, waits for them, and re-layouts  5.3 us (3%)
    ppermute x33, waiting for transfers between devices, flip(): lax.ppermute(value, axis, [(i, i ^ bit) for i in range(lax.axis_size(axis...  52.8 us
    ppermute x33, starting transfers between devices, flip(): lax.ppermute(value, axis, [(i, i ^ bit) for i in range(lax.axis_size(axis...  40.5 us
    pallas_call x24, Pallas kernels, run(): pl.pallas_call(body, grid_spec=pltpu.PrefetchScalarGridSpec(num_scalar_pr...  31.2 us
    ppermute x2, waiting for transfers between devices, sum_over_four(): near = lax.ppermute(slots[0], 'prow', [(0, 1), (3, 2)])  14.9 us
    ppermute x2, waiting for transfers between devices, sum_over_four(): total = lax.ppermute(slots[1], 'prow', [(0, 2), (2, 3), (3, 1), (1, 0)])  11.3 us
    ppermute x2, starting transfers between devices, sum_over_four(): last = lax.ppermute(both, 'prow', [(1, 3), (2, 0), (0, 1), (3, 2)])  9.01 us
    ppermute x2, starting transfers between devices, sum_over_four(): near = lax.ppermute(slots[0], 'prow', [(0, 1), (3, 2)])  5.4 us
    unnamed x22, local copies, waits for them, and re-layouts  5.3 us
  transfers between devices with their start and end apart: 41, of which 20 were waited for; matrix products, arithmetic and copies ran while one was open for 0% of the time, Pallas kernels for 12%

profile of v10, /device:TPU:0, one launch (start us, length us, event | category | flops | bytes accessed | tf_op | source)
XLA Modules:
  0.0 179.2 jit_solution(948441136483459512)
XLA Ops:
  2.6 3.0 %collective-permute-start = (f32[256,128]{1,0:T(8,128)S(1)}, f32[256,128]{1,0:T(8,128)S(1)}, u32[]{:S(2)}, u32[]{:S(2)}) collective-permute-start(f32[256,128]{1,0:T(8,128)S(1)} %get-tuple-element.52), channel_id=1, source_target_pairs={{0,2},{1,3},{2,0},{3,1},{4,6},{5,7},{6,4},{7,5},{8,10},{9,11},{10,... | collective-permute-start | bytes 393224 | tf_op jit(solution)/shard_map/ppermute | solution.py:22
  7.1 2.4 %collective-permute-done.refs_2_ = f32[256,128]{1,0:T(8,128)S(1)} collective-permute-done((f32[256,128]{1,0:T(8,128)S(1)}, f32[256,128]{1,0:T(8,128)S(1)}, u32[]{:S(2)}, u32[]{:S(2)}) %collective-permute-start) | collective-permute-done | bytes 131104 | tf_op jit(solution)/shard_map/ppermute | solution.py:22
  9.5 3.9 %collective-permute-done.1.refs_3_ = f32[256,128]{1,0:T(8,128)S(1)} collective-permute-done((f32[256,128]{1,0:T(8,128)S(1)}, f32[256,128]{1,0:T(8,128)S(1)}, u32[]{:S(2)}, u32[]{:S(2)}) %collective-permute-start.1) | collective-permute-done | bytes 131104 | tf_op jit(solution)/shard_map/ppermute | solution.py:22
  15.6 2.6 %collective-permute-start.7 = (f32[256,128]{1,0:T(8,128)S(1)}, f32[256,128]{1,0:T(8,128)S(1)}, u32[]{:S(2)}, u32[]{:S(2)}) collective-permute-start(f32[256,128]{1,0:T(8,128)S(1)} %get-tuple-element.61), channel_id=1, source_target_pairs={{0,16},{8,24},{16,0},{24,8},{1,17},{9,25},{17,1},{25,9},{2,18},{10... | collective-permute-start | bytes 393224 | tf_op jit(solution)/shard_map/ppermute | solution.py:22
  26.6 2.5 %bases.1 = (f32[2,64,512]{2,1,0:T(8,128)S(1)}, f32[1,64,512]{2,1,0:T(8,128)S(1)}) custom-call(s32[3]{0:T(128)S(1)} %pad_add_fusion.refs_0_, f32[2,512,512]{2,1,0:T(8,128)S(1)} %copy-done.6, f32[1,512,512]{2,1,0:T(8,128)S(1)} %copy-done.3, f32[256,128]{1,0:T(8,128)S(1)} %get-tuple-element.55.refs_2_.refs_3_.refs_1_), custom_call_target="tpu_custom_call" | custom-call | tf_op jit(solution)/shard_map/bases/pallas_call | solution.py:36
  34.7 3.5 %collective-permute-start.10 = (f32[256,128]{1,0:T(8,128)S(1)}, f32[256,128]{1,0:T(8,128)S(1)}, u32[]{:S(2)}, u32[]{:S(2)}) collective-permute-start(f32[256,128]{1,0:T(8,128)S(1)} %get-tuple-element.65), channel_id=1, source_target_pairs={{0,16},{8,24},{16,0},{24,8},{1,17},{9,25},{17,1},{25,9},{2,18},{10... | collective-permute-start | bytes 393224 | tf_op jit(solution)/shard_map/ppermute | solution.py:22
  39.2 5.2 %collective-permute-start.11 = (f32[256,128]{1,0:T(8,128)S(1)}, f32[256,128]{1,0:T(8,128)S(1)}, u32[]{:S(2)}, u32[]{:S(2)}) collective-permute-start(f32[256,128]{1,0:T(8,128)S(1)} %get-tuple-element.66), channel_id=1, source_target_pairs={{0,24},{8,16},{16,8},{24,0},{1,25},{9,17},{17,9},{25,1},{2,26},{10... | collective-permute-start | bytes 393224 | tf_op jit(solution)/shard_map/ppermute | solution.py:22
  44.4 2.9 %collective-permute-done.11.refs_4_.refs_6_ = f32[256,128]{1,0:T(8,128)S(1)} collective-permute-done((f32[256,128]{1,0:T(8,128)S(1)}, f32[256,128]{1,0:T(8,128)S(1)}, u32[]{:S(2)}, u32[]{:S(2)}) %collective-permute-start.11) | collective-permute-done | bytes 131104 | tf_op jit(solution)/shard_map/ppermute | solution.py:22
  47.3 5.4 %collective-permute-done.13.refs_6_.refs_2_ = f32[4,256,128]{2,1,0:T(8,128)S(1)} collective-permute-done((f32[4,256,128]{2,1,0:T(8,128)S(1)}, f32[4,256,128]{2,1,0:T(8,128)S(1)}, u32[]{:S(2)}, u32[]{:S(2)}) %collective-permute-start.13) | collective-permute-done | bytes 524320 | tf_op jit(solution)/shard_map/ppermute | solution.py:22
  57.2 7.0 %partial_product.2 = (f32[256,512]{1,0:T(8,128)S(1)}, f32[256,512]{1,0:T(8,128)S(1)}, f32[256,512]{1,0:T(8,128)S(1)}, f32[256,512]{1,0:T(8,128)S(1)}) custom-call(s32[3]{0:T(128)S(1)} %pad_add_fusion.refs_0_, s32[4,4]{1,0:T(4,128)S(1)} %copy-done.8, s32[2,8]{1,0:T(2,128)S(1)} %copy-done.7, f32[1024,2048]{1,0:T(8,128)S(1)} %bitcast.4, ...), custom_call_target="tpu_custom_call" | custom-call | tf_op jit(solution)/shard_map/partial_product/pallas_call | solution.py:36
  64.2 2.3 %collective-permute-start.19 = (f32[256,512]{1,0:T(8,128)S(1)}, f32[256,512]{1,0:T(8,128)S(1)}, u32[]{:S(2)}, u32[]{:S(2)}) collective-permute-start(f32[256,512]{1,0:T(8,128)S(1)} %get-tuple-element.68), channel_id=1, source_target_pairs={{0,16},{16,24},{24,8},{8,0},{1,17},{17,25},{25,9},{9,1},{2,18},{18... | collective-permute-start | bytes 1572872 | tf_op jit(solution)/shard_map/ppermute | solution.py:443
  66.4 3.7 %collective-permute-start.21 = (f32[256,512]{1,0:T(8,128)S(1)}, f32[256,512]{1,0:T(8,128)S(1)}, u32[]{:S(2)}, u32[]{:S(2)}) collective-permute-start(f32[256,512]{1,0:T(8,128)S(1)} %get-tuple-element.69), channel_id=1, source_target_pairs={{0,8},{24,16},{1,9},{25,17},{2,10},{26,18},{3,11},{27,19},{4,12},{... | collective-permute-start | bytes 1572872 | tf_op jit(solution)/shard_map/ppermute | solution.py:442
  70.9 9.2 %collective-permute-done.16.refs_2_ = f32[4,256,128]{2,1,0:T(8,128)S(1)} collective-permute-done((f32[4,256,128]{2,1,0:T(8,128)S(1)}, f32[4,256,128]{2,1,0:T(8,128)S(1)}, u32[]{:S(2)}, u32[]{:S(2)}) %collective-permute-start.16) | collective-permute-done | bytes 524320 | tf_op jit(solution)/shard_map/ppermute | solution.py:22
  80.1 4.1 %collective-permute-done.21.refs_6_.refs_1_ = f32[256,512]{1,0:T(8,128)S(1)} collective-permute-done((f32[256,512]{1,0:T(8,128)S(1)}, f32[256,512]{1,0:T(8,128)S(1)}, u32[]{:S(2)}, u32[]{:S(2)}) %collective-permute-start.21) | collective-permute-done | bytes 524320 | tf_op jit(solution)/shard_map/ppermute | solution.py:442
  84.5 6.5 %collective-permute-start.27 = (f32[256,512]{1,0:T(8,128)S(1)}, f32[256,512]{1,0:T(8,128)S(1)}, u32[]{:S(2)}, u32[]{:S(2)}) collective-permute-start(f32[256,512]{1,0:T(8,128)S(1)} %add_up.7), channel_id=1, source_target_pairs={{8,24},{16,0},{0,8},{24,16},{9,25},{17,1},{1,9},{25,17},{10,26},{1... | collective-permute-start | bytes 1572872 | tf_op jit(solution)/shard_map/ppermute | solution.py:446
  90.9 5.7 %partial_product.3 = (f32[256,512]{1,0:T(8,128)S(1)}, f32[256,512]{1,0:T(8,128)S(1)}, f32[256,512]{1,0:T(8,128)S(1)}, f32[256,512]{1,0:T(8,128)S(1)}) custom-call(s32[3]{0:T(128)S(1)} %pad_add_fusion.refs_0_, s32[4,4]{1,0:T(4,128)S(1)} %copy-done.8, s32[2,8]{1,0:T(2,128)S(1)} %copy-done.7, f32[1024,2048]{1,0:T(8,128)S(1)} %bitcast.4, ...), custom_call_target="tpu_custom_call" | custom-call | tf_op jit(solution)/shard_map/partial_product/pallas_call | solution.py:36
  96.6 2.3 %collective-permute-start.23 = (f32[256,512]{1,0:T(8,128)S(1)}, f32[256,512]{1,0:T(8,128)S(1)}, u32[]{:S(2)}, u32[]{:S(2)}) collective-permute-start(f32[256,512]{1,0:T(8,128)S(1)} %get-tuple-element.71), channel_id=1, source_target_pairs={{0,16},{16,24},{24,8},{8,0},{1,17},{17,25},{25,9},{9,1},{2,18},{18... | collective-permute-start | bytes 1572872 | tf_op jit(solution)/shard_map/ppermute | solution.py:443
  101.3 1.9 %collective-permute-done.27.refs_5_ = f32[256,512]{1,0:T(8,128)S(1)} collective-permute-done((f32[256,512]{1,0:T(8,128)S(1)}, f32[256,512]{1,0:T(8,128)S(1)}, u32[]{:S(2)}, u32[]{:S(2)}) %collective-permute-start.27) | collective-permute-done | bytes 524320 | tf_op jit(solution)/shard_map/ppermute | solution.py:446
  103.2 11.3 %collective-permute-done.23.refs_9_.refs_3_ = f32[256,512]{1,0:T(8,128)S(1)} collective-permute-done((f32[256,512]{1,0:T(8,128)S(1)}, f32[256,512]{1,0:T(8,128)S(1)}, u32[]{:S(2)}, u32[]{:S(2)}) %collective-permute-start.23) | collective-permute-done | bytes 524320 | tf_op jit(solution)/shard_map/ppermute | solution.py:443
  114.5 10.8 %collective-permute-done.25.refs_1_.refs_11_ = f32[256,512]{1,0:T(8,128)S(1)} collective-permute-done((f32[256,512]{1,0:T(8,128)S(1)}, f32[256,512]{1,0:T(8,128)S(1)}, u32[]{:S(2)}, u32[]{:S(2)}) %collective-permute-start.25) | collective-permute-done | bytes 524320 | tf_op jit(solution)/shard_map/ppermute | solution.py:442
  125.3 3.6 %finish.2 = (f32[2,256,512]{2,1,0:T(8,128)}, f32[2,4,64,512]{3,2,1,0:T(8,128)S(1)}, f32[2,4,64,512]{3,2,1,0:T(8,128)S(1)}, f32[512,512]{1,0:T(8,128)S(1)}, f32[512,512]{1,0:T(8,128)S(1)}) custom-call(s32[3]{0:T(128)S(1)} %pad_add_fusion.refs_0_, s32[2,8]{1,0:T(2,128)S(1)} %copy-done.7, f32[256,512]{1,0:T(8,128)S(1)} %get-tuple-element.74.refs_2_, ...), custom_call_target="tpu_custom_call" | custom-call | tf_op jit(solution)/shard_map/finish/pallas_call | solution.py:36
  128.9 2.5 %collective-permute-start.26 = (f32[256,512]{1,0:T(8,128)S(1)}, f32[256,512]{1,0:T(8,128)S(1)}, u32[]{:S(2)}, u32[]{:S(2)}) collective-permute-start(f32[256,512]{1,0:T(8,128)S(1)} %add_up.6), channel_id=1, source_target_pairs={{8,24},{16,0},{0,8},{24,16},{9,25},{17,1},{1,9},{25,17},{10,26},{1... | collective-permute-start | bytes 1572872 | tf_op jit(solution)/shard_map/ppermute | solution.py:446
  131.5 2.3 %rest.1 = (f32[512,512]{1,0:T(8,128)S(1)}, f32[256,512]{1,0:T(8,128)S(1)}) custom-call(f32[1,512,512]{2,1,0:T(8,128)S(1)} %copy-done.4, f32[512,512]{1,0:T(8,128)S(1)} %get-tuple-element.76.refs_1_, f32[512,512]{1,0:T(8,128)S(1)} %get-tuple-element.77.refs_2_, f32[2,256,512]{2,1,0:T(8,128)S(1)} %copy-done.5), custom_call_target="tpu_custom_call" | custom-call | tf_op jit(solution)/shard_map/rest/pallas_call | solution.py:36
  135.4 2.6 %collective-permute-start.31 = (f32[2,64,512]{2,1,0:T(8,128)S(1)}, f32[2,64,512]{2,1,0:T(8,128)S(1)}, u32[]{:S(2)}, u32[]{:S(2)}) collective-permute-start(f32[2,64,512]{2,1,0:T(8,128)S(1)} %get-tuple-element.86), channel_id=1, source_target_pairs={{0,6},{1,7},{2,4},{3,5},{4,2},{5,3},{6,0},{7,1},{8,14},{9,15},{10,... | collective-permute-start | bytes 786440 | tf_op jit(solution)/shard_map/ppermute | solution.py:22
  138.0 5.7 %collective-permute-done.29.refs_2_ = f32[2,64,512]{2,1,0:T(8,128)S(1)} collective-permute-done((f32[2,64,512]{2,1,0:T(8,128)S(1)}, f32[2,64,512]{2,1,0:T(8,128)S(1)}, u32[]{:S(2)}, u32[]{:S(2)}) %collective-permute-start.29) | collective-permute-done | bytes 262176 | tf_op jit(solution)/shard_map/ppermute | solution.py:22
  143.6 5.1 %collective-permute-done.30.refs_3_ = f32[2,64,512]{2,1,0:T(8,128)S(1)} collective-permute-done((f32[2,64,512]{2,1,0:T(8,128)S(1)}, f32[2,64,512]{2,1,0:T(8,128)S(1)}, u32[]{:S(2)}, u32[]{:S(2)}) %collective-permute-start.30) | collective-permute-done | bytes 262176 | tf_op jit(solution)/shard_map/ppermute | solution.py:22
  149.4 2.9 %finish.3 = (f32[2,256,512]{2,1,0:T(8,128)}, f32[1,4,64,512]{3,2,1,0:T(8,128)S(1)}, f32[1,4,64,512]{3,2,1,0:T(8,128)S(1)}) custom-call(s32[3]{0:T(128)S(1)} %pad_add_fusion.refs_0_, s32[2,8]{1,0:T(2,128)S(1)} %copy-done.7, f32[256,512]{1,0:T(8,128)S(1)} %get-tuple-element.70.refs_2_, ...), custom_call_target="tpu_custom_call", output_to_operand_aliasing={{0}: (9, {})} | custom-call | tf_op jit(solution)/shard_map/finish/pallas_call | solution.py:36
  156.2 2.1 %collective-permute-start.38 = (f32[1,64,512]{2,1,0:T(8,128)S(1)}, f32[1,64,512]{2,1,0:T(8,128)S(1)}, u32[]{:S(2)}, u32[]{:S(2)}) collective-permute-start(f32[1,64,512]{2,1,0:T(8,128)S(1)} %get-tuple-element.96), channel_id=1, source_target_pairs={{0,6},{1,7},{2,4},{3,5},{4,2},{5,3},{6,0},{7,1},{8,14},{9,15},{10,... | collective-permute-start | bytes 393224 | tf_op jit(solution)/shard_map/ppermute | solution.py:22
  161.5 2.4 %collective-permute-done.38.refs_3_ = f32[1,64,512]{2,1,0:T(8,128)S(1)} collective-permute-done((f32[1,64,512]{2,1,0:T(8,128)S(1)}, f32[1,64,512]{2,1,0:T(8,128)S(1)}, u32[]{:S(2)}, u32[]{:S(2)}) %collective-permute-start.38) | collective-permute-done | bytes 131104 | tf_op jit(solution)/shard_map/ppermute | solution.py:22
  164.7 2.5 %collective-permute-done.33.refs_1_ = f32[64,512]{1,0:T(8,128)S(1)} collective-permute-done((f32[64,512]{1,0:T(8,128)S(1)}, f32[64,512]{1,0:T(8,128)S(1)}, u32[]{:S(2)}, u32[]{:S(2)}) %collective-permute-start.33) | collective-permute-done | bytes 131104 | tf_op jit(solution)/shard_map/ppermute | solution.py:22
  167.3 3.1 %collective-permute-done.39.refs_1_ = f32[1,64,512]{2,1,0:T(8,128)S(1)} collective-permute-done((f32[1,64,512]{2,1,0:T(8,128)S(1)}, f32[1,64,512]{2,1,0:T(8,128)S(1)}, u32[]{:S(2)}, u32[]{:S(2)}) %collective-permute-start.39) | collective-permute-done | bytes 131104 | tf_op jit(solution)/shard_map/ppermute | solution.py:22
  172.7 5.1 %collective-permute-done.40.refs_6_ = f32[1,64,512]{2,1,0:T(8,128)S(1)} collective-permute-done((f32[1,64,512]{2,1,0:T(8,128)S(1)}, f32[1,64,512]{2,1,0:T(8,128)S(1)}, u32[]{:S(2)}, u32[]{:S(2)}) %collective-permute-start.40) | collective-permute-done | bytes 131104 | tf_op jit(solution)/shard_map/ppermute | solution.py:22
  (98 shorter events, 42.4 us)
Async XLA Ops:
  2.6 6.9 %collective-permute-start = (f32[256,128]{1,0:T(8,128)S(1)}, f32[256,128]{1,0:T(8,128)S(1)}, u32[]{:S(2)}, u32[]{:S(2)}) collective-permute-start(f32[256,128]{1,0:T(8,128)S(1)} %get-tuple-element.52), channel_id=1, source_target_pairs={{0,2},{1,3},{2,0},{3,1},{4,6},{5,7},{6,4},{7,5},{8,10},{9,11},{10,... | collective-permute-start | bytes 393224 | tf_op jit(solution)/shard_map/ppermute | solution.py:22
  5.6 7.8 %collective-permute-start.1 = (f32[256,128]{1,0:T(8,128)S(1)}, f32[256,128]{1,0:T(8,128)S(1)}, u32[]{:S(2)}, u32[]{:S(2)}) collective-permute-start(f32[256,128]{1,0:T(8,128)S(1)} %get-tuple-element.53), channel_id=1, source_target_pairs={{0,4},{1,5},{2,6},{3,7},{4,0},{5,1},{6,2},{7,3},{8,12},{9,13},{10,... | collective-permute-start | bytes 393224 | tf_op jit(solution)/shard_map/ppermute | solution.py:22
  14.0 8.4 %collective-permute-start.6 = (f32[256,128]{1,0:T(8,128)S(1)}, f32[256,128]{1,0:T(8,128)S(1)}, u32[]{:S(2)}, u32[]{:S(2)}) collective-permute-start(f32[256,128]{1,0:T(8,128)S(1)} %get-tuple-element.60), channel_id=1, source_target_pairs={{0,8},{8,0},{16,24},{24,16},{1,9},{9,1},{17,25},{25,17},{2,10},{10... | collective-permute-start | bytes 393224 | tf_op jit(solution)/shard_map/ppermute | solution.py:22
  15.6 13.5 %collective-permute-start.7 = (f32[256,128]{1,0:T(8,128)S(1)}, f32[256,128]{1,0:T(8,128)S(1)}, u32[]{:S(2)}, u32[]{:S(2)}) collective-permute-start(f32[256,128]{1,0:T(8,128)S(1)} %get-tuple-element.61), channel_id=1, source_target_pairs={{0,16},{8,24},{16,0},{24,8},{1,17},{9,25},{17,1},{25,9},{2,18},{10... | collective-permute-start | bytes 393224 | tf_op jit(solution)/shard_map/ppermute | solution.py:22
  18.2 11.0 %collective-permute-start.8 = (f32[256,128]{1,0:T(8,128)S(1)}, f32[256,128]{1,0:T(8,128)S(1)}, u32[]{:S(2)}, u32[]{:S(2)}) collective-permute-start(f32[256,128]{1,0:T(8,128)S(1)} %get-tuple-element.62), channel_id=1, source_target_pairs={{0,24},{8,16},{16,8},{24,0},{1,25},{9,17},{17,9},{25,1},{2,26},{10... | collective-permute-start | bytes 393224 | tf_op jit(solution)/shard_map/ppermute | solution.py:22
  20.3 8.9 %collective-permute-start.3 = (f32[256,128]{1,0:T(8,128)S(1)}, f32[256,128]{1,0:T(8,128)S(1)}, u32[]{:S(2)}, u32[]{:S(2)}) collective-permute-start(f32[256,128]{1,0:T(8,128)S(1)} %get-tuple-element.57), channel_id=1, source_target_pairs={{0,2},{1,3},{2,0},{3,1},{4,6},{5,7},{6,4},{7,5},{8,10},{9,11},{10,... | collective-permute-start | bytes 393224 | tf_op jit(solution)/shard_map/ppermute | solution.py:22
  21.5 7.6 %collective-permute-start.4 = (f32[256,128]{1,0:T(8,128)S(1)}, f32[256,128]{1,0:T(8,128)S(1)}, u32[]{:S(2)}, u32[]{:S(2)}) collective-permute-start(f32[256,128]{1,0:T(8,128)S(1)} %get-tuple-element.58), channel_id=1, source_target_pairs={{0,4},{1,5},{2,6},{3,7},{4,0},{5,1},{6,2},{7,3},{8,12},{9,13},{10,... | collective-permute-start | bytes 393224 | tf_op jit(solution)/shard_map/ppermute | solution.py:22
  22.4 6.8 %collective-permute-start.5 = (f32[256,128]{1,0:T(8,128)S(1)}, f32[256,128]{1,0:T(8,128)S(1)}, u32[]{:S(2)}, u32[]{:S(2)}) collective-permute-start(f32[256,128]{1,0:T(8,128)S(1)} %get-tuple-element.59), channel_id=1, source_target_pairs={{0,6},{1,7},{2,4},{3,5},{4,2},{5,3},{6,0},{7,1},{8,14},{9,15},{10,... | collective-permute-start | bytes 393224 | tf_op jit(solution)/shard_map/ppermute | solution.py:22
  29.8 17.6 %collective-permute-start.14 = (f32[4,256,128]{2,1,0:T(8,128)S(1)}, f32[4,256,128]{2,1,0:T(8,128)S(1)}, u32[]{:S(2)}, u32[]{:S(2)}) collective-permute-start(f32[4,256,128]{2,1,0:T(8,128)S(1)} %arrange.2.refs_0_), channel_id=1, source_target_pairs={{0,6},{1,7},{2,4},{3,5},{4,2},{5,3},{6,0},{7,1},{8,14},{9,15},{10,... | collective-permute-start | bytes 1572872 | tf_op jit(solution)/shard_map/ppermute | solution.py:22
  31.3 21.4 %collective-permute-start.13 = (f32[4,256,128]{2,1,0:T(8,128)S(1)}, f32[4,256,128]{2,1,0:T(8,128)S(1)}, u32[]{:S(2)}, u32[]{:S(2)}) collective-permute-start(f32[4,256,128]{2,1,0:T(8,128)S(1)} %arrange.2.refs_0_), channel_id=1, source_target_pairs={{0,4},{1,5},{2,6},{3,7},{4,0},{5,1},{6,2},{7,3},{8,12},{9,13},{10,... | collective-permute-start | bytes 1572872 | tf_op jit(solution)/shard_map/ppermute | solution.py:22
  32.5 20.2 %collective-permute-start.12 = (f32[4,256,128]{2,1,0:T(8,128)S(1)}, f32[4,256,128]{2,1,0:T(8,128)S(1)}, u32[]{:S(2)}, u32[]{:S(2)}) collective-permute-start(f32[4,256,128]{2,1,0:T(8,128)S(1)} %arrange.2.refs_0_), channel_id=1, source_target_pairs={{0,2},{1,3},{2,0},{3,1},{4,6},{5,7},{6,4},{7,5},{8,10},{9,11},{10,... | collective-permute-start | bytes 1572872 | tf_op jit(solution)/shard_map/ppermute | solution.py:22
  34.7 9.7 %collective-permute-start.10 = (f32[256,128]{1,0:T(8,128)S(1)}, f32[256,128]{1,0:T(8,128)S(1)}, u32[]{:S(2)}, u32[]{:S(2)}) collective-permute-start(f32[256,128]{1,0:T(8,128)S(1)} %get-tuple-element.65), channel_id=1, source_target_pairs={{0,16},{8,24},{16,0},{24,8},{1,17},{9,25},{17,1},{25,9},{2,18},{10... | collective-permute-start | bytes 393224 | tf_op jit(solution)/shard_map/ppermute | solution.py:22
  39.2 8.1 %collective-permute-start.11 = (f32[256,128]{1,0:T(8,128)S(1)}, f32[256,128]{1,0:T(8,128)S(1)}, u32[]{:S(2)}, u32[]{:S(2)}) collective-permute-start(f32[256,128]{1,0:T(8,128)S(1)} %get-tuple-element.66), channel_id=1, source_target_pairs={{0,24},{8,16},{16,8},{24,0},{1,25},{9,17},{17,9},{25,1},{2,26},{10... | collective-permute-start | bytes 393224 | tf_op jit(solution)/shard_map/ppermute | solution.py:22
  53.6 16.6 %collective-permute-start.17 = (f32[4,256,128]{2,1,0:T(8,128)S(1)}, f32[4,256,128]{2,1,0:T(8,128)S(1)}, u32[]{:S(2)}, u32[]{:S(2)}) collective-permute-start(f32[4,256,128]{2,1,0:T(8,128)S(1)} %arrange.3.refs_0_), channel_id=1, source_target_pairs={{0,6},{1,7},{2,4},{3,5},{4,2},{5,3},{6,0},{7,1},{8,14},{9,15},{10,... | collective-permute-start | bytes 1572872 | tf_op jit(solution)/shard_map/ppermute | solution.py:22
  55.3 24.8 %collective-permute-start.16 = (f32[4,256,128]{2,1,0:T(8,128)S(1)}, f32[4,256,128]{2,1,0:T(8,128)S(1)}, u32[]{:S(2)}, u32[]{:S(2)}) collective-permute-start(f32[4,256,128]{2,1,0:T(8,128)S(1)} %arrange.3.refs_0_), channel_id=1, source_target_pairs={{0,4},{1,5},{2,6},{3,7},{4,0},{5,1},{6,2},{7,3},{8,12},{9,13},{10,... | collective-permute-start | bytes 1572872 | tf_op jit(solution)/shard_map/ppermute | solution.py:22
  56.3 23.8 %collective-permute-start.15 = (f32[4,256,128]{2,1,0:T(8,128)S(1)}, f32[4,256,128]{2,1,0:T(8,128)S(1)}, u32[]{:S(2)}, u32[]{:S(2)}) collective-permute-start(f32[4,256,128]{2,1,0:T(8,128)S(1)} %arrange.3.refs_0_), channel_id=1, source_target_pairs={{0,2},{1,3},{2,0},{3,1},{4,6},{5,7},{6,4},{7,5},{8,10},{9,11},{10,... | collective-permute-start | bytes 1572872 | tf_op jit(solution)/shard_map/ppermute | solution.py:22
  64.2 15.9 %collective-permute-start.19 = (f32[256,512]{1,0:T(8,128)S(1)}, f32[256,512]{1,0:T(8,128)S(1)}, u32[]{:S(2)}, u32[]{:S(2)}) collective-permute-start(f32[256,512]{1,0:T(8,128)S(1)} %get-tuple-element.68), channel_id=1, source_target_pairs={{0,16},{16,24},{24,8},{8,0},{1,17},{17,25},{25,9},{9,1},{2,18},{18... | collective-permute-start | bytes 1572872 | tf_op jit(solution)/shard_map/ppermute | solution.py:443
  66.4 17.7 %collective-permute-start.21 = (f32[256,512]{1,0:T(8,128)S(1)}, f32[256,512]{1,0:T(8,128)S(1)}, u32[]{:S(2)}, u32[]{:S(2)}) collective-permute-start(f32[256,512]{1,0:T(8,128)S(1)} %get-tuple-element.69), channel_id=1, source_target_pairs={{0,8},{24,16},{1,9},{25,17},{2,10},{26,18},{3,11},{27,19},{4,12},{... | collective-permute-start | bytes 1572872 | tf_op jit(solution)/shard_map/ppermute | solution.py:442
  70.2 14.0 %collective-permute-start.20 = (f32[256,512]{1,0:T(8,128)S(1)}, f32[256,512]{1,0:T(8,128)S(1)}, u32[]{:S(2)}, u32[]{:S(2)}) collective-permute-start(f32[256,512]{1,0:T(8,128)S(1)} %get-tuple-element.69), channel_id=1, source_target_pairs={{8,16},{16,8},{9,17},{17,9},{10,18},{18,10},{11,19},{19,11},{12,20... | collective-permute-start | bytes 1572872 | tf_op jit(solution)/shard_map/ppermute | solution.py:444
  84.3 6.6 %collective-permute-start.22 = (f32[4,4,256,128]{3,2,1,0:T(8,128)S(1)}, f32[4,4,256,128]{3,2,1,0:T(8,128)S(1)}, u32[]{:S(2)}, u32[]{:S(2)}) collective-permute-start(f32[4,4,256,128]{3,2,1,0:T(8,128)S(1)} %pack.3.refs_4_), channel_id=1, source_target_pairs={{0,1},{1,0},{2,3},{3,2},{4,5},{5,4},{6,7},{7,6},{8,9},{9,8},{10,11... | collective-permute-start | bytes 6291464 | tf_op jit(solution)/shard_map/ppermute | solution.py:22
  84.5 18.7 %collective-permute-start.27 = (f32[256,512]{1,0:T(8,128)S(1)}, f32[256,512]{1,0:T(8,128)S(1)}, u32[]{:S(2)}, u32[]{:S(2)}) collective-permute-start(f32[256,512]{1,0:T(8,128)S(1)} %add_up.7), channel_id=1, source_target_pairs={{8,24},{16,0},{0,8},{24,16},{9,25},{17,1},{1,9},{25,17},{10,26},{1... | collective-permute-start | bytes 1572872 | tf_op jit(solution)/shard_map/ppermute | solution.py:446
  96.6 17.8 %collective-permute-start.23 = (f32[256,512]{1,0:T(8,128)S(1)}, f32[256,512]{1,0:T(8,128)S(1)}, u32[]{:S(2)}, u32[]{:S(2)}) collective-permute-start(f32[256,512]{1,0:T(8,128)S(1)} %get-tuple-element.71), channel_id=1, source_target_pairs={{0,16},{16,24},{24,8},{8,0},{1,17},{17,25},{25,9},{9,1},{2,18},{18... | collective-permute-start | bytes 1572872 | tf_op jit(solution)/shard_map/ppermute | solution.py:443
  98.9 26.4 %collective-permute-start.25 = (f32[256,512]{1,0:T(8,128)S(1)}, f32[256,512]{1,0:T(8,128)S(1)}, u32[]{:S(2)}, u32[]{:S(2)}) collective-permute-start(f32[256,512]{1,0:T(8,128)S(1)} %get-tuple-element.72), channel_id=1, source_target_pairs={{0,8},{24,16},{1,9},{25,17},{2,10},{26,18},{3,11},{27,19},{4,12},{... | collective-permute-start | bytes 1572872 | tf_op jit(solution)/shard_map/ppermute | solution.py:442
  100.6 24.7 %collective-permute-start.24 = (f32[256,512]{1,0:T(8,128)S(1)}, f32[256,512]{1,0:T(8,128)S(1)}, u32[]{:S(2)}, u32[]{:S(2)}) collective-permute-start(f32[256,512]{1,0:T(8,128)S(1)} %get-tuple-element.72), channel_id=1, source_target_pairs={{8,16},{16,8},{9,17},{17,9},{10,18},{18,10},{11,19},{19,11},{12,20... | collective-permute-start | bytes 1572872 | tf_op jit(solution)/shard_map/ppermute | solution.py:444
  128.9 20.5 %collective-permute-start.26 = (f32[256,512]{1,0:T(8,128)S(1)}, f32[256,512]{1,0:T(8,128)S(1)}, u32[]{:S(2)}, u32[]{:S(2)}) collective-permute-start(f32[256,512]{1,0:T(8,128)S(1)} %add_up.6), channel_id=1, source_target_pairs={{8,24},{16,0},{0,8},{24,16},{9,25},{17,1},{1,9},{25,17},{10,26},{1... | collective-permute-start | bytes 1572872 | tf_op jit(solution)/shard_map/ppermute | solution.py:446
  134.4 9.2 %collective-permute-start.29 = (f32[2,64,512]{2,1,0:T(8,128)S(1)}, f32[2,64,512]{2,1,0:T(8,128)S(1)}, u32[]{:S(2)}, u32[]{:S(2)}) collective-permute-start(f32[2,64,512]{2,1,0:T(8,128)S(1)} %get-tuple-element.84), channel_id=1, source_target_pairs={{0,2},{1,3},{2,0},{3,1},{4,6},{5,7},{6,4},{7,5},{8,10},{9,11},{10,... | collective-permute-start | bytes 786440 | tf_op jit(solution)/shard_map/ppermute | solution.py:22
  135.4 13.3 %collective-permute-start.30 = (f32[2,64,512]{2,1,0:T(8,128)S(1)}, f32[2,64,512]{2,1,0:T(8,128)S(1)}, u32[]{:S(2)}, u32[]{:S(2)}) collective-permute-start(f32[2,64,512]{2,1,0:T(8,128)S(1)} %get-tuple-element.85), channel_id=1, source_target_pairs={{0,4},{1,5},{2,6},{3,7},{4,0},{5,1},{6,2},{7,3},{8,12},{9,13},{10,... | collective-permute-start | bytes 786440 | tf_op jit(solution)/shard_map/ppermute | solution.py:22
  135.4 13.3 %collective-permute-start.31 = (f32[2,64,512]{2,1,0:T(8,128)S(1)}, f32[2,64,512]{2,1,0:T(8,128)S(1)}, u32[]{:S(2)}, u32[]{:S(2)}) collective-permute-start(f32[2,64,512]{2,1,0:T(8,128)S(1)} %get-tuple-element.86), channel_id=1, source_target_pairs={{0,6},{1,7},{2,4},{3,5},{4,2},{5,3},{6,0},{7,1},{8,14},{9,15},{10,... | collective-permute-start | bytes 786440 | tf_op jit(solution)/shard_map/ppermute | solution.py:22
  156.2 7.7 %collective-permute-start.38 = (f32[1,64,512]{2,1,0:T(8,128)S(1)}, f32[1,64,512]{2,1,0:T(8,128)S(1)}, u32[]{:S(2)}, u32[]{:S(2)}) collective-permute-start(f32[1,64,512]{2,1,0:T(8,128)S(1)} %get-tuple-element.96), channel_id=1, source_target_pairs={{0,6},{1,7},{2,4},{3,5},{4,2},{5,3},{6,0},{7,1},{8,14},{9,15},{10,... | collective-permute-start | bytes 393224 | tf_op jit(solution)/shard_map/ppermute | solution.py:22
  158.4 8.8 %collective-permute-start.33 = (f32[64,512]{1,0:T(8,128)S(1)}, f32[64,512]{1,0:T(8,128)S(1)}, u32[]{:S(2)}, u32[]{:S(2)}) collective-permute-start(f32[64,512]{1,0:T(8,128)S(1)} %add_up.8.refs_0_), channel_id=1, source_target_pairs={{0,16},{8,24},{16,0},{24,8},{1,17},{9,25},{17,1},{25,9},{2,18},{10... | collective-permute-start | bytes 393224 | tf_op jit(solution)/shard_map/ppermute | solution.py:22
  163.9 6.5 %collective-permute-start.39 = (f32[1,64,512]{2,1,0:T(8,128)S(1)}, f32[1,64,512]{2,1,0:T(8,128)S(1)}, u32[]{:S(2)}, u32[]{:S(2)}) collective-permute-start(f32[1,64,512]{2,1,0:T(8,128)S(1)} %add_up.10.refs_0_), channel_id=1, source_target_pairs={{0,8},{8,0},{16,24},{24,16},{1,9},{9,1},{17,25},{25,17},{2,10},{10... | collective-permute-start | bytes 393224 | tf_op jit(solution)/shard_map/ppermute | solution.py:22
  170.5 7.4 %collective-permute-start.40 = (f32[1,64,512]{2,1,0:T(8,128)S(1)}, f32[1,64,512]{2,1,0:T(8,128)S(1)}, u32[]{:S(2)}, u32[]{:S(2)}) collective-permute-start(f32[1,64,512]{2,1,0:T(8,128)S(1)} %add_up.11.refs_5_), channel_id=1, source_target_pairs={{0,16},{8,24},{16,0},{24,8},{1,17},{9,25},{17,1},{25,9},{2,18},{10... | collective-permute-start | bytes 393224 | tf_op jit(solution)/shard_map/ppermute | solution.py:22
  (20 other events, 223.5 us)

commit v11 on v10

--- a/solution.py
+++ b/solution.py
@@ -130,7 +130,7 @@
     return found
 
 
-def partial_kernel(sides, ratio, count, number, place, slots, ancestors, tile_ref, *refs):
+def partial_kernel(sides, ratio, count, number, start, place, slots, ancestors, tile_ref, *refs):
     piece_refs, out_refs, right_ref = refs[:sides], refs[sides:-1], refs[-1]
     chunk_rows, columns = out_refs[0].shape
     blocks = tile_ref.shape[1] // columns
@@ -161,7 +161,7 @@
 
     def multiply(out_ref):
         out_ref[...] = jnp.zeros_like(out_ref)
-        chunk = place[0] * count + slots[place[1], step]
+        chunk = place[0] * count + slots[place[1], start + step]
 
         @pl.when(listed(chunk * chunk_rows // columns))
         def _chunk():
@@ -183,20 +183,22 @@
         pl.when(step == index)(functools.partial(multiply, out_ref))
 
 
-def partial_product(place, slots, ancestors, tiles, pieces, ratio, columns, number, waits):
+def partial_product(
+    place, slots, ancestors, tiles, pieces, ratio, columns, number, start, stop, waits
+):
     rows, cols = tiles.shape
     count = slots.shape[0]
     out = jax.ShapeDtypeStruct((rows // count, columns), jnp.float32)
-    tile = pl.BlockSpec((rows // count, cols), lambda i, p, s, a: (s[p[1], i], 0))
+    tile = pl.BlockSpec((rows // count, cols), lambda i, p, s, a: (s[p[1], start + i], 0))
     return run(
-        functools.partial(partial_kernel, len(pieces), ratio, count, number),
+        functools.partial(partial_kernel, len(pieces), ratio, count, number, start),
         [place, slots, ancestors],
         [tiles] + pieces,
         [tile] + [whole(piece) for piece in pieces],
         waits,
-        [out] * count,
-        [whole(out)] * count,
-        grid=(count,),
+        [out] * (stop - start),
+        [whole(out)] * (stop - start),
+        grid=(stop - start,),
         scratch=[pltpu.VMEM((cols // columns, 3 * columns, columns), jnp.bfloat16)],
         name="partial_product",
     )
@@ -321,14 +323,13 @@
         out_ref[...] = keep_ref[:, chip ^ o] + received_ref[:, chip ^ o]
 
 
-def fold(place, keep, received, waits):
+def fold(place, keep, received):
     number, chips, rows, columns = keep.shape
     out = jax.ShapeDtypeStruct((number, rows, columns), jnp.float32)
     specs = [whole(keep)] * 2
     outs = [out] * chips
     return run(
-        fold_kernel, [place], [keep, received], specs, waits, outs, [whole(out)] * chips,
-        name="fold",
+        fold_kernel, [place], [keep, received], specs, [], outs, [whole(out)] * chips, name="fold"
     )
 
 
@@ -342,11 +343,12 @@
         out_ref[...] = total
 
 
-def fold_pair(place, pieces):
+def fold_pair(place, pieces, waits):
     out = jax.ShapeDtypeStruct(pieces[0].shape[1:], jnp.float32)
     specs = [whole(piece) for piece in pieces]
     return run(
-        fold_pair_kernel, [place], pieces, specs, [], [out] * 2, [whole(out)] * 2, name="fold_pair"
+        fold_pair_kernel, [place], pieces, specs, waits, [out] * 2, [whole(out)] * 2,
+        name="fold_pair",
     )
 
 
@@ -470,8 +472,8 @@
     return [mine, none if up is None else up, none if down is None else down, none, mine]
 
 
-def sum_plane(place, keep, send, waits):
-    pieces = fold(place, keep, flip(send, "pcol", 1), waits)
+def sum_plane(place, keep, send):
+    pieces = fold(place, keep, flip(send, "pcol", 1))
     return [pieces[0]] + [flip(pieces[o], "pcol", 2 * o) for o in range(1, len(pieces))]
 
 
@@ -487,8 +489,8 @@
             return pieces
 
 
-def sum_pair_near(place, pieces):
-    kept, other = fold_pair(place, pieces)
+def sum_pair_near(place, pieces, waits):
+    kept, other = fold_pair(place, pieces, waits)
     return [kept, flip(other, "prow", 1)]
 
 
@@ -525,8 +527,9 @@
             turned.append(turn(place, sent[number], waits))
             waits = [turned[0][0]]
             received.append(to_plane(turned[number]))
-    bases = bases_of(place, diag_inverse, link_factor, columns // pcol_count, [piece[0] for piece in turned[:1]])
-    rows, gathered = [], [bases[0]]
+    waits = [pieces[0] for pieces in received[:1]]
+    bases = bases_of(place, diag_inverse, link_factor, columns // pcol_count, waits)
+    rows, gathered = [], []
     for number in range(nsuper):
         if received:
             gathered += [piece for later in sent[number + 1 : number + 2] for piece in later[1:]]
@@ -534,16 +537,21 @@
             found = gather_plane(own, pcol_count)
             gathered = found[1:]
             waits = [piece for later in received[number + 1 : number + 2] for piece in later[1:]]
-            packed = pack(found, waits + (rows[-1][1:4] if rows else []))
+            packed = pack(found, waits + (rows[-1][1:4] + late if rows else [bases[0]]))
             pieces = [packed, flip(packed, "pcol", 1)]
         else:
             own = to_plane_whole(factor[number], count, ratio)
             pieces = [in_rows(lax.all_gather(own, "pcol", axis=0), count, ratio)]
-        partial = partial_product(
-            place, slots, ancestors, inverse_tiles, pieces, ratio, columns, number, [bases[0]]
-        )
-        *early, last_row, near = sum_over_line(partial, z)
-        rows.append([*early, near, last_row])
+        middle = count // 2 if number == 0 and received else count
+        partial, starts = [], [0, middle, count] if middle < count else [0, count]
+        for start, stop in zip(starts, starts[1:]):
+            partial += partial_product(
+                place, slots, ancestors, inverse_tiles, pieces, ratio, columns, number, start, stop,
+                [bases[0]],
+            )
+        rows.append(sum_over_line(partial, z))
+        rows[-1] = rows[-1][:3] + rows[-1][:2:-1]
+        late = [partial[-1]]
 
     sums, before, pending = [], [], []
     for number in range(nsuper):
@@ -555,13 +563,11 @@
         )
         if pending:
             sums += sum_pair_far(pending, count, [keep])
-        waits = []
+        group = sum_plane(place, keep, send)
         if not last:
             rest = rest_of(link_factor, *link, offdiag, number)
             before = [*rest, offdiag]
-            waits = [rest[0]]
-        group = sum_plane(place, keep, send, waits)
-        pending = [] if last else sum_pair_near(place, group)
+            pending = sum_pair_near(place, group, rest[:1])
     sums += sum_planes(group, count)
     return (offdiag, *outputs(place, bases, sums))
 

time: 180 us -> 176 us (0.978)
  waiting for transfers between devices: 80.8 us -> 71 us
  starting transfers between devices: 60.8 us -> 64.5 us
  Pallas kernels: 31.2 us -> 34 us
    ppermute x33, waiting for transfers between devices: 52.8 us -> 46.4 us  [flip(): lax.ppermute(value, axis, [(i, i ^ bit) for i in range(lax.axis_size(axis...]
    ppermute x33, starting transfers between devices: 40.5 us -> 45.8 us  [flip(): lax.ppermute(value, axis, [(i, i ^ bit) for i in range(lax.axis_size(axis...]
    ppermute x2, waiting for transfers between devices: 11.3 us -> 7.81 us  [sum_over_four(): total = lax.ppermute(slots[1], 'prow', [(0, 2), (2, 3), (3, 1), (1, 0)])]
    ppermute x2, starting transfers between devices: 9.01 us -> 5.96 us  [sum_over_four(): last = lax.ppermute(both, 'prow', [(1, 3), (2, 0), (0, 1), (3, 2)])]
    pallas_call x24 -> x25, Pallas kernels: 31.2 us -> 34 us  [run(): pl.pallas_call(body, grid_spec=pltpu.PrefetchScalarGridSpec(num_scalar_pr...]
    ppermute x2, waiting for transfers between devices: 14.9 us -> 16.8 us  [sum_over_four(): near = lax.ppermute(slots[0], 'prow', [(0, 1), (3, 2)])]
    ppermute x2, waiting for transfers between devices: 1.85 us -> 0.01 us  [sum_over_four(): last = lax.ppermute(both, 'prow', [(1, 3), (2, 0), (0, 1), (3, 2)])]
    ppermute x2, starting transfers between devices: 5.4 us -> 7.24 us  [sum_over_four(): near = lax.ppermute(slots[0], 'prow', [(0, 1), (3, 2)])]
  transfers between devices with their start and end apart: 41 -> 41, of which waited for: 20 -> 22; matrix products, arithmetic and copies ran while one was open for 0% -> 0% of each run, Pallas kernels for 12% -> 14%
where the time goes in v11:
time: 176 us
  waiting for transfers between devices  71 us (40%)
  starting transfers between devices  64.5 us (37%)
  Pallas kernels  34 us (19%)
  local copies, waits for them, and re-layouts  5.3 us (3%)
    ppermute x33, waiting for transfers between devices, flip(): lax.ppermute(value, axis, [(i, i ^ bit) for i in range(lax.axis_size(axis...  46.4 us
    ppermute x33, starting transfers between devices, flip(): lax.ppermute(value, axis, [(i, i ^ bit) for i in range(lax.axis_size(axis...  45.8 us
    pallas_call x25, Pallas kernels, run(): pl.pallas_call(body, grid_spec=pltpu.PrefetchScalarGridSpec(num_scalar_pr...  34 us
    ppermute x2, waiting for transfers between devices, sum_over_four(): near = lax.ppermute(slots[0], 'prow', [(0, 1), (3, 2)])  16.8 us
    ppermute x2, waiting for transfers between devices, sum_over_four(): total = lax.ppermute(slots[1], 'prow', [(0, 2), (2, 3), (3, 1), (1, 0)])  7.81 us
    ppermute x2, starting transfers between devices, sum_over_four(): near = lax.ppermute(slots[0], 'prow', [(0, 1), (3, 2)])  7.24 us
    ppermute x2, starting transfers between devices, sum_over_four(): last = lax.ppermute(both, 'prow', [(1, 3), (2, 0), (0, 1), (3, 2)])  5.96 us
    unnamed x22, local copies, waits for them, and re-layouts  5.3 us
  transfers between devices with their start and end apart: 41, of which 22 were waited for; matrix products, arithmetic and copies ran while one was open for 0% of the time, Pallas kernels for 14%

profile of v11, /device:TPU:0, one launch (start us, length us, event | category | flops | bytes accessed | tf_op | source)
XLA Modules:
  0.0 175.9 jit_solution(12994876461004267299)
XLA Ops:
  2.6 3.0 %collective-permute-start = (f32[256,128]{1,0:T(8,128)S(1)}, f32[256,128]{1,0:T(8,128)S(1)}, u32[]{:S(2)}, u32[]{:S(2)}) collective-permute-start(f32[256,128]{1,0:T(8,128)S(1)} %get-tuple-element.52), channel_id=1, source_target_pairs={{0,2},{1,3},{2,0},{3,1},{4,6},{5,7},{6,4},{7,5},{8,10},{9,11},{10,... | collective-permute-start | bytes 393224 | tf_op jit(solution)/shard_map/ppermute | solution.py:22
  7.1 2.4 %collective-permute-done.refs_2_ = f32[256,128]{1,0:T(8,128)S(1)} collective-permute-done((f32[256,128]{1,0:T(8,128)S(1)}, f32[256,128]{1,0:T(8,128)S(1)}, u32[]{:S(2)}, u32[]{:S(2)}) %collective-permute-start) | collective-permute-done | bytes 131104 | tf_op jit(solution)/shard_map/ppermute | solution.py:22
  9.5 3.9 %collective-permute-done.1.refs_3_ = f32[256,128]{1,0:T(8,128)S(1)} collective-permute-done((f32[256,128]{1,0:T(8,128)S(1)}, f32[256,128]{1,0:T(8,128)S(1)}, u32[]{:S(2)}, u32[]{:S(2)}) %collective-permute-start.1) | collective-permute-done | bytes 131104 | tf_op jit(solution)/shard_map/ppermute | solution.py:22
  15.6 2.6 %collective-permute-start.7 = (f32[256,128]{1,0:T(8,128)S(1)}, f32[256,128]{1,0:T(8,128)S(1)}, u32[]{:S(2)}, u32[]{:S(2)}) collective-permute-start(f32[256,128]{1,0:T(8,128)S(1)} %get-tuple-element.61), channel_id=1, source_target_pairs={{0,16},{8,24},{16,0},{24,8},{1,17},{9,25},{17,1},{25,9},{2,18},{10... | collective-permute-start | bytes 393224 | tf_op jit(solution)/shard_map/ppermute | solution.py:22
  23.8 3.4 %collective-permute-done.7.refs_6_.refs_3_ = f32[256,128]{1,0:T(8,128)S(1)} collective-permute-done((f32[256,128]{1,0:T(8,128)S(1)}, f32[256,128]{1,0:T(8,128)S(1)}, u32[]{:S(2)}, u32[]{:S(2)}) %collective-permute-start.7) | collective-permute-done | bytes 131104 | tf_op jit(solution)/shard_map/ppermute | solution.py:22
  34.0 3.2 %collective-permute-start.10 = (f32[256,128]{1,0:T(8,128)S(1)}, f32[256,128]{1,0:T(8,128)S(1)}, u32[]{:S(2)}, u32[]{:S(2)}) collective-permute-start(f32[256,128]{1,0:T(8,128)S(1)} %get-tuple-element.65), channel_id=1, source_target_pairs={{0,16},{8,24},{16,0},{24,8},{1,17},{9,25},{17,1},{25,9},{2,18},{10... | collective-permute-start | bytes 393224 | tf_op jit(solution)/shard_map/ppermute | solution.py:22
  38.3 4.9 %collective-permute-start.11 = (f32[256,128]{1,0:T(8,128)S(1)}, f32[256,128]{1,0:T(8,128)S(1)}, u32[]{:S(2)}, u32[]{:S(2)}) collective-permute-start(f32[256,128]{1,0:T(8,128)S(1)} %get-tuple-element.66), channel_id=1, source_target_pairs={{0,24},{8,16},{16,8},{24,0},{1,25},{9,17},{17,9},{25,1},{2,26},{10... | collective-permute-start | bytes 393224 | tf_op jit(solution)/shard_map/ppermute | solution.py:22
  46.0 2.5 %bases.1 = (f32[2,64,512]{2,1,0:T(8,128)S(1)}, f32[1,64,512]{2,1,0:T(8,128)S(1)}) custom-call(s32[3]{0:T(128)S(1)} %pad_add_fusion.refs_0_, f32[2,512,512]{2,1,0:T(8,128)S(1)} %copy-done.6, f32[1,512,512]{2,1,0:T(8,128)S(1)} %copy-done.3, f32[256,128]{1,0:T(8,128)S(1)} %get-tuple-element.55.refs_2_.refs_1_.refs_3_), custom_call_target="tpu_custom_call" | custom-call | tf_op jit(solution)/shard_map/bases/pallas_call | solution.py:36
  48.5 3.0 %collective-permute-done.13.refs_6_.refs_2_ = f32[4,256,128]{2,1,0:T(8,128)S(1)} collective-permute-done((f32[4,256,128]{2,1,0:T(8,128)S(1)}, f32[4,256,128]{2,1,0:T(8,128)S(1)}, u32[]{:S(2)}, u32[]{:S(2)}) %collective-permute-start.13) | collective-permute-done | bytes 524320 | tf_op jit(solution)/shard_map/ppermute | solution.py:22
  58.5 4.1 %collective-permute-start.19 = (f32[256,512]{1,0:T(8,128)S(1)}, f32[256,512]{1,0:T(8,128)S(1)}, u32[]{:S(2)}, u32[]{:S(2)}) collective-permute-start(f32[256,512]{1,0:T(8,128)S(1)} %get-tuple-element.68), channel_id=1, source_target_pairs={{0,16},{16,24},{24,8},{8,0},{1,17},{17,25},{25,9},{9,1},{2,18},{18... | collective-permute-start | bytes 1572872 | tf_op jit(solution)/shard_map/ppermute | solution.py:445
  64.5 4.3 %collective-permute-done.17.refs_3_ = f32[4,256,128]{2,1,0:T(8,128)S(1)} collective-permute-done((f32[4,256,128]{2,1,0:T(8,128)S(1)}, f32[4,256,128]{2,1,0:T(8,128)S(1)}, u32[]{:S(2)}, u32[]{:S(2)}) %collective-permute-start.17) | collective-permute-done | bytes 524320 | tf_op jit(solution)/shard_map/ppermute | solution.py:22
  69.5 4.3 %partial_product.4 = (f32[256,512]{1,0:T(8,128)S(1)}, f32[256,512]{1,0:T(8,128)S(1)}) custom-call(s32[3]{0:T(128)S(1)} %pad_add_fusion.refs_0_, s32[4,4]{1,0:T(4,128)S(1)} %copy-done.8, s32[2,8]{1,0:T(2,128)S(1)} %copy-done.7, f32[1024,2048]{1,0:T(8,128)S(1)} %bitcast.4, f32[4,4,256,128]{3,2,1,0:T(8,128)S(1)} %pack.2.refs_4_, ...), custom_call_target="tpu_custom_call" | custom-call | tf_op jit(solution)/shard_map/partial_product/pallas_call | solution.py:36
  73.8 5.1 %collective-permute-done.16.refs_2_ = f32[4,256,128]{2,1,0:T(8,128)S(1)} collective-permute-done((f32[4,256,128]{2,1,0:T(8,128)S(1)}, f32[4,256,128]{2,1,0:T(8,128)S(1)}, u32[]{:S(2)}, u32[]{:S(2)}) %collective-permute-start.16) | collective-permute-done | bytes 524320 | tf_op jit(solution)/shard_map/ppermute | solution.py:22
  79.0 6.3 %collective-permute-done.21.refs_6_.refs_1_ = f32[256,512]{1,0:T(8,128)S(1)} collective-permute-done((f32[256,512]{1,0:T(8,128)S(1)}, f32[256,512]{1,0:T(8,128)S(1)}, u32[]{:S(2)}, u32[]{:S(2)}) %collective-permute-start.21) | collective-permute-done | bytes 524320 | tf_op jit(solution)/shard_map/ppermute | solution.py:444
  85.6 3.4 %collective-permute-start.27 = (f32[256,512]{1,0:T(8,128)S(1)}, f32[256,512]{1,0:T(8,128)S(1)}, u32[]{:S(2)}, u32[]{:S(2)}) collective-permute-start(f32[256,512]{1,0:T(8,128)S(1)} %add_up.7), channel_id=1, source_target_pairs={{8,24},{16,0},{0,8},{24,16},{9,25},{17,1},{1,9},{25,17},{10,26},{1... | collective-permute-start | bytes 1572872 | tf_op jit(solution)/shard_map/ppermute | solution.py:448
  89.6 9.3 %partial_product.5 = (f32[256,512]{1,0:T(8,128)S(1)}, f32[256,512]{1,0:T(8,128)S(1)}, f32[256,512]{1,0:T(8,128)S(1)}, f32[256,512]{1,0:T(8,128)S(1)}) custom-call(s32[3]{0:T(128)S(1)} %pad_add_fusion.refs_0_, s32[4,4]{1,0:T(4,128)S(1)} %copy-done.8, s32[2,8]{1,0:T(2,128)S(1)} %copy-done.7, f32[1024,2048]{1,0:T(8,128)S(1)} %bitcast.4, ...), custom_call_target="tpu_custom_call" | custom-call | tf_op jit(solution)/shard_map/partial_product/pallas_call | solution.py:36
  99.0 5.3 %collective-permute-start.25 = (f32[256,512]{1,0:T(8,128)S(1)}, f32[256,512]{1,0:T(8,128)S(1)}, u32[]{:S(2)}, u32[]{:S(2)}) collective-permute-start(f32[256,512]{1,0:T(8,128)S(1)} %get-tuple-element.73), channel_id=1, source_target_pairs={{0,8},{24,16},{1,9},{25,17},{2,10},{26,18},{3,11},{27,19},{4,12},{... | collective-permute-start | bytes 1572872 | tf_op jit(solution)/shard_map/ppermute | solution.py:444
  105.0 7.8 %collective-permute-done.23.refs_9_.refs_3_ = f32[256,512]{1,0:T(8,128)S(1)} collective-permute-done((f32[256,512]{1,0:T(8,128)S(1)}, f32[256,512]{1,0:T(8,128)S(1)}, u32[]{:S(2)}, u32[]{:S(2)}) %collective-permute-start.23) | collective-permute-done | bytes 524320 | tf_op jit(solution)/shard_map/ppermute | solution.py:445
  112.8 10.5 %collective-permute-done.25.refs_1_.refs_11_ = f32[256,512]{1,0:T(8,128)S(1)} collective-permute-done((f32[256,512]{1,0:T(8,128)S(1)}, f32[256,512]{1,0:T(8,128)S(1)}, u32[]{:S(2)}, u32[]{:S(2)}) %collective-permute-start.25) | collective-permute-done | bytes 524320 | tf_op jit(solution)/shard_map/ppermute | solution.py:444
  123.3 3.5 %finish.2 = (f32[2,256,512]{2,1,0:T(8,128)}, f32[2,4,64,512]{3,2,1,0:T(8,128)S(1)}, f32[2,4,64,512]{3,2,1,0:T(8,128)S(1)}, f32[512,512]{1,0:T(8,128)S(1)}, f32[512,512]{1,0:T(8,128)S(1)}) custom-call(s32[3]{0:T(128)S(1)} %pad_add_fusion.refs_0_, s32[2,8]{1,0:T(2,128)S(1)} %copy-done.7, f32[256,512]{1,0:T(8,128)S(1)} %get-tuple-element.70.refs_7_.refs_2_, ...), custom_call_target="tpu_custom_call" | custom-call | tf_op jit(solution)/shard_map/finish/pallas_call | solution.py:36
  127.0 2.5 %collective-permute-start.26 = (f32[256,512]{1,0:T(8,128)S(1)}, f32[256,512]{1,0:T(8,128)S(1)}, u32[]{:S(2)}, u32[]{:S(2)}) collective-permute-start(f32[256,512]{1,0:T(8,128)S(1)} %add_up.6), channel_id=1, source_target_pairs={{8,24},{16,0},{0,8},{24,16},{9,25},{17,1},{1,9},{25,17},{10,26},{1... | collective-permute-start | bytes 1572872 | tf_op jit(solution)/shard_map/ppermute | solution.py:448
  131.4 2.4 %collective-permute-start.31 = (f32[2,64,512]{2,1,0:T(8,128)S(1)}, f32[2,64,512]{2,1,0:T(8,128)S(1)}, u32[]{:S(2)}, u32[]{:S(2)}) collective-permute-start(f32[2,64,512]{2,1,0:T(8,128)S(1)} %get-tuple-element.86), channel_id=1, source_target_pairs={{0,6},{1,7},{2,4},{3,5},{4,2},{5,3},{6,0},{7,1},{8,14},{9,15},{10,... | collective-permute-start | bytes 786440 | tf_op jit(solution)/shard_map/ppermute | solution.py:22
  133.8 2.3 %rest.1 = (f32[512,512]{1,0:T(8,128)S(1)}, f32[256,512]{1,0:T(8,128)S(1)}) custom-call(f32[1,512,512]{2,1,0:T(8,128)S(1)} %copy-done.4, f32[512,512]{1,0:T(8,128)S(1)} %get-tuple-element.76.refs_1_, f32[512,512]{1,0:T(8,128)S(1)} %get-tuple-element.77.refs_2_, f32[2,256,512]{2,1,0:T(8,128)S(1)} %copy-done.5), custom_call_target="tpu_custom_call" | custom-call | tf_op jit(solution)/shard_map/rest/pallas_call | solution.py:36
  136.1 3.4 %collective-permute-done.29.refs_2_ = f32[2,64,512]{2,1,0:T(8,128)S(1)} collective-permute-done((f32[2,64,512]{2,1,0:T(8,128)S(1)}, f32[2,64,512]{2,1,0:T(8,128)S(1)}, u32[]{:S(2)}, u32[]{:S(2)}) %collective-permute-start.29) | collective-permute-done | bytes 262176 | tf_op jit(solution)/shard_map/ppermute | solution.py:22
  139.5 5.2 %collective-permute-done.30.refs_3_ = f32[2,64,512]{2,1,0:T(8,128)S(1)} collective-permute-done((f32[2,64,512]{2,1,0:T(8,128)S(1)}, f32[2,64,512]{2,1,0:T(8,128)S(1)}, u32[]{:S(2)}, u32[]{:S(2)}) %collective-permute-start.30) | collective-permute-done | bytes 262176 | tf_op jit(solution)/shard_map/ppermute | solution.py:22
  145.3 2.9 %finish.3 = (f32[2,256,512]{2,1,0:T(8,128)}, f32[1,4,64,512]{3,2,1,0:T(8,128)S(1)}, f32[1,4,64,512]{3,2,1,0:T(8,128)S(1)}) custom-call(s32[3]{0:T(128)S(1)} %pad_add_fusion.refs_0_, s32[2,8]{1,0:T(2,128)S(1)} %copy-done.7, f32[256,512]{1,0:T(8,128)S(1)} %get-tuple-element.71.refs_2_, ...), custom_call_target="tpu_custom_call", output_to_operand_aliasing={{0}: (9, {})} | custom-call | tf_op jit(solution)/shard_map/finish/pallas_call | solution.py:36
  148.2 2.8 %collective-permute-start.32 = (f32[64,512]{1,0:T(8,128)S(1)}, f32[64,512]{1,0:T(8,128)S(1)}, u32[]{:S(2)}, u32[]{:S(2)}) collective-permute-start(f32[64,512]{1,0:T(8,128)S(1)} %get-tuple-element.90), channel_id=1, source_target_pairs={{0,8},{8,0},{16,24},{24,16},{1,9},{9,1},{17,25},{25,17},{2,10},{10... | collective-permute-start | bytes 393224 | tf_op jit(solution)/shard_map/ppermute | solution.py:22
  152.7 2.5 %collective-permute-start.38 = (f32[1,64,512]{2,1,0:T(8,128)S(1)}, f32[1,64,512]{2,1,0:T(8,128)S(1)}, u32[]{:S(2)}, u32[]{:S(2)}) collective-permute-start(f32[1,64,512]{2,1,0:T(8,128)S(1)} %get-tuple-element.96), channel_id=1, source_target_pairs={{0,6},{1,7},{2,4},{3,5},{4,2},{5,3},{6,0},{7,1},{8,14},{9,15},{10,... | collective-permute-start | bytes 393224 | tf_op jit(solution)/shard_map/ppermute | solution.py:22
  155.2 2.7 %collective-permute-start.33 = (f32[64,512]{1,0:T(8,128)S(1)}, f32[64,512]{1,0:T(8,128)S(1)}, u32[]{:S(2)}, u32[]{:S(2)}) collective-permute-start(f32[64,512]{1,0:T(8,128)S(1)} %add_up.8.refs_0_), channel_id=1, source_target_pairs={{0,16},{8,24},{16,0},{24,8},{1,17},{9,25},{17,1},{25,9},{2,18},{10... | collective-permute-start | bytes 393224 | tf_op jit(solution)/shard_map/ppermute | solution.py:22
  162.1 2.3 %collective-permute-done.33.refs_1_ = f32[64,512]{1,0:T(8,128)S(1)} collective-permute-done((f32[64,512]{1,0:T(8,128)S(1)}, f32[64,512]{1,0:T(8,128)S(1)}, u32[]{:S(2)}, u32[]{:S(2)}) %collective-permute-start.33) | collective-permute-done | bytes 131104 | tf_op jit(solution)/shard_map/ppermute | solution.py:22
  166.4 2.3 %collective-permute-start.40 = (f32[1,64,512]{2,1,0:T(8,128)S(1)}, f32[1,64,512]{2,1,0:T(8,128)S(1)}, u32[]{:S(2)}, u32[]{:S(2)}) collective-permute-start(f32[1,64,512]{2,1,0:T(8,128)S(1)} %add_up.11.refs_5_), channel_id=1, source_target_pairs={{0,16},{8,24},{16,0},{24,8},{1,17},{9,25},{17,1},{25,9},{2,18},{10... | collective-permute-start | bytes 393224 | tf_op jit(solution)/shard_map/ppermute | solution.py:22
  170.3 4.2 %collective-permute-done.40.refs_6_ = f32[1,64,512]{2,1,0:T(8,128)S(1)} collective-permute-done((f32[1,64,512]{2,1,0:T(8,128)S(1)}, f32[1,64,512]{2,1,0:T(8,128)S(1)}, u32[]{:S(2)}, u32[]{:S(2)}) %collective-permute-start.40) | collective-permute-done | bytes 131104 | tf_op jit(solution)/shard_map/ppermute | solution.py:22
  (99 shorter events, 46.5 us)
Async XLA Ops:
  2.6 6.9 %collective-permute-start = (f32[256,128]{1,0:T(8,128)S(1)}, f32[256,128]{1,0:T(8,128)S(1)}, u32[]{:S(2)}, u32[]{:S(2)}) collective-permute-start(f32[256,128]{1,0:T(8,128)S(1)} %get-tuple-element.52), channel_id=1, source_target_pairs={{0,2},{1,3},{2,0},{3,1},{4,6},{5,7},{6,4},{7,5},{8,10},{9,11},{10,... | collective-permute-start | bytes 393224 | tf_op jit(solution)/shard_map/ppermute | solution.py:22
  5.6 7.8 %collective-permute-start.1 = (f32[256,128]{1,0:T(8,128)S(1)}, f32[256,128]{1,0:T(8,128)S(1)}, u32[]{:S(2)}, u32[]{:S(2)}) collective-permute-start(f32[256,128]{1,0:T(8,128)S(1)} %get-tuple-element.53), channel_id=1, source_target_pairs={{0,4},{1,5},{2,6},{3,7},{4,0},{5,1},{6,2},{7,3},{8,12},{9,13},{10,... | collective-permute-start | bytes 393224 | tf_op jit(solution)/shard_map/ppermute | solution.py:22
  7.1 6.3 %collective-permute-start.2 = (f32[256,128]{1,0:T(8,128)S(1)}, f32[256,128]{1,0:T(8,128)S(1)}, u32[]{:S(2)}, u32[]{:S(2)}) collective-permute-start(f32[256,128]{1,0:T(8,128)S(1)} %get-tuple-element.54), channel_id=1, source_target_pairs={{0,6},{1,7},{2,4},{3,5},{4,2},{5,3},{6,0},{7,1},{8,14},{9,15},{10,... | collective-permute-start | bytes 393224 | tf_op jit(solution)/shard_map/ppermute | solution.py:22
  14.0 8.4 %collective-permute-start.6 = (f32[256,128]{1,0:T(8,128)S(1)}, f32[256,128]{1,0:T(8,128)S(1)}, u32[]{:S(2)}, u32[]{:S(2)}) collective-permute-start(f32[256,128]{1,0:T(8,128)S(1)} %get-tuple-element.60), channel_id=1, source_target_pairs={{0,8},{8,0},{16,24},{24,16},{1,9},{9,1},{17,25},{25,17},{2,10},{10... | collective-permute-start | bytes 393224 | tf_op jit(solution)/shard_map/ppermute | solution.py:22
  15.6 11.6 %collective-permute-start.7 = (f32[256,128]{1,0:T(8,128)S(1)}, f32[256,128]{1,0:T(8,128)S(1)}, u32[]{:S(2)}, u32[]{:S(2)}) collective-permute-start(f32[256,128]{1,0:T(8,128)S(1)} %get-tuple-element.61), channel_id=1, source_target_pairs={{0,16},{8,24},{16,0},{24,8},{1,17},{9,25},{17,1},{25,9},{2,18},{10... | collective-permute-start | bytes 393224 | tf_op jit(solution)/shard_map/ppermute | solution.py:22
  18.2 9.0 %collective-permute-start.8 = (f32[256,128]{1,0:T(8,128)S(1)}, f32[256,128]{1,0:T(8,128)S(1)}, u32[]{:S(2)}, u32[]{:S(2)}) collective-permute-start(f32[256,128]{1,0:T(8,128)S(1)} %get-tuple-element.62), channel_id=1, source_target_pairs={{0,24},{8,16},{16,8},{24,0},{1,25},{9,17},{17,9},{25,1},{2,26},{10... | collective-permute-start | bytes 393224 | tf_op jit(solution)/shard_map/ppermute | solution.py:22
  20.3 6.9 %collective-permute-start.3 = (f32[256,128]{1,0:T(8,128)S(1)}, f32[256,128]{1,0:T(8,128)S(1)}, u32[]{:S(2)}, u32[]{:S(2)}) collective-permute-start(f32[256,128]{1,0:T(8,128)S(1)} %get-tuple-element.57), channel_id=1, source_target_pairs={{0,2},{1,3},{2,0},{3,1},{4,6},{5,7},{6,4},{7,5},{8,10},{9,11},{10,... | collective-permute-start | bytes 393224 | tf_op jit(solution)/shard_map/ppermute | solution.py:22
  28.8 19.7 %collective-permute-start.14 = (f32[4,256,128]{2,1,0:T(8,128)S(1)}, f32[4,256,128]{2,1,0:T(8,128)S(1)}, u32[]{:S(2)}, u32[]{:S(2)}) collective-permute-start(f32[4,256,128]{2,1,0:T(8,128)S(1)} %arrange.2.refs_0_), channel_id=1, source_target_pairs={{0,6},{1,7},{2,4},{3,5},{4,2},{5,3},{6,0},{7,1},{8,14},{9,15},{10,... | collective-permute-start | bytes 1572872 | tf_op jit(solution)/shard_map/ppermute | solution.py:22
  30.3 21.2 %collective-permute-start.13 = (f32[4,256,128]{2,1,0:T(8,128)S(1)}, f32[4,256,128]{2,1,0:T(8,128)S(1)}, u32[]{:S(2)}, u32[]{:S(2)}) collective-permute-start(f32[4,256,128]{2,1,0:T(8,128)S(1)} %arrange.2.refs_0_), channel_id=1, source_target_pairs={{0,4},{1,5},{2,6},{3,7},{4,0},{5,1},{6,2},{7,3},{8,12},{9,13},{10,... | collective-permute-start | bytes 1572872 | tf_op jit(solution)/shard_map/ppermute | solution.py:22
  31.8 20.4 %collective-permute-start.12 = (f32[4,256,128]{2,1,0:T(8,128)S(1)}, f32[4,256,128]{2,1,0:T(8,128)S(1)}, u32[]{:S(2)}, u32[]{:S(2)}) collective-permute-start(f32[4,256,128]{2,1,0:T(8,128)S(1)} %arrange.2.refs_0_), channel_id=1, source_target_pairs={{0,2},{1,3},{2,0},{3,1},{4,6},{5,7},{6,4},{7,5},{8,10},{9,11},{10,... | collective-permute-start | bytes 1572872 | tf_op jit(solution)/shard_map/ppermute | solution.py:22
  34.0 14.5 %collective-permute-start.10 = (f32[256,128]{1,0:T(8,128)S(1)}, f32[256,128]{1,0:T(8,128)S(1)}, u32[]{:S(2)}, u32[]{:S(2)}) collective-permute-start(f32[256,128]{1,0:T(8,128)S(1)} %get-tuple-element.65), channel_id=1, source_target_pairs={{0,16},{8,24},{16,0},{24,8},{1,17},{9,25},{17,1},{25,9},{2,18},{10... | collective-permute-start | bytes 393224 | tf_op jit(solution)/shard_map/ppermute | solution.py:22
  38.3 10.2 %collective-permute-start.11 = (f32[256,128]{1,0:T(8,128)S(1)}, f32[256,128]{1,0:T(8,128)S(1)}, u32[]{:S(2)}, u32[]{:S(2)}) collective-permute-start(f32[256,128]{1,0:T(8,128)S(1)} %get-tuple-element.66), channel_id=1, source_target_pairs={{0,24},{8,16},{16,8},{24,0},{1,25},{9,17},{17,9},{25,1},{2,26},{10... | collective-permute-start | bytes 393224 | tf_op jit(solution)/shard_map/ppermute | solution.py:22
  53.0 15.7 %collective-permute-start.17 = (f32[4,256,128]{2,1,0:T(8,128)S(1)}, f32[4,256,128]{2,1,0:T(8,128)S(1)}, u32[]{:S(2)}, u32[]{:S(2)}) collective-permute-start(f32[4,256,128]{2,1,0:T(8,128)S(1)} %arrange.3.refs_0_), channel_id=1, source_target_pairs={{0,6},{1,7},{2,4},{3,5},{4,2},{5,3},{6,0},{7,1},{8,14},{9,15},{10,... | collective-permute-start | bytes 1572872 | tf_op jit(solution)/shard_map/ppermute | solution.py:22
  53.7 25.3 %collective-permute-start.16 = (f32[4,256,128]{2,1,0:T(8,128)S(1)}, f32[4,256,128]{2,1,0:T(8,128)S(1)}, u32[]{:S(2)}, u32[]{:S(2)}) collective-permute-start(f32[4,256,128]{2,1,0:T(8,128)S(1)} %arrange.3.refs_0_), channel_id=1, source_target_pairs={{0,4},{1,5},{2,6},{3,7},{4,0},{5,1},{6,2},{7,3},{8,12},{9,13},{10,... | collective-permute-start | bytes 1572872 | tf_op jit(solution)/shard_map/ppermute | solution.py:22
  54.8 24.1 %collective-permute-start.15 = (f32[4,256,128]{2,1,0:T(8,128)S(1)}, f32[4,256,128]{2,1,0:T(8,128)S(1)}, u32[]{:S(2)}, u32[]{:S(2)}) collective-permute-start(f32[4,256,128]{2,1,0:T(8,128)S(1)} %arrange.3.refs_0_), channel_id=1, source_target_pairs={{0,2},{1,3},{2,0},{3,1},{4,6},{5,7},{6,4},{7,5},{8,10},{9,11},{10,... | collective-permute-start | bytes 1572872 | tf_op jit(solution)/shard_map/ppermute | solution.py:22
  58.5 20.5 %collective-permute-start.19 = (f32[256,512]{1,0:T(8,128)S(1)}, f32[256,512]{1,0:T(8,128)S(1)}, u32[]{:S(2)}, u32[]{:S(2)}) collective-permute-start(f32[256,512]{1,0:T(8,128)S(1)} %get-tuple-element.68), channel_id=1, source_target_pairs={{0,16},{16,24},{24,8},{8,0},{1,17},{17,25},{25,9},{9,1},{2,18},{18... | collective-permute-start | bytes 1572872 | tf_op jit(solution)/shard_map/ppermute | solution.py:445
  62.6 22.7 %collective-permute-start.21 = (f32[256,512]{1,0:T(8,128)S(1)}, f32[256,512]{1,0:T(8,128)S(1)}, u32[]{:S(2)}, u32[]{:S(2)}) collective-permute-start(f32[256,512]{1,0:T(8,128)S(1)} %get-tuple-element.69), channel_id=1, source_target_pairs={{0,8},{24,16},{1,9},{25,17},{2,10},{26,18},{3,11},{27,19},{4,12},{... | collective-permute-start | bytes 1572872 | tf_op jit(solution)/shard_map/ppermute | solution.py:444
  68.8 16.5 %collective-permute-start.20 = (f32[256,512]{1,0:T(8,128)S(1)}, f32[256,512]{1,0:T(8,128)S(1)}, u32[]{:S(2)}, u32[]{:S(2)}) collective-permute-start(f32[256,512]{1,0:T(8,128)S(1)} %get-tuple-element.69), channel_id=1, source_target_pairs={{8,16},{16,8},{9,17},{17,9},{10,18},{18,10},{11,19},{19,11},{12,20... | collective-permute-start | bytes 1572872 | tf_op jit(solution)/shard_map/ppermute | solution.py:446
  85.6 19.5 %collective-permute-start.27 = (f32[256,512]{1,0:T(8,128)S(1)}, f32[256,512]{1,0:T(8,128)S(1)}, u32[]{:S(2)}, u32[]{:S(2)}) collective-permute-start(f32[256,512]{1,0:T(8,128)S(1)} %add_up.7), channel_id=1, source_target_pairs={{8,24},{16,0},{0,8},{24,16},{9,25},{17,1},{1,9},{25,17},{10,26},{1... | collective-permute-start | bytes 1572872 | tf_op jit(solution)/shard_map/ppermute | solution.py:448
  98.9 13.9 %collective-permute-start.23 = (f32[256,512]{1,0:T(8,128)S(1)}, f32[256,512]{1,0:T(8,128)S(1)}, u32[]{:S(2)}, u32[]{:S(2)}) collective-permute-start(f32[256,512]{1,0:T(8,128)S(1)} %get-tuple-element.72), channel_id=1, source_target_pairs={{0,16},{16,24},{24,8},{8,0},{1,17},{17,25},{25,9},{9,1},{2,18},{18... | collective-permute-start | bytes 1572872 | tf_op jit(solution)/shard_map/ppermute | solution.py:445
  99.0 24.3 %collective-permute-start.25 = (f32[256,512]{1,0:T(8,128)S(1)}, f32[256,512]{1,0:T(8,128)S(1)}, u32[]{:S(2)}, u32[]{:S(2)}) collective-permute-start(f32[256,512]{1,0:T(8,128)S(1)} %get-tuple-element.73), channel_id=1, source_target_pairs={{0,8},{24,16},{1,9},{25,17},{2,10},{26,18},{3,11},{27,19},{4,12},{... | collective-permute-start | bytes 1572872 | tf_op jit(solution)/shard_map/ppermute | solution.py:444
  104.3 19.0 %collective-permute-start.24 = (f32[256,512]{1,0:T(8,128)S(1)}, f32[256,512]{1,0:T(8,128)S(1)}, u32[]{:S(2)}, u32[]{:S(2)}) collective-permute-start(f32[256,512]{1,0:T(8,128)S(1)} %get-tuple-element.73), channel_id=1, source_target_pairs={{8,16},{16,8},{9,17},{17,9},{10,18},{18,10},{11,19},{19,11},{12,20... | collective-permute-start | bytes 1572872 | tf_op jit(solution)/shard_map/ppermute | solution.py:446
  127.0 18.4 %collective-permute-start.26 = (f32[256,512]{1,0:T(8,128)S(1)}, f32[256,512]{1,0:T(8,128)S(1)}, u32[]{:S(2)}, u32[]{:S(2)}) collective-permute-start(f32[256,512]{1,0:T(8,128)S(1)} %add_up.6), channel_id=1, source_target_pairs={{8,24},{16,0},{0,8},{24,16},{9,25},{17,1},{1,9},{25,17},{10,26},{1... | collective-permute-start | bytes 1572872 | tf_op jit(solution)/shard_map/ppermute | solution.py:448
  130.3 9.2 %collective-permute-start.29 = (f32[2,64,512]{2,1,0:T(8,128)S(1)}, f32[2,64,512]{2,1,0:T(8,128)S(1)}, u32[]{:S(2)}, u32[]{:S(2)}) collective-permute-start(f32[2,64,512]{2,1,0:T(8,128)S(1)} %get-tuple-element.84), channel_id=1, source_target_pairs={{0,2},{1,3},{2,0},{3,1},{4,6},{5,7},{6,4},{7,5},{8,10},{9,11},{10,... | collective-permute-start | bytes 786440 | tf_op jit(solution)/shard_map/ppermute | solution.py:22
  131.4 13.3 %collective-permute-start.30 = (f32[2,64,512]{2,1,0:T(8,128)S(1)}, f32[2,64,512]{2,1,0:T(8,128)S(1)}, u32[]{:S(2)}, u32[]{:S(2)}) collective-permute-start(f32[2,64,512]{2,1,0:T(8,128)S(1)} %get-tuple-element.85), channel_id=1, source_target_pairs={{0,4},{1,5},{2,6},{3,7},{4,0},{5,1},{6,2},{7,3},{8,12},{9,13},{10,... | collective-permute-start | bytes 786440 | tf_op jit(solution)/shard_map/ppermute | solution.py:22
  131.4 13.3 %collective-permute-start.31 = (f32[2,64,512]{2,1,0:T(8,128)S(1)}, f32[2,64,512]{2,1,0:T(8,128)S(1)}, u32[]{:S(2)}, u32[]{:S(2)}) collective-permute-start(f32[2,64,512]{2,1,0:T(8,128)S(1)} %get-tuple-element.86), channel_id=1, source_target_pairs={{0,6},{1,7},{2,4},{3,5},{4,2},{5,3},{6,0},{7,1},{8,14},{9,15},{10,... | collective-permute-start | bytes 786440 | tf_op jit(solution)/shard_map/ppermute | solution.py:22
  148.2 7.0 %collective-permute-start.32 = (f32[64,512]{1,0:T(8,128)S(1)}, f32[64,512]{1,0:T(8,128)S(1)}, u32[]{:S(2)}, u32[]{:S(2)}) collective-permute-start(f32[64,512]{1,0:T(8,128)S(1)} %get-tuple-element.90), channel_id=1, source_target_pairs={{0,8},{8,0},{16,24},{24,16},{1,9},{9,1},{17,25},{25,17},{2,10},{10... | collective-permute-start | bytes 393224 | tf_op jit(solution)/shard_map/ppermute | solution.py:22
  151.6 6.4 %collective-permute-start.36 = (f32[1,64,512]{2,1,0:T(8,128)S(1)}, f32[1,64,512]{2,1,0:T(8,128)S(1)}, u32[]{:S(2)}, u32[]{:S(2)}) collective-permute-start(f32[1,64,512]{2,1,0:T(8,128)S(1)} %get-tuple-element.94), channel_id=1, source_target_pairs={{0,2},{1,3},{2,0},{3,1},{4,6},{5,7},{6,4},{7,5},{8,10},{9,11},{10,... | collective-permute-start | bytes 393224 | tf_op jit(solution)/shard_map/ppermute | solution.py:22
  152.0 8.3 %collective-permute-start.37 = (f32[1,64,512]{2,1,0:T(8,128)S(1)}, f32[1,64,512]{2,1,0:T(8,128)S(1)}, u32[]{:S(2)}, u32[]{:S(2)}) collective-permute-start(f32[1,64,512]{2,1,0:T(8,128)S(1)} %get-tuple-element.95), channel_id=1, source_target_pairs={{0,4},{1,5},{2,6},{3,7},{4,0},{5,1},{6,2},{7,3},{8,12},{9,13},{10,... | collective-permute-start | bytes 393224 | tf_op jit(solution)/shard_map/ppermute | solution.py:22
  152.7 7.5 %collective-permute-start.38 = (f32[1,64,512]{2,1,0:T(8,128)S(1)}, f32[1,64,512]{2,1,0:T(8,128)S(1)}, u32[]{:S(2)}, u32[]{:S(2)}) collective-permute-start(f32[1,64,512]{2,1,0:T(8,128)S(1)} %get-tuple-element.96), channel_id=1, source_target_pairs={{0,6},{1,7},{2,4},{3,5},{4,2},{5,3},{6,0},{7,1},{8,14},{9,15},{10,... | collective-permute-start | bytes 393224 | tf_op jit(solution)/shard_map/ppermute | solution.py:22
  155.2 9.2 %collective-permute-start.33 = (f32[64,512]{1,0:T(8,128)S(1)}, f32[64,512]{1,0:T(8,128)S(1)}, u32[]{:S(2)}, u32[]{:S(2)}) collective-permute-start(f32[64,512]{1,0:T(8,128)S(1)} %add_up.8.refs_0_), channel_id=1, source_target_pairs={{0,16},{8,24},{16,0},{24,8},{1,17},{9,25},{17,1},{25,9},{2,18},{10... | collective-permute-start | bytes 393224 | tf_op jit(solution)/shard_map/ppermute | solution.py:22
  166.4 8.1 %collective-permute-start.40 = (f32[1,64,512]{2,1,0:T(8,128)S(1)}, f32[1,64,512]{2,1,0:T(8,128)S(1)}, u32[]{:S(2)}, u32[]{:S(2)}) collective-permute-start(f32[1,64,512]{2,1,0:T(8,128)S(1)} %add_up.11.refs_5_), channel_id=1, source_target_pairs={{0,16},{8,24},{16,0},{24,8},{1,17},{9,25},{17,1},{25,9},{2,18},{10... | collective-permute-start | bytes 393224 | tf_op jit(solution)/shard_map/ppermute | solution.py:22
  (20 other events, 211.9 us)

commit v12 on v11

--- a/solution.py
+++ b/solution.py
@@ -556,7 +556,7 @@
     sums, before, pending = [], [], []
     for number in range(nsuper):
         last = number + 1 == nsuper
-        waits = [] if last else rows[number + 1][1:4]
+        waits = [] if last else rows[number + 1][2:4]
         offdiag, keep, send, *link = finish(
             number, own_block, place, ancestors, rows[number][:3] + rows[number][4:], factor, before,
             link_factor, pcol_count // 2, waits + pending[:1],

time: 176 us -> 175 us (level)
  waiting for transfers between devices: 71 us -> 77.9 us
  starting transfers between devices: 64.5 us -> 59.4 us
  Pallas kernels: 34 us -> 30.5 us
    ppermute x2, waiting for transfers between devices: 0.01 us -> 10.9 us  [sum_over_four(): last = lax.ppermute(both, 'prow', [(1, 3), (2, 0), (0, 1), (3, 2)])]
    ppermute x2, waiting for transfers between devices: 7.81 us -> 0.01 us  [sum_over_four(): total = lax.ppermute(slots[1], 'prow', [(0, 2), (2, 3), (3, 1), (1, 0)])]
    ppermute x33, starting transfers between devices: 45.8 us -> 38.7 us  [flip(): lax.ppermute(value, axis, [(i, i ^ bit) for i in range(lax.axis_size(axis...]
    ppermute x33, waiting for transfers between devices: 46.4 us -> 52.8 us  [flip(): lax.ppermute(value, axis, [(i, i ^ bit) for i in range(lax.axis_size(axis...]
    pallas_call x25, Pallas kernels: 34 us -> 30.5 us  [run(): pl.pallas_call(body, grid_spec=pltpu.PrefetchScalarGridSpec(num_scalar_pr...]
    ppermute x2, waiting for transfers between devices: 16.8 us -> 14.3 us  [sum_over_four(): near = lax.ppermute(slots[0], 'prow', [(0, 1), (3, 2)])]
  transfers between devices with their start and end apart: 41 -> 41, of which waited for: 22 -> 22; matrix products, arithmetic and copies ran while one was open for 0% -> 0% of each run, Pallas kernels for 14% -> 12%
where the time goes in v12:
time: 175 us; the launch traced here: 174 us
  waiting for transfers between devices  77.9 us (45%)
  starting transfers between devices  59.4 us (34%)
  Pallas kernels  30.5 us (17%)
  local copies, waits for them, and re-layouts  5.3 us (3%)
    ppermute x33, waiting for transfers between devices, flip(): lax.ppermute(value, axis, [(i, i ^ bit) for i in range(lax.axis_size(axis...  52.8 us
    ppermute x33, starting transfers between devices, flip(): lax.ppermute(value, axis, [(i, i ^ bit) for i in range(lax.axis_size(axis...  38.7 us
    pallas_call x25, Pallas kernels, run(): pl.pallas_call(body, grid_spec=pltpu.PrefetchScalarGridSpec(num_scalar_pr...  30.5 us
    ppermute x2, waiting for transfers between devices, sum_over_four(): near = lax.ppermute(slots[0], 'prow', [(0, 1), (3, 2)])  14.3 us
    ppermute x2, waiting for transfers between devices, sum_over_four(): last = lax.ppermute(both, 'prow', [(1, 3), (2, 0), (0, 1), (3, 2)])  10.9 us
    ppermute x2, starting transfers between devices, sum_over_four(): near = lax.ppermute(slots[0], 'prow', [(0, 1), (3, 2)])  7.86 us
    ppermute x2, starting transfers between devices, sum_over_four(): last = lax.ppermute(both, 'prow', [(1, 3), (2, 0), (0, 1), (3, 2)])  6.89 us
    unnamed x22, local copies, waits for them, and re-layouts  5.3 us
  transfers between devices with their start and end apart: 41, of which 22 were waited for; matrix products, arithmetic and copies ran while one was open for 0% of the time, Pallas kernels for 12%

profile of v12, /device:TPU:0, one launch (start us, length us, event | category | flops | bytes accessed | tf_op | source)
XLA Modules:
  0.0 174.2 jit_solution(7695179594231300079)
XLA Ops:
  2.6 3.0 %collective-permute-start = (f32[256,128]{1,0:T(8,128)S(1)}, f32[256,128]{1,0:T(8,128)S(1)}, u32[]{:S(2)}, u32[]{:S(2)}) collective-permute-start(f32[256,128]{1,0:T(8,128)S(1)} %get-tuple-element.52), channel_id=1, source_target_pairs={{0,2},{1,3},{2,0},{3,1},{4,6},{5,7},{6,4},{7,5},{8,10},{9,11},{10,... | collective-permute-start | bytes 393224 | tf_op jit(solution)/shard_map/ppermute | solution.py:22
  7.1 2.4 %collective-permute-done.refs_2_ = f32[256,128]{1,0:T(8,128)S(1)} collective-permute-done((f32[256,128]{1,0:T(8,128)S(1)}, f32[256,128]{1,0:T(8,128)S(1)}, u32[]{:S(2)}, u32[]{:S(2)}) %collective-permute-start) | collective-permute-done | bytes 131104 | tf_op jit(solution)/shard_map/ppermute | solution.py:22
  9.5 3.9 %collective-permute-done.1.refs_3_ = f32[256,128]{1,0:T(8,128)S(1)} collective-permute-done((f32[256,128]{1,0:T(8,128)S(1)}, f32[256,128]{1,0:T(8,128)S(1)}, u32[]{:S(2)}, u32[]{:S(2)}) %collective-permute-start.1) | collective-permute-done | bytes 131104 | tf_op jit(solution)/shard_map/ppermute | solution.py:22
  15.6 2.6 %collective-permute-start.7 = (f32[256,128]{1,0:T(8,128)S(1)}, f32[256,128]{1,0:T(8,128)S(1)}, u32[]{:S(2)}, u32[]{:S(2)}) collective-permute-start(f32[256,128]{1,0:T(8,128)S(1)} %get-tuple-element.61), channel_id=1, source_target_pairs={{0,16},{8,24},{16,0},{24,8},{1,17},{9,25},{17,1},{25,9},{2,18},{10... | collective-permute-start | bytes 393224 | tf_op jit(solution)/shard_map/ppermute | solution.py:22
  23.8 3.4 %collective-permute-done.7.refs_6_.refs_3_ = f32[256,128]{1,0:T(8,128)S(1)} collective-permute-done((f32[256,128]{1,0:T(8,128)S(1)}, f32[256,128]{1,0:T(8,128)S(1)}, u32[]{:S(2)}, u32[]{:S(2)}) %collective-permute-start.7) | collective-permute-done | bytes 131104 | tf_op jit(solution)/shard_map/ppermute | solution.py:22
  34.0 3.2 %collective-permute-start.10 = (f32[256,128]{1,0:T(8,128)S(1)}, f32[256,128]{1,0:T(8,128)S(1)}, u32[]{:S(2)}, u32[]{:S(2)}) collective-permute-start(f32[256,128]{1,0:T(8,128)S(1)} %get-tuple-element.65), channel_id=1, source_target_pairs={{0,16},{8,24},{16,0},{24,8},{1,17},{9,25},{17,1},{25,9},{2,18},{10... | collective-permute-start | bytes 393224 | tf_op jit(solution)/shard_map/ppermute | solution.py:22
  38.3 4.9 %collective-permute-start.11 = (f32[256,128]{1,0:T(8,128)S(1)}, f32[256,128]{1,0:T(8,128)S(1)}, u32[]{:S(2)}, u32[]{:S(2)}) collective-permute-start(f32[256,128]{1,0:T(8,128)S(1)} %get-tuple-element.66), channel_id=1, source_target_pairs={{0,24},{8,16},{16,8},{24,0},{1,25},{9,17},{17,9},{25,1},{2,26},{10... | collective-permute-start | bytes 393224 | tf_op jit(solution)/shard_map/ppermute | solution.py:22
  46.0 2.5 %bases.1 = (f32[2,64,512]{2,1,0:T(8,128)S(1)}, f32[1,64,512]{2,1,0:T(8,128)S(1)}) custom-call(s32[3]{0:T(128)S(1)} %pad_add_fusion.refs_0_, f32[2,512,512]{2,1,0:T(8,128)S(1)} %copy-done.6, f32[1,512,512]{2,1,0:T(8,128)S(1)} %copy-done.3, f32[256,128]{1,0:T(8,128)S(1)} %get-tuple-element.55.refs_2_.refs_1_.refs_3_), custom_call_target="tpu_custom_call" | custom-call | tf_op jit(solution)/shard_map/bases/pallas_call | solution.py:36
  48.5 3.0 %collective-permute-done.13.refs_6_.refs_2_ = f32[4,256,128]{2,1,0:T(8,128)S(1)} collective-permute-done((f32[4,256,128]{2,1,0:T(8,128)S(1)}, f32[4,256,128]{2,1,0:T(8,128)S(1)}, u32[]{:S(2)}, u32[]{:S(2)}) %collective-permute-start.13) | collective-permute-done | bytes 524320 | tf_op jit(solution)/shard_map/ppermute | solution.py:22
  58.5 2.9 %collective-permute-start.19 = (f32[256,512]{1,0:T(8,128)S(1)}, f32[256,512]{1,0:T(8,128)S(1)}, u32[]{:S(2)}, u32[]{:S(2)}) collective-permute-start(f32[256,512]{1,0:T(8,128)S(1)} %get-tuple-element.68), channel_id=1, source_target_pairs={{0,16},{16,24},{24,8},{8,0},{1,17},{17,25},{25,9},{9,1},{2,18},{18... | collective-permute-start | bytes 1572872 | tf_op jit(solution)/shard_map/ppermute | solution.py:445
  61.4 3.1 %collective-permute-start.21 = (f32[256,512]{1,0:T(8,128)S(1)}, f32[256,512]{1,0:T(8,128)S(1)}, u32[]{:S(2)}, u32[]{:S(2)}) collective-permute-start(f32[256,512]{1,0:T(8,128)S(1)} %get-tuple-element.69), channel_id=1, source_target_pairs={{0,8},{24,16},{1,9},{25,17},{2,10},{26,18},{3,11},{27,19},{4,12},{... | collective-permute-start | bytes 1572872 | tf_op jit(solution)/shard_map/ppermute | solution.py:444
  64.5 4.3 %collective-permute-done.17.refs_3_ = f32[4,256,128]{2,1,0:T(8,128)S(1)} collective-permute-done((f32[4,256,128]{2,1,0:T(8,128)S(1)}, f32[4,256,128]{2,1,0:T(8,128)S(1)}, u32[]{:S(2)}, u32[]{:S(2)}) %collective-permute-start.17) | collective-permute-done | bytes 524320 | tf_op jit(solution)/shard_map/ppermute | solution.py:22
  69.5 4.4 %partial_product.4 = (f32[256,512]{1,0:T(8,128)S(1)}, f32[256,512]{1,0:T(8,128)S(1)}) custom-call(s32[3]{0:T(128)S(1)} %pad_add_fusion.refs_0_, s32[4,4]{1,0:T(4,128)S(1)} %copy-done.8, s32[2,8]{1,0:T(2,128)S(1)} %copy-done.7, f32[1024,2048]{1,0:T(8,128)S(1)} %bitcast.4, f32[4,4,256,128]{3,2,1,0:T(8,128)S(1)} %pack.2.refs_4_, ...), custom_call_target="tpu_custom_call" | custom-call | tf_op jit(solution)/shard_map/partial_product/pallas_call | solution.py:36
  73.8 5.1 %collective-permute-done.16.refs_2_ = f32[4,256,128]{2,1,0:T(8,128)S(1)} collective-permute-done((f32[4,256,128]{2,1,0:T(8,128)S(1)}, f32[4,256,128]{2,1,0:T(8,128)S(1)}, u32[]{:S(2)}, u32[]{:S(2)}) %collective-permute-start.16) | collective-permute-done | bytes 524320 | tf_op jit(solution)/shard_map/ppermute | solution.py:22
  78.9 5.1 %collective-permute-done.21.refs_6_.refs_1_ = f32[256,512]{1,0:T(8,128)S(1)} collective-permute-done((f32[256,512]{1,0:T(8,128)S(1)}, f32[256,512]{1,0:T(8,128)S(1)}, u32[]{:S(2)}, u32[]{:S(2)}) %collective-permute-start.21) | collective-permute-done | bytes 524320 | tf_op jit(solution)/shard_map/ppermute | solution.py:444
  84.4 5.5 %collective-permute-start.27 = (f32[256,512]{1,0:T(8,128)S(1)}, f32[256,512]{1,0:T(8,128)S(1)}, u32[]{:S(2)}, u32[]{:S(2)}) collective-permute-start(f32[256,512]{1,0:T(8,128)S(1)} %add_up.7), channel_id=1, source_target_pairs={{8,24},{16,0},{0,8},{24,16},{9,25},{17,1},{1,9},{25,17},{10,26},{1... | collective-permute-start | bytes 1572872 | tf_op jit(solution)/shard_map/ppermute | solution.py:448
  89.9 5.7 %partial_product.5 = (f32[256,512]{1,0:T(8,128)S(1)}, f32[256,512]{1,0:T(8,128)S(1)}, f32[256,512]{1,0:T(8,128)S(1)}, f32[256,512]{1,0:T(8,128)S(1)}) custom-call(s32[3]{0:T(128)S(1)} %pad_add_fusion.refs_0_, s32[4,4]{1,0:T(4,128)S(1)} %copy-done.8, s32[2,8]{1,0:T(2,128)S(1)} %copy-done.7, f32[1024,2048]{1,0:T(8,128)S(1)} %bitcast.4, ...), custom_call_target="tpu_custom_call" | custom-call | tf_op jit(solution)/shard_map/partial_product/pallas_call | solution.py:36
  95.6 4.7 %collective-permute-start.25 = (f32[256,512]{1,0:T(8,128)S(1)}, f32[256,512]{1,0:T(8,128)S(1)}, u32[]{:S(2)}, u32[]{:S(2)}) collective-permute-start(f32[256,512]{1,0:T(8,128)S(1)} %get-tuple-element.73), channel_id=1, source_target_pairs={{0,8},{24,16},{1,9},{25,17},{2,10},{26,18},{3,11},{27,19},{4,12},{... | collective-permute-start | bytes 1572872 | tf_op jit(solution)/shard_map/ppermute | solution.py:444
  102.6 9.1 %collective-permute-done.25.refs_1_.refs_10_ = f32[256,512]{1,0:T(8,128)S(1)} collective-permute-done((f32[256,512]{1,0:T(8,128)S(1)}, f32[256,512]{1,0:T(8,128)S(1)}, u32[]{:S(2)}, u32[]{:S(2)}) %collective-permute-start.25) | collective-permute-done | bytes 524320 | tf_op jit(solution)/shard_map/ppermute | solution.py:444
  111.7 3.6 %finish.2 = (f32[2,256,512]{2,1,0:T(8,128)}, f32[2,4,64,512]{3,2,1,0:T(8,128)S(1)}, f32[2,4,64,512]{3,2,1,0:T(8,128)S(1)}, f32[512,512]{1,0:T(8,128)S(1)}, f32[512,512]{1,0:T(8,128)S(1)}) custom-call(s32[3]{0:T(128)S(1)} %pad_add_fusion.refs_0_, s32[2,8]{1,0:T(2,128)S(1)} %copy-done.7, f32[256,512]{1,0:T(8,128)S(1)} %get-tuple-element.70.refs_7_.refs_2_, ...), custom_call_target="tpu_custom_call" | custom-call | tf_op jit(solution)/shard_map/finish/pallas_call | solution.py:36
  121.3 2.9 %collective-permute-start.31 = (f32[2,64,512]{2,1,0:T(8,128)S(1)}, f32[2,64,512]{2,1,0:T(8,128)S(1)}, u32[]{:S(2)}, u32[]{:S(2)}) collective-permute-start(f32[2,64,512]{2,1,0:T(8,128)S(1)} %get-tuple-element.86), channel_id=1, source_target_pairs={{0,6},{1,7},{2,4},{3,5},{4,2},{5,3},{6,0},{7,1},{8,14},{9,15},{10,... | collective-permute-start | bytes 786440 | tf_op jit(solution)/shard_map/ppermute | solution.py:22
  124.1 2.3 %rest.1 = (f32[512,512]{1,0:T(8,128)S(1)}, f32[256,512]{1,0:T(8,128)S(1)}) custom-call(f32[1,512,512]{2,1,0:T(8,128)S(1)} %copy-done.4, f32[512,512]{1,0:T(8,128)S(1)} %get-tuple-element.76.refs_1_, f32[512,512]{1,0:T(8,128)S(1)} %get-tuple-element.77.refs_2_, f32[2,256,512]{2,1,0:T(8,128)S(1)} %copy-done.5), custom_call_target="tpu_custom_call" | custom-call | tf_op jit(solution)/shard_map/rest/pallas_call | solution.py:36
  126.4 3.4 %collective-permute-done.29.refs_2_ = f32[2,64,512]{2,1,0:T(8,128)S(1)} collective-permute-done((f32[2,64,512]{2,1,0:T(8,128)S(1)}, f32[2,64,512]{2,1,0:T(8,128)S(1)}, u32[]{:S(2)}, u32[]{:S(2)}) %collective-permute-start.29) | collective-permute-done | bytes 262176 | tf_op jit(solution)/shard_map/ppermute | solution.py:22
  129.9 4.5 %collective-permute-done.30.refs_3_ = f32[2,64,512]{2,1,0:T(8,128)S(1)} collective-permute-done((f32[2,64,512]{2,1,0:T(8,128)S(1)}, f32[2,64,512]{2,1,0:T(8,128)S(1)}, u32[]{:S(2)}, u32[]{:S(2)}) %collective-permute-start.30) | collective-permute-done | bytes 262176 | tf_op jit(solution)/shard_map/ppermute | solution.py:22
  135.0 9.4 %collective-permute-done.26.refs_5_ = f32[256,512]{1,0:T(8,128)S(1)} collective-permute-done((f32[256,512]{1,0:T(8,128)S(1)}, f32[256,512]{1,0:T(8,128)S(1)}, u32[]{:S(2)}, u32[]{:S(2)}) %collective-permute-start.26) | collective-permute-done | bytes 524320 | tf_op jit(solution)/shard_map/ppermute | solution.py:448
  144.3 2.9 %finish.3 = (f32[2,256,512]{2,1,0:T(8,128)}, f32[1,4,64,512]{3,2,1,0:T(8,128)S(1)}, f32[1,4,64,512]{3,2,1,0:T(8,128)S(1)}) custom-call(s32[3]{0:T(128)S(1)} %pad_add_fusion.refs_0_, s32[2,8]{1,0:T(2,128)S(1)} %copy-done.7, f32[256,512]{1,0:T(8,128)S(1)} %get-tuple-element.71.refs_2_, ...), custom_call_target="tpu_custom_call", output_to_operand_aliasing={{0}: (9, {})} | custom-call | tf_op jit(solution)/shard_map/finish/pallas_call | solution.py:36
  150.6 2.8 %collective-permute-start.38 = (f32[1,64,512]{2,1,0:T(8,128)S(1)}, f32[1,64,512]{2,1,0:T(8,128)S(1)}, u32[]{:S(2)}, u32[]{:S(2)}) collective-permute-start(f32[1,64,512]{2,1,0:T(8,128)S(1)} %get-tuple-element.96), channel_id=1, source_target_pairs={{0,6},{1,7},{2,4},{3,5},{4,2},{5,3},{6,0},{7,1},{8,14},{9,15},{10,... | collective-permute-start | bytes 393224 | tf_op jit(solution)/shard_map/ppermute | solution.py:22
  156.2 2.5 %collective-permute-done.37.refs_2_ = f32[1,64,512]{2,1,0:T(8,128)S(1)} collective-permute-done((f32[1,64,512]{2,1,0:T(8,128)S(1)}, f32[1,64,512]{2,1,0:T(8,128)S(1)}, u32[]{:S(2)}, u32[]{:S(2)}) %collective-permute-start.37) | collective-permute-done | bytes 131104 | tf_op jit(solution)/shard_map/ppermute | solution.py:22
  158.9 3.2 %collective-permute-done.33.refs_1_ = f32[64,512]{1,0:T(8,128)S(1)} collective-permute-done((f32[64,512]{1,0:T(8,128)S(1)}, f32[64,512]{1,0:T(8,128)S(1)}, u32[]{:S(2)}, u32[]{:S(2)}) %collective-permute-start.33) | collective-permute-done | bytes 131104 | tf_op jit(solution)/shard_map/ppermute | solution.py:22
  162.2 2.7 %collective-permute-done.39.refs_1_ = f32[1,64,512]{2,1,0:T(8,128)S(1)} collective-permute-done((f32[1,64,512]{2,1,0:T(8,128)S(1)}, f32[1,64,512]{2,1,0:T(8,128)S(1)}, u32[]{:S(2)}, u32[]{:S(2)}) %collective-permute-start.39) | collective-permute-done | bytes 131104 | tf_op jit(solution)/shard_map/ppermute | solution.py:22
  164.9 2.7 %collective-permute-done.34.refs_4_ = f32[64,512]{1,0:T(8,128)S(1)} collective-permute-done((f32[64,512]{1,0:T(8,128)S(1)}, f32[64,512]{1,0:T(8,128)S(1)}, u32[]{:S(2)}, u32[]{:S(2)}) %collective-permute-start.34) | collective-permute-done | bytes 131104 | tf_op jit(solution)/shard_map/ppermute | solution.py:22
  167.6 5.2 %collective-permute-done.40.refs_6_ = f32[1,64,512]{2,1,0:T(8,128)S(1)} collective-permute-done((f32[1,64,512]{2,1,0:T(8,128)S(1)}, f32[1,64,512]{2,1,0:T(8,128)S(1)}, u32[]{:S(2)}, u32[]{:S(2)}) %collective-permute-start.40) | collective-permute-done | bytes 131104 | tf_op jit(solution)/shard_map/ppermute | solution.py:22
  (99 shorter events, 46.7 us)
Async XLA Ops:
  2.6 6.9 %collective-permute-start = (f32[256,128]{1,0:T(8,128)S(1)}, f32[256,128]{1,0:T(8,128)S(1)}, u32[]{:S(2)}, u32[]{:S(2)}) collective-permute-start(f32[256,128]{1,0:T(8,128)S(1)} %get-tuple-element.52), channel_id=1, source_target_pairs={{0,2},{1,3},{2,0},{3,1},{4,6},{5,7},{6,4},{7,5},{8,10},{9,11},{10,... | collective-permute-start | bytes 393224 | tf_op jit(solution)/shard_map/ppermute | solution.py:22
  5.6 7.8 %collective-permute-start.1 = (f32[256,128]{1,0:T(8,128)S(1)}, f32[256,128]{1,0:T(8,128)S(1)}, u32[]{:S(2)}, u32[]{:S(2)}) collective-permute-start(f32[256,128]{1,0:T(8,128)S(1)} %get-tuple-element.53), channel_id=1, source_target_pairs={{0,4},{1,5},{2,6},{3,7},{4,0},{5,1},{6,2},{7,3},{8,12},{9,13},{10,... | collective-permute-start | bytes 393224 | tf_op jit(solution)/shard_map/ppermute | solution.py:22
  7.1 6.3 %collective-permute-start.2 = (f32[256,128]{1,0:T(8,128)S(1)}, f32[256,128]{1,0:T(8,128)S(1)}, u32[]{:S(2)}, u32[]{:S(2)}) collective-permute-start(f32[256,128]{1,0:T(8,128)S(1)} %get-tuple-element.54), channel_id=1, source_target_pairs={{0,6},{1,7},{2,4},{3,5},{4,2},{5,3},{6,0},{7,1},{8,14},{9,15},{10,... | collective-permute-start | bytes 393224 | tf_op jit(solution)/shard_map/ppermute | solution.py:22
  14.0 8.4 %collective-permute-start.6 = (f32[256,128]{1,0:T(8,128)S(1)}, f32[256,128]{1,0:T(8,128)S(1)}, u32[]{:S(2)}, u32[]{:S(2)}) collective-permute-start(f32[256,128]{1,0:T(8,128)S(1)} %get-tuple-element.60), channel_id=1, source_target_pairs={{0,8},{8,0},{16,24},{24,16},{1,9},{9,1},{17,25},{25,17},{2,10},{10... | collective-permute-start | bytes 393224 | tf_op jit(solution)/shard_map/ppermute | solution.py:22
  15.6 11.6 %collective-permute-start.7 = (f32[256,128]{1,0:T(8,128)S(1)}, f32[256,128]{1,0:T(8,128)S(1)}, u32[]{:S(2)}, u32[]{:S(2)}) collective-permute-start(f32[256,128]{1,0:T(8,128)S(1)} %get-tuple-element.61), channel_id=1, source_target_pairs={{0,16},{8,24},{16,0},{24,8},{1,17},{9,25},{17,1},{25,9},{2,18},{10... | collective-permute-start | bytes 393224 | tf_op jit(solution)/shard_map/ppermute | solution.py:22
  18.2 9.0 %collective-permute-start.8 = (f32[256,128]{1,0:T(8,128)S(1)}, f32[256,128]{1,0:T(8,128)S(1)}, u32[]{:S(2)}, u32[]{:S(2)}) collective-permute-start(f32[256,128]{1,0:T(8,128)S(1)} %get-tuple-element.62), channel_id=1, source_target_pairs={{0,24},{8,16},{16,8},{24,0},{1,25},{9,17},{17,9},{25,1},{2,26},{10... | collective-permute-start | bytes 393224 | tf_op jit(solution)/shard_map/ppermute | solution.py:22
  20.3 6.9 %collective-permute-start.3 = (f32[256,128]{1,0:T(8,128)S(1)}, f32[256,128]{1,0:T(8,128)S(1)}, u32[]{:S(2)}, u32[]{:S(2)}) collective-permute-start(f32[256,128]{1,0:T(8,128)S(1)} %get-tuple-element.57), channel_id=1, source_target_pairs={{0,2},{1,3},{2,0},{3,1},{4,6},{5,7},{6,4},{7,5},{8,10},{9,11},{10,... | collective-permute-start | bytes 393224 | tf_op jit(solution)/shard_map/ppermute | solution.py:22
  28.8 19.7 %collective-permute-start.14 = (f32[4,256,128]{2,1,0:T(8,128)S(1)}, f32[4,256,128]{2,1,0:T(8,128)S(1)}, u32[]{:S(2)}, u32[]{:S(2)}) collective-permute-start(f32[4,256,128]{2,1,0:T(8,128)S(1)} %arrange.2.refs_0_), channel_id=1, source_target_pairs={{0,6},{1,7},{2,4},{3,5},{4,2},{5,3},{6,0},{7,1},{8,14},{9,15},{10,... | collective-permute-start | bytes 1572872 | tf_op jit(solution)/shard_map/ppermute | solution.py:22
  30.3 21.2 %collective-permute-start.13 = (f32[4,256,128]{2,1,0:T(8,128)S(1)}, f32[4,256,128]{2,1,0:T(8,128)S(1)}, u32[]{:S(2)}, u32[]{:S(2)}) collective-permute-start(f32[4,256,128]{2,1,0:T(8,128)S(1)} %arrange.2.refs_0_), channel_id=1, source_target_pairs={{0,4},{1,5},{2,6},{3,7},{4,0},{5,1},{6,2},{7,3},{8,12},{9,13},{10,... | collective-permute-start | bytes 1572872 | tf_op jit(solution)/shard_map/ppermute | solution.py:22
  31.8 20.4 %collective-permute-start.12 = (f32[4,256,128]{2,1,0:T(8,128)S(1)}, f32[4,256,128]{2,1,0:T(8,128)S(1)}, u32[]{:S(2)}, u32[]{:S(2)}) collective-permute-start(f32[4,256,128]{2,1,0:T(8,128)S(1)} %arrange.2.refs_0_), channel_id=1, source_target_pairs={{0,2},{1,3},{2,0},{3,1},{4,6},{5,7},{6,4},{7,5},{8,10},{9,11},{10,... | collective-permute-start | bytes 1572872 | tf_op jit(solution)/shard_map/ppermute | solution.py:22
  34.0 14.5 %collective-permute-start.10 = (f32[256,128]{1,0:T(8,128)S(1)}, f32[256,128]{1,0:T(8,128)S(1)}, u32[]{:S(2)}, u32[]{:S(2)}) collective-permute-start(f32[256,128]{1,0:T(8,128)S(1)} %get-tuple-element.65), channel_id=1, source_target_pairs={{0,16},{8,24},{16,0},{24,8},{1,17},{9,25},{17,1},{25,9},{2,18},{10... | collective-permute-start | bytes 393224 | tf_op jit(solution)/shard_map/ppermute | solution.py:22
  38.3 10.2 %collective-permute-start.11 = (f32[256,128]{1,0:T(8,128)S(1)}, f32[256,128]{1,0:T(8,128)S(1)}, u32[]{:S(2)}, u32[]{:S(2)}) collective-permute-start(f32[256,128]{1,0:T(8,128)S(1)} %get-tuple-element.66), channel_id=1, source_target_pairs={{0,24},{8,16},{16,8},{24,0},{1,25},{9,17},{17,9},{25,1},{2,26},{10... | collective-permute-start | bytes 393224 | tf_op jit(solution)/shard_map/ppermute | solution.py:22
  53.0 15.7 %collective-permute-start.17 = (f32[4,256,128]{2,1,0:T(8,128)S(1)}, f32[4,256,128]{2,1,0:T(8,128)S(1)}, u32[]{:S(2)}, u32[]{:S(2)}) collective-permute-start(f32[4,256,128]{2,1,0:T(8,128)S(1)} %arrange.3.refs_0_), channel_id=1, source_target_pairs={{0,6},{1,7},{2,4},{3,5},{4,2},{5,3},{6,0},{7,1},{8,14},{9,15},{10,... | collective-permute-start | bytes 1572872 | tf_op jit(solution)/shard_map/ppermute | solution.py:22
  53.7 25.3 %collective-permute-start.16 = (f32[4,256,128]{2,1,0:T(8,128)S(1)}, f32[4,256,128]{2,1,0:T(8,128)S(1)}, u32[]{:S(2)}, u32[]{:S(2)}) collective-permute-start(f32[4,256,128]{2,1,0:T(8,128)S(1)} %arrange.3.refs_0_), channel_id=1, source_target_pairs={{0,4},{1,5},{2,6},{3,7},{4,0},{5,1},{6,2},{7,3},{8,12},{9,13},{10,... | collective-permute-start | bytes 1572872 | tf_op jit(solution)/shard_map/ppermute | solution.py:22
  54.8 24.1 %collective-permute-start.15 = (f32[4,256,128]{2,1,0:T(8,128)S(1)}, f32[4,256,128]{2,1,0:T(8,128)S(1)}, u32[]{:S(2)}, u32[]{:S(2)}) collective-permute-start(f32[4,256,128]{2,1,0:T(8,128)S(1)} %arrange.3.refs_0_), channel_id=1, source_target_pairs={{0,2},{1,3},{2,0},{3,1},{4,6},{5,7},{6,4},{7,5},{8,10},{9,11},{10,... | collective-permute-start | bytes 1572872 | tf_op jit(solution)/shard_map/ppermute | solution.py:22
  58.5 20.5 %collective-permute-start.19 = (f32[256,512]{1,0:T(8,128)S(1)}, f32[256,512]{1,0:T(8,128)S(1)}, u32[]{:S(2)}, u32[]{:S(2)}) collective-permute-start(f32[256,512]{1,0:T(8,128)S(1)} %get-tuple-element.68), channel_id=1, source_target_pairs={{0,16},{16,24},{24,8},{8,0},{1,17},{17,25},{25,9},{9,1},{2,18},{18... | collective-permute-start | bytes 1572872 | tf_op jit(solution)/shard_map/ppermute | solution.py:445
  61.4 22.7 %collective-permute-start.21 = (f32[256,512]{1,0:T(8,128)S(1)}, f32[256,512]{1,0:T(8,128)S(1)}, u32[]{:S(2)}, u32[]{:S(2)}) collective-permute-start(f32[256,512]{1,0:T(8,128)S(1)} %get-tuple-element.69), channel_id=1, source_target_pairs={{0,8},{24,16},{1,9},{25,17},{2,10},{26,18},{3,11},{27,19},{4,12},{... | collective-permute-start | bytes 1572872 | tf_op jit(solution)/shard_map/ppermute | solution.py:444
  68.8 15.3 %collective-permute-start.20 = (f32[256,512]{1,0:T(8,128)S(1)}, f32[256,512]{1,0:T(8,128)S(1)}, u32[]{:S(2)}, u32[]{:S(2)}) collective-permute-start(f32[256,512]{1,0:T(8,128)S(1)} %get-tuple-element.69), channel_id=1, source_target_pairs={{8,16},{16,8},{9,17},{17,9},{10,18},{18,10},{11,19},{19,11},{12,20... | collective-permute-start | bytes 1572872 | tf_op jit(solution)/shard_map/ppermute | solution.py:446
  84.4 18.2 %collective-permute-start.27 = (f32[256,512]{1,0:T(8,128)S(1)}, f32[256,512]{1,0:T(8,128)S(1)}, u32[]{:S(2)}, u32[]{:S(2)}) collective-permute-start(f32[256,512]{1,0:T(8,128)S(1)} %add_up.7), channel_id=1, source_target_pairs={{8,24},{16,0},{0,8},{24,16},{9,25},{17,1},{1,9},{25,17},{10,26},{1... | collective-permute-start | bytes 1572872 | tf_op jit(solution)/shard_map/ppermute | solution.py:448
  95.6 16.1 %collective-permute-start.25 = (f32[256,512]{1,0:T(8,128)S(1)}, f32[256,512]{1,0:T(8,128)S(1)}, u32[]{:S(2)}, u32[]{:S(2)}) collective-permute-start(f32[256,512]{1,0:T(8,128)S(1)} %get-tuple-element.73), channel_id=1, source_target_pairs={{0,8},{24,16},{1,9},{25,17},{2,10},{26,18},{3,11},{27,19},{4,12},{... | collective-permute-start | bytes 1572872 | tf_op jit(solution)/shard_map/ppermute | solution.py:444
  100.3 11.3 %collective-permute-start.24 = (f32[256,512]{1,0:T(8,128)S(1)}, f32[256,512]{1,0:T(8,128)S(1)}, u32[]{:S(2)}, u32[]{:S(2)}) collective-permute-start(f32[256,512]{1,0:T(8,128)S(1)} %get-tuple-element.73), channel_id=1, source_target_pairs={{8,16},{16,8},{9,17},{17,9},{10,18},{18,10},{11,19},{19,11},{12,20... | collective-permute-start | bytes 1572872 | tf_op jit(solution)/shard_map/ppermute | solution.py:446
  116.7 18.3 %collective-permute-start.23 = (f32[256,512]{1,0:T(8,128)S(1)}, f32[256,512]{1,0:T(8,128)S(1)}, u32[]{:S(2)}, u32[]{:S(2)}) collective-permute-start(f32[256,512]{1,0:T(8,128)S(1)} %get-tuple-element.72), channel_id=1, source_target_pairs={{0,16},{16,24},{24,8},{8,0},{1,17},{17,25},{25,9},{9,1},{2,18},{18... | collective-permute-start | bytes 1572872 | tf_op jit(solution)/shard_map/ppermute | solution.py:445
  118.6 25.8 %collective-permute-start.26 = (f32[256,512]{1,0:T(8,128)S(1)}, f32[256,512]{1,0:T(8,128)S(1)}, u32[]{:S(2)}, u32[]{:S(2)}) collective-permute-start(f32[256,512]{1,0:T(8,128)S(1)} %add_up.6), channel_id=1, source_target_pairs={{8,24},{16,0},{0,8},{24,16},{9,25},{17,1},{1,9},{25,17},{10,26},{1... | collective-permute-start | bytes 1572872 | tf_op jit(solution)/shard_map/ppermute | solution.py:448
  120.6 9.3 %collective-permute-start.29 = (f32[2,64,512]{2,1,0:T(8,128)S(1)}, f32[2,64,512]{2,1,0:T(8,128)S(1)}, u32[]{:S(2)}, u32[]{:S(2)}) collective-permute-start(f32[2,64,512]{2,1,0:T(8,128)S(1)} %get-tuple-element.84), channel_id=1, source_target_pairs={{0,2},{1,3},{2,0},{3,1},{4,6},{5,7},{6,4},{7,5},{8,10},{9,11},{10,... | collective-permute-start | bytes 786440 | tf_op jit(solution)/shard_map/ppermute | solution.py:22
  120.7 13.7 %collective-permute-start.30 = (f32[2,64,512]{2,1,0:T(8,128)S(1)}, f32[2,64,512]{2,1,0:T(8,128)S(1)}, u32[]{:S(2)}, u32[]{:S(2)}) collective-permute-start(f32[2,64,512]{2,1,0:T(8,128)S(1)} %get-tuple-element.85), channel_id=1, source_target_pairs={{0,4},{1,5},{2,6},{3,7},{4,0},{5,1},{6,2},{7,3},{8,12},{9,13},{10,... | collective-permute-start | bytes 786440 | tf_op jit(solution)/shard_map/ppermute | solution.py:22
  121.3 13.1 %collective-permute-start.31 = (f32[2,64,512]{2,1,0:T(8,128)S(1)}, f32[2,64,512]{2,1,0:T(8,128)S(1)}, u32[]{:S(2)}, u32[]{:S(2)}) collective-permute-start(f32[2,64,512]{2,1,0:T(8,128)S(1)} %get-tuple-element.86), channel_id=1, source_target_pairs={{0,6},{1,7},{2,4},{3,5},{4,2},{5,3},{6,0},{7,1},{8,14},{9,15},{10,... | collective-permute-start | bytes 786440 | tf_op jit(solution)/shard_map/ppermute | solution.py:22
  149.8 6.4 %collective-permute-start.36 = (f32[1,64,512]{2,1,0:T(8,128)S(1)}, f32[1,64,512]{2,1,0:T(8,128)S(1)}, u32[]{:S(2)}, u32[]{:S(2)}) collective-permute-start(f32[1,64,512]{2,1,0:T(8,128)S(1)} %get-tuple-element.94), channel_id=1, source_target_pairs={{0,2},{1,3},{2,0},{3,1},{4,6},{5,7},{6,4},{7,5},{8,10},{9,11},{10,... | collective-permute-start | bytes 393224 | tf_op jit(solution)/shard_map/ppermute | solution.py:22
  150.6 8.1 %collective-permute-start.37 = (f32[1,64,512]{2,1,0:T(8,128)S(1)}, f32[1,64,512]{2,1,0:T(8,128)S(1)}, u32[]{:S(2)}, u32[]{:S(2)}) collective-permute-start(f32[1,64,512]{2,1,0:T(8,128)S(1)} %get-tuple-element.95), channel_id=1, source_target_pairs={{0,4},{1,5},{2,6},{3,7},{4,0},{5,1},{6,2},{7,3},{8,12},{9,13},{10,... | collective-permute-start | bytes 393224 | tf_op jit(solution)/shard_map/ppermute | solution.py:22
  150.6 8.1 %collective-permute-start.38 = (f32[1,64,512]{2,1,0:T(8,128)S(1)}, f32[1,64,512]{2,1,0:T(8,128)S(1)}, u32[]{:S(2)}, u32[]{:S(2)}) collective-permute-start(f32[1,64,512]{2,1,0:T(8,128)S(1)} %get-tuple-element.96), channel_id=1, source_target_pairs={{0,6},{1,7},{2,4},{3,5},{4,2},{5,3},{6,0},{7,1},{8,14},{9,15},{10,... | collective-permute-start | bytes 393224 | tf_op jit(solution)/shard_map/ppermute | solution.py:22
  153.3 8.8 %collective-permute-start.33 = (f32[64,512]{1,0:T(8,128)S(1)}, f32[64,512]{1,0:T(8,128)S(1)}, u32[]{:S(2)}, u32[]{:S(2)}) collective-permute-start(f32[64,512]{1,0:T(8,128)S(1)} %add_up.8.refs_0_), channel_id=1, source_target_pairs={{0,16},{8,24},{16,0},{24,8},{1,17},{9,25},{17,1},{25,9},{2,18},{10... | collective-permute-start | bytes 393224 | tf_op jit(solution)/shard_map/ppermute | solution.py:22
  158.7 6.2 %collective-permute-start.39 = (f32[1,64,512]{2,1,0:T(8,128)S(1)}, f32[1,64,512]{2,1,0:T(8,128)S(1)}, u32[]{:S(2)}, u32[]{:S(2)}) collective-permute-start(f32[1,64,512]{2,1,0:T(8,128)S(1)} %add_up.10.refs_0_), channel_id=1, source_target_pairs={{0,8},{8,0},{16,24},{24,16},{1,9},{9,1},{17,25},{25,17},{2,10},{10... | collective-permute-start | bytes 393224 | tf_op jit(solution)/shard_map/ppermute | solution.py:22
  164.9 7.9 %collective-permute-start.40 = (f32[1,64,512]{2,1,0:T(8,128)S(1)}, f32[1,64,512]{2,1,0:T(8,128)S(1)}, u32[]{:S(2)}, u32[]{:S(2)}) collective-permute-start(f32[1,64,512]{2,1,0:T(8,128)S(1)} %add_up.11.refs_5_), channel_id=1, source_target_pairs={{0,16},{8,24},{16,0},{24,8},{1,17},{9,25},{17,1},{25,9},{2,18},{10... | collective-permute-start | bytes 393224 | tf_op jit(solution)/shard_map/ppermute | solution.py:22
  (20 other events, 195.1 us)

commit v13 on v12

--- a/solution.py
+++ b/solution.py
@@ -529,7 +529,7 @@
             received.append(to_plane(turned[number]))
     waits = [pieces[0] for pieces in received[:1]]
     bases = bases_of(place, diag_inverse, link_factor, columns // pcol_count, waits)
-    rows, gathered = [], []
+    rows, lates, gathered = [], [], []
     for number in range(nsuper):
         if received:
             gathered += [piece for later in sent[number + 1 : number + 2] for piece in later[1:]]
@@ -542,8 +542,8 @@
         else:
             own = to_plane_whole(factor[number], count, ratio)
             pieces = [in_rows(lax.all_gather(own, "pcol", axis=0), count, ratio)]
-        middle = count // 2 if number == 0 and received else count
-        partial, starts = [], [0, middle, count] if middle < count else [0, count]
+        middle = 1 if rows else count // 2
+        partial, starts = [], [0, middle, count] if received else [0, count]
         for start, stop in zip(starts, starts[1:]):
             partial += partial_product(
                 place, slots, ancestors, inverse_tiles, pieces, ratio, columns, number, start, stop,
@@ -552,11 +552,12 @@
         rows.append(sum_over_line(partial, z))
         rows[-1] = rows[-1][:3] + rows[-1][:2:-1]
         late = [partial[-1]]
+        lates.append(late)
 
     sums, before, pending = [], [], []
     for number in range(nsuper):
         last = number + 1 == nsuper
-        waits = [] if last else rows[number + 1][2:4]
+        waits = [] if last else rows[number + 1][2:4] + lates[number + 1]
         offdiag, keep, send, *link = finish(
             number, own_block, place, ancestors, rows[number][:3] + rows[number][4:], factor, before,
             link_factor, pcol_count // 2, waits + pending[:1],

time: 175 us -> 172 us (0.983)
  Pallas kernels: 30.5 us -> 28.1 us
    ppermute x2, starting transfers between devices: 6.89 us -> 3.59 us  [sum_over_four(): last = lax.ppermute(both, 'prow', [(1, 3), (2, 0), (0, 1), (3, 2)])]
    ppermute x2, starting transfers between devices: 4.66 us -> 7.93 us  [sum_over_four(): total = lax.ppermute(slots[1], 'prow', [(0, 2), (2, 3), (3, 1), (1, 0)])]
    ppermute x33, starting transfers between devices: 38.7 us -> 41.5 us  [flip(): lax.ppermute(value, axis, [(i, i ^ bit) for i in range(lax.axis_size(axis...]
    pallas_call x25 -> x26, Pallas kernels: 30.5 us -> 28.1 us  [run(): pl.pallas_call(body, grid_spec=pltpu.PrefetchScalarGridSpec(num_scalar_pr...]
    ppermute x2, waiting for transfers between devices: 10.9 us -> 8.57 us  [sum_over_four(): last = lax.ppermute(both, 'prow', [(1, 3), (2, 0), (0, 1), (3, 2)])]
  transfers between devices with their start and end apart: 41 -> 41, of which waited for: 22 -> 24; matrix products, arithmetic and copies ran while one was open for 0% -> 0% of each run, Pallas kernels for 12% -> 12%
where the time goes in v13:
time: 172 us
  waiting for transfers between devices  76.5 us (44%)
  starting transfers between devices  60.8 us (35%)
  Pallas kernels  28.1 us (16%)
  local copies, waits for them, and re-layouts  5.3 us (3%)
    ppermute x33, waiting for transfers between devices, flip(): lax.ppermute(value, axis, [(i, i ^ bit) for i in range(lax.axis_size(axis...  53.4 us
    ppermute x33, starting transfers between devices, flip(): lax.ppermute(value, axis, [(i, i ^ bit) for i in range(lax.axis_size(axis...  41.5 us
    pallas_call x26, Pallas kernels, run(): pl.pallas_call(body, grid_spec=pltpu.PrefetchScalarGridSpec(num_scalar_pr...  28.1 us
    ppermute x2, waiting for transfers between devices, sum_over_four(): near = lax.ppermute(slots[0], 'prow', [(0, 1), (3, 2)])  14.5 us
    ppermute x2, waiting for transfers between devices, sum_over_four(): last = lax.ppermute(both, 'prow', [(1, 3), (2, 0), (0, 1), (3, 2)])  8.57 us
    ppermute x2, starting transfers between devices, sum_over_four(): total = lax.ppermute(slots[1], 'prow', [(0, 2), (2, 3), (3, 1), (1, 0)])  7.93 us
    ppermute x2, starting transfers between devices, sum_over_four(): near = lax.ppermute(slots[0], 'prow', [(0, 1), (3, 2)])  6.27 us
    unnamed x22, local copies, waits for them, and re-layouts  5.3 us
  transfers between devices with their start and end apart: 41, of which 24 were waited for; matrix products, arithmetic and copies ran while one was open for 0% of the time, Pallas kernels for 12%

profile of v13, /device:TPU:0, one launch (start us, length us, event | category | flops | bytes accessed | tf_op | source)
XLA Modules:
  0.0 171.8 jit_solution(2565920059309694244)
XLA Ops:
  2.6 3.0 %collective-permute-start = (f32[256,128]{1,0:T(8,128)S(1)}, f32[256,128]{1,0:T(8,128)S(1)}, u32[]{:S(2)}, u32[]{:S(2)}) collective-permute-start(f32[256,128]{1,0:T(8,128)S(1)} %get-tuple-element.51), channel_id=1, source_target_pairs={{0,2},{1,3},{2,0},{3,1},{4,6},{5,7},{6,4},{7,5},{8,10},{9,11},{10,... | collective-permute-start | bytes 393224 | tf_op jit(solution)/shard_map/ppermute | solution.py:22
  7.1 2.4 %collective-permute-done.refs_2_ = f32[256,128]{1,0:T(8,128)S(1)} collective-permute-done((f32[256,128]{1,0:T(8,128)S(1)}, f32[256,128]{1,0:T(8,128)S(1)}, u32[]{:S(2)}, u32[]{:S(2)}) %collective-permute-start) | collective-permute-done | bytes 131104 | tf_op jit(solution)/shard_map/ppermute | solution.py:22
  9.5 3.9 %collective-permute-done.1.refs_3_ = f32[256,128]{1,0:T(8,128)S(1)} collective-permute-done((f32[256,128]{1,0:T(8,128)S(1)}, f32[256,128]{1,0:T(8,128)S(1)}, u32[]{:S(2)}, u32[]{:S(2)}) %collective-permute-start.1) | collective-permute-done | bytes 131104 | tf_op jit(solution)/shard_map/ppermute | solution.py:22
  15.6 2.6 %collective-permute-start.7 = (f32[256,128]{1,0:T(8,128)S(1)}, f32[256,128]{1,0:T(8,128)S(1)}, u32[]{:S(2)}, u32[]{:S(2)}) collective-permute-start(f32[256,128]{1,0:T(8,128)S(1)} %get-tuple-element.60), channel_id=1, source_target_pairs={{0,16},{8,24},{16,0},{24,8},{1,17},{9,25},{17,1},{25,9},{2,18},{10... | collective-permute-start | bytes 393224 | tf_op jit(solution)/shard_map/ppermute | solution.py:22
  23.8 3.4 %collective-permute-done.7.refs_6_.refs_3_ = f32[256,128]{1,0:T(8,128)S(1)} collective-permute-done((f32[256,128]{1,0:T(8,128)S(1)}, f32[256,128]{1,0:T(8,128)S(1)}, u32[]{:S(2)}, u32[]{:S(2)}) %collective-permute-start.7) | collective-permute-done | bytes 131104 | tf_op jit(solution)/shard_map/ppermute | solution.py:22
  34.0 3.2 %collective-permute-start.10 = (f32[256,128]{1,0:T(8,128)S(1)}, f32[256,128]{1,0:T(8,128)S(1)}, u32[]{:S(2)}, u32[]{:S(2)}) collective-permute-start(f32[256,128]{1,0:T(8,128)S(1)} %get-tuple-element.64), channel_id=1, source_target_pairs={{0,16},{8,24},{16,0},{24,8},{1,17},{9,25},{17,1},{25,9},{2,18},{10... | collective-permute-start | bytes 393224 | tf_op jit(solution)/shard_map/ppermute | solution.py:22
  38.3 4.9 %collective-permute-start.11 = (f32[256,128]{1,0:T(8,128)S(1)}, f32[256,128]{1,0:T(8,128)S(1)}, u32[]{:S(2)}, u32[]{:S(2)}) collective-permute-start(f32[256,128]{1,0:T(8,128)S(1)} %get-tuple-element.65), channel_id=1, source_target_pairs={{0,24},{8,16},{16,8},{24,0},{1,25},{9,17},{17,9},{25,1},{2,26},{10... | collective-permute-start | bytes 393224 | tf_op jit(solution)/shard_map/ppermute | solution.py:22
  46.0 2.5 %bases.1 = (f32[2,64,512]{2,1,0:T(8,128)S(1)}, f32[1,64,512]{2,1,0:T(8,128)S(1)}) custom-call(s32[3]{0:T(128)S(1)} %pad_add_fusion.refs_0_, f32[2,512,512]{2,1,0:T(8,128)S(1)} %copy-done.6, f32[1,512,512]{2,1,0:T(8,128)S(1)} %copy-done.3, f32[256,128]{1,0:T(8,128)S(1)} %get-tuple-element.54.refs_2_.refs_1_.refs_3_), custom_call_target="tpu_custom_call" | custom-call | tf_op jit(solution)/shard_map/bases/pallas_call | solution.py:36
  48.5 3.0 %collective-permute-done.13.refs_6_.refs_2_ = f32[4,256,128]{2,1,0:T(8,128)S(1)} collective-permute-done((f32[4,256,128]{2,1,0:T(8,128)S(1)}, f32[4,256,128]{2,1,0:T(8,128)S(1)}, u32[]{:S(2)}, u32[]{:S(2)}) %collective-permute-start.13) | collective-permute-done | bytes 524320 | tf_op jit(solution)/shard_map/ppermute | solution.py:22
  58.5 4.6 %collective-permute-start.19 = (f32[256,512]{1,0:T(8,128)S(1)}, f32[256,512]{1,0:T(8,128)S(1)}, u32[]{:S(2)}, u32[]{:S(2)}) collective-permute-start(f32[256,512]{1,0:T(8,128)S(1)} %get-tuple-element.67), channel_id=1, source_target_pairs={{0,16},{16,24},{24,8},{8,0},{1,17},{17,25},{25,9},{9,1},{2,18},{18... | collective-permute-start | bytes 1572872 | tf_op jit(solution)/shard_map/ppermute | solution.py:445
  64.4 4.3 %collective-permute-done.17.refs_3_ = f32[4,256,128]{2,1,0:T(8,128)S(1)} collective-permute-done((f32[4,256,128]{2,1,0:T(8,128)S(1)}, f32[4,256,128]{2,1,0:T(8,128)S(1)}, u32[]{:S(2)}, u32[]{:S(2)}) %collective-permute-start.17) | collective-permute-done | bytes 524320 | tf_op jit(solution)/shard_map/ppermute | solution.py:22
  69.5 3.2 %partial_product.5 = (f32[256,512]{1,0:T(8,128)S(1)}, f32[256,512]{1,0:T(8,128)S(1)}) custom-call(s32[3]{0:T(128)S(1)} %pad_add_fusion.refs_0_, s32[4,4]{1,0:T(4,128)S(1)} %copy-done.8, s32[2,8]{1,0:T(2,128)S(1)} %copy-done.7, f32[1024,2048]{1,0:T(8,128)S(1)} %bitcast.4, f32[4,4,256,128]{3,2,1,0:T(8,128)S(1)} %pack.2.refs_4_, ...), custom_call_target="tpu_custom_call" | custom-call | tf_op jit(solution)/shard_map/partial_product/pallas_call | solution.py:36
  72.6 6.3 %collective-permute-done.16.refs_2_ = f32[4,256,128]{2,1,0:T(8,128)S(1)} collective-permute-done((f32[4,256,128]{2,1,0:T(8,128)S(1)}, f32[4,256,128]{2,1,0:T(8,128)S(1)}, u32[]{:S(2)}, u32[]{:S(2)}) %collective-permute-start.16) | collective-permute-done | bytes 524320 | tf_op jit(solution)/shard_map/ppermute | solution.py:22
  78.9 5.0 %collective-permute-done.21.refs_6_.refs_1_ = f32[256,512]{1,0:T(8,128)S(1)} collective-permute-done((f32[256,512]{1,0:T(8,128)S(1)}, f32[256,512]{1,0:T(8,128)S(1)}, u32[]{:S(2)}, u32[]{:S(2)}) %collective-permute-start.21) | collective-permute-done | bytes 524320 | tf_op jit(solution)/shard_map/ppermute | solution.py:444
  84.3 3.5 %collective-permute-start.27 = (f32[256,512]{1,0:T(8,128)S(1)}, f32[256,512]{1,0:T(8,128)S(1)}, u32[]{:S(2)}, u32[]{:S(2)}) collective-permute-start(f32[256,512]{1,0:T(8,128)S(1)} %add_up.7), channel_id=1, source_target_pairs={{8,24},{16,0},{0,8},{24,16},{9,25},{17,1},{1,9},{25,17},{10,26},{1... | collective-permute-start | bytes 1572872 | tf_op jit(solution)/shard_map/ppermute | solution.py:448
  88.4 3.0 %partial_product.7 = f32[256,512]{1,0:T(8,128)S(1)} custom-call(s32[3]{0:T(128)S(1)} %pad_add_fusion.refs_0_, s32[4,4]{1,0:T(4,128)S(1)} %copy-done.8, s32[2,8]{1,0:T(2,128)S(1)} %copy-done.7, f32[1024,2048]{1,0:T(8,128)S(1)} %bitcast.4, f32[4,4,256,128]{3,2,1,0:T(8,128)S(1)} %pack.3.refs_4_, f32[4,4,256,128]{3,2,1,0:T(8,128)S(1)} %collective-permute-done.22.refs_5_, ...), custom_call_target="tpu_custom_call" | custom-call | tf_op jit(solution)/shard_map/partial_product/pallas_call | solution.py:36
  91.4 5.0 %collective-permute-start.25 = (f32[256,512]{1,0:T(8,128)S(1)}, f32[256,512]{1,0:T(8,128)S(1)}, u32[]{:S(2)}, u32[]{:S(2)}) collective-permute-start(f32[256,512]{1,0:T(8,128)S(1)} %partial_product.7), channel_id=1, source_target_pairs={{0,8},{24,16},{1,9},{25,17},{2,10},{26,18},{3,11},{27,19},{4,12},{... | collective-permute-start | bytes 1572872 | tf_op jit(solution)/shard_map/ppermute | solution.py:444
  97.3 3.2 %partial_product.6 = (f32[256,512]{1,0:T(8,128)S(1)}, f32[256,512]{1,0:T(8,128)S(1)}, f32[256,512]{1,0:T(8,128)S(1)}) custom-call(s32[3]{0:T(128)S(1)} %pad_add_fusion.refs_0_, s32[4,4]{1,0:T(4,128)S(1)} %copy-done.8, s32[2,8]{1,0:T(2,128)S(1)} %copy-done.7, f32[1024,2048]{1,0:T(8,128)S(1)} %bitcast.4, f32[4,4,256,128]{3,2,1,0:T(8,128)S(1)} %pack.3.refs_4_, ...), custom_call_target="tpu_custom_call" | custom-call | tf_op jit(solution)/shard_map/partial_product/pallas_call | solution.py:36
  101.4 9.4 %collective-permute-done.25.refs_1_.refs_10_ = f32[256,512]{1,0:T(8,128)S(1)} collective-permute-done((f32[256,512]{1,0:T(8,128)S(1)}, f32[256,512]{1,0:T(8,128)S(1)}, u32[]{:S(2)}, u32[]{:S(2)}) %collective-permute-start.25) | collective-permute-done | bytes 524320 | tf_op jit(solution)/shard_map/ppermute | solution.py:444
  110.9 2.7 %finish.2 = (f32[2,256,512]{2,1,0:T(8,128)}, f32[2,4,64,512]{3,2,1,0:T(8,128)S(1)}, f32[2,4,64,512]{3,2,1,0:T(8,128)S(1)}, f32[512,512]{1,0:T(8,128)S(1)}, f32[512,512]{1,0:T(8,128)S(1)}) custom-call(s32[3]{0:T(128)S(1)} %pad_add_fusion.refs_0_, s32[2,8]{1,0:T(2,128)S(1)} %copy-done.7, f32[256,512]{1,0:T(8,128)S(1)} %get-tuple-element.69.refs_7_.refs_2_, ...), custom_call_target="tpu_custom_call" | custom-call | tf_op jit(solution)/shard_map/finish/pallas_call | solution.py:36
  113.6 3.3 %collective-permute-start.23 = (f32[256,512]{1,0:T(8,128)S(1)}, f32[256,512]{1,0:T(8,128)S(1)}, u32[]{:S(2)}, u32[]{:S(2)}) collective-permute-start(f32[256,512]{1,0:T(8,128)S(1)} %get-tuple-element.71), channel_id=1, source_target_pairs={{0,16},{16,24},{24,8},{8,0},{1,17},{17,25},{25,9},{9,1},{2,18},{18... | collective-permute-start | bytes 1572872 | tf_op jit(solution)/shard_map/ppermute | solution.py:445
  117.7 2.5 %collective-permute-start.29 = (f32[2,64,512]{2,1,0:T(8,128)S(1)}, f32[2,64,512]{2,1,0:T(8,128)S(1)}, u32[]{:S(2)}, u32[]{:S(2)}) collective-permute-start(f32[2,64,512]{2,1,0:T(8,128)S(1)} %get-tuple-element.82), channel_id=1, source_target_pairs={{0,2},{1,3},{2,0},{3,1},{4,6},{5,7},{6,4},{7,5},{8,10},{9,11},{10,... | collective-permute-start | bytes 786440 | tf_op jit(solution)/shard_map/ppermute | solution.py:22
  122.2 2.3 %rest.1 = (f32[512,512]{1,0:T(8,128)S(1)}, f32[256,512]{1,0:T(8,128)S(1)}) custom-call(f32[1,512,512]{2,1,0:T(8,128)S(1)} %copy-done.4, f32[512,512]{1,0:T(8,128)S(1)} %get-tuple-element.74.refs_1_, f32[512,512]{1,0:T(8,128)S(1)} %get-tuple-element.75.refs_2_, f32[2,256,512]{2,1,0:T(8,128)S(1)} %copy-done.5), custom_call_target="tpu_custom_call" | custom-call | tf_op jit(solution)/shard_map/rest/pallas_call | solution.py:36
  124.5 2.9 %collective-permute-done.29.refs_2_ = f32[2,64,512]{2,1,0:T(8,128)S(1)} collective-permute-done((f32[2,64,512]{2,1,0:T(8,128)S(1)}, f32[2,64,512]{2,1,0:T(8,128)S(1)}, u32[]{:S(2)}, u32[]{:S(2)}) %collective-permute-start.29) | collective-permute-done | bytes 262176 | tf_op jit(solution)/shard_map/ppermute | solution.py:22
  127.4 5.2 %collective-permute-done.30.refs_3_ = f32[2,64,512]{2,1,0:T(8,128)S(1)} collective-permute-done((f32[2,64,512]{2,1,0:T(8,128)S(1)}, f32[2,64,512]{2,1,0:T(8,128)S(1)}, u32[]{:S(2)}, u32[]{:S(2)}) %collective-permute-start.30) | collective-permute-done | bytes 262176 | tf_op jit(solution)/shard_map/ppermute | solution.py:22
  134.4 7.6 %collective-permute-done.26.refs_5_ = f32[256,512]{1,0:T(8,128)S(1)} collective-permute-done((f32[256,512]{1,0:T(8,128)S(1)}, f32[256,512]{1,0:T(8,128)S(1)}, u32[]{:S(2)}, u32[]{:S(2)}) %collective-permute-start.26) | collective-permute-done | bytes 524320 | tf_op jit(solution)/shard_map/ppermute | solution.py:448
  142.0 2.1 %finish.3 = (f32[2,256,512]{2,1,0:T(8,128)}, f32[1,4,64,512]{3,2,1,0:T(8,128)S(1)}, f32[1,4,64,512]{3,2,1,0:T(8,128)S(1)}) custom-call(s32[3]{0:T(128)S(1)} %pad_add_fusion.refs_0_, s32[2,8]{1,0:T(2,128)S(1)} %copy-done.7, f32[256,512]{1,0:T(8,128)S(1)} %get-tuple-element.70.refs_11_.refs_2_, ...), custom_call_target="tpu_custom_call", output_to_operand_aliasing={{0}: (9, {})} | custom-call | tf_op jit(solution)/shard_map/finish/pallas_call | solution.py:36
  148.1 2.6 %collective-permute-start.37 = (f32[1,64,512]{2,1,0:T(8,128)S(1)}, f32[1,64,512]{2,1,0:T(8,128)S(1)}, u32[]{:S(2)}, u32[]{:S(2)}) collective-permute-start(f32[1,64,512]{2,1,0:T(8,128)S(1)} %get-tuple-element.93), channel_id=1, source_target_pairs={{0,4},{1,5},{2,6},{3,7},{4,0},{5,1},{6,2},{7,3},{8,12},{9,13},{10,... | collective-permute-start | bytes 393224 | tf_op jit(solution)/shard_map/ppermute | solution.py:22
  153.1 4.1 %collective-permute-done.37.refs_2_ = f32[1,64,512]{2,1,0:T(8,128)S(1)} collective-permute-done((f32[1,64,512]{2,1,0:T(8,128)S(1)}, f32[1,64,512]{2,1,0:T(8,128)S(1)}, u32[]{:S(2)}, u32[]{:S(2)}) %collective-permute-start.37) | collective-permute-done | bytes 131104 | tf_op jit(solution)/shard_map/ppermute | solution.py:22
  159.8 3.0 %collective-permute-done.39.refs_1_ = f32[1,64,512]{2,1,0:T(8,128)S(1)} collective-permute-done((f32[1,64,512]{2,1,0:T(8,128)S(1)}, f32[1,64,512]{2,1,0:T(8,128)S(1)}, u32[]{:S(2)}, u32[]{:S(2)}) %collective-permute-start.39) | collective-permute-done | bytes 131104 | tf_op jit(solution)/shard_map/ppermute | solution.py:22
  164.1 2.3 %collective-permute-done.34.refs_4_ = f32[64,512]{1,0:T(8,128)S(1)} collective-permute-done((f32[64,512]{1,0:T(8,128)S(1)}, f32[64,512]{1,0:T(8,128)S(1)}, u32[]{:S(2)}, u32[]{:S(2)}) %collective-permute-start.34) | collective-permute-done | bytes 131104 | tf_op jit(solution)/shard_map/ppermute | solution.py:22
  166.5 4.0 %collective-permute-done.40.refs_6_ = f32[1,64,512]{2,1,0:T(8,128)S(1)} collective-permute-done((f32[1,64,512]{2,1,0:T(8,128)S(1)}, f32[1,64,512]{2,1,0:T(8,128)S(1)}, u32[]{:S(2)}, u32[]{:S(2)}) %collective-permute-start.40) | collective-permute-done | bytes 131104 | tf_op jit(solution)/shard_map/ppermute | solution.py:22
  (100 shorter events, 49.9 us)
Async XLA Ops:
  2.6 6.9 %collective-permute-start = (f32[256,128]{1,0:T(8,128)S(1)}, f32[256,128]{1,0:T(8,128)S(1)}, u32[]{:S(2)}, u32[]{:S(2)}) collective-permute-start(f32[256,128]{1,0:T(8,128)S(1)} %get-tuple-element.51), channel_id=1, source_target_pairs={{0,2},{1,3},{2,0},{3,1},{4,6},{5,7},{6,4},{7,5},{8,10},{9,11},{10,... | collective-permute-start | bytes 393224 | tf_op jit(solution)/shard_map/ppermute | solution.py:22
  5.6 7.8 %collective-permute-start.1 = (f32[256,128]{1,0:T(8,128)S(1)}, f32[256,128]{1,0:T(8,128)S(1)}, u32[]{:S(2)}, u32[]{:S(2)}) collective-permute-start(f32[256,128]{1,0:T(8,128)S(1)} %get-tuple-element.52), channel_id=1, source_target_pairs={{0,4},{1,5},{2,6},{3,7},{4,0},{5,1},{6,2},{7,3},{8,12},{9,13},{10,... | collective-permute-start | bytes 393224 | tf_op jit(solution)/shard_map/ppermute | solution.py:22
  7.1 6.3 %collective-permute-start.2 = (f32[256,128]{1,0:T(8,128)S(1)}, f32[256,128]{1,0:T(8,128)S(1)}, u32[]{:S(2)}, u32[]{:S(2)}) collective-permute-start(f32[256,128]{1,0:T(8,128)S(1)} %get-tuple-element.53), channel_id=1, source_target_pairs={{0,6},{1,7},{2,4},{3,5},{4,2},{5,3},{6,0},{7,1},{8,14},{9,15},{10,... | collective-permute-start | bytes 393224 | tf_op jit(solution)/shard_map/ppermute | solution.py:22
  14.0 8.4 %collective-permute-start.6 = (f32[256,128]{1,0:T(8,128)S(1)}, f32[256,128]{1,0:T(8,128)S(1)}, u32[]{:S(2)}, u32[]{:S(2)}) collective-permute-start(f32[256,128]{1,0:T(8,128)S(1)} %get-tuple-element.59), channel_id=1, source_target_pairs={{0,8},{8,0},{16,24},{24,16},{1,9},{9,1},{17,25},{25,17},{2,10},{10... | collective-permute-start | bytes 393224 | tf_op jit(solution)/shard_map/ppermute | solution.py:22
  15.6 11.6 %collective-permute-start.7 = (f32[256,128]{1,0:T(8,128)S(1)}, f32[256,128]{1,0:T(8,128)S(1)}, u32[]{:S(2)}, u32[]{:S(2)}) collective-permute-start(f32[256,128]{1,0:T(8,128)S(1)} %get-tuple-element.60), channel_id=1, source_target_pairs={{0,16},{8,24},{16,0},{24,8},{1,17},{9,25},{17,1},{25,9},{2,18},{10... | collective-permute-start | bytes 393224 | tf_op jit(solution)/shard_map/ppermute | solution.py:22
  18.2 9.0 %collective-permute-start.8 = (f32[256,128]{1,0:T(8,128)S(1)}, f32[256,128]{1,0:T(8,128)S(1)}, u32[]{:S(2)}, u32[]{:S(2)}) collective-permute-start(f32[256,128]{1,0:T(8,128)S(1)} %get-tuple-element.61), channel_id=1, source_target_pairs={{0,24},{8,16},{16,8},{24,0},{1,25},{9,17},{17,9},{25,1},{2,26},{10... | collective-permute-start | bytes 393224 | tf_op jit(solution)/shard_map/ppermute | solution.py:22
  20.3 6.9 %collective-permute-start.3 = (f32[256,128]{1,0:T(8,128)S(1)}, f32[256,128]{1,0:T(8,128)S(1)}, u32[]{:S(2)}, u32[]{:S(2)}) collective-permute-start(f32[256,128]{1,0:T(8,128)S(1)} %get-tuple-element.56), channel_id=1, source_target_pairs={{0,2},{1,3},{2,0},{3,1},{4,6},{5,7},{6,4},{7,5},{8,10},{9,11},{10,... | collective-permute-start | bytes 393224 | tf_op jit(solution)/shard_map/ppermute | solution.py:22
  28.8 19.7 %collective-permute-start.14 = (f32[4,256,128]{2,1,0:T(8,128)S(1)}, f32[4,256,128]{2,1,0:T(8,128)S(1)}, u32[]{:S(2)}, u32[]{:S(2)}) collective-permute-start(f32[4,256,128]{2,1,0:T(8,128)S(1)} %arrange.2.refs_0_), channel_id=1, source_target_pairs={{0,6},{1,7},{2,4},{3,5},{4,2},{5,3},{6,0},{7,1},{8,14},{9,15},{10,... | collective-permute-start | bytes 1572872 | tf_op jit(solution)/shard_map/ppermute | solution.py:22
  30.3 21.2 %collective-permute-start.13 = (f32[4,256,128]{2,1,0:T(8,128)S(1)}, f32[4,256,128]{2,1,0:T(8,128)S(1)}, u32[]{:S(2)}, u32[]{:S(2)}) collective-permute-start(f32[4,256,128]{2,1,0:T(8,128)S(1)} %arrange.2.refs_0_), channel_id=1, source_target_pairs={{0,4},{1,5},{2,6},{3,7},{4,0},{5,1},{6,2},{7,3},{8,12},{9,13},{10,... | collective-permute-start | bytes 1572872 | tf_op jit(solution)/shard_map/ppermute | solution.py:22
  31.8 20.4 %collective-permute-start.12 = (f32[4,256,128]{2,1,0:T(8,128)S(1)}, f32[4,256,128]{2,1,0:T(8,128)S(1)}, u32[]{:S(2)}, u32[]{:S(2)}) collective-permute-start(f32[4,256,128]{2,1,0:T(8,128)S(1)} %arrange.2.refs_0_), channel_id=1, source_target_pairs={{0,2},{1,3},{2,0},{3,1},{4,6},{5,7},{6,4},{7,5},{8,10},{9,11},{10,... | collective-permute-start | bytes 1572872 | tf_op jit(solution)/shard_map/ppermute | solution.py:22
  34.0 14.5 %collective-permute-start.10 = (f32[256,128]{1,0:T(8,128)S(1)}, f32[256,128]{1,0:T(8,128)S(1)}, u32[]{:S(2)}, u32[]{:S(2)}) collective-permute-start(f32[256,128]{1,0:T(8,128)S(1)} %get-tuple-element.64), channel_id=1, source_target_pairs={{0,16},{8,24},{16,0},{24,8},{1,17},{9,25},{17,1},{25,9},{2,18},{10... | collective-permute-start | bytes 393224 | tf_op jit(solution)/shard_map/ppermute | solution.py:22
  38.3 10.2 %collective-permute-start.11 = (f32[256,128]{1,0:T(8,128)S(1)}, f32[256,128]{1,0:T(8,128)S(1)}, u32[]{:S(2)}, u32[]{:S(2)}) collective-permute-start(f32[256,128]{1,0:T(8,128)S(1)} %get-tuple-element.65), channel_id=1, source_target_pairs={{0,24},{8,16},{16,8},{24,0},{1,25},{9,17},{17,9},{25,1},{2,26},{10... | collective-permute-start | bytes 393224 | tf_op jit(solution)/shard_map/ppermute | solution.py:22
  53.0 15.7 %collective-permute-start.17 = (f32[4,256,128]{2,1,0:T(8,128)S(1)}, f32[4,256,128]{2,1,0:T(8,128)S(1)}, u32[]{:S(2)}, u32[]{:S(2)}) collective-permute-start(f32[4,256,128]{2,1,0:T(8,128)S(1)} %arrange.3.refs_0_), channel_id=1, source_target_pairs={{0,6},{1,7},{2,4},{3,5},{4,2},{5,3},{6,0},{7,1},{8,14},{9,15},{10,... | collective-permute-start | bytes 1572872 | tf_op jit(solution)/shard_map/ppermute | solution.py:22
  53.7 25.3 %collective-permute-start.16 = (f32[4,256,128]{2,1,0:T(8,128)S(1)}, f32[4,256,128]{2,1,0:T(8,128)S(1)}, u32[]{:S(2)}, u32[]{:S(2)}) collective-permute-start(f32[4,256,128]{2,1,0:T(8,128)S(1)} %arrange.3.refs_0_), channel_id=1, source_target_pairs={{0,4},{1,5},{2,6},{3,7},{4,0},{5,1},{6,2},{7,3},{8,12},{9,13},{10,... | collective-permute-start | bytes 1572872 | tf_op jit(solution)/shard_map/ppermute | solution.py:22
  54.8 24.1 %collective-permute-start.15 = (f32[4,256,128]{2,1,0:T(8,128)S(1)}, f32[4,256,128]{2,1,0:T(8,128)S(1)}, u32[]{:S(2)}, u32[]{:S(2)}) collective-permute-start(f32[4,256,128]{2,1,0:T(8,128)S(1)} %arrange.3.refs_0_), channel_id=1, source_target_pairs={{0,2},{1,3},{2,0},{3,1},{4,6},{5,7},{6,4},{7,5},{8,10},{9,11},{10,... | collective-permute-start | bytes 1572872 | tf_op jit(solution)/shard_map/ppermute | solution.py:22
  58.5 20.5 %collective-permute-start.19 = (f32[256,512]{1,0:T(8,128)S(1)}, f32[256,512]{1,0:T(8,128)S(1)}, u32[]{:S(2)}, u32[]{:S(2)}) collective-permute-start(f32[256,512]{1,0:T(8,128)S(1)} %get-tuple-element.67), channel_id=1, source_target_pairs={{0,16},{16,24},{24,8},{8,0},{1,17},{17,25},{25,9},{9,1},{2,18},{18... | collective-permute-start | bytes 1572872 | tf_op jit(solution)/shard_map/ppermute | solution.py:445
  63.1 20.9 %collective-permute-start.21 = (f32[256,512]{1,0:T(8,128)S(1)}, f32[256,512]{1,0:T(8,128)S(1)}, u32[]{:S(2)}, u32[]{:S(2)}) collective-permute-start(f32[256,512]{1,0:T(8,128)S(1)} %get-tuple-element.68), channel_id=1, source_target_pairs={{0,8},{24,16},{1,9},{25,17},{2,10},{26,18},{3,11},{27,19},{4,12},{... | collective-permute-start | bytes 1572872 | tf_op jit(solution)/shard_map/ppermute | solution.py:444
  68.8 15.2 %collective-permute-start.20 = (f32[256,512]{1,0:T(8,128)S(1)}, f32[256,512]{1,0:T(8,128)S(1)}, u32[]{:S(2)}, u32[]{:S(2)}) collective-permute-start(f32[256,512]{1,0:T(8,128)S(1)} %get-tuple-element.68), channel_id=1, source_target_pairs={{8,16},{16,8},{9,17},{17,9},{10,18},{18,10},{11,19},{19,11},{12,20... | collective-permute-start | bytes 1572872 | tf_op jit(solution)/shard_map/ppermute | solution.py:446
  84.3 17.2 %collective-permute-start.27 = (f32[256,512]{1,0:T(8,128)S(1)}, f32[256,512]{1,0:T(8,128)S(1)}, u32[]{:S(2)}, u32[]{:S(2)}) collective-permute-start(f32[256,512]{1,0:T(8,128)S(1)} %add_up.7), channel_id=1, source_target_pairs={{8,24},{16,0},{0,8},{24,16},{9,25},{17,1},{1,9},{25,17},{10,26},{1... | collective-permute-start | bytes 1572872 | tf_op jit(solution)/shard_map/ppermute | solution.py:448
  91.4 19.5 %collective-permute-start.25 = (f32[256,512]{1,0:T(8,128)S(1)}, f32[256,512]{1,0:T(8,128)S(1)}, u32[]{:S(2)}, u32[]{:S(2)}) collective-permute-start(f32[256,512]{1,0:T(8,128)S(1)} %partial_product.7), channel_id=1, source_target_pairs={{0,8},{24,16},{1,9},{25,17},{2,10},{26,18},{3,11},{27,19},{4,12},{... | collective-permute-start | bytes 1572872 | tf_op jit(solution)/shard_map/ppermute | solution.py:444
  96.4 14.5 %collective-permute-start.24 = (f32[256,512]{1,0:T(8,128)S(1)}, f32[256,512]{1,0:T(8,128)S(1)}, u32[]{:S(2)}, u32[]{:S(2)}) collective-permute-start(f32[256,512]{1,0:T(8,128)S(1)} %partial_product.7), channel_id=1, source_target_pairs={{8,16},{16,8},{9,17},{17,9},{10,18},{18,10},{11,19},{19,11},{12,20... | collective-permute-start | bytes 1572872 | tf_op jit(solution)/shard_map/ppermute | solution.py:446
  113.6 20.8 %collective-permute-start.23 = (f32[256,512]{1,0:T(8,128)S(1)}, f32[256,512]{1,0:T(8,128)S(1)}, u32[]{:S(2)}, u32[]{:S(2)}) collective-permute-start(f32[256,512]{1,0:T(8,128)S(1)} %get-tuple-element.71), channel_id=1, source_target_pairs={{0,16},{16,24},{24,8},{8,0},{1,17},{17,25},{25,9},{9,1},{2,18},{18... | collective-permute-start | bytes 1572872 | tf_op jit(solution)/shard_map/ppermute | solution.py:445
  117.0 25.0 %collective-permute-start.26 = (f32[256,512]{1,0:T(8,128)S(1)}, f32[256,512]{1,0:T(8,128)S(1)}, u32[]{:S(2)}, u32[]{:S(2)}) collective-permute-start(f32[256,512]{1,0:T(8,128)S(1)} %add_up.6), channel_id=1, source_target_pairs={{8,24},{16,0},{0,8},{24,16},{9,25},{17,1},{1,9},{25,17},{10,26},{1... | collective-permute-start | bytes 1572872 | tf_op jit(solution)/shard_map/ppermute | solution.py:448
  117.7 9.6 %collective-permute-start.29 = (f32[2,64,512]{2,1,0:T(8,128)S(1)}, f32[2,64,512]{2,1,0:T(8,128)S(1)}, u32[]{:S(2)}, u32[]{:S(2)}) collective-permute-start(f32[2,64,512]{2,1,0:T(8,128)S(1)} %get-tuple-element.82), channel_id=1, source_target_pairs={{0,2},{1,3},{2,0},{3,1},{4,6},{5,7},{6,4},{7,5},{8,10},{9,11},{10,... | collective-permute-start | bytes 786440 | tf_op jit(solution)/shard_map/ppermute | solution.py:22
  120.2 12.3 %collective-permute-start.30 = (f32[2,64,512]{2,1,0:T(8,128)S(1)}, f32[2,64,512]{2,1,0:T(8,128)S(1)}, u32[]{:S(2)}, u32[]{:S(2)}) collective-permute-start(f32[2,64,512]{2,1,0:T(8,128)S(1)} %get-tuple-element.83), channel_id=1, source_target_pairs={{0,4},{1,5},{2,6},{3,7},{4,0},{5,1},{6,2},{7,3},{8,12},{9,13},{10,... | collective-permute-start | bytes 786440 | tf_op jit(solution)/shard_map/ppermute | solution.py:22
  121.6 12.2 %collective-permute-start.31 = (f32[2,64,512]{2,1,0:T(8,128)S(1)}, f32[2,64,512]{2,1,0:T(8,128)S(1)}, u32[]{:S(2)}, u32[]{:S(2)}) collective-permute-start(f32[2,64,512]{2,1,0:T(8,128)S(1)} %get-tuple-element.84), channel_id=1, source_target_pairs={{0,6},{1,7},{2,4},{3,5},{4,2},{5,3},{6,0},{7,1},{8,14},{9,15},{10,... | collective-permute-start | bytes 786440 | tf_op jit(solution)/shard_map/ppermute | solution.py:22
  147.1 6.0 %collective-permute-start.36 = (f32[1,64,512]{2,1,0:T(8,128)S(1)}, f32[1,64,512]{2,1,0:T(8,128)S(1)}, u32[]{:S(2)}, u32[]{:S(2)}) collective-permute-start(f32[1,64,512]{2,1,0:T(8,128)S(1)} %get-tuple-element.92), channel_id=1, source_target_pairs={{0,2},{1,3},{2,0},{3,1},{4,6},{5,7},{6,4},{7,5},{8,10},{9,11},{10,... | collective-permute-start | bytes 393224 | tf_op jit(solution)/shard_map/ppermute | solution.py:22
  148.1 9.1 %collective-permute-start.37 = (f32[1,64,512]{2,1,0:T(8,128)S(1)}, f32[1,64,512]{2,1,0:T(8,128)S(1)}, u32[]{:S(2)}, u32[]{:S(2)}) collective-permute-start(f32[1,64,512]{2,1,0:T(8,128)S(1)} %get-tuple-element.93), channel_id=1, source_target_pairs={{0,4},{1,5},{2,6},{3,7},{4,0},{5,1},{6,2},{7,3},{8,12},{9,13},{10,... | collective-permute-start | bytes 393224 | tf_op jit(solution)/shard_map/ppermute | solution.py:22
  150.6 6.5 %collective-permute-start.38 = (f32[1,64,512]{2,1,0:T(8,128)S(1)}, f32[1,64,512]{2,1,0:T(8,128)S(1)}, u32[]{:S(2)}, u32[]{:S(2)}) collective-permute-start(f32[1,64,512]{2,1,0:T(8,128)S(1)} %get-tuple-element.94), channel_id=1, source_target_pairs={{0,6},{1,7},{2,4},{3,5},{4,2},{5,3},{6,0},{7,1},{8,14},{9,15},{10,... | collective-permute-start | bytes 393224 | tf_op jit(solution)/shard_map/ppermute | solution.py:22
  150.7 9.0 %collective-permute-start.33 = (f32[64,512]{1,0:T(8,128)S(1)}, f32[64,512]{1,0:T(8,128)S(1)}, u32[]{:S(2)}, u32[]{:S(2)}) collective-permute-start(f32[64,512]{1,0:T(8,128)S(1)} %add_up.8.refs_0_), channel_id=1, source_target_pairs={{0,16},{8,24},{16,0},{24,8},{1,17},{9,25},{17,1},{25,9},{2,18},{10... | collective-permute-start | bytes 393224 | tf_op jit(solution)/shard_map/ppermute | solution.py:22
  159.7 6.7 %collective-permute-start.34 = (f32[64,512]{1,0:T(8,128)S(1)}, f32[64,512]{1,0:T(8,128)S(1)}, u32[]{:S(2)}, u32[]{:S(2)}) collective-permute-start(f32[64,512]{1,0:T(8,128)S(1)} %add_up.9.refs_3_), channel_id=1, source_target_pairs={{0,8},{8,0},{16,24},{24,16},{1,9},{9,1},{17,25},{25,17},{2,10},{10... | collective-permute-start | bytes 393224 | tf_op jit(solution)/shard_map/ppermute | solution.py:22
  162.8 7.6 %collective-permute-start.40 = (f32[1,64,512]{2,1,0:T(8,128)S(1)}, f32[1,64,512]{2,1,0:T(8,128)S(1)}, u32[]{:S(2)}, u32[]{:S(2)}) collective-permute-start(f32[1,64,512]{2,1,0:T(8,128)S(1)} %add_up.11.refs_5_), channel_id=1, source_target_pairs={{0,16},{8,24},{16,0},{24,8},{1,17},{9,25},{17,1},{25,9},{2,18},{10... | collective-permute-start | bytes 393224 | tf_op jit(solution)/shard_map/ppermute | solution.py:22
  (20 other events, 176.7 us)

commit v14 on v13

--- a/solution.py
+++ b/solution.py
@@ -121,6 +121,22 @@
     out = jax.ShapeDtypeStruct(arrays[0].shape, arrays[0].dtype)
     specs = [whole(array) for array in arrays]
     return run(add_kernel, [], arrays, specs, waits, out, whole(out), name="add_up")
+
+
+def pass_on_kernel(place, onward_ref, own_ref, near_ref, both_ref, mine_ref):
+    near = near_ref[...]
+    inside = (place[1] == 1) | (place[1] == 2)
+    both_ref[...] = onward_ref[...] + jnp.where(inside, near, 0.0)
+    mine_ref[...] = own_ref[...] + jnp.where(inside, 0.0, near)
+
+
+def pass_on(place, onward, own, near):
+    out = jax.ShapeDtypeStruct(own.shape, own.dtype)
+    specs = [whole(own)] * 3
+    outs = [out] * 2
+    return run(
+        pass_on_kernel, [place], [onward, own, near], specs, [], outs, specs[:2], name="pass_on"
+    )
 
 
 def is_listed(ancestors, number, block):
@@ -433,26 +449,26 @@
     return rows.reshape(ratio * count * unit_rows, count * width)
 
 
-FOUR_SLOTS = ((3, 2, 1, 0), (2, 0, 3, 1), (1, 3, 0, 2), (0, 1, 2, 3))
+FOUR_SLOTS = ((3, 2, 1, 0), (0, 2, 3, 1), (3, 1, 0, 2), (0, 1, 2, 3))
 
 
 def slots_of(count):
     return FOUR_SLOTS if count == len(FOUR_SLOTS) else (tuple(range(count)),) * count
 
 
-def sum_over_four(slots):
-    near = lax.ppermute(slots[0], "prow", [(0, 1), (3, 2)])
-    total = lax.ppermute(slots[1], "prow", [(0, 2), (2, 3), (3, 1), (1, 0)])
-    middle = lax.ppermute(slots[0], "prow", [(1, 2), (2, 1)])
-    both = add_up([slots[2], near], [])
+def sum_over_four(place, slots):
+    near = lax.ppermute(slots[0], "prow", [(0, 1), (3, 2), (1, 0), (2, 3)])
+    middle = lax.ppermute(slots[1], "prow", [(1, 2), (2, 1)])
+    total = lax.ppermute(slots[1], "prow", [(0, 2), (3, 1)])
+    both, mine = pass_on(place, slots[2], slots[3], near)
     last = lax.ppermute(both, "prow", [(1, 3), (2, 0), (0, 1), (3, 2)])
-    return [slots[3], total, middle, last, near]
-
-
-def sum_over_line(slots, z):
+    return [mine, total, middle, last, near]
+
+
+def sum_over_line(place, slots, z):
     count = len(slots)
     if count == len(FOUR_SLOTS):
-        return sum_over_four(slots)
+        return sum_over_four(place, slots)
     chunks = jnp.stack(slots)
 
     def chunk(index):
@@ -542,14 +558,14 @@
         else:
             own = to_plane_whole(factor[number], count, ratio)
             pieces = [in_rows(lax.all_gather(own, "pcol", axis=0), count, ratio)]
-        middle = 1 if rows else count // 2
+        middle = count // 2
         partial, starts = [], [0, middle, count] if received else [0, count]
         for start, stop in zip(starts, starts[1:]):
             partial += partial_product(
                 place, slots, ancestors, inverse_tiles, pieces, ratio, columns, number, start, stop,
                 [bases[0]],
             )
-        rows.append(sum_over_line(partial, z))
+        rows.append(sum_over_line(place, partial, z))
         rows[-1] = rows[-1][:3] + rows[-1][:2:-1]
         late = [partial[-1]]
         lates.append(late)

time: 172 us -> 187 us (1.087)
  waiting for transfers between devices: 76.5 us -> 84.4 us
  starting transfers between devices: 60.8 us -> 66.1 us
    ppermute x2, starting transfers between devices: 3.59 us -> 12.5 us  [sum_over_four(): last = lax.ppermute(both, 'prow', [(1, 3), (2, 0), (0, 1), (3, 2)])]
    ppermute x33, starting transfers between devices: 41.5 us -> 37.1 us  [flip(): lax.ppermute(value, axis, [(i, i ^ bit) for i in range(lax.axis_size(axis...]
    ppermute x2, waiting for transfers between devices: 8.57 us -> 12.3 us  [sum_over_four(): last = lax.ppermute(both, 'prow', [(1, 3), (2, 0), (0, 1), (3, 2)])]
    ppermute x6, waiting for transfers between devices: 14.5 us -> 17.4 us  [the longest x2 11 us: sum_over_four(): near = lax.ppermute(slots[0], 'prow', [(0, 1), (3, 2), (1, 0), (2, 3)])]
  transfers between devices with their start and end apart: 41 -> 41, of which waited for: 24 -> 21; matrix products, arithmetic and copies ran while one was open for 0% -> 0% of each run, Pallas kernels for 12% -> 11%
where the time goes in v14:
time: 187 us
  waiting for transfers between devices  84.4 us (45%)
  starting transfers between devices  66.1 us (35%)
  Pallas kernels  29.4 us (16%)
  local copies, waits for them, and re-layouts  5.64 us (3%)
    ppermute x33, waiting for transfers between devices, flip(): lax.ppermute(value, axis, [(i, i ^ bit) for i in range(lax.axis_size(axis...  54.7 us
    ppermute x33, starting transfers between devices, flip(): lax.ppermute(value, axis, [(i, i ^ bit) for i in range(lax.axis_size(axis...  37.1 us
    pallas_call x26, Pallas kernels, run(): pl.pallas_call(body, grid_spec=pltpu.PrefetchScalarGridSpec(num_scalar_pr...  29.4 us
    ppermute x2, starting transfers between devices, sum_over_four(): last = lax.ppermute(both, 'prow', [(1, 3), (2, 0), (0, 1), (3, 2)])  12.5 us
    ppermute x2, waiting for transfers between devices, sum_over_four(): last = lax.ppermute(both, 'prow', [(1, 3), (2, 0), (0, 1), (3, 2)])  12.3 us
    ppermute x2, waiting for transfers between devices, sum_over_four(): near = lax.ppermute(slots[0], 'prow', [(0, 1), (3, 2), (1, 0), (2, 3)])  11 us
    ppermute x2, starting transfers between devices, sum_over_four(): total = lax.ppermute(slots[1], 'prow', [(0, 2), (3, 1)])  7.8 us
    ppermute x2, starting transfers between devices, sum_over_four(): near = lax.ppermute(slots[0], 'prow', [(0, 1), (3, 2), (1, 0), (2, 3)])  7.02 us
  transfers between devices with their start and end apart: 41, of which 21 were waited for; matrix products, arithmetic and copies ran while one was open for 0% of the time, Pallas kernels for 11%

profile of v14, /device:TPU:0, one launch (start us, length us, event | category | flops | bytes accessed | tf_op | source)
XLA Modules:
  0.0 186.6 jit_solution(8707666952146344483)
XLA Ops:
  2.6 3.0 %collective-permute-start = (f32[256,128]{1,0:T(8,128)S(1)}, f32[256,128]{1,0:T(8,128)S(1)}, u32[]{:S(2)}, u32[]{:S(2)}) collective-permute-start(f32[256,128]{1,0:T(8,128)S(1)} %get-tuple-element.56), channel_id=1, source_target_pairs={{0,2},{1,3},{2,0},{3,1},{4,6},{5,7},{6,4},{7,5},{8,10},{9,11},{10,... | collective-permute-start | bytes 393224 | tf_op jit(solution)/shard_map/ppermute | solution.py:22
  7.1 2.4 %collective-permute-done.refs_2_ = f32[256,128]{1,0:T(8,128)S(1)} collective-permute-done((f32[256,128]{1,0:T(8,128)S(1)}, f32[256,128]{1,0:T(8,128)S(1)}, u32[]{:S(2)}, u32[]{:S(2)}) %collective-permute-start) | collective-permute-done | bytes 131104 | tf_op jit(solution)/shard_map/ppermute | solution.py:22
  9.5 3.9 %collective-permute-done.1.refs_3_ = f32[256,128]{1,0:T(8,128)S(1)} collective-permute-done((f32[256,128]{1,0:T(8,128)S(1)}, f32[256,128]{1,0:T(8,128)S(1)}, u32[]{:S(2)}, u32[]{:S(2)}) %collective-permute-start.1) | collective-permute-done | bytes 131104 | tf_op jit(solution)/shard_map/ppermute | solution.py:22
  20.9 2.6 %collective-permute-start.7 = (f32[256,128]{1,0:T(8,128)S(1)}, f32[256,128]{1,0:T(8,128)S(1)}, u32[]{:S(2)}, u32[]{:S(2)}) collective-permute-start(f32[256,128]{1,0:T(8,128)S(1)} %get-tuple-element.65), channel_id=1, source_target_pairs={{0,16},{8,24},{16,0},{24,8},{1,17},{9,25},{17,1},{25,9},{2,18},{10... | collective-permute-start | bytes 393224 | tf_op jit(solution)/shard_map/ppermute | solution.py:22
  23.5 2.2 %collective-permute-start.8 = (f32[256,128]{1,0:T(8,128)S(1)}, f32[256,128]{1,0:T(8,128)S(1)}, u32[]{:S(2)}, u32[]{:S(2)}) collective-permute-start(f32[256,128]{1,0:T(8,128)S(1)} %get-tuple-element.66), channel_id=1, source_target_pairs={{0,24},{8,16},{16,8},{24,0},{1,25},{9,17},{17,9},{25,1},{2,26},{10... | collective-permute-start | bytes 393224 | tf_op jit(solution)/shard_map/ppermute | solution.py:22
  25.7 5.9 %collective-permute-done.7.refs_6_.refs_3_ = f32[256,128]{1,0:T(8,128)S(1)} collective-permute-done((f32[256,128]{1,0:T(8,128)S(1)}, f32[256,128]{1,0:T(8,128)S(1)}, u32[]{:S(2)}, u32[]{:S(2)}) %collective-permute-start.7) | collective-permute-done | bytes 131104 | tf_op jit(solution)/shard_map/ppermute | solution.py:22
  36.4 3.1 %collective-permute-start.10 = (f32[256,128]{1,0:T(8,128)S(1)}, f32[256,128]{1,0:T(8,128)S(1)}, u32[]{:S(2)}, u32[]{:S(2)}) collective-permute-start(f32[256,128]{1,0:T(8,128)S(1)} %get-tuple-element.69), channel_id=1, source_target_pairs={{0,16},{8,24},{16,0},{24,8},{1,17},{9,25},{17,1},{25,9},{2,18},{10... | collective-permute-start | bytes 393224 | tf_op jit(solution)/shard_map/ppermute | solution.py:22
  40.8 6.5 %collective-permute-done.10.refs_3_.refs_5_ = f32[256,128]{1,0:T(8,128)S(1)} collective-permute-done((f32[256,128]{1,0:T(8,128)S(1)}, f32[256,128]{1,0:T(8,128)S(1)}, u32[]{:S(2)}, u32[]{:S(2)}) %collective-permute-start.10) | collective-permute-done | bytes 131104 | tf_op jit(solution)/shard_map/ppermute | solution.py:22
  50.5 2.5 %bases.1 = (f32[2,64,512]{2,1,0:T(8,128)S(1)}, f32[1,64,512]{2,1,0:T(8,128)S(1)}) custom-call(s32[3]{0:T(128)S(1)} %pad_add_fusion.refs_0_, f32[2,512,512]{2,1,0:T(8,128)S(1)} %copy-done.6, f32[1,512,512]{2,1,0:T(8,128)S(1)} %copy-done.3, f32[256,128]{1,0:T(8,128)S(1)} %get-tuple-element.59.refs_2_.refs_1_.refs_3_), custom_call_target="tpu_custom_call" | custom-call | tf_op jit(solution)/shard_map/bases/pallas_call | solution.py:36
  61.0 4.8 %collective-permute-start.21 = (f32[256,512]{1,0:T(8,128)S(1)}, f32[256,512]{1,0:T(8,128)S(1)}, u32[]{:S(2)}, u32[]{:S(2)}) collective-permute-start(f32[256,512]{1,0:T(8,128)S(1)} %get-tuple-element.73), channel_id=1, source_target_pairs={{0,8},{24,16},{8,0},{16,24},{1,9},{25,17},{9,1},{17,25},{2,10},{26... | collective-permute-start | bytes 1572872 | tf_op jit(solution)/shard_map/ppermute | solution.py:460
  65.8 4.1 %collective-permute-start.19 = (f32[256,512]{1,0:T(8,128)S(1)}, f32[256,512]{1,0:T(8,128)S(1)}, u32[]{:S(2)}, u32[]{:S(2)}) collective-permute-start(f32[256,512]{1,0:T(8,128)S(1)} %get-tuple-element.72), channel_id=1, source_target_pairs={{0,16},{24,8},{1,17},{25,9},{2,18},{26,10},{3,19},{27,11},{4,20},{... | collective-permute-start | bytes 1572872 | tf_op jit(solution)/shard_map/ppermute | solution.py:462
  71.0 3.2 %partial_product.5 = (f32[256,512]{1,0:T(8,128)S(1)}, f32[256,512]{1,0:T(8,128)S(1)}) custom-call(s32[3]{0:T(128)S(1)} %pad_add_fusion.refs_0_, s32[4,4]{1,0:T(4,128)S(1)} %copy-done.8, s32[2,8]{1,0:T(2,128)S(1)} %copy-done.7, f32[1024,2048]{1,0:T(8,128)S(1)} %bitcast.4, f32[4,4,256,128]{3,2,1,0:T(8,128)S(1)} %pack.2.refs_4_, ...), custom_call_target="tpu_custom_call" | custom-call | tf_op jit(solution)/shard_map/partial_product/pallas_call | solution.py:36
  74.2 7.2 %collective-permute-done.16.refs_2_ = f32[4,256,128]{2,1,0:T(8,128)S(1)} collective-permute-done((f32[4,256,128]{2,1,0:T(8,128)S(1)}, f32[4,256,128]{2,1,0:T(8,128)S(1)}, u32[]{:S(2)}, u32[]{:S(2)}) %collective-permute-start.16) | collective-permute-done | bytes 524320 | tf_op jit(solution)/shard_map/ppermute | solution.py:22
  81.4 6.4 %collective-permute-done.19.refs_4_.refs_3_ = f32[256,512]{1,0:T(8,128)S(1)} collective-permute-done((f32[256,512]{1,0:T(8,128)S(1)}, f32[256,512]{1,0:T(8,128)S(1)}, u32[]{:S(2)}, u32[]{:S(2)}) %collective-permute-start.19) | collective-permute-done | bytes 524320 | tf_op jit(solution)/shard_map/ppermute | solution.py:462
  88.8 12.4 %collective-permute-start.27 = (f32[256,512]{1,0:T(8,128)S(1)}, f32[256,512]{1,0:T(8,128)S(1)}, u32[]{:S(2)}, u32[]{:S(2)}) collective-permute-start(f32[256,512]{1,0:T(8,128)S(1)} %get-tuple-element.83), channel_id=1, source_target_pairs={{8,24},{16,0},{0,8},{24,16},{9,25},{17,1},{1,9},{25,17},{10,26},{1... | collective-permute-start | bytes 1572872 | tf_op jit(solution)/shard_map/ppermute | solution.py:464
  101.2 4.3 %partial_product.7 = (f32[256,512]{1,0:T(8,128)S(1)}, f32[256,512]{1,0:T(8,128)S(1)}) custom-call(s32[3]{0:T(128)S(1)} %pad_add_fusion.refs_0_, s32[4,4]{1,0:T(4,128)S(1)} %copy-done.8, s32[2,8]{1,0:T(2,128)S(1)} %copy-done.7, f32[1024,2048]{1,0:T(8,128)S(1)} %bitcast.4, f32[4,4,256,128]{3,2,1,0:T(8,128)S(1)} %pack.3.refs_4_, ...), custom_call_target="tpu_custom_call" | custom-call | tf_op jit(solution)/shard_map/partial_product/pallas_call | solution.py:36
  105.5 2.2 %collective-permute-start.23 = (f32[256,512]{1,0:T(8,128)S(1)}, f32[256,512]{1,0:T(8,128)S(1)}, u32[]{:S(2)}, u32[]{:S(2)}) collective-permute-start(f32[256,512]{1,0:T(8,128)S(1)} %get-tuple-element.77), channel_id=1, source_target_pairs={{0,8},{24,16},{8,0},{16,24},{1,9},{25,17},{9,1},{17,25},{2,10},{26... | collective-permute-start | bytes 1572872 | tf_op jit(solution)/shard_map/ppermute | solution.py:460
  110.6 4.4 %collective-permute-done.27.refs_5_ = f32[256,512]{1,0:T(8,128)S(1)} collective-permute-done((f32[256,512]{1,0:T(8,128)S(1)}, f32[256,512]{1,0:T(8,128)S(1)}, u32[]{:S(2)}, u32[]{:S(2)}) %collective-permute-start.27) | collective-permute-done | bytes 524320 | tf_op jit(solution)/shard_map/ppermute | solution.py:464
  115.0 11.0 %collective-permute-done.23.refs_3_.refs_10_ = f32[256,512]{1,0:T(8,128)S(1)} collective-permute-done((f32[256,512]{1,0:T(8,128)S(1)}, f32[256,512]{1,0:T(8,128)S(1)}, u32[]{:S(2)}, u32[]{:S(2)}) %collective-permute-start.23) | collective-permute-done | bytes 524320 | tf_op jit(solution)/shard_map/ppermute | solution.py:460
  126.0 2.7 %finish.2 = (f32[2,256,512]{2,1,0:T(8,128)}, f32[2,4,64,512]{3,2,1,0:T(8,128)S(1)}, f32[2,4,64,512]{3,2,1,0:T(8,128)S(1)}, f32[512,512]{1,0:T(8,128)S(1)}, f32[512,512]{1,0:T(8,128)S(1)}) custom-call(s32[3]{0:T(128)S(1)} %pad_add_fusion.refs_0_, s32[2,8]{1,0:T(2,128)S(1)} %copy-done.7, f32[256,512]{1,0:T(8,128)S(1)} %get-tuple-element.82.refs_2_, ...), custom_call_target="tpu_custom_call" | custom-call | tf_op jit(solution)/shard_map/finish/pallas_call | solution.py:36
  128.8 3.7 %collective-permute-start.24 = (f32[256,512]{1,0:T(8,128)S(1)}, f32[256,512]{1,0:T(8,128)S(1)}, u32[]{:S(2)}, u32[]{:S(2)}) collective-permute-start(f32[256,512]{1,0:T(8,128)S(1)} %get-tuple-element.79), channel_id=1, source_target_pairs={{0,16},{24,8},{1,17},{25,9},{2,18},{26,10},{3,19},{27,11},{4,20},{... | collective-permute-start | bytes 1572872 | tf_op jit(solution)/shard_map/ppermute | solution.py:462
  134.8 2.1 %collective-permute-start.30 = (f32[2,64,512]{2,1,0:T(8,128)S(1)}, f32[2,64,512]{2,1,0:T(8,128)S(1)}, u32[]{:S(2)}, u32[]{:S(2)}) collective-permute-start(f32[2,64,512]{2,1,0:T(8,128)S(1)} %get-tuple-element.93), channel_id=1, source_target_pairs={{0,4},{1,5},{2,6},{3,7},{4,0},{5,1},{6,2},{7,3},{8,12},{9,13},{10,... | collective-permute-start | bytes 786440 | tf_op jit(solution)/shard_map/ppermute | solution.py:22
  137.5 2.3 %rest.1 = (f32[512,512]{1,0:T(8,128)S(1)}, f32[256,512]{1,0:T(8,128)S(1)}) custom-call(f32[1,512,512]{2,1,0:T(8,128)S(1)} %copy-done.4, f32[512,512]{1,0:T(8,128)S(1)} %get-tuple-element.84.refs_1_, f32[512,512]{1,0:T(8,128)S(1)} %get-tuple-element.85.refs_2_, f32[2,256,512]{2,1,0:T(8,128)S(1)} %copy-done.5), custom_call_target="tpu_custom_call" | custom-call | tf_op jit(solution)/shard_map/rest/pallas_call | solution.py:36
  139.8 3.4 %collective-permute-done.29.refs_2_ = f32[2,64,512]{2,1,0:T(8,128)S(1)} collective-permute-done((f32[2,64,512]{2,1,0:T(8,128)S(1)}, f32[2,64,512]{2,1,0:T(8,128)S(1)}, u32[]{:S(2)}, u32[]{:S(2)}) %collective-permute-start.29) | collective-permute-done | bytes 262176 | tf_op jit(solution)/shard_map/ppermute | solution.py:22
  143.2 5.6 %collective-permute-done.30.refs_3_ = f32[2,64,512]{2,1,0:T(8,128)S(1)} collective-permute-done((f32[2,64,512]{2,1,0:T(8,128)S(1)}, f32[2,64,512]{2,1,0:T(8,128)S(1)}, u32[]{:S(2)}, u32[]{:S(2)}) %collective-permute-start.30) | collective-permute-done | bytes 262176 | tf_op jit(solution)/shard_map/ppermute | solution.py:22
  149.4 7.9 %collective-permute-done.26.refs_5_ = f32[256,512]{1,0:T(8,128)S(1)} collective-permute-done((f32[256,512]{1,0:T(8,128)S(1)}, f32[256,512]{1,0:T(8,128)S(1)}, u32[]{:S(2)}, u32[]{:S(2)}) %collective-permute-start.26) | collective-permute-done | bytes 524320 | tf_op jit(solution)/shard_map/ppermute | solution.py:464
  157.3 2.1 %finish.3 = (f32[2,256,512]{2,1,0:T(8,128)}, f32[1,4,64,512]{3,2,1,0:T(8,128)S(1)}, f32[1,4,64,512]{3,2,1,0:T(8,128)S(1)}) custom-call(s32[3]{0:T(128)S(1)} %pad_add_fusion.refs_0_, s32[2,8]{1,0:T(2,128)S(1)} %copy-done.7, f32[256,512]{1,0:T(8,128)S(1)} %get-tuple-element.78.refs_2_, ...), custom_call_target="tpu_custom_call", output_to_operand_aliasing={{0}: (9, {})} | custom-call | tf_op jit(solution)/shard_map/finish/pallas_call | solution.py:36
  162.6 2.2 %collective-permute-start.37 = (f32[1,64,512]{2,1,0:T(8,128)S(1)}, f32[1,64,512]{2,1,0:T(8,128)S(1)}, u32[]{:S(2)}, u32[]{:S(2)}) collective-permute-start(f32[1,64,512]{2,1,0:T(8,128)S(1)} %get-tuple-element.103), channel_id=1, source_target_pairs={{0,4},{1,5},{2,6},{3,7},{4,0},{5,1},{6,2},{7,3},{8,12},{9,13},{10,... | collective-permute-start | bytes 393224 | tf_op jit(solution)/shard_map/ppermute | solution.py:22
  168.3 2.1 %collective-permute-done.37.refs_2_ = f32[1,64,512]{2,1,0:T(8,128)S(1)} collective-permute-done((f32[1,64,512]{2,1,0:T(8,128)S(1)}, f32[1,64,512]{2,1,0:T(8,128)S(1)}, u32[]{:S(2)}, u32[]{:S(2)}) %collective-permute-start.37) | collective-permute-done | bytes 131104 | tf_op jit(solution)/shard_map/ppermute | solution.py:22
  174.5 3.1 %collective-permute-done.39.refs_1_ = f32[1,64,512]{2,1,0:T(8,128)S(1)} collective-permute-done((f32[1,64,512]{2,1,0:T(8,128)S(1)}, f32[1,64,512]{2,1,0:T(8,128)S(1)}, u32[]{:S(2)}, u32[]{:S(2)}) %collective-permute-start.39) | collective-permute-done | bytes 131104 | tf_op jit(solution)/shard_map/ppermute | solution.py:22
  178.2 2.9 %collective-permute-done.34.refs_4_ = f32[64,512]{1,0:T(8,128)S(1)} collective-permute-done((f32[64,512]{1,0:T(8,128)S(1)}, f32[64,512]{1,0:T(8,128)S(1)}, u32[]{:S(2)}, u32[]{:S(2)}) %collective-permute-start.34) | collective-permute-done | bytes 131104 | tf_op jit(solution)/shard_map/ppermute | solution.py:22
  181.2 4.1 %collective-permute-done.40.refs_6_ = f32[1,64,512]{2,1,0:T(8,128)S(1)} collective-permute-done((f32[1,64,512]{2,1,0:T(8,128)S(1)}, f32[1,64,512]{2,1,0:T(8,128)S(1)}, u32[]{:S(2)}, u32[]{:S(2)}) %collective-permute-start.40) | collective-permute-done | bytes 131104 | tf_op jit(solution)/shard_map/ppermute | solution.py:22
  (100 shorter events, 49.3 us)
Async XLA Ops:
  2.6 6.9 %collective-permute-start = (f32[256,128]{1,0:T(8,128)S(1)}, f32[256,128]{1,0:T(8,128)S(1)}, u32[]{:S(2)}, u32[]{:S(2)}) collective-permute-start(f32[256,128]{1,0:T(8,128)S(1)} %get-tuple-element.56), channel_id=1, source_target_pairs={{0,2},{1,3},{2,0},{3,1},{4,6},{5,7},{6,4},{7,5},{8,10},{9,11},{10,... | collective-permute-start | bytes 393224 | tf_op jit(solution)/shard_map/ppermute | solution.py:22
  5.6 7.8 %collective-permute-start.1 = (f32[256,128]{1,0:T(8,128)S(1)}, f32[256,128]{1,0:T(8,128)S(1)}, u32[]{:S(2)}, u32[]{:S(2)}) collective-permute-start(f32[256,128]{1,0:T(8,128)S(1)} %get-tuple-element.57), channel_id=1, source_target_pairs={{0,4},{1,5},{2,6},{3,7},{4,0},{5,1},{6,2},{7,3},{8,12},{9,13},{10,... | collective-permute-start | bytes 393224 | tf_op jit(solution)/shard_map/ppermute | solution.py:22
  15.8 7.7 %collective-permute-start.3 = (f32[256,128]{1,0:T(8,128)S(1)}, f32[256,128]{1,0:T(8,128)S(1)}, u32[]{:S(2)}, u32[]{:S(2)}) collective-permute-start(f32[256,128]{1,0:T(8,128)S(1)} %get-tuple-element.61), channel_id=1, source_target_pairs={{0,2},{1,3},{2,0},{3,1},{4,6},{5,7},{6,4},{7,5},{8,10},{9,11},{10,... | collective-permute-start | bytes 393224 | tf_op jit(solution)/shard_map/ppermute | solution.py:22
  17.1 8.6 %collective-permute-start.4 = (f32[256,128]{1,0:T(8,128)S(1)}, f32[256,128]{1,0:T(8,128)S(1)}, u32[]{:S(2)}, u32[]{:S(2)}) collective-permute-start(f32[256,128]{1,0:T(8,128)S(1)} %get-tuple-element.62), channel_id=1, source_target_pairs={{0,4},{1,5},{2,6},{3,7},{4,0},{5,1},{6,2},{7,3},{8,12},{9,13},{10,... | collective-permute-start | bytes 393224 | tf_op jit(solution)/shard_map/ppermute | solution.py:22
  17.9 7.8 %collective-permute-start.5 = (f32[256,128]{1,0:T(8,128)S(1)}, f32[256,128]{1,0:T(8,128)S(1)}, u32[]{:S(2)}, u32[]{:S(2)}) collective-permute-start(f32[256,128]{1,0:T(8,128)S(1)} %get-tuple-element.63), channel_id=1, source_target_pairs={{0,6},{1,7},{2,4},{3,5},{4,2},{5,3},{6,0},{7,1},{8,14},{9,15},{10,... | collective-permute-start | bytes 393224 | tf_op jit(solution)/shard_map/ppermute | solution.py:22
  20.9 10.7 %collective-permute-start.7 = (f32[256,128]{1,0:T(8,128)S(1)}, f32[256,128]{1,0:T(8,128)S(1)}, u32[]{:S(2)}, u32[]{:S(2)}) collective-permute-start(f32[256,128]{1,0:T(8,128)S(1)} %get-tuple-element.65), channel_id=1, source_target_pairs={{0,16},{8,24},{16,0},{24,8},{1,17},{9,25},{17,1},{25,9},{2,18},{10... | collective-permute-start | bytes 393224 | tf_op jit(solution)/shard_map/ppermute | solution.py:22
  23.5 8.2 %collective-permute-start.8 = (f32[256,128]{1,0:T(8,128)S(1)}, f32[256,128]{1,0:T(8,128)S(1)}, u32[]{:S(2)}, u32[]{:S(2)}) collective-permute-start(f32[256,128]{1,0:T(8,128)S(1)} %get-tuple-element.66), channel_id=1, source_target_pairs={{0,24},{8,16},{16,8},{24,0},{1,25},{9,17},{17,9},{25,1},{2,26},{10... | collective-permute-start | bytes 393224 | tf_op jit(solution)/shard_map/ppermute | solution.py:22
  32.3 20.8 %collective-permute-start.12 = (f32[4,256,128]{2,1,0:T(8,128)S(1)}, f32[4,256,128]{2,1,0:T(8,128)S(1)}, u32[]{:S(2)}, u32[]{:S(2)}) collective-permute-start(f32[4,256,128]{2,1,0:T(8,128)S(1)} %arrange.2.refs_0_), channel_id=1, source_target_pairs={{0,2},{1,3},{2,0},{3,1},{4,6},{5,7},{6,4},{7,5},{8,10},{9,11},{10,... | collective-permute-start | bytes 1572872 | tf_op jit(solution)/shard_map/ppermute | solution.py:22
  34.0 20.7 %collective-permute-start.13 = (f32[4,256,128]{2,1,0:T(8,128)S(1)}, f32[4,256,128]{2,1,0:T(8,128)S(1)}, u32[]{:S(2)}, u32[]{:S(2)}) collective-permute-start(f32[4,256,128]{2,1,0:T(8,128)S(1)} %arrange.2.refs_0_), channel_id=1, source_target_pairs={{0,4},{1,5},{2,6},{3,7},{4,0},{5,1},{6,2},{7,3},{8,12},{9,13},{10,... | collective-permute-start | bytes 1572872 | tf_op jit(solution)/shard_map/ppermute | solution.py:22
  34.5 20.2 %collective-permute-start.14 = (f32[4,256,128]{2,1,0:T(8,128)S(1)}, f32[4,256,128]{2,1,0:T(8,128)S(1)}, u32[]{:S(2)}, u32[]{:S(2)}) collective-permute-start(f32[4,256,128]{2,1,0:T(8,128)S(1)} %arrange.2.refs_0_), channel_id=1, source_target_pairs={{0,6},{1,7},{2,4},{3,5},{4,2},{5,3},{6,0},{7,1},{8,14},{9,15},{10,... | collective-permute-start | bytes 1572872 | tf_op jit(solution)/shard_map/ppermute | solution.py:22
  36.4 10.9 %collective-permute-start.10 = (f32[256,128]{1,0:T(8,128)S(1)}, f32[256,128]{1,0:T(8,128)S(1)}, u32[]{:S(2)}, u32[]{:S(2)}) collective-permute-start(f32[256,128]{1,0:T(8,128)S(1)} %get-tuple-element.69), channel_id=1, source_target_pairs={{0,16},{8,24},{16,0},{24,8},{1,17},{9,25},{17,1},{25,9},{2,18},{10... | collective-permute-start | bytes 393224 | tf_op jit(solution)/shard_map/ppermute | solution.py:22
  39.5 13.5 %collective-permute-start.11 = (f32[256,128]{1,0:T(8,128)S(1)}, f32[256,128]{1,0:T(8,128)S(1)}, u32[]{:S(2)}, u32[]{:S(2)}) collective-permute-start(f32[256,128]{1,0:T(8,128)S(1)} %get-tuple-element.70), channel_id=1, source_target_pairs={{0,24},{8,16},{16,8},{24,0},{1,25},{9,17},{17,9},{25,1},{2,26},{10... | collective-permute-start | bytes 393224 | tf_op jit(solution)/shard_map/ppermute | solution.py:22
  55.5 14.8 %collective-permute-start.15 = (f32[4,256,128]{2,1,0:T(8,128)S(1)}, f32[4,256,128]{2,1,0:T(8,128)S(1)}, u32[]{:S(2)}, u32[]{:S(2)}) collective-permute-start(f32[4,256,128]{2,1,0:T(8,128)S(1)} %arrange.3.refs_0_), channel_id=1, source_target_pairs={{0,2},{1,3},{2,0},{3,1},{4,6},{5,7},{6,4},{7,5},{8,10},{9,11},{10,... | collective-permute-start | bytes 1572872 | tf_op jit(solution)/shard_map/ppermute | solution.py:22
  56.2 25.3 %collective-permute-start.16 = (f32[4,256,128]{2,1,0:T(8,128)S(1)}, f32[4,256,128]{2,1,0:T(8,128)S(1)}, u32[]{:S(2)}, u32[]{:S(2)}) collective-permute-start(f32[4,256,128]{2,1,0:T(8,128)S(1)} %arrange.3.refs_0_), channel_id=1, source_target_pairs={{0,4},{1,5},{2,6},{3,7},{4,0},{5,1},{6,2},{7,3},{8,12},{9,13},{10,... | collective-permute-start | bytes 1572872 | tf_op jit(solution)/shard_map/ppermute | solution.py:22
  57.3 24.1 %collective-permute-start.17 = (f32[4,256,128]{2,1,0:T(8,128)S(1)}, f32[4,256,128]{2,1,0:T(8,128)S(1)}, u32[]{:S(2)}, u32[]{:S(2)}) collective-permute-start(f32[4,256,128]{2,1,0:T(8,128)S(1)} %arrange.3.refs_0_), channel_id=1, source_target_pairs={{0,6},{1,7},{2,4},{3,5},{4,2},{5,3},{6,0},{7,1},{8,14},{9,15},{10,... | collective-permute-start | bytes 1572872 | tf_op jit(solution)/shard_map/ppermute | solution.py:22
  61.0 20.4 %collective-permute-start.21 = (f32[256,512]{1,0:T(8,128)S(1)}, f32[256,512]{1,0:T(8,128)S(1)}, u32[]{:S(2)}, u32[]{:S(2)}) collective-permute-start(f32[256,512]{1,0:T(8,128)S(1)} %get-tuple-element.73), channel_id=1, source_target_pairs={{0,8},{24,16},{8,0},{16,24},{1,9},{25,17},{9,1},{17,25},{2,10},{26... | collective-permute-start | bytes 1572872 | tf_op jit(solution)/shard_map/ppermute | solution.py:460
  65.8 22.1 %collective-permute-start.19 = (f32[256,512]{1,0:T(8,128)S(1)}, f32[256,512]{1,0:T(8,128)S(1)}, u32[]{:S(2)}, u32[]{:S(2)}) collective-permute-start(f32[256,512]{1,0:T(8,128)S(1)} %get-tuple-element.72), channel_id=1, source_target_pairs={{0,16},{24,8},{1,17},{25,9},{2,18},{26,10},{3,19},{27,11},{4,20},{... | collective-permute-start | bytes 1572872 | tf_op jit(solution)/shard_map/ppermute | solution.py:462
  70.3 17.5 %collective-permute-start.20 = (f32[256,512]{1,0:T(8,128)S(1)}, f32[256,512]{1,0:T(8,128)S(1)}, u32[]{:S(2)}, u32[]{:S(2)}) collective-permute-start(f32[256,512]{1,0:T(8,128)S(1)} %get-tuple-element.72), channel_id=1, source_target_pairs={{8,16},{16,8},{9,17},{17,9},{10,18},{18,10},{11,19},{19,11},{12,20... | collective-permute-start | bytes 1572872 | tf_op jit(solution)/shard_map/ppermute | solution.py:461
  88.0 13.1 %collective-permute-start.22 = (f32[4,4,256,128]{3,2,1,0:T(8,128)S(1)}, f32[4,4,256,128]{3,2,1,0:T(8,128)S(1)}, u32[]{:S(2)}, u32[]{:S(2)}) collective-permute-start(f32[4,4,256,128]{3,2,1,0:T(8,128)S(1)} %pack.3.refs_4_), channel_id=1, source_target_pairs={{0,1},{1,0},{2,3},{3,2},{4,5},{5,4},{6,7},{7,6},{8,9},{9,8},{10,11... | collective-permute-start | bytes 6291464 | tf_op jit(solution)/shard_map/ppermute | solution.py:22
  88.8 26.2 %collective-permute-start.27 = (f32[256,512]{1,0:T(8,128)S(1)}, f32[256,512]{1,0:T(8,128)S(1)}, u32[]{:S(2)}, u32[]{:S(2)}) collective-permute-start(f32[256,512]{1,0:T(8,128)S(1)} %get-tuple-element.83), channel_id=1, source_target_pairs={{8,24},{16,0},{0,8},{24,16},{9,25},{17,1},{1,9},{25,17},{10,26},{1... | collective-permute-start | bytes 1572872 | tf_op jit(solution)/shard_map/ppermute | solution.py:464
  105.5 20.5 %collective-permute-start.23 = (f32[256,512]{1,0:T(8,128)S(1)}, f32[256,512]{1,0:T(8,128)S(1)}, u32[]{:S(2)}, u32[]{:S(2)}) collective-permute-start(f32[256,512]{1,0:T(8,128)S(1)} %get-tuple-element.77), channel_id=1, source_target_pairs={{0,8},{24,16},{8,0},{16,24},{1,9},{25,17},{9,1},{17,25},{2,10},{26... | collective-permute-start | bytes 1572872 | tf_op jit(solution)/shard_map/ppermute | solution.py:460
  107.7 18.3 %collective-permute-start.25 = (f32[256,512]{1,0:T(8,128)S(1)}, f32[256,512]{1,0:T(8,128)S(1)}, u32[]{:S(2)}, u32[]{:S(2)}) collective-permute-start(f32[256,512]{1,0:T(8,128)S(1)} %get-tuple-element.79), channel_id=1, source_target_pairs={{8,16},{16,8},{9,17},{17,9},{10,18},{18,10},{11,19},{19,11},{12,20... | collective-permute-start | bytes 1572872 | tf_op jit(solution)/shard_map/ppermute | solution.py:461
  128.8 20.6 %collective-permute-start.24 = (f32[256,512]{1,0:T(8,128)S(1)}, f32[256,512]{1,0:T(8,128)S(1)}, u32[]{:S(2)}, u32[]{:S(2)}) collective-permute-start(f32[256,512]{1,0:T(8,128)S(1)} %get-tuple-element.79), channel_id=1, source_target_pairs={{0,16},{24,8},{1,17},{25,9},{2,18},{26,10},{3,19},{27,11},{4,20},{... | collective-permute-start | bytes 1572872 | tf_op jit(solution)/shard_map/ppermute | solution.py:462
  133.2 24.1 %collective-permute-start.26 = (f32[256,512]{1,0:T(8,128)S(1)}, f32[256,512]{1,0:T(8,128)S(1)}, u32[]{:S(2)}, u32[]{:S(2)}) collective-permute-start(f32[256,512]{1,0:T(8,128)S(1)} %get-tuple-element.80), channel_id=1, source_target_pairs={{8,24},{16,0},{0,8},{24,16},{9,25},{17,1},{1,9},{25,17},{10,26},{1... | collective-permute-start | bytes 1572872 | tf_op jit(solution)/shard_map/ppermute | solution.py:464
  133.9 9.2 %collective-permute-start.29 = (f32[2,64,512]{2,1,0:T(8,128)S(1)}, f32[2,64,512]{2,1,0:T(8,128)S(1)}, u32[]{:S(2)}, u32[]{:S(2)}) collective-permute-start(f32[2,64,512]{2,1,0:T(8,128)S(1)} %get-tuple-element.92), channel_id=1, source_target_pairs={{0,2},{1,3},{2,0},{3,1},{4,6},{5,7},{6,4},{7,5},{8,10},{9,11},{10,... | collective-permute-start | bytes 786440 | tf_op jit(solution)/shard_map/ppermute | solution.py:22
  134.8 14.0 %collective-permute-start.30 = (f32[2,64,512]{2,1,0:T(8,128)S(1)}, f32[2,64,512]{2,1,0:T(8,128)S(1)}, u32[]{:S(2)}, u32[]{:S(2)}) collective-permute-start(f32[2,64,512]{2,1,0:T(8,128)S(1)} %get-tuple-element.93), channel_id=1, source_target_pairs={{0,4},{1,5},{2,6},{3,7},{4,0},{5,1},{6,2},{7,3},{8,12},{9,13},{10,... | collective-permute-start | bytes 786440 | tf_op jit(solution)/shard_map/ppermute | solution.py:22
  136.9 11.9 %collective-permute-start.31 = (f32[2,64,512]{2,1,0:T(8,128)S(1)}, f32[2,64,512]{2,1,0:T(8,128)S(1)}, u32[]{:S(2)}, u32[]{:S(2)}) collective-permute-start(f32[2,64,512]{2,1,0:T(8,128)S(1)} %get-tuple-element.94), channel_id=1, source_target_pairs={{0,6},{1,7},{2,4},{3,5},{4,2},{5,3},{6,0},{7,1},{8,14},{9,15},{10,... | collective-permute-start | bytes 786440 | tf_op jit(solution)/shard_map/ppermute | solution.py:22
  162.6 7.8 %collective-permute-start.37 = (f32[1,64,512]{2,1,0:T(8,128)S(1)}, f32[1,64,512]{2,1,0:T(8,128)S(1)}, u32[]{:S(2)}, u32[]{:S(2)}) collective-permute-start(f32[1,64,512]{2,1,0:T(8,128)S(1)} %get-tuple-element.103), channel_id=1, source_target_pairs={{0,4},{1,5},{2,6},{3,7},{4,0},{5,1},{6,2},{7,3},{8,12},{9,13},{10,... | collective-permute-start | bytes 393224 | tf_op jit(solution)/shard_map/ppermute | solution.py:22
  164.8 7.1 %collective-permute-start.38 = (f32[1,64,512]{2,1,0:T(8,128)S(1)}, f32[1,64,512]{2,1,0:T(8,128)S(1)}, u32[]{:S(2)}, u32[]{:S(2)}) collective-permute-start(f32[1,64,512]{2,1,0:T(8,128)S(1)} %get-tuple-element.104), channel_id=1, source_target_pairs={{0,6},{1,7},{2,4},{3,5},{4,2},{5,3},{6,0},{7,1},{8,14},{9,15},{10,... | collective-permute-start | bytes 393224 | tf_op jit(solution)/shard_map/ppermute | solution.py:22
  165.6 8.8 %collective-permute-start.33 = (f32[64,512]{1,0:T(8,128)S(1)}, f32[64,512]{1,0:T(8,128)S(1)}, u32[]{:S(2)}, u32[]{:S(2)}) collective-permute-start(f32[64,512]{1,0:T(8,128)S(1)} %add_up.4.refs_0_), channel_id=1, source_target_pairs={{0,16},{8,24},{16,0},{24,8},{1,17},{9,25},{17,1},{25,9},{2,18},{10... | collective-permute-start | bytes 393224 | tf_op jit(solution)/shard_map/ppermute | solution.py:22
  174.4 6.8 %collective-permute-start.34 = (f32[64,512]{1,0:T(8,128)S(1)}, f32[64,512]{1,0:T(8,128)S(1)}, u32[]{:S(2)}, u32[]{:S(2)}) collective-permute-start(f32[64,512]{1,0:T(8,128)S(1)} %add_up.5.refs_3_), channel_id=1, source_target_pairs={{0,8},{8,0},{16,24},{24,16},{1,9},{9,1},{17,25},{25,17},{2,10},{10... | collective-permute-start | bytes 393224 | tf_op jit(solution)/shard_map/ppermute | solution.py:22
  177.7 7.6 %collective-permute-start.40 = (f32[1,64,512]{2,1,0:T(8,128)S(1)}, f32[1,64,512]{2,1,0:T(8,128)S(1)}, u32[]{:S(2)}, u32[]{:S(2)}) collective-permute-start(f32[1,64,512]{2,1,0:T(8,128)S(1)} %add_up.7.refs_5_), channel_id=1, source_target_pairs={{0,16},{8,24},{16,0},{24,8},{1,17},{9,25},{17,1},{25,9},{2,18},{10... | collective-permute-start | bytes 393224 | tf_op jit(solution)/shard_map/ppermute | solution.py:22
  (20 other events, 175.5 us)

commit v15 on v13

--- a/solution.py
+++ b/solution.py
@@ -560,7 +560,7 @@
         waits = [] if last else rows[number + 1][2:4] + lates[number + 1]
         offdiag, keep, send, *link = finish(
             number, own_block, place, ancestors, rows[number][:3] + rows[number][4:], factor, before,
-            link_factor, pcol_count // 2, waits + pending[:1],
+            link_factor, pcol_count // 2, waits + pending,
         )
         if pending:
             sums += sum_pair_far(pending, count, [keep])

time: 172 us -> 175 us (1.017)
  Pallas kernels: 28.1 us -> 32 us
  starting transfers between devices: 60.8 us -> 58.1 us
    ppermute x2, starting transfers between devices: 7.93 us -> 3.53 us  [sum_over_four(): total = lax.ppermute(slots[1], 'prow', [(0, 2), (2, 3), (3, 1), (1, 0)])]
    pallas_call x26, Pallas kernels: 28.1 us -> 32 us  [run(): pl.pallas_call(body, grid_spec=pltpu.PrefetchScalarGridSpec(num_scalar_pr...]
    ppermute x2, starting transfers between devices: 6.27 us -> 8.61 us  [sum_over_four(): near = lax.ppermute(slots[0], 'prow', [(0, 1), (3, 2)])]
    ppermute x33, starting transfers between devices: 41.5 us -> 39.6 us  [flip(): lax.ppermute(value, axis, [(i, i ^ bit) for i in range(lax.axis_size(axis...]
  transfers between devices with their start and end apart: 41 -> 41, of which waited for: 24 -> 23; matrix products, arithmetic and copies ran while one was open for 0% -> 0% of each run, Pallas kernels for 12% -> 12%
where the time goes in v15:
time: 175 us; the launch traced here: 174 us
  waiting for transfers between devices  78 us (45%)
  starting transfers between devices  58.1 us (33%)
  Pallas kernels  32 us (18%)
  local copies, waits for them, and re-layouts  5.3 us (3%)
    ppermute x33, waiting for transfers between devices, flip(): lax.ppermute(value, axis, [(i, i ^ bit) for i in range(lax.axis_size(axis...  54.9 us
    ppermute x33, starting transfers between devices, flip(): lax.ppermute(value, axis, [(i, i ^ bit) for i in range(lax.axis_size(axis...  39.6 us
    pallas_call x26, Pallas kernels, run(): pl.pallas_call(body, grid_spec=pltpu.PrefetchScalarGridSpec(num_scalar_pr...  32 us
    ppermute x2, waiting for transfers between devices, sum_over_four(): near = lax.ppermute(slots[0], 'prow', [(0, 1), (3, 2)])  15.4 us
    ppermute x2, starting transfers between devices, sum_over_four(): near = lax.ppermute(slots[0], 'prow', [(0, 1), (3, 2)])  8.61 us
    ppermute x2, waiting for transfers between devices, sum_over_four(): last = lax.ppermute(both, 'prow', [(1, 3), (2, 0), (0, 1), (3, 2)])  7.77 us
    unnamed x22, local copies, waits for them, and re-layouts  5.3 us
    ppermute x2, starting transfers between devices, sum_over_four(): last = lax.ppermute(both, 'prow', [(1, 3), (2, 0), (0, 1), (3, 2)])  4.83 us
  transfers between devices with their start and end apart: 41, of which 23 were waited for; matrix products, arithmetic and copies ran while one was open for 0% of the time, Pallas kernels for 12%

profile of v15, /device:TPU:0, one launch (start us, length us, event | category | flops | bytes accessed | tf_op | source)
XLA Modules:
  0.0 174.5 jit_solution(397647336220952611)
XLA Ops:
  2.6 3.0 %collective-permute-start = (f32[256,128]{1,0:T(8,128)S(1)}, f32[256,128]{1,0:T(8,128)S(1)}, u32[]{:S(2)}, u32[]{:S(2)}) collective-permute-start(f32[256,128]{1,0:T(8,128)S(1)} %get-tuple-element.51), channel_id=1, source_target_pairs={{0,2},{1,3},{2,0},{3,1},{4,6},{5,7},{6,4},{7,5},{8,10},{9,11},{10,... | collective-permute-start | bytes 393224 | tf_op jit(solution)/shard_map/ppermute | solution.py:22
  7.1 2.4 %collective-permute-done.refs_2_ = f32[256,128]{1,0:T(8,128)S(1)} collective-permute-done((f32[256,128]{1,0:T(8,128)S(1)}, f32[256,128]{1,0:T(8,128)S(1)}, u32[]{:S(2)}, u32[]{:S(2)}) %collective-permute-start) | collective-permute-done | bytes 131104 | tf_op jit(solution)/shard_map/ppermute | solution.py:22
  9.5 3.9 %collective-permute-done.1.refs_3_ = f32[256,128]{1,0:T(8,128)S(1)} collective-permute-done((f32[256,128]{1,0:T(8,128)S(1)}, f32[256,128]{1,0:T(8,128)S(1)}, u32[]{:S(2)}, u32[]{:S(2)}) %collective-permute-start.1) | collective-permute-done | bytes 131104 | tf_op jit(solution)/shard_map/ppermute | solution.py:22
  15.6 2.6 %collective-permute-start.7 = (f32[256,128]{1,0:T(8,128)S(1)}, f32[256,128]{1,0:T(8,128)S(1)}, u32[]{:S(2)}, u32[]{:S(2)}) collective-permute-start(f32[256,128]{1,0:T(8,128)S(1)} %get-tuple-element.60), channel_id=1, source_target_pairs={{0,16},{8,24},{16,0},{24,8},{1,17},{9,25},{17,1},{25,9},{2,18},{10... | collective-permute-start | bytes 393224 | tf_op jit(solution)/shard_map/ppermute | solution.py:22
  23.8 3.4 %collective-permute-done.7.refs_6_.refs_3_ = f32[256,128]{1,0:T(8,128)S(1)} collective-permute-done((f32[256,128]{1,0:T(8,128)S(1)}, f32[256,128]{1,0:T(8,128)S(1)}, u32[]{:S(2)}, u32[]{:S(2)}) %collective-permute-start.7) | collective-permute-done | bytes 131104 | tf_op jit(solution)/shard_map/ppermute | solution.py:22
  34.0 3.2 %collective-permute-start.10 = (f32[256,128]{1,0:T(8,128)S(1)}, f32[256,128]{1,0:T(8,128)S(1)}, u32[]{:S(2)}, u32[]{:S(2)}) collective-permute-start(f32[256,128]{1,0:T(8,128)S(1)} %get-tuple-element.64), channel_id=1, source_target_pairs={{0,16},{8,24},{16,0},{24,8},{1,17},{9,25},{17,1},{25,9},{2,18},{10... | collective-permute-start | bytes 393224 | tf_op jit(solution)/shard_map/ppermute | solution.py:22
  38.3 4.9 %collective-permute-start.11 = (f32[256,128]{1,0:T(8,128)S(1)}, f32[256,128]{1,0:T(8,128)S(1)}, u32[]{:S(2)}, u32[]{:S(2)}) collective-permute-start(f32[256,128]{1,0:T(8,128)S(1)} %get-tuple-element.65), channel_id=1, source_target_pairs={{0,24},{8,16},{16,8},{24,0},{1,25},{9,17},{17,9},{25,1},{2,26},{10... | collective-permute-start | bytes 393224 | tf_op jit(solution)/shard_map/ppermute | solution.py:22
  46.0 2.5 %bases.1 = (f32[2,64,512]{2,1,0:T(8,128)S(1)}, f32[1,64,512]{2,1,0:T(8,128)S(1)}) custom-call(s32[3]{0:T(128)S(1)} %pad_add_fusion.refs_0_, f32[2,512,512]{2,1,0:T(8,128)S(1)} %copy-done.6, f32[1,512,512]{2,1,0:T(8,128)S(1)} %copy-done.3, f32[256,128]{1,0:T(8,128)S(1)} %get-tuple-element.54.refs_2_.refs_1_.refs_3_), custom_call_target="tpu_custom_call" | custom-call | tf_op jit(solution)/shard_map/bases/pallas_call | solution.py:36
  48.5 3.0 %collective-permute-done.13.refs_6_.refs_2_ = f32[4,256,128]{2,1,0:T(8,128)S(1)} collective-permute-done((f32[4,256,128]{2,1,0:T(8,128)S(1)}, f32[4,256,128]{2,1,0:T(8,128)S(1)}, u32[]{:S(2)}, u32[]{:S(2)}) %collective-permute-start.13) | collective-permute-done | bytes 524320 | tf_op jit(solution)/shard_map/ppermute | solution.py:22
  56.6 4.3 %partial_product.4 = (f32[256,512]{1,0:T(8,128)S(1)}, f32[256,512]{1,0:T(8,128)S(1)}) custom-call(s32[3]{0:T(128)S(1)} %pad_add_fusion.refs_0_, s32[4,4]{1,0:T(4,128)S(1)} %copy-done.8, s32[2,8]{1,0:T(2,128)S(1)} %copy-done.7, f32[1024,2048]{1,0:T(8,128)S(1)} %bitcast.4, f32[4,4,256,128]{3,2,1,0:T(8,128)S(1)} %pack.2.refs_4_, ...), custom_call_target="tpu_custom_call" | custom-call | tf_op jit(solution)/shard_map/partial_product/pallas_call | solution.py:36
  62.6 2.5 %collective-permute-start.21 = (f32[256,512]{1,0:T(8,128)S(1)}, f32[256,512]{1,0:T(8,128)S(1)}, u32[]{:S(2)}, u32[]{:S(2)}) collective-permute-start(f32[256,512]{1,0:T(8,128)S(1)} %get-tuple-element.68), channel_id=1, source_target_pairs={{0,8},{24,16},{1,9},{25,17},{2,10},{26,18},{3,11},{27,19},{4,12},{... | collective-permute-start | bytes 1572872 | tf_op jit(solution)/shard_map/ppermute | solution.py:444
  65.2 3.6 %collective-permute-done.17.refs_3_ = f32[4,256,128]{2,1,0:T(8,128)S(1)} collective-permute-done((f32[4,256,128]{2,1,0:T(8,128)S(1)}, f32[4,256,128]{2,1,0:T(8,128)S(1)}, u32[]{:S(2)}, u32[]{:S(2)}) %collective-permute-start.17) | collective-permute-done | bytes 524320 | tf_op jit(solution)/shard_map/ppermute | solution.py:22
  69.5 4.3 %partial_product.5 = (f32[256,512]{1,0:T(8,128)S(1)}, f32[256,512]{1,0:T(8,128)S(1)}) custom-call(s32[3]{0:T(128)S(1)} %pad_add_fusion.refs_0_, s32[4,4]{1,0:T(4,128)S(1)} %copy-done.8, s32[2,8]{1,0:T(2,128)S(1)} %copy-done.7, f32[1024,2048]{1,0:T(8,128)S(1)} %bitcast.4, f32[4,4,256,128]{3,2,1,0:T(8,128)S(1)} %pack.2.refs_4_, ...), custom_call_target="tpu_custom_call" | custom-call | tf_op jit(solution)/shard_map/partial_product/pallas_call | solution.py:36
  73.8 5.1 %collective-permute-done.16.refs_2_ = f32[4,256,128]{2,1,0:T(8,128)S(1)} collective-permute-done((f32[4,256,128]{2,1,0:T(8,128)S(1)}, f32[4,256,128]{2,1,0:T(8,128)S(1)}, u32[]{:S(2)}, u32[]{:S(2)}) %collective-permute-start.16) | collective-permute-done | bytes 524320 | tf_op jit(solution)/shard_map/ppermute | solution.py:22
  78.9 5.0 %collective-permute-done.21.refs_6_.refs_1_ = f32[256,512]{1,0:T(8,128)S(1)} collective-permute-done((f32[256,512]{1,0:T(8,128)S(1)}, f32[256,512]{1,0:T(8,128)S(1)}, u32[]{:S(2)}, u32[]{:S(2)}) %collective-permute-start.21) | collective-permute-done | bytes 524320 | tf_op jit(solution)/shard_map/ppermute | solution.py:444
  84.3 4.1 %collective-permute-start.27 = (f32[256,512]{1,0:T(8,128)S(1)}, f32[256,512]{1,0:T(8,128)S(1)}, u32[]{:S(2)}, u32[]{:S(2)}) collective-permute-start(f32[256,512]{1,0:T(8,128)S(1)} %add_up.7), channel_id=1, source_target_pairs={{8,24},{16,0},{0,8},{24,16},{9,25},{17,1},{1,9},{25,17},{10,26},{1... | collective-permute-start | bytes 1572872 | tf_op jit(solution)/shard_map/ppermute | solution.py:448
  90.2 6.1 %collective-permute-start.25 = (f32[256,512]{1,0:T(8,128)S(1)}, f32[256,512]{1,0:T(8,128)S(1)}, u32[]{:S(2)}, u32[]{:S(2)}) collective-permute-start(f32[256,512]{1,0:T(8,128)S(1)} %partial_product.7), channel_id=1, source_target_pairs={{0,8},{24,16},{1,9},{25,17},{2,10},{26,18},{3,11},{27,19},{4,12},{... | collective-permute-start | bytes 1572872 | tf_op jit(solution)/shard_map/ppermute | solution.py:444
  97.2 3.2 %partial_product.6 = (f32[256,512]{1,0:T(8,128)S(1)}, f32[256,512]{1,0:T(8,128)S(1)}, f32[256,512]{1,0:T(8,128)S(1)}) custom-call(s32[3]{0:T(128)S(1)} %pad_add_fusion.refs_0_, s32[4,4]{1,0:T(4,128)S(1)} %copy-done.8, s32[2,8]{1,0:T(2,128)S(1)} %copy-done.7, f32[1024,2048]{1,0:T(8,128)S(1)} %bitcast.4, f32[4,4,256,128]{3,2,1,0:T(8,128)S(1)} %pack.3.refs_4_, ...), custom_call_target="tpu_custom_call" | custom-call | tf_op jit(solution)/shard_map/partial_product/pallas_call | solution.py:36
  101.2 10.3 %collective-permute-done.25.refs_1_.refs_10_ = f32[256,512]{1,0:T(8,128)S(1)} collective-permute-done((f32[256,512]{1,0:T(8,128)S(1)}, f32[256,512]{1,0:T(8,128)S(1)}, u32[]{:S(2)}, u32[]{:S(2)}) %collective-permute-start.25) | collective-permute-done | bytes 524320 | tf_op jit(solution)/shard_map/ppermute | solution.py:444
  111.5 3.4 %finish.2 = (f32[2,256,512]{2,1,0:T(8,128)}, f32[2,4,64,512]{3,2,1,0:T(8,128)S(1)}, f32[2,4,64,512]{3,2,1,0:T(8,128)S(1)}, f32[512,512]{1,0:T(8,128)S(1)}, f32[512,512]{1,0:T(8,128)S(1)}) custom-call(s32[3]{0:T(128)S(1)} %pad_add_fusion.refs_0_, s32[2,8]{1,0:T(2,128)S(1)} %copy-done.7, f32[256,512]{1,0:T(8,128)S(1)} %get-tuple-element.69.refs_7_.refs_2_, ...), custom_call_target="tpu_custom_call" | custom-call | tf_op jit(solution)/shard_map/finish/pallas_call | solution.py:36
  121.8 2.3 %rest.1 = (f32[512,512]{1,0:T(8,128)S(1)}, f32[256,512]{1,0:T(8,128)S(1)}) custom-call(f32[1,512,512]{2,1,0:T(8,128)S(1)} %copy-done.4, f32[512,512]{1,0:T(8,128)S(1)} %get-tuple-element.74.refs_1_, f32[512,512]{1,0:T(8,128)S(1)} %get-tuple-element.75.refs_2_, f32[2,256,512]{2,1,0:T(8,128)S(1)} %copy-done.5), custom_call_target="tpu_custom_call" | custom-call | tf_op jit(solution)/shard_map/rest/pallas_call | solution.py:36
  124.1 3.4 %collective-permute-done.29.refs_2_ = f32[2,64,512]{2,1,0:T(8,128)S(1)} collective-permute-done((f32[2,64,512]{2,1,0:T(8,128)S(1)}, f32[2,64,512]{2,1,0:T(8,128)S(1)}, u32[]{:S(2)}, u32[]{:S(2)}) %collective-permute-start.29) | collective-permute-done | bytes 262176 | tf_op jit(solution)/shard_map/ppermute | solution.py:22
  127.4 6.0 %collective-permute-done.30.refs_3_ = f32[2,64,512]{2,1,0:T(8,128)S(1)} collective-permute-done((f32[2,64,512]{2,1,0:T(8,128)S(1)}, f32[2,64,512]{2,1,0:T(8,128)S(1)}, u32[]{:S(2)}, u32[]{:S(2)}) %collective-permute-start.30) | collective-permute-done | bytes 262176 | tf_op jit(solution)/shard_map/ppermute | solution.py:22
  136.2 7.0 %collective-permute-done.26.refs_5_ = f32[256,512]{1,0:T(8,128)S(1)} collective-permute-done((f32[256,512]{1,0:T(8,128)S(1)}, f32[256,512]{1,0:T(8,128)S(1)}, u32[]{:S(2)}, u32[]{:S(2)}) %collective-permute-start.26) | collective-permute-done | bytes 524320 | tf_op jit(solution)/shard_map/ppermute | solution.py:448
  143.2 2.7 %collective-permute-done.32.refs_11_.refs_1_ = f32[64,512]{1,0:T(8,128)S(1)} collective-permute-done((f32[64,512]{1,0:T(8,128)S(1)}, f32[64,512]{1,0:T(8,128)S(1)}, u32[]{:S(2)}, u32[]{:S(2)}) %collective-permute-start.32) | collective-permute-done | bytes 131104 | tf_op jit(solution)/shard_map/ppermute | solution.py:22
  145.9 2.9 %finish.3 = (f32[2,256,512]{2,1,0:T(8,128)}, f32[1,4,64,512]{3,2,1,0:T(8,128)S(1)}, f32[1,4,64,512]{3,2,1,0:T(8,128)S(1)}) custom-call(s32[3]{0:T(128)S(1)} %pad_add_fusion.refs_0_, s32[2,8]{1,0:T(2,128)S(1)} %copy-done.7, f32[256,512]{1,0:T(8,128)S(1)} %get-tuple-element.70.refs_11_.refs_2_, ...), custom_call_target="tpu_custom_call", output_to_operand_aliasing={{0}: (9, {})} | custom-call | tf_op jit(solution)/shard_map/finish/pallas_call | solution.py:36
  151.4 2.7 %collective-permute-start.37 = (f32[1,64,512]{2,1,0:T(8,128)S(1)}, f32[1,64,512]{2,1,0:T(8,128)S(1)}, u32[]{:S(2)}, u32[]{:S(2)}) collective-permute-start(f32[1,64,512]{2,1,0:T(8,128)S(1)} %get-tuple-element.93), channel_id=1, source_target_pairs={{0,4},{1,5},{2,6},{3,7},{4,0},{5,1},{6,2},{7,3},{8,12},{9,13},{10,... | collective-permute-start | bytes 393224 | tf_op jit(solution)/shard_map/ppermute | solution.py:22
  155.0 2.7 %collective-permute-done.36.refs_1_ = f32[1,64,512]{2,1,0:T(8,128)S(1)} collective-permute-done((f32[1,64,512]{2,1,0:T(8,128)S(1)}, f32[1,64,512]{2,1,0:T(8,128)S(1)}, u32[]{:S(2)}, u32[]{:S(2)}) %collective-permute-start.36) | collective-permute-done | bytes 131104 | tf_op jit(solution)/shard_map/ppermute | solution.py:22
  157.7 2.7 %collective-permute-done.37.refs_2_ = f32[1,64,512]{2,1,0:T(8,128)S(1)} collective-permute-done((f32[1,64,512]{2,1,0:T(8,128)S(1)}, f32[1,64,512]{2,1,0:T(8,128)S(1)}, u32[]{:S(2)}, u32[]{:S(2)}) %collective-permute-start.37) | collective-permute-done | bytes 131104 | tf_op jit(solution)/shard_map/ppermute | solution.py:22
  162.9 2.7 %collective-permute-done.39.refs_1_ = f32[1,64,512]{2,1,0:T(8,128)S(1)} collective-permute-done((f32[1,64,512]{2,1,0:T(8,128)S(1)}, f32[1,64,512]{2,1,0:T(8,128)S(1)}, u32[]{:S(2)}, u32[]{:S(2)}) %collective-permute-start.39) | collective-permute-done | bytes 131104 | tf_op jit(solution)/shard_map/ppermute | solution.py:22
  166.4 3.0 %collective-permute-done.34.refs_4_ = f32[64,512]{1,0:T(8,128)S(1)} collective-permute-done((f32[64,512]{1,0:T(8,128)S(1)}, f32[64,512]{1,0:T(8,128)S(1)}, u32[]{:S(2)}, u32[]{:S(2)}) %collective-permute-start.34) | collective-permute-done | bytes 131104 | tf_op jit(solution)/shard_map/ppermute | solution.py:22
  169.3 3.8 %collective-permute-done.40.refs_6_ = f32[1,64,512]{2,1,0:T(8,128)S(1)} collective-permute-done((f32[1,64,512]{2,1,0:T(8,128)S(1)}, f32[1,64,512]{2,1,0:T(8,128)S(1)}, u32[]{:S(2)}, u32[]{:S(2)}) %collective-permute-start.40) | collective-permute-done | bytes 131104 | tf_op jit(solution)/shard_map/ppermute | solution.py:22
  (100 shorter events, 50.8 us)
Async XLA Ops:
  2.6 6.9 %collective-permute-start = (f32[256,128]{1,0:T(8,128)S(1)}, f32[256,128]{1,0:T(8,128)S(1)}, u32[]{:S(2)}, u32[]{:S(2)}) collective-permute-start(f32[256,128]{1,0:T(8,128)S(1)} %get-tuple-element.51), channel_id=1, source_target_pairs={{0,2},{1,3},{2,0},{3,1},{4,6},{5,7},{6,4},{7,5},{8,10},{9,11},{10,... | collective-permute-start | bytes 393224 | tf_op jit(solution)/shard_map/ppermute | solution.py:22
  5.6 7.8 %collective-permute-start.1 = (f32[256,128]{1,0:T(8,128)S(1)}, f32[256,128]{1,0:T(8,128)S(1)}, u32[]{:S(2)}, u32[]{:S(2)}) collective-permute-start(f32[256,128]{1,0:T(8,128)S(1)} %get-tuple-element.52), channel_id=1, source_target_pairs={{0,4},{1,5},{2,6},{3,7},{4,0},{5,1},{6,2},{7,3},{8,12},{9,13},{10,... | collective-permute-start | bytes 393224 | tf_op jit(solution)/shard_map/ppermute | solution.py:22
  14.0 8.4 %collective-permute-start.6 = (f32[256,128]{1,0:T(8,128)S(1)}, f32[256,128]{1,0:T(8,128)S(1)}, u32[]{:S(2)}, u32[]{:S(2)}) collective-permute-start(f32[256,128]{1,0:T(8,128)S(1)} %get-tuple-element.59), channel_id=1, source_target_pairs={{0,8},{8,0},{16,24},{24,16},{1,9},{9,1},{17,25},{25,17},{2,10},{10... | collective-permute-start | bytes 393224 | tf_op jit(solution)/shard_map/ppermute | solution.py:22
  15.6 11.6 %collective-permute-start.7 = (f32[256,128]{1,0:T(8,128)S(1)}, f32[256,128]{1,0:T(8,128)S(1)}, u32[]{:S(2)}, u32[]{:S(2)}) collective-permute-start(f32[256,128]{1,0:T(8,128)S(1)} %get-tuple-element.60), channel_id=1, source_target_pairs={{0,16},{8,24},{16,0},{24,8},{1,17},{9,25},{17,1},{25,9},{2,18},{10... | collective-permute-start | bytes 393224 | tf_op jit(solution)/shard_map/ppermute | solution.py:22
  18.2 9.0 %collective-permute-start.8 = (f32[256,128]{1,0:T(8,128)S(1)}, f32[256,128]{1,0:T(8,128)S(1)}, u32[]{:S(2)}, u32[]{:S(2)}) collective-permute-start(f32[256,128]{1,0:T(8,128)S(1)} %get-tuple-element.61), channel_id=1, source_target_pairs={{0,24},{8,16},{16,8},{24,0},{1,25},{9,17},{17,9},{25,1},{2,26},{10... | collective-permute-start | bytes 393224 | tf_op jit(solution)/shard_map/ppermute | solution.py:22
  20.3 6.9 %collective-permute-start.3 = (f32[256,128]{1,0:T(8,128)S(1)}, f32[256,128]{1,0:T(8,128)S(1)}, u32[]{:S(2)}, u32[]{:S(2)}) collective-permute-start(f32[256,128]{1,0:T(8,128)S(1)} %get-tuple-element.56), channel_id=1, source_target_pairs={{0,2},{1,3},{2,0},{3,1},{4,6},{5,7},{6,4},{7,5},{8,10},{9,11},{10,... | collective-permute-start | bytes 393224 | tf_op jit(solution)/shard_map/ppermute | solution.py:22
  28.8 19.7 %collective-permute-start.14 = (f32[4,256,128]{2,1,0:T(8,128)S(1)}, f32[4,256,128]{2,1,0:T(8,128)S(1)}, u32[]{:S(2)}, u32[]{:S(2)}) collective-permute-start(f32[4,256,128]{2,1,0:T(8,128)S(1)} %arrange.2.refs_0_), channel_id=1, source_target_pairs={{0,6},{1,7},{2,4},{3,5},{4,2},{5,3},{6,0},{7,1},{8,14},{9,15},{10,... | collective-permute-start | bytes 1572872 | tf_op jit(solution)/shard_map/ppermute | solution.py:22
  30.3 21.2 %collective-permute-start.13 = (f32[4,256,128]{2,1,0:T(8,128)S(1)}, f32[4,256,128]{2,1,0:T(8,128)S(1)}, u32[]{:S(2)}, u32[]{:S(2)}) collective-permute-start(f32[4,256,128]{2,1,0:T(8,128)S(1)} %arrange.2.refs_0_), channel_id=1, source_target_pairs={{0,4},{1,5},{2,6},{3,7},{4,0},{5,1},{6,2},{7,3},{8,12},{9,13},{10,... | collective-permute-start | bytes 1572872 | tf_op jit(solution)/shard_map/ppermute | solution.py:22
  31.8 20.4 %collective-permute-start.12 = (f32[4,256,128]{2,1,0:T(8,128)S(1)}, f32[4,256,128]{2,1,0:T(8,128)S(1)}, u32[]{:S(2)}, u32[]{:S(2)}) collective-permute-start(f32[4,256,128]{2,1,0:T(8,128)S(1)} %arrange.2.refs_0_), channel_id=1, source_target_pairs={{0,2},{1,3},{2,0},{3,1},{4,6},{5,7},{6,4},{7,5},{8,10},{9,11},{10,... | collective-permute-start | bytes 1572872 | tf_op jit(solution)/shard_map/ppermute | solution.py:22
  34.0 14.5 %collective-permute-start.10 = (f32[256,128]{1,0:T(8,128)S(1)}, f32[256,128]{1,0:T(8,128)S(1)}, u32[]{:S(2)}, u32[]{:S(2)}) collective-permute-start(f32[256,128]{1,0:T(8,128)S(1)} %get-tuple-element.64), channel_id=1, source_target_pairs={{0,16},{8,24},{16,0},{24,8},{1,17},{9,25},{17,1},{25,9},{2,18},{10... | collective-permute-start | bytes 393224 | tf_op jit(solution)/shard_map/ppermute | solution.py:22
  38.3 10.2 %collective-permute-start.11 = (f32[256,128]{1,0:T(8,128)S(1)}, f32[256,128]{1,0:T(8,128)S(1)}, u32[]{:S(2)}, u32[]{:S(2)}) collective-permute-start(f32[256,128]{1,0:T(8,128)S(1)} %get-tuple-element.65), channel_id=1, source_target_pairs={{0,24},{8,16},{16,8},{24,0},{1,25},{9,17},{17,9},{25,1},{2,26},{10... | collective-permute-start | bytes 393224 | tf_op jit(solution)/shard_map/ppermute | solution.py:22
  53.0 15.7 %collective-permute-start.17 = (f32[4,256,128]{2,1,0:T(8,128)S(1)}, f32[4,256,128]{2,1,0:T(8,128)S(1)}, u32[]{:S(2)}, u32[]{:S(2)}) collective-permute-start(f32[4,256,128]{2,1,0:T(8,128)S(1)} %arrange.3.refs_0_), channel_id=1, source_target_pairs={{0,6},{1,7},{2,4},{3,5},{4,2},{5,3},{6,0},{7,1},{8,14},{9,15},{10,... | collective-permute-start | bytes 1572872 | tf_op jit(solution)/shard_map/ppermute | solution.py:22
  53.7 25.3 %collective-permute-start.16 = (f32[4,256,128]{2,1,0:T(8,128)S(1)}, f32[4,256,128]{2,1,0:T(8,128)S(1)}, u32[]{:S(2)}, u32[]{:S(2)}) collective-permute-start(f32[4,256,128]{2,1,0:T(8,128)S(1)} %arrange.3.refs_0_), channel_id=1, source_target_pairs={{0,4},{1,5},{2,6},{3,7},{4,0},{5,1},{6,2},{7,3},{8,12},{9,13},{10,... | collective-permute-start | bytes 1572872 | tf_op jit(solution)/shard_map/ppermute | solution.py:22
  54.8 24.1 %collective-permute-start.15 = (f32[4,256,128]{2,1,0:T(8,128)S(1)}, f32[4,256,128]{2,1,0:T(8,128)S(1)}, u32[]{:S(2)}, u32[]{:S(2)}) collective-permute-start(f32[4,256,128]{2,1,0:T(8,128)S(1)} %arrange.3.refs_0_), channel_id=1, source_target_pairs={{0,2},{1,3},{2,0},{3,1},{4,6},{5,7},{6,4},{7,5},{8,10},{9,11},{10,... | collective-permute-start | bytes 1572872 | tf_op jit(solution)/shard_map/ppermute | solution.py:22
  61.0 18.0 %collective-permute-start.19 = (f32[256,512]{1,0:T(8,128)S(1)}, f32[256,512]{1,0:T(8,128)S(1)}, u32[]{:S(2)}, u32[]{:S(2)}) collective-permute-start(f32[256,512]{1,0:T(8,128)S(1)} %get-tuple-element.67), channel_id=1, source_target_pairs={{0,16},{16,24},{24,8},{8,0},{1,17},{17,25},{25,9},{9,1},{2,18},{18... | collective-permute-start | bytes 1572872 | tf_op jit(solution)/shard_map/ppermute | solution.py:445
  62.6 21.4 %collective-permute-start.21 = (f32[256,512]{1,0:T(8,128)S(1)}, f32[256,512]{1,0:T(8,128)S(1)}, u32[]{:S(2)}, u32[]{:S(2)}) collective-permute-start(f32[256,512]{1,0:T(8,128)S(1)} %get-tuple-element.68), channel_id=1, source_target_pairs={{0,8},{24,16},{1,9},{25,17},{2,10},{26,18},{3,11},{27,19},{4,12},{... | collective-permute-start | bytes 1572872 | tf_op jit(solution)/shard_map/ppermute | solution.py:444
  68.8 15.2 %collective-permute-start.20 = (f32[256,512]{1,0:T(8,128)S(1)}, f32[256,512]{1,0:T(8,128)S(1)}, u32[]{:S(2)}, u32[]{:S(2)}) collective-permute-start(f32[256,512]{1,0:T(8,128)S(1)} %get-tuple-element.68), channel_id=1, source_target_pairs={{8,16},{16,8},{9,17},{17,9},{10,18},{18,10},{11,19},{19,11},{12,20... | collective-permute-start | bytes 1572872 | tf_op jit(solution)/shard_map/ppermute | solution.py:446
  84.3 16.9 %collective-permute-start.27 = (f32[256,512]{1,0:T(8,128)S(1)}, f32[256,512]{1,0:T(8,128)S(1)}, u32[]{:S(2)}, u32[]{:S(2)}) collective-permute-start(f32[256,512]{1,0:T(8,128)S(1)} %add_up.7), channel_id=1, source_target_pairs={{8,24},{16,0},{0,8},{24,16},{9,25},{17,1},{1,9},{25,17},{10,26},{1... | collective-permute-start | bytes 1572872 | tf_op jit(solution)/shard_map/ppermute | solution.py:448
  90.2 21.3 %collective-permute-start.25 = (f32[256,512]{1,0:T(8,128)S(1)}, f32[256,512]{1,0:T(8,128)S(1)}, u32[]{:S(2)}, u32[]{:S(2)}) collective-permute-start(f32[256,512]{1,0:T(8,128)S(1)} %partial_product.7), channel_id=1, source_target_pairs={{0,8},{24,16},{1,9},{25,17},{2,10},{26,18},{3,11},{27,19},{4,12},{... | collective-permute-start | bytes 1572872 | tf_op jit(solution)/shard_map/ppermute | solution.py:444
  96.3 15.2 %collective-permute-start.24 = (f32[256,512]{1,0:T(8,128)S(1)}, f32[256,512]{1,0:T(8,128)S(1)}, u32[]{:S(2)}, u32[]{:S(2)}) collective-permute-start(f32[256,512]{1,0:T(8,128)S(1)} %partial_product.7), channel_id=1, source_target_pairs={{8,16},{16,8},{9,17},{17,9},{10,18},{18,10},{11,19},{19,11},{12,20... | collective-permute-start | bytes 1572872 | tf_op jit(solution)/shard_map/ppermute | solution.py:446
  114.9 21.3 %collective-permute-start.23 = (f32[256,512]{1,0:T(8,128)S(1)}, f32[256,512]{1,0:T(8,128)S(1)}, u32[]{:S(2)}, u32[]{:S(2)}) collective-permute-start(f32[256,512]{1,0:T(8,128)S(1)} %get-tuple-element.71), channel_id=1, source_target_pairs={{0,16},{16,24},{24,8},{8,0},{1,17},{17,25},{25,9},{9,1},{2,18},{18... | collective-permute-start | bytes 1572872 | tf_op jit(solution)/shard_map/ppermute | solution.py:445
  116.8 26.3 %collective-permute-start.26 = (f32[256,512]{1,0:T(8,128)S(1)}, f32[256,512]{1,0:T(8,128)S(1)}, u32[]{:S(2)}, u32[]{:S(2)}) collective-permute-start(f32[256,512]{1,0:T(8,128)S(1)} %add_up.6), channel_id=1, source_target_pairs={{8,24},{16,0},{0,8},{24,16},{9,25},{17,1},{1,9},{25,17},{10,26},{1... | collective-permute-start | bytes 1572872 | tf_op jit(solution)/shard_map/ppermute | solution.py:448
  118.2 9.2 %collective-permute-start.29 = (f32[2,64,512]{2,1,0:T(8,128)S(1)}, f32[2,64,512]{2,1,0:T(8,128)S(1)}, u32[]{:S(2)}, u32[]{:S(2)}) collective-permute-start(f32[2,64,512]{2,1,0:T(8,128)S(1)} %get-tuple-element.82), channel_id=1, source_target_pairs={{0,2},{1,3},{2,0},{3,1},{4,6},{5,7},{6,4},{7,5},{8,10},{9,11},{10,... | collective-permute-start | bytes 786440 | tf_op jit(solution)/shard_map/ppermute | solution.py:22
  119.3 14.2 %collective-permute-start.30 = (f32[2,64,512]{2,1,0:T(8,128)S(1)}, f32[2,64,512]{2,1,0:T(8,128)S(1)}, u32[]{:S(2)}, u32[]{:S(2)}) collective-permute-start(f32[2,64,512]{2,1,0:T(8,128)S(1)} %get-tuple-element.83), channel_id=1, source_target_pairs={{0,4},{1,5},{2,6},{3,7},{4,0},{5,1},{6,2},{7,3},{8,12},{9,13},{10,... | collective-permute-start | bytes 786440 | tf_op jit(solution)/shard_map/ppermute | solution.py:22
  121.5 12.0 %collective-permute-start.31 = (f32[2,64,512]{2,1,0:T(8,128)S(1)}, f32[2,64,512]{2,1,0:T(8,128)S(1)}, u32[]{:S(2)}, u32[]{:S(2)}) collective-permute-start(f32[2,64,512]{2,1,0:T(8,128)S(1)} %get-tuple-element.84), channel_id=1, source_target_pairs={{0,6},{1,7},{2,4},{3,5},{4,2},{5,3},{6,0},{7,1},{8,14},{9,15},{10,... | collective-permute-start | bytes 786440 | tf_op jit(solution)/shard_map/ppermute | solution.py:22
  134.1 11.8 %collective-permute-start.32 = (f32[64,512]{1,0:T(8,128)S(1)}, f32[64,512]{1,0:T(8,128)S(1)}, u32[]{:S(2)}, u32[]{:S(2)}) collective-permute-start(f32[64,512]{1,0:T(8,128)S(1)} %get-tuple-element.86), channel_id=1, source_target_pairs={{0,8},{8,0},{16,24},{24,16},{1,9},{9,1},{17,25},{25,17},{2,10},{10... | collective-permute-start | bytes 393224 | tf_op jit(solution)/shard_map/ppermute | solution.py:22
  151.3 6.4 %collective-permute-start.36 = (f32[1,64,512]{2,1,0:T(8,128)S(1)}, f32[1,64,512]{2,1,0:T(8,128)S(1)}, u32[]{:S(2)}, u32[]{:S(2)}) collective-permute-start(f32[1,64,512]{2,1,0:T(8,128)S(1)} %get-tuple-element.92), channel_id=1, source_target_pairs={{0,2},{1,3},{2,0},{3,1},{4,6},{5,7},{6,4},{7,5},{8,10},{9,11},{10,... | collective-permute-start | bytes 393224 | tf_op jit(solution)/shard_map/ppermute | solution.py:22
  151.4 9.0 %collective-permute-start.37 = (f32[1,64,512]{2,1,0:T(8,128)S(1)}, f32[1,64,512]{2,1,0:T(8,128)S(1)}, u32[]{:S(2)}, u32[]{:S(2)}) collective-permute-start(f32[1,64,512]{2,1,0:T(8,128)S(1)} %get-tuple-element.93), channel_id=1, source_target_pairs={{0,4},{1,5},{2,6},{3,7},{4,0},{5,1},{6,2},{7,3},{8,12},{9,13},{10,... | collective-permute-start | bytes 393224 | tf_op jit(solution)/shard_map/ppermute | solution.py:22
  154.0 6.3 %collective-permute-start.38 = (f32[1,64,512]{2,1,0:T(8,128)S(1)}, f32[1,64,512]{2,1,0:T(8,128)S(1)}, u32[]{:S(2)}, u32[]{:S(2)}) collective-permute-start(f32[1,64,512]{2,1,0:T(8,128)S(1)} %get-tuple-element.94), channel_id=1, source_target_pairs={{0,6},{1,7},{2,4},{3,5},{4,2},{5,3},{6,0},{7,1},{8,14},{9,15},{10,... | collective-permute-start | bytes 393224 | tf_op jit(solution)/shard_map/ppermute | solution.py:22
  154.8 7.9 %collective-permute-start.33 = (f32[64,512]{1,0:T(8,128)S(1)}, f32[64,512]{1,0:T(8,128)S(1)}, u32[]{:S(2)}, u32[]{:S(2)}) collective-permute-start(f32[64,512]{1,0:T(8,128)S(1)} %add_up.8.refs_0_), channel_id=1, source_target_pairs={{0,16},{8,24},{16,0},{24,8},{1,17},{9,25},{17,1},{25,9},{2,18},{10... | collective-permute-start | bytes 393224 | tf_op jit(solution)/shard_map/ppermute | solution.py:22
  162.8 6.5 %collective-permute-start.34 = (f32[64,512]{1,0:T(8,128)S(1)}, f32[64,512]{1,0:T(8,128)S(1)}, u32[]{:S(2)}, u32[]{:S(2)}) collective-permute-start(f32[64,512]{1,0:T(8,128)S(1)} %add_up.9.refs_3_), channel_id=1, source_target_pairs={{0,8},{8,0},{16,24},{24,16},{1,9},{9,1},{17,25},{25,17},{2,10},{10... | collective-permute-start | bytes 393224 | tf_op jit(solution)/shard_map/ppermute | solution.py:22
  165.6 7.5 %collective-permute-start.40 = (f32[1,64,512]{2,1,0:T(8,128)S(1)}, f32[1,64,512]{2,1,0:T(8,128)S(1)}, u32[]{:S(2)}, u32[]{:S(2)}) collective-permute-start(f32[1,64,512]{2,1,0:T(8,128)S(1)} %add_up.11.refs_5_), channel_id=1, source_target_pairs={{0,16},{8,24},{16,0},{24,8},{1,17},{9,25},{17,1},{25,9},{2,18},{10... | collective-permute-start | bytes 393224 | tf_op jit(solution)/shard_map/ppermute | solution.py:22
  (20 other events, 177.6 us)

commit v16 on v13

--- a/solution.py
+++ b/solution.py
@@ -226,7 +226,7 @@
 
 def finish_kernel(number, last, first, block, place, ancestors, *refs):
     refs = list(refs)
-    sums, factor_ref = [refs.pop(0) for _ in range(4)], refs.pop(0)
+    sums, factor_ref = [refs.pop(0) for _ in range(2)], refs.pop(0)
     if not first:
         old_rest, old_rows, _ = (refs.pop(0) for _ in range(3))
     if not last:
@@ -242,7 +242,7 @@
 
     @pl.when(is_listed(ancestors, number, own))
     def _own():
-        summed = ((sums[0][...] + sums[1][...]) + sums[2][...]) + sums[3][...]
+        summed = sums[0][...] + sums[1][...]
         part_ref[...] += dot(factor_ref[0], summed, 0)
         offdiag_ref[0] = -(summed if first else summed + old_rows[...])
 
@@ -559,7 +559,7 @@
         last = number + 1 == nsuper
         waits = [] if last else rows[number + 1][2:4] + lates[number + 1]
         offdiag, keep, send, *link = finish(
-            number, own_block, place, ancestors, rows[number][:3] + rows[number][4:], factor, before,
+            number, own_block, place, ancestors, [add_up(rows[number][:3], []), rows[number][4]], factor, before,
             link_factor, pcol_count // 2, waits + pending[:1],
         )
         if pending:

time: 172 us -> 173 us (level)
  waiting for transfers between devices: 76.5 us -> 83.3 us
  starting transfers between devices: 60.8 us -> 55.5 us
    ppermute x2, waiting for transfers between devices: 0.01 us -> 5.67 us  [sum_over_four(): total = lax.ppermute(slots[1], 'prow', [(0, 2), (2, 3), (3, 1), (1, 0)])]
    ppermute x33, waiting for transfers between devices: 53.4 us -> 49.5 us  [flip(): lax.ppermute(value, axis, [(i, i ^ bit) for i in range(lax.axis_size(axis...]
    ppermute x33, starting transfers between devices: 41.5 us -> 37.9 us  [flip(): lax.ppermute(value, axis, [(i, i ^ bit) for i in range(lax.axis_size(axis...]
    ppermute x2, waiting for transfers between devices: 8.57 us -> 11.8 us  [sum_over_four(): last = lax.ppermute(both, 'prow', [(1, 3), (2, 0), (0, 1), (3, 2)])]
    ppermute x2, waiting for transfers between devices: 14.5 us -> 16.4 us  [sum_over_four(): near = lax.ppermute(slots[0], 'prow', [(0, 1), (3, 2)])]
    pallas_call x26 -> x28, Pallas kernels: 28.1 us -> 26.9 us  [run(): pl.pallas_call(body, grid_spec=pltpu.PrefetchScalarGridSpec(num_scalar_pr...]
  transfers between devices with their start and end apart: 41 -> 41, of which waited for: 24 -> 24; matrix products, arithmetic and copies ran while one was open for 0% -> 0% of each run, Pallas kernels for 12% -> 11%
where the time goes in v16:
time: 173 us; the launch traced here: 172 us
  waiting for transfers between devices  83.3 us (48%)
  starting transfers between devices  55.5 us (32%)
  Pallas kernels  26.9 us (16%)
  local copies, waits for them, and re-layouts  5.3 us (3%)
    ppermute x33, waiting for transfers between devices, flip(): lax.ppermute(value, axis, [(i, i ^ bit) for i in range(lax.axis_size(axis...  49.5 us
    ppermute x33, starting transfers between devices, flip(): lax.ppermute(value, axis, [(i, i ^ bit) for i in range(lax.axis_size(axis...  37.9 us
    pallas_call x28, Pallas kernels, run(): pl.pallas_call(body, grid_spec=pltpu.PrefetchScalarGridSpec(num_scalar_pr...  26.9 us
    ppermute x2, waiting for transfers between devices, sum_over_four(): near = lax.ppermute(slots[0], 'prow', [(0, 1), (3, 2)])  16.4 us
    ppermute x2, waiting for transfers between devices, sum_over_four(): last = lax.ppermute(both, 'prow', [(1, 3), (2, 0), (0, 1), (3, 2)])  11.8 us
    ppermute x2, starting transfers between devices, sum_over_four(): total = lax.ppermute(slots[1], 'prow', [(0, 2), (2, 3), (3, 1), (1, 0)])  7.69 us
    ppermute x2, starting transfers between devices, sum_over_four(): near = lax.ppermute(slots[0], 'prow', [(0, 1), (3, 2)])  5.73 us
    ppermute x2, waiting for transfers between devices, sum_over_four(): total = lax.ppermute(slots[1], 'prow', [(0, 2), (2, 3), (3, 1), (1, 0)])  5.67 us
  transfers between devices with their start and end apart: 41, of which 24 were waited for; matrix products, arithmetic and copies ran while one was open for 0% of the time, Pallas kernels for 11%

profile of v16, /device:TPU:0, one launch (start us, length us, event | category | flops | bytes accessed | tf_op | source)
XLA Modules:
  0.0 172.1 jit_solution(9600995236632656788)
XLA Ops:
  2.6 3.0 %collective-permute-start = (f32[256,128]{1,0:T(8,128)S(1)}, f32[256,128]{1,0:T(8,128)S(1)}, u32[]{:S(2)}, u32[]{:S(2)}) collective-permute-start(f32[256,128]{1,0:T(8,128)S(1)} %get-tuple-element.51), channel_id=1, source_target_pairs={{0,2},{1,3},{2,0},{3,1},{4,6},{5,7},{6,4},{7,5},{8,10},{9,11},{10,... | collective-permute-start | bytes 393224 | tf_op jit(solution)/shard_map/ppermute | solution.py:22
  7.1 2.4 %collective-permute-done.refs_2_ = f32[256,128]{1,0:T(8,128)S(1)} collective-permute-done((f32[256,128]{1,0:T(8,128)S(1)}, f32[256,128]{1,0:T(8,128)S(1)}, u32[]{:S(2)}, u32[]{:S(2)}) %collective-permute-start) | collective-permute-done | bytes 131104 | tf_op jit(solution)/shard_map/ppermute | solution.py:22
  9.5 3.9 %collective-permute-done.1.refs_3_ = f32[256,128]{1,0:T(8,128)S(1)} collective-permute-done((f32[256,128]{1,0:T(8,128)S(1)}, f32[256,128]{1,0:T(8,128)S(1)}, u32[]{:S(2)}, u32[]{:S(2)}) %collective-permute-start.1) | collective-permute-done | bytes 131104 | tf_op jit(solution)/shard_map/ppermute | solution.py:22
  15.6 2.6 %collective-permute-start.7 = (f32[256,128]{1,0:T(8,128)S(1)}, f32[256,128]{1,0:T(8,128)S(1)}, u32[]{:S(2)}, u32[]{:S(2)}) collective-permute-start(f32[256,128]{1,0:T(8,128)S(1)} %get-tuple-element.60), channel_id=1, source_target_pairs={{0,16},{8,24},{16,0},{24,8},{1,17},{9,25},{17,1},{25,9},{2,18},{10... | collective-permute-start | bytes 393224 | tf_op jit(solution)/shard_map/ppermute | solution.py:22
  23.8 3.4 %collective-permute-done.7.refs_6_.refs_3_ = f32[256,128]{1,0:T(8,128)S(1)} collective-permute-done((f32[256,128]{1,0:T(8,128)S(1)}, f32[256,128]{1,0:T(8,128)S(1)}, u32[]{:S(2)}, u32[]{:S(2)}) %collective-permute-start.7) | collective-permute-done | bytes 131104 | tf_op jit(solution)/shard_map/ppermute | solution.py:22
  34.0 3.2 %collective-permute-start.10 = (f32[256,128]{1,0:T(8,128)S(1)}, f32[256,128]{1,0:T(8,128)S(1)}, u32[]{:S(2)}, u32[]{:S(2)}) collective-permute-start(f32[256,128]{1,0:T(8,128)S(1)} %get-tuple-element.64), channel_id=1, source_target_pairs={{0,16},{8,24},{16,0},{24,8},{1,17},{9,25},{17,1},{25,9},{2,18},{10... | collective-permute-start | bytes 393224 | tf_op jit(solution)/shard_map/ppermute | solution.py:22
  38.3 4.9 %collective-permute-start.11 = (f32[256,128]{1,0:T(8,128)S(1)}, f32[256,128]{1,0:T(8,128)S(1)}, u32[]{:S(2)}, u32[]{:S(2)}) collective-permute-start(f32[256,128]{1,0:T(8,128)S(1)} %get-tuple-element.65), channel_id=1, source_target_pairs={{0,24},{8,16},{16,8},{24,0},{1,25},{9,17},{17,9},{25,1},{2,26},{10... | collective-permute-start | bytes 393224 | tf_op jit(solution)/shard_map/ppermute | solution.py:22
  46.0 2.5 %bases.1 = (f32[2,64,512]{2,1,0:T(8,128)S(1)}, f32[1,64,512]{2,1,0:T(8,128)S(1)}) custom-call(s32[3]{0:T(128)S(1)} %pad_add_fusion.refs_0_, f32[2,512,512]{2,1,0:T(8,128)S(1)} %copy-done.6, f32[1,512,512]{2,1,0:T(8,128)S(1)} %copy-done.3, f32[256,128]{1,0:T(8,128)S(1)} %get-tuple-element.54.refs_2_.refs_1_.refs_3_), custom_call_target="tpu_custom_call" | custom-call | tf_op jit(solution)/shard_map/bases/pallas_call | solution.py:36
  48.5 3.0 %collective-permute-done.13.refs_6_.refs_2_ = f32[4,256,128]{2,1,0:T(8,128)S(1)} collective-permute-done((f32[4,256,128]{2,1,0:T(8,128)S(1)}, f32[4,256,128]{2,1,0:T(8,128)S(1)}, u32[]{:S(2)}, u32[]{:S(2)}) %collective-permute-start.13) | collective-permute-done | bytes 524320 | tf_op jit(solution)/shard_map/ppermute | solution.py:22
  58.5 4.6 %collective-permute-start.19 = (f32[256,512]{1,0:T(8,128)S(1)}, f32[256,512]{1,0:T(8,128)S(1)}, u32[]{:S(2)}, u32[]{:S(2)}) collective-permute-start(f32[256,512]{1,0:T(8,128)S(1)} %get-tuple-element.67), channel_id=1, source_target_pairs={{0,16},{16,24},{24,8},{8,0},{1,17},{17,25},{25,9},{9,1},{2,18},{18... | collective-permute-start | bytes 1572872 | tf_op jit(solution)/shard_map/ppermute | solution.py:445
  64.4 4.3 %collective-permute-done.17.refs_3_ = f32[4,256,128]{2,1,0:T(8,128)S(1)} collective-permute-done((f32[4,256,128]{2,1,0:T(8,128)S(1)}, f32[4,256,128]{2,1,0:T(8,128)S(1)}, u32[]{:S(2)}, u32[]{:S(2)}) %collective-permute-start.17) | collective-permute-done | bytes 524320 | tf_op jit(solution)/shard_map/ppermute | solution.py:22
  69.5 4.3 %partial_product.5 = (f32[256,512]{1,0:T(8,128)S(1)}, f32[256,512]{1,0:T(8,128)S(1)}) custom-call(s32[3]{0:T(128)S(1)} %pad_add_fusion.refs_0_, s32[4,4]{1,0:T(4,128)S(1)} %copy-done.8, s32[2,8]{1,0:T(2,128)S(1)} %copy-done.7, f32[1024,2048]{1,0:T(8,128)S(1)} %bitcast.4, f32[4,4,256,128]{3,2,1,0:T(8,128)S(1)} %pack.2.refs_4_, ...), custom_call_target="tpu_custom_call" | custom-call | tf_op jit(solution)/shard_map/partial_product/pallas_call | solution.py:36
  73.8 5.1 %collective-permute-done.16.refs_2_ = f32[4,256,128]{2,1,0:T(8,128)S(1)} collective-permute-done((f32[4,256,128]{2,1,0:T(8,128)S(1)}, f32[4,256,128]{2,1,0:T(8,128)S(1)}, u32[]{:S(2)}, u32[]{:S(2)}) %collective-permute-start.16) | collective-permute-done | bytes 524320 | tf_op jit(solution)/shard_map/ppermute | solution.py:22
  78.9 6.9 %collective-permute-done.21.refs_6_.refs_1_ = f32[256,512]{1,0:T(8,128)S(1)} collective-permute-done((f32[256,512]{1,0:T(8,128)S(1)}, f32[256,512]{1,0:T(8,128)S(1)}, u32[]{:S(2)}, u32[]{:S(2)}) %collective-permute-start.21) | collective-permute-done | bytes 524320 | tf_op jit(solution)/shard_map/ppermute | solution.py:444
  86.2 2.5 %collective-permute-start.27 = (f32[256,512]{1,0:T(8,128)S(1)}, f32[256,512]{1,0:T(8,128)S(1)}, u32[]{:S(2)}, u32[]{:S(2)}) collective-permute-start(f32[256,512]{1,0:T(8,128)S(1)} %add_up.11), channel_id=1, source_target_pairs={{8,24},{16,0},{0,8},{24,16},{9,25},{17,1},{1,9},{25,17},{10,26},{1... | collective-permute-start | bytes 1572872 | tf_op jit(solution)/shard_map/ppermute | solution.py:448
  92.0 4.4 %collective-permute-start.25 = (f32[256,512]{1,0:T(8,128)S(1)}, f32[256,512]{1,0:T(8,128)S(1)}, u32[]{:S(2)}, u32[]{:S(2)}) collective-permute-start(f32[256,512]{1,0:T(8,128)S(1)} %partial_product.7), channel_id=1, source_target_pairs={{0,8},{24,16},{1,9},{25,17},{2,10},{26,18},{3,11},{27,19},{4,12},{... | collective-permute-start | bytes 1572872 | tf_op jit(solution)/shard_map/ppermute | solution.py:444
  97.4 1.9 %partial_product.6 = (f32[256,512]{1,0:T(8,128)S(1)}, f32[256,512]{1,0:T(8,128)S(1)}, f32[256,512]{1,0:T(8,128)S(1)}) custom-call(s32[3]{0:T(128)S(1)} %pad_add_fusion.refs_0_, s32[4,4]{1,0:T(4,128)S(1)} %copy-done.8, s32[2,8]{1,0:T(2,128)S(1)} %copy-done.7, f32[1024,2048]{1,0:T(8,128)S(1)} %bitcast.4, f32[4,4,256,128]{3,2,1,0:T(8,128)S(1)} %pack.3.refs_4_, ...), custom_call_target="tpu_custom_call" | custom-call | tf_op jit(solution)/shard_map/partial_product/pallas_call | solution.py:36
  99.3 3.0 %collective-permute-done.27.refs_3_ = f32[256,512]{1,0:T(8,128)S(1)} collective-permute-done((f32[256,512]{1,0:T(8,128)S(1)}, f32[256,512]{1,0:T(8,128)S(1)}, u32[]{:S(2)}, u32[]{:S(2)}) %collective-permute-start.27) | collective-permute-done | bytes 524320 | tf_op jit(solution)/shard_map/ppermute | solution.py:448
  102.3 9.4 %collective-permute-done.25.refs_1_.refs_8_ = f32[256,512]{1,0:T(8,128)S(1)} collective-permute-done((f32[256,512]{1,0:T(8,128)S(1)}, f32[256,512]{1,0:T(8,128)S(1)}, u32[]{:S(2)}, u32[]{:S(2)}) %collective-permute-start.25) | collective-permute-done | bytes 524320 | tf_op jit(solution)/shard_map/ppermute | solution.py:444
  111.8 2.7 %finish.2 = (f32[2,256,512]{2,1,0:T(8,128)}, f32[2,4,64,512]{3,2,1,0:T(8,128)S(1)}, f32[2,4,64,512]{3,2,1,0:T(8,128)S(1)}, f32[512,512]{1,0:T(8,128)S(1)}, f32[512,512]{1,0:T(8,128)S(1)}) custom-call(s32[3]{0:T(128)S(1)} %pad_add_fusion.refs_0_, s32[2,8]{1,0:T(2,128)S(1)} %copy-done.7, f32[256,512]{1,0:T(8,128)S(1)} %add_up.10.refs_2_, ...), custom_call_target="tpu_custom_call" | custom-call | tf_op jit(solution)/shard_map/finish/pallas_call | solution.py:36
  114.4 3.1 %collective-permute-start.23 = (f32[256,512]{1,0:T(8,128)S(1)}, f32[256,512]{1,0:T(8,128)S(1)}, u32[]{:S(2)}, u32[]{:S(2)}) collective-permute-start(f32[256,512]{1,0:T(8,128)S(1)} %get-tuple-element.71), channel_id=1, source_target_pairs={{0,16},{16,24},{24,8},{8,0},{1,17},{17,25},{25,9},{9,1},{2,18},{18... | collective-permute-start | bytes 1572872 | tf_op jit(solution)/shard_map/ppermute | solution.py:445
  121.9 2.3 %rest.1 = (f32[512,512]{1,0:T(8,128)S(1)}, f32[256,512]{1,0:T(8,128)S(1)}) custom-call(f32[1,512,512]{2,1,0:T(8,128)S(1)} %copy-done.4, f32[512,512]{1,0:T(8,128)S(1)} %get-tuple-element.74.refs_1_, f32[512,512]{1,0:T(8,128)S(1)} %get-tuple-element.75.refs_2_, f32[2,256,512]{2,1,0:T(8,128)S(1)} %copy-done.5), custom_call_target="tpu_custom_call" | custom-call | tf_op jit(solution)/shard_map/rest/pallas_call | solution.py:36
  124.2 5.7 %collective-permute-done.23.refs_1_ = f32[256,512]{1,0:T(8,128)S(1)} collective-permute-done((f32[256,512]{1,0:T(8,128)S(1)}, f32[256,512]{1,0:T(8,128)S(1)}, u32[]{:S(2)}, u32[]{:S(2)}) %collective-permute-start.23) | collective-permute-done | bytes 524320 | tf_op jit(solution)/shard_map/ppermute | solution.py:445
  130.0 3.4 %collective-permute-done.30.refs_3_ = f32[2,64,512]{2,1,0:T(8,128)S(1)} collective-permute-done((f32[2,64,512]{2,1,0:T(8,128)S(1)}, f32[2,64,512]{2,1,0:T(8,128)S(1)}, u32[]{:S(2)}, u32[]{:S(2)}) %collective-permute-start.30) | collective-permute-done | bytes 262176 | tf_op jit(solution)/shard_map/ppermute | solution.py:22
  134.0 8.8 %collective-permute-done.26.refs_3_ = f32[256,512]{1,0:T(8,128)S(1)} collective-permute-done((f32[256,512]{1,0:T(8,128)S(1)}, f32[256,512]{1,0:T(8,128)S(1)}, u32[]{:S(2)}, u32[]{:S(2)}) %collective-permute-start.26) | collective-permute-done | bytes 524320 | tf_op jit(solution)/shard_map/ppermute | solution.py:448
  142.8 2.1 %finish.3 = (f32[2,256,512]{2,1,0:T(8,128)}, f32[1,4,64,512]{3,2,1,0:T(8,128)S(1)}, f32[1,4,64,512]{3,2,1,0:T(8,128)S(1)}) custom-call(s32[3]{0:T(128)S(1)} %pad_add_fusion.refs_0_, s32[2,8]{1,0:T(2,128)S(1)} %copy-done.7, f32[256,512]{1,0:T(8,128)S(1)} %add_up.8.refs_2_, ...), custom_call_target="tpu_custom_call", output_to_operand_aliasing={{0}: (7, {})} | custom-call | tf_op jit(solution)/shard_map/finish/pallas_call | solution.py:36
  147.6 2.3 %collective-permute-start.37 = (f32[1,64,512]{2,1,0:T(8,128)S(1)}, f32[1,64,512]{2,1,0:T(8,128)S(1)}, u32[]{:S(2)}, u32[]{:S(2)}) collective-permute-start(f32[1,64,512]{2,1,0:T(8,128)S(1)} %get-tuple-element.93), channel_id=1, source_target_pairs={{0,4},{1,5},{2,6},{3,7},{4,0},{5,1},{6,2},{7,3},{8,12},{9,13},{10,... | collective-permute-start | bytes 393224 | tf_op jit(solution)/shard_map/ppermute | solution.py:22
  151.8 2.2 %collective-permute-done.36.refs_1_ = f32[1,64,512]{2,1,0:T(8,128)S(1)} collective-permute-done((f32[1,64,512]{2,1,0:T(8,128)S(1)}, f32[1,64,512]{2,1,0:T(8,128)S(1)}, u32[]{:S(2)}, u32[]{:S(2)}) %collective-permute-start.36) | collective-permute-done | bytes 131104 | tf_op jit(solution)/shard_map/ppermute | solution.py:22
  157.5 2.3 %collective-permute-done.33.refs_1_ = f32[64,512]{1,0:T(8,128)S(1)} collective-permute-done((f32[64,512]{1,0:T(8,128)S(1)}, f32[64,512]{1,0:T(8,128)S(1)}, u32[]{:S(2)}, u32[]{:S(2)}) %collective-permute-start.33) | collective-permute-done | bytes 131104 | tf_op jit(solution)/shard_map/ppermute | solution.py:22
  159.9 2.7 %collective-permute-done.39.refs_1_ = f32[1,64,512]{2,1,0:T(8,128)S(1)} collective-permute-done((f32[1,64,512]{2,1,0:T(8,128)S(1)}, f32[1,64,512]{2,1,0:T(8,128)S(1)}, u32[]{:S(2)}, u32[]{:S(2)}) %collective-permute-start.39) | collective-permute-done | bytes 131104 | tf_op jit(solution)/shard_map/ppermute | solution.py:22
  163.0 2.3 %collective-permute-done.34.refs_4_ = f32[64,512]{1,0:T(8,128)S(1)} collective-permute-done((f32[64,512]{1,0:T(8,128)S(1)}, f32[64,512]{1,0:T(8,128)S(1)}, u32[]{:S(2)}, u32[]{:S(2)}) %collective-permute-start.34) | collective-permute-done | bytes 131104 | tf_op jit(solution)/shard_map/ppermute | solution.py:22
  165.3 5.4 %collective-permute-done.40.refs_6_ = f32[1,64,512]{2,1,0:T(8,128)S(1)} collective-permute-done((f32[1,64,512]{2,1,0:T(8,128)S(1)}, f32[1,64,512]{2,1,0:T(8,128)S(1)}, u32[]{:S(2)}, u32[]{:S(2)}) %collective-permute-start.40) | collective-permute-done | bytes 131104 | tf_op jit(solution)/shard_map/ppermute | solution.py:22
  (102 shorter events, 50.4 us)
Async XLA Ops:
  2.6 6.9 %collective-permute-start = (f32[256,128]{1,0:T(8,128)S(1)}, f32[256,128]{1,0:T(8,128)S(1)}, u32[]{:S(2)}, u32[]{:S(2)}) collective-permute-start(f32[256,128]{1,0:T(8,128)S(1)} %get-tuple-element.51), channel_id=1, source_target_pairs={{0,2},{1,3},{2,0},{3,1},{4,6},{5,7},{6,4},{7,5},{8,10},{9,11},{10,... | collective-permute-start | bytes 393224 | tf_op jit(solution)/shard_map/ppermute | solution.py:22
  5.6 7.8 %collective-permute-start.1 = (f32[256,128]{1,0:T(8,128)S(1)}, f32[256,128]{1,0:T(8,128)S(1)}, u32[]{:S(2)}, u32[]{:S(2)}) collective-permute-start(f32[256,128]{1,0:T(8,128)S(1)} %get-tuple-element.52), channel_id=1, source_target_pairs={{0,4},{1,5},{2,6},{3,7},{4,0},{5,1},{6,2},{7,3},{8,12},{9,13},{10,... | collective-permute-start | bytes 393224 | tf_op jit(solution)/shard_map/ppermute | solution.py:22
  7.1 6.3 %collective-permute-start.2 = (f32[256,128]{1,0:T(8,128)S(1)}, f32[256,128]{1,0:T(8,128)S(1)}, u32[]{:S(2)}, u32[]{:S(2)}) collective-permute-start(f32[256,128]{1,0:T(8,128)S(1)} %get-tuple-element.53), channel_id=1, source_target_pairs={{0,6},{1,7},{2,4},{3,5},{4,2},{5,3},{6,0},{7,1},{8,14},{9,15},{10,... | collective-permute-start | bytes 393224 | tf_op jit(solution)/shard_map/ppermute | solution.py:22
  14.0 8.4 %collective-permute-start.6 = (f32[256,128]{1,0:T(8,128)S(1)}, f32[256,128]{1,0:T(8,128)S(1)}, u32[]{:S(2)}, u32[]{:S(2)}) collective-permute-start(f32[256,128]{1,0:T(8,128)S(1)} %get-tuple-element.59), channel_id=1, source_target_pairs={{0,8},{8,0},{16,24},{24,16},{1,9},{9,1},{17,25},{25,17},{2,10},{10... | collective-permute-start | bytes 393224 | tf_op jit(solution)/shard_map/ppermute | solution.py:22
  15.6 11.6 %collective-permute-start.7 = (f32[256,128]{1,0:T(8,128)S(1)}, f32[256,128]{1,0:T(8,128)S(1)}, u32[]{:S(2)}, u32[]{:S(2)}) collective-permute-start(f32[256,128]{1,0:T(8,128)S(1)} %get-tuple-element.60), channel_id=1, source_target_pairs={{0,16},{8,24},{16,0},{24,8},{1,17},{9,25},{17,1},{25,9},{2,18},{10... | collective-permute-start | bytes 393224 | tf_op jit(solution)/shard_map/ppermute | solution.py:22
  18.2 9.0 %collective-permute-start.8 = (f32[256,128]{1,0:T(8,128)S(1)}, f32[256,128]{1,0:T(8,128)S(1)}, u32[]{:S(2)}, u32[]{:S(2)}) collective-permute-start(f32[256,128]{1,0:T(8,128)S(1)} %get-tuple-element.61), channel_id=1, source_target_pairs={{0,24},{8,16},{16,8},{24,0},{1,25},{9,17},{17,9},{25,1},{2,26},{10... | collective-permute-start | bytes 393224 | tf_op jit(solution)/shard_map/ppermute | solution.py:22
  20.3 6.9 %collective-permute-start.3 = (f32[256,128]{1,0:T(8,128)S(1)}, f32[256,128]{1,0:T(8,128)S(1)}, u32[]{:S(2)}, u32[]{:S(2)}) collective-permute-start(f32[256,128]{1,0:T(8,128)S(1)} %get-tuple-element.56), channel_id=1, source_target_pairs={{0,2},{1,3},{2,0},{3,1},{4,6},{5,7},{6,4},{7,5},{8,10},{9,11},{10,... | collective-permute-start | bytes 393224 | tf_op jit(solution)/shard_map/ppermute | solution.py:22
  28.8 19.7 %collective-permute-start.14 = (f32[4,256,128]{2,1,0:T(8,128)S(1)}, f32[4,256,128]{2,1,0:T(8,128)S(1)}, u32[]{:S(2)}, u32[]{:S(2)}) collective-permute-start(f32[4,256,128]{2,1,0:T(8,128)S(1)} %arrange.2.refs_0_), channel_id=1, source_target_pairs={{0,6},{1,7},{2,4},{3,5},{4,2},{5,3},{6,0},{7,1},{8,14},{9,15},{10,... | collective-permute-start | bytes 1572872 | tf_op jit(solution)/shard_map/ppermute | solution.py:22
  30.3 21.2 %collective-permute-start.13 = (f32[4,256,128]{2,1,0:T(8,128)S(1)}, f32[4,256,128]{2,1,0:T(8,128)S(1)}, u32[]{:S(2)}, u32[]{:S(2)}) collective-permute-start(f32[4,256,128]{2,1,0:T(8,128)S(1)} %arrange.2.refs_0_), channel_id=1, source_target_pairs={{0,4},{1,5},{2,6},{3,7},{4,0},{5,1},{6,2},{7,3},{8,12},{9,13},{10,... | collective-permute-start | bytes 1572872 | tf_op jit(solution)/shard_map/ppermute | solution.py:22
  31.8 20.4 %collective-permute-start.12 = (f32[4,256,128]{2,1,0:T(8,128)S(1)}, f32[4,256,128]{2,1,0:T(8,128)S(1)}, u32[]{:S(2)}, u32[]{:S(2)}) collective-permute-start(f32[4,256,128]{2,1,0:T(8,128)S(1)} %arrange.2.refs_0_), channel_id=1, source_target_pairs={{0,2},{1,3},{2,0},{3,1},{4,6},{5,7},{6,4},{7,5},{8,10},{9,11},{10,... | collective-permute-start | bytes 1572872 | tf_op jit(solution)/shard_map/ppermute | solution.py:22
  34.0 14.5 %collective-permute-start.10 = (f32[256,128]{1,0:T(8,128)S(1)}, f32[256,128]{1,0:T(8,128)S(1)}, u32[]{:S(2)}, u32[]{:S(2)}) collective-permute-start(f32[256,128]{1,0:T(8,128)S(1)} %get-tuple-element.64), channel_id=1, source_target_pairs={{0,16},{8,24},{16,0},{24,8},{1,17},{9,25},{17,1},{25,9},{2,18},{10... | collective-permute-start | bytes 393224 | tf_op jit(solution)/shard_map/ppermute | solution.py:22
  38.3 10.2 %collective-permute-start.11 = (f32[256,128]{1,0:T(8,128)S(1)}, f32[256,128]{1,0:T(8,128)S(1)}, u32[]{:S(2)}, u32[]{:S(2)}) collective-permute-start(f32[256,128]{1,0:T(8,128)S(1)} %get-tuple-element.65), channel_id=1, source_target_pairs={{0,24},{8,16},{16,8},{24,0},{1,25},{9,17},{17,9},{25,1},{2,26},{10... | collective-permute-start | bytes 393224 | tf_op jit(solution)/shard_map/ppermute | solution.py:22
  53.0 15.7 %collective-permute-start.17 = (f32[4,256,128]{2,1,0:T(8,128)S(1)}, f32[4,256,128]{2,1,0:T(8,128)S(1)}, u32[]{:S(2)}, u32[]{:S(2)}) collective-permute-start(f32[4,256,128]{2,1,0:T(8,128)S(1)} %arrange.3.refs_0_), channel_id=1, source_target_pairs={{0,6},{1,7},{2,4},{3,5},{4,2},{5,3},{6,0},{7,1},{8,14},{9,15},{10,... | collective-permute-start | bytes 1572872 | tf_op jit(solution)/shard_map/ppermute | solution.py:22
  53.7 25.3 %collective-permute-start.16 = (f32[4,256,128]{2,1,0:T(8,128)S(1)}, f32[4,256,128]{2,1,0:T(8,128)S(1)}, u32[]{:S(2)}, u32[]{:S(2)}) collective-permute-start(f32[4,256,128]{2,1,0:T(8,128)S(1)} %arrange.3.refs_0_), channel_id=1, source_target_pairs={{0,4},{1,5},{2,6},{3,7},{4,0},{5,1},{6,2},{7,3},{8,12},{9,13},{10,... | collective-permute-start | bytes 1572872 | tf_op jit(solution)/shard_map/ppermute | solution.py:22
  54.8 24.1 %collective-permute-start.15 = (f32[4,256,128]{2,1,0:T(8,128)S(1)}, f32[4,256,128]{2,1,0:T(8,128)S(1)}, u32[]{:S(2)}, u32[]{:S(2)}) collective-permute-start(f32[4,256,128]{2,1,0:T(8,128)S(1)} %arrange.3.refs_0_), channel_id=1, source_target_pairs={{0,2},{1,3},{2,0},{3,1},{4,6},{5,7},{6,4},{7,5},{8,10},{9,11},{10,... | collective-permute-start | bytes 1572872 | tf_op jit(solution)/shard_map/ppermute | solution.py:22
  58.5 20.5 %collective-permute-start.19 = (f32[256,512]{1,0:T(8,128)S(1)}, f32[256,512]{1,0:T(8,128)S(1)}, u32[]{:S(2)}, u32[]{:S(2)}) collective-permute-start(f32[256,512]{1,0:T(8,128)S(1)} %get-tuple-element.67), channel_id=1, source_target_pairs={{0,16},{16,24},{24,8},{8,0},{1,17},{17,25},{25,9},{9,1},{2,18},{18... | collective-permute-start | bytes 1572872 | tf_op jit(solution)/shard_map/ppermute | solution.py:445
  63.1 22.7 %collective-permute-start.21 = (f32[256,512]{1,0:T(8,128)S(1)}, f32[256,512]{1,0:T(8,128)S(1)}, u32[]{:S(2)}, u32[]{:S(2)}) collective-permute-start(f32[256,512]{1,0:T(8,128)S(1)} %get-tuple-element.68), channel_id=1, source_target_pairs={{0,8},{24,16},{1,9},{25,17},{2,10},{26,18},{3,11},{27,19},{4,12},{... | collective-permute-start | bytes 1572872 | tf_op jit(solution)/shard_map/ppermute | solution.py:444
  68.8 17.1 %collective-permute-start.20 = (f32[256,512]{1,0:T(8,128)S(1)}, f32[256,512]{1,0:T(8,128)S(1)}, u32[]{:S(2)}, u32[]{:S(2)}) collective-permute-start(f32[256,512]{1,0:T(8,128)S(1)} %get-tuple-element.68), channel_id=1, source_target_pairs={{8,16},{16,8},{9,17},{17,9},{10,18},{18,10},{11,19},{19,11},{12,20... | collective-permute-start | bytes 1572872 | tf_op jit(solution)/shard_map/ppermute | solution.py:446
  86.2 16.2 %collective-permute-start.27 = (f32[256,512]{1,0:T(8,128)S(1)}, f32[256,512]{1,0:T(8,128)S(1)}, u32[]{:S(2)}, u32[]{:S(2)}) collective-permute-start(f32[256,512]{1,0:T(8,128)S(1)} %add_up.11), channel_id=1, source_target_pairs={{8,24},{16,0},{0,8},{24,16},{9,25},{17,1},{1,9},{25,17},{10,26},{1... | collective-permute-start | bytes 1572872 | tf_op jit(solution)/shard_map/ppermute | solution.py:448
  92.0 19.8 %collective-permute-start.25 = (f32[256,512]{1,0:T(8,128)S(1)}, f32[256,512]{1,0:T(8,128)S(1)}, u32[]{:S(2)}, u32[]{:S(2)}) collective-permute-start(f32[256,512]{1,0:T(8,128)S(1)} %partial_product.7), channel_id=1, source_target_pairs={{0,8},{24,16},{1,9},{25,17},{2,10},{26,18},{3,11},{27,19},{4,12},{... | collective-permute-start | bytes 1572872 | tf_op jit(solution)/shard_map/ppermute | solution.py:444
  96.4 15.4 %collective-permute-start.24 = (f32[256,512]{1,0:T(8,128)S(1)}, f32[256,512]{1,0:T(8,128)S(1)}, u32[]{:S(2)}, u32[]{:S(2)}) collective-permute-start(f32[256,512]{1,0:T(8,128)S(1)} %partial_product.7), channel_id=1, source_target_pairs={{8,16},{16,8},{9,17},{17,9},{10,18},{18,10},{11,19},{19,11},{12,20... | collective-permute-start | bytes 1572872 | tf_op jit(solution)/shard_map/ppermute | solution.py:446
  114.4 15.4 %collective-permute-start.23 = (f32[256,512]{1,0:T(8,128)S(1)}, f32[256,512]{1,0:T(8,128)S(1)}, u32[]{:S(2)}, u32[]{:S(2)}) collective-permute-start(f32[256,512]{1,0:T(8,128)S(1)} %get-tuple-element.71), channel_id=1, source_target_pairs={{0,16},{16,24},{24,8},{8,0},{1,17},{17,25},{25,9},{9,1},{2,18},{18... | collective-permute-start | bytes 1572872 | tf_op jit(solution)/shard_map/ppermute | solution.py:445
  117.6 25.3 %collective-permute-start.26 = (f32[256,512]{1,0:T(8,128)S(1)}, f32[256,512]{1,0:T(8,128)S(1)}, u32[]{:S(2)}, u32[]{:S(2)}) collective-permute-start(f32[256,512]{1,0:T(8,128)S(1)} %add_up.9), channel_id=1, source_target_pairs={{8,24},{16,0},{0,8},{24,16},{9,25},{17,1},{1,9},{25,17},{10,26},{1... | collective-permute-start | bytes 1572872 | tf_op jit(solution)/shard_map/ppermute | solution.py:448
  118.3 11.6 %collective-permute-start.29 = (f32[2,64,512]{2,1,0:T(8,128)S(1)}, f32[2,64,512]{2,1,0:T(8,128)S(1)}, u32[]{:S(2)}, u32[]{:S(2)}) collective-permute-start(f32[2,64,512]{2,1,0:T(8,128)S(1)} %get-tuple-element.82), channel_id=1, source_target_pairs={{0,2},{1,3},{2,0},{3,1},{4,6},{5,7},{6,4},{7,5},{8,10},{9,11},{10,... | collective-permute-start | bytes 786440 | tf_op jit(solution)/shard_map/ppermute | solution.py:22
  119.7 13.7 %collective-permute-start.30 = (f32[2,64,512]{2,1,0:T(8,128)S(1)}, f32[2,64,512]{2,1,0:T(8,128)S(1)}, u32[]{:S(2)}, u32[]{:S(2)}) collective-permute-start(f32[2,64,512]{2,1,0:T(8,128)S(1)} %get-tuple-element.83), channel_id=1, source_target_pairs={{0,4},{1,5},{2,6},{3,7},{4,0},{5,1},{6,2},{7,3},{8,12},{9,13},{10,... | collective-permute-start | bytes 786440 | tf_op jit(solution)/shard_map/ppermute | solution.py:22
  121.3 12.1 %collective-permute-start.31 = (f32[2,64,512]{2,1,0:T(8,128)S(1)}, f32[2,64,512]{2,1,0:T(8,128)S(1)}, u32[]{:S(2)}, u32[]{:S(2)}) collective-permute-start(f32[2,64,512]{2,1,0:T(8,128)S(1)} %get-tuple-element.84), channel_id=1, source_target_pairs={{0,6},{1,7},{2,4},{3,5},{4,2},{5,3},{6,0},{7,1},{8,14},{9,15},{10,... | collective-permute-start | bytes 786440 | tf_op jit(solution)/shard_map/ppermute | solution.py:22
  145.0 6.1 %collective-permute-start.32 = (f32[64,512]{1,0:T(8,128)S(1)}, f32[64,512]{1,0:T(8,128)S(1)}, u32[]{:S(2)}, u32[]{:S(2)}) collective-permute-start(f32[64,512]{1,0:T(8,128)S(1)} %get-tuple-element.88), channel_id=1, source_target_pairs={{0,8},{8,0},{16,24},{24,16},{1,9},{9,1},{17,25},{25,17},{2,10},{10... | collective-permute-start | bytes 393224 | tf_op jit(solution)/shard_map/ppermute | solution.py:22
  147.5 6.4 %collective-permute-start.36 = (f32[1,64,512]{2,1,0:T(8,128)S(1)}, f32[1,64,512]{2,1,0:T(8,128)S(1)}, u32[]{:S(2)}, u32[]{:S(2)}) collective-permute-start(f32[1,64,512]{2,1,0:T(8,128)S(1)} %get-tuple-element.92), channel_id=1, source_target_pairs={{0,2},{1,3},{2,0},{3,1},{4,6},{5,7},{6,4},{7,5},{8,10},{9,11},{10,... | collective-permute-start | bytes 393224 | tf_op jit(solution)/shard_map/ppermute | solution.py:22
  147.6 8.1 %collective-permute-start.37 = (f32[1,64,512]{2,1,0:T(8,128)S(1)}, f32[1,64,512]{2,1,0:T(8,128)S(1)}, u32[]{:S(2)}, u32[]{:S(2)}) collective-permute-start(f32[1,64,512]{2,1,0:T(8,128)S(1)} %get-tuple-element.93), channel_id=1, source_target_pairs={{0,4},{1,5},{2,6},{3,7},{4,0},{5,1},{6,2},{7,3},{8,12},{9,13},{10,... | collective-permute-start | bytes 393224 | tf_op jit(solution)/shard_map/ppermute | solution.py:22
  149.9 6.8 %collective-permute-start.38 = (f32[1,64,512]{2,1,0:T(8,128)S(1)}, f32[1,64,512]{2,1,0:T(8,128)S(1)}, u32[]{:S(2)}, u32[]{:S(2)}) collective-permute-start(f32[1,64,512]{2,1,0:T(8,128)S(1)} %get-tuple-element.94), channel_id=1, source_target_pairs={{0,6},{1,7},{2,4},{3,5},{4,2},{5,3},{6,0},{7,1},{8,14},{9,15},{10,... | collective-permute-start | bytes 393224 | tf_op jit(solution)/shard_map/ppermute | solution.py:22
  151.1 8.7 %collective-permute-start.33 = (f32[64,512]{1,0:T(8,128)S(1)}, f32[64,512]{1,0:T(8,128)S(1)}, u32[]{:S(2)}, u32[]{:S(2)}) collective-permute-start(f32[64,512]{1,0:T(8,128)S(1)} %add_up.12.refs_0_), channel_id=1, source_target_pairs={{0,16},{8,24},{16,0},{24,8},{1,17},{9,25},{17,1},{25,9},{2,18},{10... | collective-permute-start | bytes 393224 | tf_op jit(solution)/shard_map/ppermute | solution.py:22
  162.6 8.1 %collective-permute-start.40 = (f32[1,64,512]{2,1,0:T(8,128)S(1)}, f32[1,64,512]{2,1,0:T(8,128)S(1)}, u32[]{:S(2)}, u32[]{:S(2)}) collective-permute-start(f32[1,64,512]{2,1,0:T(8,128)S(1)} %add_up.15.refs_5_), channel_id=1, source_target_pairs={{0,16},{8,24},{16,0},{24,8},{1,17},{9,25},{17,1},{25,9},{2,18},{10... | collective-permute-start | bytes 393224 | tf_op jit(solution)/shard_map/ppermute | solution.py:22
  (20 other events, 164.7 us)
